TPU v7x, 32 devices: a whole 2x2x4 slice. The times are simulated.
32 devices in a mesh: gx: 8 (over z, y), gy: 4 (over x, core).
Axes of the slice: x: 2, y: 2, z: 4, core: 2. Of those that a mesh axis runs over, the one named last changes fastest.
Arguments:
- phi: float32 [256, 128, 1024], P('gx', 'gy'), may hold values from -6 to 6
- kappa: float32 [256, 128, 1024], P('gx', 'gy'), may hold values from 0.02 to 0.12
- stiffness: float32 [512, 2048], P('gx', 'gy'), may hold values from 0.5 to 4
- face_cell: int32 [8, 4, 32, 128], P('gx', 'gy'), may hold values from 0 to 131071
- load_dof: int32 [8, 4, 32, 128], P('gx', 'gy'), may hold values from 0 to 32767
- displacement: float32 [512, 2048], P('gx', 'gy'), may hold values from -6 to 6
- v_hist: float32 [40, 512, 2048], P(None, 'gx', 'gy'), may hold values from -100 to 100
- w_hist: float32 [40, 512, 2048], P(None, 'gx', 'gy'), may hold values from -100 to 100
- r_prev: float32 [512, 2048], P('gx', 'gy'), may hold values from -6 to 6
- w_prev: float32 [512, 2048], P('gx', 'gy'), may hold values from -6 to 6
Outputs:
- phi_out: float32 [256, 128, 1024], P('gx', 'gy')
- x_next: float32 [512, 2048], P('gx', 'gy')
All inputs are finite; a program needn't handle non-finite values.
Results may differ from a plain program's by a relative error of at most 0.0003.
Values sent between devices are 32-bit elements; how exact they have to be, the bound alone decides.
No kernel may reach another device: no remote copies, remote signals or barrier semaphores. Data moves between devices by JAX's collectives and lax.ppermute only.
A program may use at most 128 MiB of HBM per device.

v0:
```python
import functools

import jax
import jax.numpy as jnp
from jax import lax
from jax.experimental import pallas as pl
from jax.experimental.pallas import tpu as pltpu
from jax.sharding import PartitionSpec as P

NSUB = 4
SWEEPS = 3
HIST = 40
VMEM_BYTES = 56 * 1024 * 1024
F32 = jnp.float32
BF16 = jnp.bfloat16


def params():
    return pltpu.CompilerParams(vmem_limit_bytes=VMEM_BYTES)


def vmem_specs(count):
    return [pl.BlockSpec(memory_space=pltpu.VMEM)] * count


def any_specs(count):
    return [pl.BlockSpec(memory_space=pl.ANY)] * count


def pieces(value, count):
    parts = []
    for _ in range(count):
        part = value.astype(BF16)
        parts.append(part)
        value = value - part.astype(F32)
    return parts


def as_row(block):
    return jnp.concatenate([block[i : i + 1] for i in range(block.shape[0])], axis=1)


def one_hot(keys, rows):
    ids = lax.broadcasted_iota(jnp.int32, (rows, keys.shape[1]), 0)
    return jnp.where(ids == keys, 1.0, 0.0).astype(BF16)


def select_sum(table, lane, group, rows, parts):
    total = table[:rows]
    for part in range(1, parts):
        total = total + table[part * rows : (part + 1) * rows]
    ids = lax.broadcasted_iota(jnp.int32, total.shape, 0)
    return jnp.sum(jnp.where(ids == lane, total, 0.0), axis=0, keepdims=True)


def pick(table_t, index_ref, out_rows, rows, lane_bits, chunk_bits, parts, step=8):
    lanes = 1 << lane_bits
    for base in range(0, index_ref.shape[0], step):
        index = as_row(index_ref[base : base + step, :])
        lane = index & (lanes - 1)
        keys = ((index >> lane_bits) & ((1 << chunk_bits) - 1)) * rows + (
            index >> (lane_bits + chunk_bits)
        )
        hot = one_hot(keys, rows << chunk_bits)
        found = lax.dot_general(
            table_t, hot, (((1,), (0,)), ((), ())), preferred_element_type=F32
        )
        out_rows(base, select_sum(found, lane, step, lanes, parts))


def spread_values(values, lane, lanes, parts):
    ids = lax.broadcasted_iota(jnp.int32, (lanes, lane.shape[1]), 0)
    match = ids == lane
    return jnp.concatenate(
        [jnp.where(match, part.astype(F32), 0.0).astype(BF16) for part in pieces(values, parts)],
        axis=0,
    )


NEAR = ((0, 0), (1, 0), (-1, 0), (0, 1), (0, -1), (1, 1), (1, -1), (-1, 1), (-1, -1))


def tile_of(ref, plane, number):
    at = (number % 8) * 128
    return ref[plane + number // 8, :, at : at + 128]


def starter(sems):
    used = [0]

    def copy(src, dst):
        made = pltpu.make_async_copy(src, dst, sems.at[used[0]])
        used[0] += 1
        made.start()
        return made

    return copy


def gather_disp(n_gy, disp_ref, index_ref, out_ref, own_ref):
    sx, sy = disp_ref.shape
    peers, blk = index_ref.shape
    chunk_bits = (sy // 128).bit_length() - 1
    columns = []
    for q in range(sy // 128):
        columns.append(jnp.transpose(disp_ref[:, q * 128 : (q + 1) * 128]))
    table_t = jnp.concatenate(pieces(jnp.concatenate(columns, axis=1), 3), axis=0)

    def write(base, row):
        for i in range(8):
            own_ref[base + i : base + i + 1, :] = row[:, i * blk : (i + 1) * blk]

    pick(table_t, index_ref, write, sx, 7, chunk_bits, 3)
    own = own_ref[...]
    beside = lax.broadcasted_iota(jnp.int32, own.shape, 0) % n_gy
    out_ref[:, 0, 0:blk] = own
    out_ref[:, 0, blk : 2 * blk] = jnp.where(
        beside == n_gy - 1, 0.0, pltpu.roll(own, peers - 1, axis=0)
    )
    out_ref[:, 0, 2 * blk : 3 * blk] = jnp.where(beside == 0, 0.0, pltpu.roll(own, 1, axis=0))


def scatter_disp(cx, cy, cz, disp_ref, cells_ref, up_ref, down_ref, out_ref, acc_ref, side_ref, near_ref, sems):
    planes = out_ref.shape[0]
    peers, blk = cells_ref.shape
    rows = planes * cy
    chunks = cz // 256
    row_bits = cz.bit_length() - 1
    step = 8
    extra = near_ref.shape[1]
    copy = starter(sems)
    copies = [
        copy(ref.at[pl.ds(cx, extra)], near_ref.at[side])
        for side, ref in enumerate((up_ref, down_ref))
    ]

    def accumulate(target, first, keys, height, lane, values):
        added = lax.dot_general(
            one_hot(keys, height), spread_values(values, lane, 256, 2),
            (((1,), (1,)), ((), ())), preferred_element_type=F32,
        )
        if first:
            target[...] = added
        else:
            target[...] += added

    for base in range(0, peers, step):
        index = as_row(cells_ref[base : base + step, :])
        values = 0.5 * as_row(disp_ref[base : base + step, 0, 0:blk])
        keys = ((index >> 8) & (chunks - 1)) * rows + (index >> row_bits)
        accumulate(acc_ref, base == 0, keys, rows * chunks, index & 255, values)
    for made in copies:
        made.wait()
    for side in range(2):
        for base in range(0, peers, step):
            index = as_row(tile_of(near_ref.at[side], 0, base // step).astype(jnp.int32))
            values = 0.5 * as_row(
                disp_ref[base : base + step, 0, (side + 1) * blk : (side + 2) * blk]
            )
            row = index >> row_bits
            plane = row // cy
            column = row - plane * cy
            inside = column < 4 if side == 0 else column >= cy - 4
            place = column if side == 0 else column - (cy - 8)
            keys = ((index >> 8) & (chunks - 1)) * (planes * 8) + plane * 8 + place
            keys = jnp.where(inside, keys, -1)
            accumulate(
                side_ref, base == 0 and side == 0, keys, planes * 8 * chunks, index & 255, values
            )
    for q in range(chunks):
        part = acc_ref[q * rows : (q + 1) * rows, :]
        out_ref[:, 0:cy, q * 256 : (q + 1) * 256] = (part[:, :256] + part[:, 256:]).reshape(
            planes, cy, 256
        )
        part = side_ref[q * planes * 8 : (q + 1) * planes * 8, :]
        out_ref[:, cy : cy + 8, q * 256 : (q + 1) * 256] = (
            part[:, :256] + part[:, 256:]
        ).reshape(planes, 8, 256)


def gather_press(n_gx, n_gy, wet_ref, index_ref, gram_ref, out_ref, own_ref):
    planes, cy, cz = wet_ref.shape
    peers, blk = index_ref.shape
    rows = planes * cy
    chunks = cz // 256
    columns = []
    for q in range(chunks):
        part = wet_ref[:, :, q * 256 : (q + 1) * 256].reshape(rows, 256)
        columns.append(jnp.transpose(part))
    table_t = jnp.concatenate(pieces(jnp.concatenate(columns, axis=1), 2), axis=0)

    def write(base, row):
        for i in range(8):
            own_ref[base + i : base + i + 1, :] = row[:, i * blk : (i + 1) * blk]

    pick(table_t, index_ref, write, rows, 8, chunks.bit_length() - 1, 2)
    own = own_ref[...]
    number = lax.broadcasted_iota(jnp.int32, own.shape, 0)
    at_x, at_y = number // n_gy, number % n_gy
    for k, (dx, dy) in enumerate(NEAR):
        ok = (at_x + dx >= 0) & (at_x + dx < n_gx) & (at_y + dy >= 0) & (at_y + dy < n_gy)
        moved = pltpu.roll(own, (-(dx * n_gy + dy)) % peers, axis=0) if k else own
        out_ref[:, 0, k * blk : (k + 1) * blk] = jnp.where(ok, moved, 0.0)
    out_ref[:, 0, len(NEAR) * blk : (len(NEAR) + 1) * blk] = gram_ref[...]


def gram_rows(v_ref, out_ref, v, same, cross, wide, sems):
    hist, sx, sy = v_ref.shape
    tiles = sx // 8
    copy = starter(sems)
    copies = [
        copy(v_ref.at[:, pl.ds(8 * t, 8), :], v.at[t]) for t in range(tiles)
    ]
    for t in range(tiles):
        copies[t].wait()
        high, low = pieces(v[t].reshape(hist * 8, sy), 2)

        def dot(x, y):
            return lax.dot_general(x, y, (((1,), (1,)), ((), ())), preferred_element_type=F32)

        if t == 0:
            same[...] = dot(high, high) + dot(low, low)
            cross[...] = dot(high, low)
        else:
            same[...] += dot(high, high) + dot(low, low)
            cross[...] += dot(high, low)
    size = hist * 8
    row = lax.broadcasted_iota(jnp.int32, (size, size), 0)
    column = lax.broadcasted_iota(jnp.int32, (size, size), 1)
    match = (row & 7) == (column & 7)
    group = (
        lax.broadcasted_iota(jnp.int32, (size, 128), 0) // 8
        == lax.broadcasted_iota(jnp.int32, (size, 128), 1)
    ).astype(F32)

    def reduced(ref):
        part = jnp.sum(jnp.where(match, ref[...], 0.0).reshape(hist, 8, size), axis=1)
        return jnp.dot(part, group, precision=lax.Precision.HIGHEST, preferred_element_type=F32)

    wide[...] = jnp.zeros_like(wide)
    wide[0:hist, :] = reduced(cross)
    turned = jnp.transpose(wide[0:128, :])
    wide[0:128, :] = wide[0:128, :] + turned
    wide[0:hist, :] = wide[0:hist, :] + reduced(same)
    peers = out_ref.shape[0]
    if peers >= hist:
        out_ref[...] = wide[0:peers, :]
    else:
        out_ref[...] = wide[0:peers, :] + pltpu.roll(wide[peers : 2 * peers, :], 64, axis=1)


def shell(recv_ref, index_ref, disp_ref, stiff_ref, prev_ref, v_ref, up_ref, down_ref, low_ref,
          low_up_ref, low_down_ref, high_ref, resp_ref, late_ref, v, packs, acc, rows_acc, cols_acc,
          corner_acc, ext, dots, sems, v_sem):
    sx, sy = disp_ref.shape
    peers, blk = index_ref.shape
    extra = packs.shape[1]
    index_planes = extra - 2
    load_tiles = peers // 8
    chunks = sy // 128
    hist = v_ref.shape[0]
    v_copy = pltpu.make_async_copy(v_ref, v, v_sem.at[0])
    v_copy.start()
    copy = starter(sems)
    top = up_ref.shape[0] - extra
    corner = low_up_ref.shape[0] - extra
    low_planes = low_ref.shape[0] - (-(-extra // 4))
    copies = [
        copy(high_ref.at[pl.ds(0, extra)], packs.at[0]),
        copy(up_ref.at[pl.ds(top, extra)], packs.at[2]),
        copy(down_ref.at[pl.ds(top, extra)], packs.at[3]),
        copy(high_ref.at[pl.ds(extra, extra)], packs.at[4]),
        copy(high_ref.at[pl.ds(2 * extra, extra)], packs.at[5]),
        copy(low_up_ref.at[pl.ds(corner, extra)], packs.at[6]),
        copy(low_down_ref.at[pl.ds(corner, extra)], packs.at[7]),
    ]
    for e in range(extra):
        copies.append(
            copy(low_ref.at[low_planes + e // 4, pl.ds(8 * (e % 4), 8)], packs.at[1, e])
        )

    def accumulate(target, first, keys, height, lane, lanes, values):
        added = lax.dot_general(
            one_hot(keys, height), spread_values(values, lane, lanes, 2),
            (((1,), (1,)), ((), ())), preferred_element_type=F32,
        )
        if first:
            target[...] = added
        else:
            target[...] += added

    def values_of(k, base):
        return as_row(recv_ref[base : base + 8, 0, k * blk : (k + 1) * blk])

    for base in range(0, peers, 8):
        index = as_row(index_ref[base : base + 8, :])
        keys = ((index >> 7) & (chunks - 1)) * sx + index // sy
        accumulate(acc, base == 0, keys, sx * chunks, index & 127, 128, values_of(0, base))
    for made in copies:
        made.wait()
    for k, (dx, dy) in enumerate(NEAR):
        if k == 0:
            continue
        for base in range(0, peers, 8):
            number = load_tiles + base // 8
            index = as_row(tile_of(packs.at[k - 1], 0, number).astype(jnp.int32))
            row = index // sy
            lane = index & (sy - 1)
            if dx == 1:
                row8 = jnp.where(row < 4, row, -1)
            elif dx == -1:
                row8 = jnp.where(row >= sx - 4, row - (sx - 8), -1)
            if dy == 1:
                lane8 = jnp.where(lane < 4, lane, -1)
            elif dy == -1:
                lane8 = jnp.where(lane >= sy - 4, lane - (sy - 8), -1)
            values = values_of(k, base)
            if dy == 0:
                keys = jnp.where(row8 < 0, -1, (lane >> 7) * 8 + row8)
                accumulate(
                    rows_acc, k == 1 and base == 0, keys, 8 * chunks, lane & 127, 128, values
                )
            elif dx == 0:
                accumulate(cols_acc, k == 3 and base == 0, row, sx, lane8, 8, values)
            else:
                accumulate(corner_acc, k == 5 and base == 0, row8, 8, lane8, 8, values)

    ids = lax.broadcasted_iota(jnp.int32, (8, 128), 0)
    lanes = lax.broadcasted_iota(jnp.int32, (8, 128), 1)
    placed = (jnp.where(ids < 4, ids, ids + 120) == lanes).astype(F32)

    def widened(ref):
        both = ref[:, 0:8] + ref[:, 8:16]
        return jnp.dot(both, placed, precision=lax.Precision.HIGHEST, preferred_element_type=F32)

    force, disp, stiff = ext.at[0], ext.at[1], ext.at[2]
    for q in range(chunks):
        at = slice(q * 128, (q + 1) * 128)
        part = acc[q * sx : (q + 1) * sx, :]
        force[0:sx, at] = part[:, 0:128] + part[:, 128:256]
        part = rows_acc[q * 8 : (q + 1) * 8, :]
        force[sx : sx + 8, at] = part[:, 0:128] + part[:, 128:256]
    side = slice(sy, sy + 128)
    force[0:sx, side] = widened(cols_acc)
    force[sx : sx + 8, side] = widened(corner_acc)
    sub = lax.broadcasted_iota(jnp.int32, (8, sy), 0) < 4
    sub1 = lax.broadcasted_iota(jnp.int32, (8, 128), 0) < 4
    lane = lax.broadcasted_iota(jnp.int32, (sx, 128), 1)
    lane1 = lax.broadcasted_iota(jnp.int32, (8, 128), 1)
    for kind, (target, own) in enumerate(((disp, disp_ref), (stiff, stiff_ref))):

        def row_tile(pack, start, size):
            at = kind * sy + start
            return packs[pack, index_planes, :, at : at + size]

        def col_tile(pack):
            return jnp.concatenate(
                [tile_of(packs.at[pack], index_planes + 1, m) for m in range(sx // 8)], axis=0
            )

        target[0:sx, 0:sy] = own[...]
        target[sx : sx + 8, 0:sy] = jnp.where(sub, row_tile(0, 0, sy), row_tile(1, 0, sy))
        ahead, behind = col_tile(2), col_tile(3)
        if kind == 0:
            behind = pltpu.roll(behind, 64, axis=1)
        else:
            ahead = pltpu.roll(ahead, 64, axis=1)
        target[0:sx, side] = jnp.where(lane < 32, ahead, jnp.where(lane >= 96, behind, 0.0))

        def corner_tile(pack_ahead, pack_behind):
            return jnp.where(
                lane1 < 32, row_tile(pack_ahead, 0, 128),
                jnp.where(lane1 >= 96, row_tile(pack_behind, sy - 128, 128), 0.0),
            )

        target[sx : sx + 8, side] = jnp.where(sub1, corner_tile(4, 5), corner_tile(6, 7))

    load = force[...]
    k = stiff[...]
    diag = 1.0 + 4.0 * k
    scale = 0.8 / diag
    resp = disp[...]
    high, wide = sx + 8, sy + 128
    for sweep in range(SWEEPS):
        beside = (pltpu.roll(resp, 1, axis=0) + pltpu.roll(resp, high - 1, axis=0)) + (
            pltpu.roll(resp, 1, axis=1) + pltpu.roll(resp, wide - 1, axis=1)
        )
        resp = resp + scale * (load - (diag * resp - k * beside))
    own = resp[0:sx, 0:sy]
    resp_ref[...] = own
    resid = own - disp_ref[...]
    newest = resid - prev_ref[...]
    dots[...] = jnp.zeros_like(dots)

    def folded(value):
        total = value[0:8]
        for t in range(1, sx // 8):
            total = total + value[8 * t : 8 * t + 8]
        out = total[:, 0:128]
        for q in range(1, chunks):
            out = out + total[:, q * 128 : (q + 1) * 128]
        return jnp.sum(out, axis=0, keepdims=True)

    dots[0:1, :] = folded(newest * newest)
    dots[64:65, :] = folded(resid * newest)
    v_copy.wait()
    for number in range(1, hist):
        column = v[number]
        dots[number : number + 1, :] = folded(column * newest)
        dots[64 + number : 65 + number, :] = folded(column * resid)
    late = lax.dot_general(
        jnp.ones((8, 128), F32), dots[...], (((1,), (1,)), ((), ())),
        precision=lax.Precision.HIGHEST, preferred_element_type=F32,
    )
    gram_at = len(NEAR) * blk
    gram = jnp.sum(recv_ref[:, 0, gram_at : gram_at + 128], axis=0, keepdims=True)
    late_ref[:, 0, 0:128] = jnp.broadcast_to(late[0:1], (peers, 128))
    late_ref[:, 0, 128:256] = jnp.broadcast_to(gram, (peers, 128))


def solve(recv_ref, resp_ref, prev_ref, w_ref, out_ref, w, sems):
    peers = recv_ref.shape[0]
    hist = w_ref.shape[0]
    sx, sy = resp_ref.shape
    w_copy = pltpu.make_async_copy(w_ref, w, sems.at[0])
    w_copy.start()
    late = jnp.sum(recv_ref[:, 0, 0:128], axis=0, keepdims=True)
    rows = recv_ref[:, 0, 128:256]
    if peers >= hist:
        gram = rows[0:hist]
    else:
        gram = jnp.concatenate(
            [rows, pltpu.roll(rows, 64, axis=1)[0 : hist - peers]], axis=0
        )
    row = lax.broadcasted_iota(jnp.int32, (hist, 128), 0)
    lane = lax.broadcasted_iota(jnp.int32, (hist, 128), 1)
    turned = jnp.transpose(jnp.broadcast_to(late, (128, 128)))
    gram = jnp.where(row == 0, jnp.broadcast_to(late, (hist, 128)), gram)
    gram = jnp.where(lane == 0, turned[0:hist], gram)
    gram = jnp.where(lane < hist, gram, 0.0)
    unit = row == lane
    trace = jnp.sum(jnp.where(unit, gram, 0.0), keepdims=True)
    a = gram + jnp.where(unit, 0.001 * trace / hist, 0.0)
    a = jnp.where(lane == 64, -turned[64 : 64 + hist], a)
    for j in range(hist):
        column = jnp.broadcast_to(a[:, j : j + 1], (hist, 128))
        scaled = a[j : j + 1, :] / column[j : j + 1, :]
        a = jnp.where(row == j, scaled, a - column * scaled)
    coef = jnp.broadcast_to(a[:, 64:65], (hist, 128))
    coef = jnp.concatenate([coef] * (sy // 128), axis=1)
    resp = resp_ref[...]
    total = resp + coef[0:1] * (resp - prev_ref[...])
    w_copy.wait()
    for number in range(1, hist):
        total = total + coef[number : number + 1] * w[number]
    out_ref[...] = total


def pack(phi_ref, kappa_ref, disp_ref, stiff_ref, cells_ref, loads_ref, up_ref, down_ref, low_ref,
         low_up_ref, low_down_ref, own_ref, phi_lo, kap_lo, phi_hi, kap_hi, up, down, own,
         in_sems, out_sems):
    cx, cy, cz = phi_ref.shape
    sx, sy = disp_ref.shape
    peers = cells_ref.shape[0]
    extra = own.shape[0]
    copy_in, copy_out = starter(in_sems), starter(out_sems)
    depth = 8
    groups = []
    for x in range(0, cx, depth):
        at = pl.ds(x, depth)
        groups.append([
            copy_in(phi_ref.at[at, pl.ds(0, 8)], phi_lo.at[at]),
            copy_in(kappa_ref.at[at, pl.ds(0, 8)], kap_lo.at[at]),
            copy_in(phi_ref.at[at, pl.ds(cy - 8, 8)], phi_hi.at[at]),
            copy_in(kappa_ref.at[at, pl.ds(cy - 8, 8)], kap_hi.at[at]),
        ])
    outs = [
        copy_out(phi_ref.at[pl.ds(cx - 4, 4)], low_ref.at[pl.ds(0, 4)]),
        copy_out(kappa_ref.at[pl.ds(cx - 3, 3)], low_ref.at[pl.ds(4, 3)]),
    ]
    for n in range(2 * peers // 8):
        source = cells_ref if n < peers // 8 else loads_ref
        base = 8 * (n % (peers // 8))
        own[n // 8, :, (n % 8) * 128 : (n % 8 + 1) * 128] = source[base : base + 8, :].astype(F32)
    if 2 * peers % 64:
        own[2 * peers // 64, :, 2 * peers % 64 * 16 :] = jnp.zeros(
            (8, 1024 - 2 * peers % 64 * 16), F32
        )
    sub = lax.broadcasted_iota(jnp.int32, (8, sy), 0) < 4
    for kind, ref in enumerate((disp_ref, stiff_ref)):
        own[extra - 2, :, kind * sy : (kind + 1) * sy] = jnp.where(
            sub, ref[0:8, :], ref[sx - 8 : sx, :]
        )
    lane = lax.broadcasted_iota(jnp.int32, (sx, 128), 1)
    first, final = slice(0, 128), slice(sy - 128, sy)
    columns = jnp.where(
        lane < 32, disp_ref[:, first],
        jnp.where(
            lane < 64, pltpu.roll(disp_ref[:, final], 64, axis=1),
            jnp.where(lane < 96, pltpu.roll(stiff_ref[:, first], 64, axis=1), stiff_ref[:, final]),
        ),
    )
    for m in range(sx // 8):
        own[extra - 1, :, m * 128 : (m + 1) * 128] = columns[8 * m : 8 * m + 8, :]
    outs += [
        copy_out(own, own_ref),
        copy_out(own, up_ref.at[pl.ds(cx, extra)]),
        copy_out(own, down_ref.at[pl.ds(cx, extra)]),
        copy_out(own, low_up_ref.at[pl.ds(4, extra)]),
        copy_out(own, low_down_ref.at[pl.ds(4, extra)]),
    ]
    for e in range(extra):
        outs.append(copy_out(own.at[e], low_ref.at[7 + e // 4, pl.ds(8 * (e % 4), 8)]))
    upper = lax.broadcasted_iota(jnp.int32, (depth, 8, cz), 1) < 4
    for number, copies in enumerate(groups):
        for made in copies:
            made.wait()
        x = number * depth
        at = slice(x, x + depth)
        up[at] = jnp.where(upper, phi_lo[at], pltpu.roll(kap_lo[at], 4, axis=1))
        down[at] = jnp.where(upper, pltpu.roll(kap_hi[at], 4, axis=1), phi_hi[at])
        at = pl.ds(x, depth)
        outs.append(copy_out(up.at[at], up_ref.at[at]))
        outs.append(copy_out(down.at[at], down_ref.at[at]))
    at = pl.ds(cx - 4, 4)
    outs.append(copy_out(up.at[at], low_up_ref.at[pl.ds(0, 4)]))
    outs.append(copy_out(down.at[at], low_down_ref.at[pl.ds(0, 4)]))
    for made in outs:
        made.wait()


def packed(phi, kappa, displacement, stiffness, cells, loads):
    cx, cy, cz = phi.shape
    peers = cells.shape[0]
    extra = -(-2 * peers // 64) + 2

    def shape(planes, rows=8):
        return jax.ShapeDtypeStruct((planes, rows, cz), F32)

    return pl.pallas_call(
        pack,
        in_specs=any_specs(2) + vmem_specs(4),
        out_specs=any_specs(6),
        out_shape=[
            shape(cx + extra), shape(cx + extra), shape(7 + -(-extra // 4), cy),
            shape(4 + extra), shape(4 + extra), shape(extra),
        ],
        scratch_shapes=[pltpu.VMEM((cx, 8, cz), F32)] * 6
        + [
            pltpu.VMEM((extra, 8, cz), F32),
            pltpu.SemaphoreType.DMA((cx // 2,)),
            pltpu.SemaphoreType.DMA((32,)),
        ],
        compiler_params=params(),
        name="pack",
    )(phi, kappa, displacement, stiffness, cells, loads)


def substep(src, kap, coef, dst, plane, advect, cy, cz):
    wide = cy + 8
    chunks = cz // 128
    lane = lax.broadcasted_iota(jnp.int32, (wide, 128), 1)
    first, last = lane == 0, lane == 127

    def take(ref, at, q):
        return ref[at, :, q * 128 : (q + 1) * 128]

    zero = jnp.zeros((wide, 128), F32)
    now = take(src, plane, 0)
    back, back_before = pltpu.roll(now, 1, axis=1), zero
    ahead = pltpu.roll(now, 127, axis=1)
    for q in range(chunks):
        if q + 1 < chunks:
            later = take(src, plane, q + 1)
            ahead_later = pltpu.roll(later, 127, axis=1)
        else:
            later, ahead_later = None, zero
        before = take(src, plane - 1, q)
        above = jnp.concatenate([now[8:], pltpu.roll(now[:8], 7, axis=0)], axis=0)
        below = jnp.concatenate([pltpu.roll(now[wide - 8 :], 1, axis=0), now[: wide - 8]], axis=0)
        total = (before + take(src, plane + 1, q)) + (above + below)
        total = total + (jnp.where(first, back_before, back) + jnp.where(last, ahead_later, ahead))
        dst[plane, :, q * 128 : (q + 1) * 128] = (
            take(coef, plane, q) * now + advect * before + take(kap, plane, q) * total
        )
        if later is not None:
            back_before, back = back, pltpu.roll(later, 1, axis=1)
            now, ahead = later, ahead_later


def fluid(x0, x1, cx, cy, cz, with_wet, *refs):
    planes = x1 - x0 + 8
    wide = cy + 8
    chunks = cz // 128
    names = ["phi", "kappa", "up", "down", "forced"]
    names += ["low", "low_up", "low_down"] if x0 - 4 < 0 else []
    names += ["high"] if x1 + 4 > cx else []
    names += ["wet"] if with_wet else []
    names += ["out"] + ([] if with_wet else ["send"])
    names += ["nat", "knat", "a", "b", "kap", "coef", "upb", "downb", "sems", "out_sems"]
    r = dict(zip(names, refs))
    nat, knat, a, b, kap, coef = (r[n] for n in ("nat", "knat", "a", "b", "kap", "coef"))
    upb, downb = r["upb"], r["downb"]
    is_last = lax.axis_index("gx") == lax.axis_size("gx") - 1
    copy, copy_out = starter(r["sems"]), starter(r["out_sems"])

    def chunked(src, s0, count, dst, d0, rows, start=copy):
        return [
            start(
                src.at[pl.ds(s0, count), pl.ds(0, rows), pl.ds(q * 128, 128)],
                dst.at[pl.ds(d0, count), q, pl.ds(0, rows)],
            )
            for q in range(chunks)
        ]

    def unchunked(src, s0, count, dst, d0, rows):
        return [
            copy_out(
                src.at[pl.ds(s0, count), q, pl.ds(0, rows)],
                dst.at[pl.ds(d0, count), pl.ds(0, rows), pl.ds(q * 128, 128)],
            )
            for q in range(chunks)
        ]

    outs = []
    groups = []
    if x0 - 4 < 0:
        groups.append((0, 4, True, chunked(r["low"], 0, 4, nat, 0, cy)
                       + chunked(r["low"], 4, 3, knat, 1, cy) + [
            copy(r["low_up"].at[pl.ds(0, 4)], upb.at[pl.ds(0, 4)]),
            copy(r["low_down"].at[pl.ds(0, 4)], downb.at[pl.ds(0, 4)]),
        ]))
    own0, own1 = max(0, x0 - 4), min(cx, x1 + 4)
    start = own0
    while start < own1:
        count = min(8, own1 - start)
        i = start - (x0 - 4)
        groups.append((i, i + count, True, chunked(r["phi"], start, count, nat, i, cy)
                       + chunked(r["kappa"], start, count, knat, i, cy) + [
            copy(r["up"].at[pl.ds(start, count)], upb.at[pl.ds(i, count)]),
            copy(r["down"].at[pl.ds(start, count)], downb.at[pl.ds(i, count)]),
        ]))
        start += count
    if x1 + 4 > cx:
        i = cx - (x0 - 4)
        groups.append((i, i + 4, False, chunked(r["high"], 0, 4, nat, i, wide)
                       + chunked(r["high"], 4, 3, knat, i, wide)))
    if with_wet:
        outs.append(copy_out(r["wet"], r["out"].at[pl.ds(0, x0)]))

    upper = lax.broadcasted_iota(jnp.int32, (8, cz), 0) < 4
    tiles = wide // 8

    def prepare(i, halo, wet):
        if halo:
            up, down = upb[i], downb[i]
            edge = jnp.where(upper, up, down)
            kedge = pltpu.roll(jnp.where(upper, down, up), 4, axis=0)
            for q in range(chunks):
                nat[i, q, cy:wide, :] = edge[:, q * 128 : (q + 1) * 128]
                knat[i, q, cy:wide, :] = kedge[:, q * 128 : (q + 1) * 128]
        for q in range(chunks):
            at = slice(q * 128, (q + 1) * 128)
            if wet:
                nat[i, q] = nat[i, q] + r["forced"][i + (x0 - 4), :, at]
            for j in range(tiles):
                rows = slice(8 * j, 8 * j + 8)
                a[i, rows, at] = nat[i, q, pl.ds(j, 8, stride=tiles), :]
                k = knat[i, q, pl.ds(j, 8, stride=tiles), :]
                kap[i, rows, at] = k
                coef[i, rows, at] = 0.75 - 6.0 * k

    def step(src, dst, i):
        outside = jnp.logical_and(is_last, i + (x0 - 4) >= cx)
        substep(src, kap, coef, dst, i, jnp.where(outside, 0.0, 0.25), cy, cz)

    def loop(lo, hi, *work):
        def body(i, carry):
            for one in work:
                one(i)
            return carry

        if hi > lo:
            lax.fori_loop(lo, hi, body, 0)

    wet_lo, wet_hi = 4 - x0, 4 - x0 + r["forced"].shape[0]
    for i0, i1, halo, copies in groups:
        for made in copies:
            made.wait()
        edges = sorted({i0, i1, min(max(2, i0), i1), min(max(wet_lo, i0), i1), min(max(wet_hi, i0), i1)})
        for lo, hi in zip(edges[:-1], edges[1:]):
            wet = wet_lo <= lo < wet_hi
            work = [lambda i: prepare(i, halo, wet)]
            if lo >= 2:
                work.append(lambda i: step(a, b, i - 1))
            loop(lo, hi, *work)
        if not with_wet and i0 == 4:
            outs += unchunked(nat, 4, 4, r["send"], 0, wide)
            outs += unchunked(knat, 4, 3, r["send"], 4, wide)
    loop(2, planes - 2, lambda i: step(b, a, i))
    loop(3, planes - 3, lambda i: step(a, b, i))

    def finish(i):
        step(b, a, i)
        for q in range(chunks):
            for j in range(tiles):
                rows = slice(8 * j, 8 * j + 8)
                done[i, q, pl.ds(j, 8, stride=tiles), :] = a[i, rows, q * 128 : (q + 1) * 128]

    done = nat if with_wet else knat
    if not with_wet:
        for made in outs:
            made.wait()
        outs = []
    start = 4
    while start < planes - 4:
        count = min(8, planes - 4 - start)
        loop(start, start + count, finish)
        x = x0 + start - 4
        outs += unchunked(done, start, count, r["out"], x if with_wet else x - x0, cy)
        start += count
    for made in outs:
        made.wait()


def fluid_call(x0, x1, phi, kappa, up, down, forced, low=None, high=None, wet=None):
    cx, cy, cz = phi.shape
    planes = x1 - x0 + 8
    args = [phi, kappa, up, down, forced]
    specs = any_specs(4) + vmem_specs(1)
    if low is not None:
        args += list(low)
        specs += any_specs(3)
    if high is not None:
        args.append(high)
        specs += any_specs(1)
    if wet is not None:
        args.append(wet)
        specs += any_specs(1)
        out_shape = jax.ShapeDtypeStruct((cx, cy, cz), F32)
        out_specs = pl.BlockSpec(memory_space=pl.ANY)
    else:
        out_shape = [
            jax.ShapeDtypeStruct((x1 - x0, cy, cz), F32),
            jax.ShapeDtypeStruct((7, cy + 8, cz), F32),
        ]
        out_specs = any_specs(2)
    cells = planes * (cy + 8) * cz
    natural = pltpu.VMEM((planes, cz // 128, cy + 8, 128), F32)
    stored = pltpu.VMEM((planes, cy + 8, cz), F32)
    return pl.pallas_call(
        functools.partial(fluid, x0, x1, cx, cy, cz, wet is not None),
        in_specs=specs,
        out_specs=out_specs,
        out_shape=out_shape,
        scratch_shapes=[natural, natural, stored, stored, stored, stored]
        + [pltpu.VMEM((planes, 8, cz), F32)] * 2
        + [pltpu.SemaphoreType.DMA((128,)), pltpu.SemaphoreType.DMA((64,))],
        compiler_params=params(),
        cost_estimate=pl.CostEstimate(
            flops=48 * cells, bytes_accessed=12 * cells, transcendentals=0
        ),
        name="fluid_wet" if wet is None else "fluid_rest",
    )(*args)


def shifted_pairs(n_gx, n_gy, dx, dy):
    pairs = []
    for gx in range(n_gx):
        for gy in range(n_gy):
            tx, ty = gx + dx, gy + dy
            if 0 <= tx < n_gx and 0 <= ty < n_gy:
                pairs.append((gx * n_gy + gy, tx * n_gy + ty))
    return pairs


def local(phi, kappa, stiffness, face_cell, load_dof, displacement, v_hist, w_hist, r_prev, w_prev):
    n_gx, n_gy = lax.axis_size("gx"), lax.axis_size("gy")
    peers, blk = face_cell.shape[2:]
    cx, cy, cz = phi.shape
    sx, sy = displacement.shape
    hist = v_hist.shape[0]
    wet_planes = cx // 8
    fcell = face_cell.reshape(peers, blk)
    ldof = load_dof.reshape(peers, blk)
    axes = ("gx", "gy")

    def shift(value, dx, dy):
        return lax.ppermute(value, axes, shifted_pairs(n_gx, n_gy, dx, dy))

    def exchange(value):
        return lax.all_to_all(value, axes, split_axis=0, concat_axis=0, tiled=True)

    def call(body, out_shape, scratch, name, specs, *args):
        several = isinstance(out_shape, list)
        return pl.pallas_call(
            body,
            in_specs=specs,
            out_specs=vmem_specs(len(out_shape)) if several else vmem_specs(1)[0],
            out_shape=out_shape,
            scratch_shapes=scratch,
            compiler_params=params(),
            name=name,
        )(*args)

    def f32(*shape):
        return jax.ShapeDtypeStruct(shape, F32)

    up_send, down_send, low_send, low_up_send, low_down_send, own = packed(
        phi, kappa, displacement, stiffness, fcell, ldof
    )
    extra = own.shape[0]
    low = shift(low_send, 1, 0)
    up = shift(up_send, 0, -1)
    down = shift(down_send, 0, 1)
    low_up = shift(low_up_send, 1, -1)
    low_down = shift(low_down_send, 1, 1)
    near = shift(jnp.concatenate([own, up[cx:], down[cx:]], axis=0), -1, 0)

    sent = call(
        functools.partial(gather_disp, n_gy), f32(peers, 1, 3 * blk),
        [pltpu.VMEM((peers, blk), F32)], "gather_disp", vmem_specs(2), displacement, ldof,
    )
    disp = exchange(sent)
    chunks = cz // 256
    forced = call(
        functools.partial(scatter_disp, cx, cy, cz), f32(wet_planes, cy + 8, cz),
        [
            pltpu.VMEM((wet_planes * cy * chunks, 512), F32),
            pltpu.VMEM((wet_planes * 8 * chunks, 512), F32),
            pltpu.VMEM((2, (extra - 2) // 2 + (extra - 2) % 2, 8, cz), F32),
            pltpu.SemaphoreType.DMA((2,)),
        ],
        "scatter_disp", vmem_specs(2) + any_specs(2), disp, fcell, up, down,
    )
    wet, send = fluid_call(
        0, wet_planes, phi, kappa, up, down, forced, low=(low, low_up, low_down)
    )
    size = 8 * hist
    gram = call(
        gram_rows, f32(peers, 128),
        [
            pltpu.VMEM((sx // 8, hist, 8, sy), F32), pltpu.VMEM((size, size), F32),
            pltpu.VMEM((size, size), F32),
            pltpu.VMEM((max(128, peers, 2 * peers if peers < hist else 0), 128), F32),
            pltpu.SemaphoreType.DMA((sx // 8,)),
        ],
        "gram_rows", any_specs(1), v_hist,
    )
    press = call(
        functools.partial(gather_press, n_gx, n_gy), f32(peers, 1, (len(NEAR) + 1) * blk),
        [pltpu.VMEM((peers, blk), F32)], "gather_press", vmem_specs(3), wet, fcell, gram,
    )
    loads = exchange(press)
    high = shift(send, -1, 0)
    resp, late = call(
        shell, [f32(sx, sy), f32(peers, 1, 256)],
        [
            pltpu.VMEM((hist, sx, sy), F32),
            pltpu.VMEM((8, extra, 8, cz), F32),
            pltpu.VMEM((sx * (sy // 128), 256), F32),
            pltpu.VMEM((8 * (sy // 128), 256), F32),
            pltpu.VMEM((sx, 16), F32),
            pltpu.VMEM((8, 16), F32),
            pltpu.VMEM((3, sx + 8, sy + 128), F32),
            pltpu.VMEM((128, 128), F32),
            pltpu.SemaphoreType.DMA((7 + extra,)),
            pltpu.SemaphoreType.DMA((1,)),
        ],
        "shell", vmem_specs(5) + any_specs(7),
        loads, ldof, displacement, stiffness, r_prev, v_hist, up, down, low, low_up, low_down, near,
    )
    x_next = call(
        solve, f32(sx, sy),
        [pltpu.VMEM((hist, sx, sy), F32), pltpu.SemaphoreType.DMA((1,))],
        "solve", vmem_specs(3) + any_specs(1), exchange(late), resp, w_prev, w_hist,
    )
    field = fluid_call(wet_planes, cx, phi, kappa, up, down, forced, high=high, wet=wet)
    return (field, x_next)


def solution(mesh):
    in_specs = (
        P("gx", "gy", None),
        P("gx", "gy", None),
        P("gx", "gy"),
        P("gx", "gy", None, None),
        P("gx", "gy", None, None),
        P("gx", "gy"),
        P(None, "gx", "gy"),
        P(None, "gx", "gy"),
        P("gx", "gy"),
        P("gx", "gy"),
    )
    out_specs = (P("gx", "gy", None), P("gx", "gy"))
    return jax.shard_map(local, mesh=mesh, in_specs=in_specs, out_specs=out_specs, check_vma=False)
```

profile of v0, /device:TPU:0, one launch (start us, length us, event | category | flops | bytes accessed | tf_op | source)
XLA Modules:
  0.0 197.6 jit_solution(9331371026127440701)
XLA Ops:
  0.6 30.3 %pack.1 = (f32[35,8,1024]{2,1,0:T(8,128)}, f32[35,8,1024]{2,1,0:T(8,128)}, f32[8,32,1024]{2,1,0:T(8,128)}, f32[7,8,1024]{2,1,0:T(8,128)}, f32[7,8,1024]{2,1,0:T(8,128)}, /*index=5*/f32[3,8,1024]{2,1,0:T(8,128)}) custom-call(f32[32,32,1024]{2,1,0:T(8,128)} %refs_0_.3, f32[32,32,1024]{2,1,0:T(8,128)} %refs_1_.3, f32[64,512]{1,0:T(8,128)} %disp_ref.5, ...), custom_call_target="tpu_custom_call" | custom-call | tf_op jit(solution)/shard_map/pack/pallas_call | solution.py:540
  31.0 1.3 collective-permute-start
  32.3 3.1 %collective-permute-start.1 = (f32[35,8,1024]{2,1,0:T(8,128)}, f32[35,8,1024]{2,1,0:T(8,128)S(1)}, u32[]{:S(2)}, u32[]{:S(2)}) collective-permute-start(f32[35,8,1024]{2,1,0:T(8,128)} %get-tuple-element.13), channel_id=1, source_target_pairs={{0,1},{1,2},{2,3},{4,5},{5,6},{6,7},{8,9},{9,10},{10,11},{12,13},{... | collective-permute-start | bytes 3440648 | tf_op jit(solution)/shard_map/ppermute | solution.py:789
  35.4 4.9 %collective-permute-start.2 = (f32[8,32,1024]{2,1,0:T(8,128)}, f32[8,32,1024]{2,1,0:T(8,128)S(1)}, u32[]{:S(2)}, u32[]{:S(2)}) collective-permute-start(f32[8,32,1024]{2,1,0:T(8,128)} %get-tuple-element.14), channel_id=1, source_target_pairs={{0,4},{1,5},{2,6},{3,7},{4,8},{5,9},{6,10},{7,11},{8,12},{9,13},{1... | collective-permute-start | bytes 3145736 | tf_op jit(solution)/shard_map/ppermute | solution.py:789
  41.0 5.8 %collective-permute-start.4 = (f32[7,8,1024]{2,1,0:T(8,128)}, f32[7,8,1024]{2,1,0:T(8,128)S(1)}, u32[]{:S(2)}, u32[]{:S(2)}) collective-permute-start(f32[7,8,1024]{2,1,0:T(8,128)} %get-tuple-element.16), channel_id=1, source_target_pairs={{0,5},{1,6},{2,7},{4,9},{5,10},{6,11},{8,13},{9,14},{10,15},{12,17... | collective-permute-start | bytes 688136 | tf_op jit(solution)/shard_map/ppermute | solution.py:789
  46.9 3.0 %gather_disp.1 = f32[32,1,384]{2,1,0:T(1,128)} custom-call(f32[64,512]{1,0:T(8,128)} %disp_ref.5, s32[32,128]{1,0:T(8,128)} %bitcast.6), custom_call_target="tpu_custom_call" | custom-call | tf_op jit(solution)/shard_map/gather_disp/pallas_call | solution.py:796
  49.9 22.0 %all_to_all.15.disp_ref = f32[32,1,384]{2,1,0:T(1,128)} all-to-all(f32[32,1,384]{2,1,0:T(1,128)} %gather_disp.1), channel_id=1, replica_groups=mesh['gx'=8,'gy'=4] {'gx','gy'}, dimensions={0} | all-to-all | bytes 98304 | tf_op jit(solution)/shard_map/all_to_all | solution.py:792
  71.9 1.0 copy-done
  72.9 1.0 copy-done.1
  73.9 10.9 %scatter_disp.1.refs_4_ = f32[4,40,1024]{2,1,0:T(8,128)} custom-call(f32[32,1,384]{2,1,0:T(1,128)} %all_to_all.15.disp_ref, s32[32,128]{1,0:T(8,128)} %bitcast.3, f32[35,8,1024]{2,1,0:T(8,128)} %copy-done, f32[35,8,1024]{2,1,0:T(8,128)} %copy-done.1), custom_call_target="tpu_custom_call" | custom-call | tf_op jit(solution)/shard_map/scatter_disp/pallas_call | solution.py:796
  85.6 1.0 copy-done.2
  86.6 10.4 %fluid_wet.1 = (f32[4,32,1024]{2,1,0:T(8,128)}, f32[7,40,1024]{2,1,0:T(8,128)}) custom-call(f32[32,32,1024]{2,1,0:T(8,128)} %refs_0_.3, f32[32,32,1024]{2,1,0:T(8,128)} %refs_1_.3, f32[35,8,1024]{2,1,0:T(8,128)} %copy-done, f32[35,8,1024]{2,1,0:T(8,128)} %copy-done.1, f32[4,40,1024]{2,1,0:T(8,128)} %scatter_disp.1.refs_4_, f32[8,32,1024]{2,1,0:T(8,128)} %copy-done.2, ...), custom_call_target="tpu_custom_call" | custom-call | flops 23592960 | bytes 5898240 | tf_op jit(solution)/shard_map/fluid_wet/pallas_call | solution.py:751
  97.0 1.5 collective-permute-start.5
  98.4 7.9 %gram_rows.1.gram_ref = f32[32,128]{1,0:T(8,128)} custom-call(f32[40,64,512]{2,1,0:T(8,128)} %v_ref.3), custom_call_target="tpu_custom_call" | custom-call | tf_op jit(solution)/shard_map/gram_rows/pallas_call | solution.py:796
  106.4 4.4 %gather_press.1 = f32[32,1,1280]{2,1,0:T(1,128)} custom-call(f32[4,32,1024]{2,1,0:T(8,128)} %get-tuple-element.18.refs_6_.wet_ref, s32[32,128]{1,0:T(8,128)} %bitcast.4, f32[32,128]{1,0:T(8,128)} %gram_rows.1.gram_ref), custom_call_target="tpu_custom_call" | custom-call | tf_op jit(solution)/shard_map/gather_press/pallas_call | solution.py:796
  110.8 12.0 %all-to-all-start.1 = ((f32[32,1,1280]{2,1,0:T(1,128)}), f32[32,1,1280]{2,1,0:T(1,128)S(1)}, u32[]{:S(2)}, u32[]{:S(2)}) async-start(f32[32,1,1280]{2,1,0:T(1,128)} %gather_press.1), calls=%async_computation.1 | async-start | bytes 327680 | tf_op jit(solution)/shard_map/all_to_all | solution.py:792
  122.9 1.5 collective-permute-start.6
  124.4 11.1 %collective-permute-done.6.high_ref = f32[9,8,1024]{2,1,0:T(8,128)S(1)} collective-permute-done((f32[9,8,1024]{2,1,0:T(8,128)S(1)}, f32[9,8,1024]{2,1,0:T(8,128)S(1)}, u32[]{:S(2)}, u32[]{:S(2)}) %collective-permute-start.6) | collective-permute-done | bytes 294944 | tf_op jit(solution)/shard_map/ppermute | solution.py:789
  135.5 2.3 %all-to-all-done.1.recv_ref = f32[32,1,1280]{2,1,0:T(1,128)S(1)} async-done(((f32[32,1,1280]{2,1,0:T(1,128)}), f32[32,1,1280]{2,1,0:T(1,128)S(1)}, u32[]{:S(2)}, u32[]{:S(2)}) %all-to-all-start.1) | async-done | bytes 163872 | tf_op jit(solution)/shard_map/all_to_all | solution.py:792
  138.5 8.9 %shell.1 = (f32[64,512]{1,0:T(8,128)}, f32[32,1,256]{2,1,0:T(1,128)}) custom-call(f32[32,1,1280]{2,1,0:T(1,128)} %copy-done.6, s32[32,128]{1,0:T(8,128)} %bitcast.7, f32[64,512]{1,0:T(8,128)} %disp_ref.5, f32[64,512]{1,0:T(8,128)} %stiff_ref.3, f32[64,512]{1,0:T(8,128)} %prev_ref.2, f32[40,64,512]{2,1,0:T(8,128)} %v_ref.3, f32[35,8,1024]{2,1,0:T(8,128)} %copy-done, ...), custom_call_target="tpu_custom_call" | custom-call | tf_op jit(solution)/shard_map/shell/pallas_call | solution.py:796
  147.4 16.5 %all_to_all.16.recv_ref = f32[32,1,256]{2,1,0:T(1,128)} all-to-all(f32[32,1,256]{2,1,0:T(1,128)} %get-tuple-element.20), channel_id=1, replica_groups=mesh['gx'=8,'gy'=4] {'gx','gy'}, dimensions={0} | all-to-all | bytes 65536 | tf_op jit(solution)/shard_map/all_to_all | solution.py:792
  163.9 5.6 %solve.1 = f32[64,512]{1,0:T(8,128)} custom-call(f32[32,1,256]{2,1,0:T(1,128)} %all_to_all.16.recv_ref, f32[64,512]{1,0:T(8,128)} %get-tuple-element.21.resp_ref, f32[64,512]{1,0:T(8,128)} %prev_ref.3, f32[40,64,512]{2,1,0:T(8,128)} %w_ref.1), custom_call_target="tpu_custom_call" | custom-call | tf_op jit(solution)/shard_map/solve/pallas_call | solution.py:796
  169.6 1.0 copy-done.3
  170.6 26.8 %fluid_rest.1 = f32[32,32,1024]{2,1,0:T(8,128)} custom-call(f32[32,32,1024]{2,1,0:T(8,128)} %refs_0_.3, f32[32,32,1024]{2,1,0:T(8,128)} %refs_1_.3, f32[35,8,1024]{2,1,0:T(8,128)} %copy-done, f32[35,8,1024]{2,1,0:T(8,128)} %copy-done.1, f32[4,40,1024]{2,1,0:T(8,128)} %scatter_disp.1.refs_4_, f32[7,40,1024]{2,1,0:T(8,128)} %copy-done.3, ...), custom_call_target="tpu_custom_call" | custom-call | flops 70778880 | bytes 17694720 | tf_op jit(solution)/shard_map/fluid_rest/pallas_call | solution.py:751
  (26 shorter events, 2.2 us)
Async XLA Ops:
  31.0 40.9 %collective-permute-start = (f32[35,8,1024]{2,1,0:T(8,128)}, f32[35,8,1024]{2,1,0:T(8,128)S(1)}, u32[]{:S(2)}, u32[]{:S(2)}) collective-permute-start(f32[35,8,1024]{2,1,0:T(8,128)} %get-tuple-element.12), channel_id=1, source_target_pairs={{1,0},{2,1},{3,2},{5,4},{6,5},{7,6},{9,8},{10,9},{11,10},{13,12},{... | collective-permute-start | bytes 3440648 | tf_op jit(solution)/shard_map/ppermute | solution.py:789
  32.3 39.6 %collective-permute-start.1 = (f32[35,8,1024]{2,1,0:T(8,128)}, f32[35,8,1024]{2,1,0:T(8,128)S(1)}, u32[]{:S(2)}, u32[]{:S(2)}) collective-permute-start(f32[35,8,1024]{2,1,0:T(8,128)} %get-tuple-element.13), channel_id=1, source_target_pairs={{0,1},{1,2},{2,3},{4,5},{5,6},{6,7},{8,9},{9,10},{10,11},{12,13},{... | collective-permute-start | bytes 3440648 | tf_op jit(solution)/shard_map/ppermute | solution.py:789
  35.4 49.5 %collective-permute-start.2 = (f32[8,32,1024]{2,1,0:T(8,128)}, f32[8,32,1024]{2,1,0:T(8,128)S(1)}, u32[]{:S(2)}, u32[]{:S(2)}) collective-permute-start(f32[8,32,1024]{2,1,0:T(8,128)} %get-tuple-element.14), channel_id=1, source_target_pairs={{0,4},{1,5},{2,6},{3,7},{4,8},{5,9},{6,10},{7,11},{8,12},{9,13},{1... | collective-permute-start | bytes 3145736 | tf_op jit(solution)/shard_map/ppermute | solution.py:789
  40.3 44.5 %collective-permute-start.3 = (f32[7,8,1024]{2,1,0:T(8,128)}, f32[7,8,1024]{2,1,0:T(8,128)S(1)}, u32[]{:S(2)}, u32[]{:S(2)}) collective-permute-start(f32[7,8,1024]{2,1,0:T(8,128)} %get-tuple-element.15), channel_id=1, source_target_pairs={{1,4},{2,5},{3,6},{5,8},{6,9},{7,10},{9,12},{10,13},{11,14},{13,16... | collective-permute-start | bytes 688136 | tf_op jit(solution)/shard_map/ppermute | solution.py:789
  41.0 43.8 %collective-permute-start.4 = (f32[7,8,1024]{2,1,0:T(8,128)}, f32[7,8,1024]{2,1,0:T(8,128)S(1)}, u32[]{:S(2)}, u32[]{:S(2)}) collective-permute-start(f32[7,8,1024]{2,1,0:T(8,128)} %get-tuple-element.16), channel_id=1, source_target_pairs={{0,5},{1,6},{2,7},{4,9},{5,10},{6,11},{8,13},{9,14},{10,15},{12,17... | collective-permute-start | bytes 688136 | tf_op jit(solution)/shard_map/ppermute | solution.py:789
  71.9 1.0 copy-start
  72.9 1.0 copy-start.1
  84.8 0.7 copy-start.4
  84.8 0.8 copy-start.5
  85.6 1.0 copy-start.2
  97.0 72.6 %collective-permute-start.5 = (f32[7,40,1024]{2,1,0:T(8,128)}, f32[7,40,1024]{2,1,0:T(8,128)S(1)}, u32[]{:S(2)}, u32[]{:S(2)}) collective-permute-start(f32[7,40,1024]{2,1,0:T(8,128)} %get-tuple-element.17), channel_id=1, source_target_pairs={{4,0},{5,1},{6,2},{7,3},{8,4},{9,5},{10,6},{11,7},{12,8},{13,9},{1... | collective-permute-start | bytes 3440648 | tf_op jit(solution)/shard_map/ppermute | solution.py:789
  106.3 16.5 %slice-start = ((f32[35,8,1024]{2,1,0:T(8,128)}), f32[3,8,1024]{2,1,0:T(8,128)S(1)}, s32[]{:S(2)}) async-start(f32[35,8,1024]{2,1,0:T(8,128)} %copy-done), calls=%async_computation.3 | async-start | bytes 196608 | tf_op jit(solution)/shard_map/slice | solution.py:818
  106.4 16.5 %slice-start.1 = ((f32[35,8,1024]{2,1,0:T(8,128)}), f32[3,8,1024]{2,1,0:T(8,128)S(1)}, s32[]{:S(2)}) async-start(f32[35,8,1024]{2,1,0:T(8,128)} %copy-done.1), calls=%async_computation.4 | async-start | bytes 196608 | tf_op jit(solution)/shard_map/slice | solution.py:818
  106.4 16.5 %copy-start.8 = (f32[3,8,1024]{2,1,0:T(8,128)S(1)}, f32[3,8,1024]{2,1,0:T(8,128)}, u32[]{:S(2)}) copy-start(f32[3,8,1024]{2,1,0:T(8,128)} %get-tuple-element.19) | copy-start | bytes 294916
  110.8 27.0 %all-to-all-start.1 = ((f32[32,1,1280]{2,1,0:T(1,128)}), f32[32,1,1280]{2,1,0:T(1,128)S(1)}, u32[]{:S(2)}, u32[]{:S(2)}) async-start(f32[32,1,1280]{2,1,0:T(1,128)} %gather_press.1), calls=%async_computation.1 | async-start | bytes 327680 | tf_op jit(solution)/shard_map/all_to_all | solution.py:792
  122.9 12.7 %collective-permute-start.6 = (f32[9,8,1024]{2,1,0:T(8,128)S(1)}, f32[9,8,1024]{2,1,0:T(8,128)S(1)}, u32[]{:S(2)}, u32[]{:S(2)}) collective-permute-start(f32[9,8,1024]{2,1,0:T(8,128)S(1)} %pad_maximum_fusion), channel_id=1, source_target_pairs={{4,0},{5,1},{6,2},{7,3},{8,4},{9,5},{10,6},{11,7},{12,8},{13,9},{1... | collective-permute-start | bytes 884744 | tf_op jit(solution)/shard_map/ppermute | solution.py:789
  135.5 2.3 %copy-start.7 = (f32[9,8,1024]{2,1,0:T(8,128)}, f32[9,8,1024]{2,1,0:T(8,128)S(1)}, u32[]{:S(2)}) copy-start(f32[9,8,1024]{2,1,0:T(8,128)S(1)} %collective-permute-done.6.high_ref) | copy-start | bytes 884740
  137.8 0.7 copy-start.6
  169.6 1.0 copy-start.3
where the time goes:
time: 198 us
  Pallas kernels  108 us (55%)
  blocking collectives  38.5 us (19%)
  starting transfers between devices  30.9 us (16%)
  waiting for transfers between devices  13.4 us (7%)
  local copies, waits for them, and re-layouts  5.47 us (3%)
    pallas_call x6, Pallas kernels, call(): pl.pallas_call(body, in_specs=specs, out_specs=vmem_specs(len(out_shape))...  40.7 us
    all_to_all x2, blocking collectives, exchange(): return lax.all_to_all(value, axes, split_axis=0, concat_axis=0, tiled=True)  38.5 us
    pallas_call x2, Pallas kernels, fluid_call(): pl.pallas_call(functools.partial(fluid, x0, x1, cx, cy, cz, wet is not No...  37.1 us
    pallas_call x1, Pallas kernels, packed(): pl.pallas_call(pack, in_specs=any_specs(2) + vmem_specs(4), out_specs=any...  30.3 us
    ppermute x7, starting transfers between devices, shift(): return lax.ppermute(value, axes, shifted_pairs(n_gx, n_gy, dx, dy))  18.8 us
    all_to_all x1, starting transfers between devices, exchange(): return lax.all_to_all(value, axes, split_axis=0, concat_axis=0, tiled=True)  12 us
    ppermute x7, waiting for transfers between devices, shift(): return lax.ppermute(value, axes, shifted_pairs(n_gx, n_gy, dx, dy))  11.2 us
    unnamed x18, local copies, waits for them, and re-layouts  5.46 us
  transfers between devices with their start and end apart: 8, of which 2 were waited for; matrix products, arithmetic and copies ran while one was open for 0% of the time, Pallas kernels for 21%

commit v1 on v0

--- a/solution.py
+++ b/solution.py
@@ -23,8 +23,8 @@
     return [pl.BlockSpec(memory_space=pltpu.VMEM)] * count
 
 
-def any_specs(count):
-    return [pl.BlockSpec(memory_space=pl.ANY)] * count
+def hbm_specs(count):
+    return [pl.BlockSpec(memory_space=pltpu.HBM)] * count
 
 
 def pieces(value, count):
@@ -124,7 +124,7 @@
     planes = out_ref.shape[0]
     peers, blk = cells_ref.shape
     rows = planes * cy
-    chunks = cz // 256
+    chunks = cz // 128
     row_bits = cz.bit_length() - 1
     step = 8
     extra = near_ref.shape[1]
@@ -134,10 +134,9 @@
         for side, ref in enumerate((up_ref, down_ref))
     ]
 
-    def accumulate(target, first, keys, height, lane, values):
+    def accumulate(target, first, left, right):
         added = lax.dot_general(
-            one_hot(keys, height), spread_values(values, lane, 256, 2),
-            (((1,), (1,)), ((), ())), preferred_element_type=F32,
+            left, right, (((1,), (1,)), ((), ())), preferred_element_type=F32
         )
         if first:
             target[...] = added
@@ -147,12 +146,15 @@
     for base in range(0, peers, step):
         index = as_row(cells_ref[base : base + step, :])
         values = 0.5 * as_row(disp_ref[base : base + step, 0, 0:blk])
-        keys = ((index >> 8) & (chunks - 1)) * rows + (index >> row_bits)
-        accumulate(acc_ref, base == 0, keys, rows * chunks, index & 255, values)
+        keys = ((index >> 7) & (chunks - 1)) * rows + (index >> row_bits)
+        accumulate(
+            acc_ref, base == 0, one_hot(keys, rows * chunks),
+            spread_values(values, index & 127, 128, 2),
+        )
     for made in copies:
         made.wait()
-    for side in range(2):
-        for base in range(0, peers, step):
+    for base in range(0, peers, step):
+        for side in range(2):
             index = as_row(tile_of(near_ref.at[side], 0, base // step).astype(jnp.int32))
             values = 0.5 * as_row(
                 disp_ref[base : base + step, 0, (side + 1) * blk : (side + 2) * blk]
@@ -162,23 +164,24 @@
             column = row - plane * cy
             inside = column < 4 if side == 0 else column >= cy - 4
             place = column if side == 0 else column - (cy - 8)
-            keys = ((index >> 8) & (chunks - 1)) * (planes * 8) + plane * 8 + place
+            keys = ((index >> 8) & (chunks // 2 - 1)) * (planes * 8) + plane * 8 + place
             keys = jnp.where(inside, keys, -1)
             accumulate(
-                side_ref, base == 0 and side == 0, keys, planes * 8 * chunks, index & 255, values
+                side_ref, base == 0 and side == 0, spread_values(values, index & 255, 256, 2),
+                one_hot(keys, planes * 4 * chunks),
             )
     for q in range(chunks):
         part = acc_ref[q * rows : (q + 1) * rows, :]
-        out_ref[:, 0:cy, q * 256 : (q + 1) * 256] = (part[:, :256] + part[:, 256:]).reshape(
-            planes, cy, 256
-        )
-        part = side_ref[q * planes * 8 : (q + 1) * planes * 8, :]
-        out_ref[:, cy : cy + 8, q * 256 : (q + 1) * 256] = (
-            part[:, :256] + part[:, 256:]
-        ).reshape(planes, 8, 256)
-
-
-def gather_press(n_gx, n_gy, wet_ref, index_ref, gram_ref, out_ref, own_ref):
+        out_ref[:, 0:cy, q * 128 : (q + 1) * 128] = (part[:, :128] + part[:, 128:]).reshape(
+            planes, cy, 128
+        )
+    both = jnp.transpose(side_ref[0:256, :] + side_ref[256:512, :])
+    for q in range(chunks // 2):
+        part = both[q * planes * 8 : (q + 1) * planes * 8, :]
+        out_ref[:, cy : cy + 8, q * 256 : (q + 1) * 256] = part.reshape(planes, 8, 256)
+
+
+def gather_press(n_gx, n_gy, wet_ref, index_ref, gram_ref, after_ref, out_ref, own_ref):
     planes, cy, cz = wet_ref.shape
     peers, blk = index_ref.shape
     rows = planes * cy
@@ -456,8 +459,8 @@
     out_ref[...] = total
 
 
-def pack(phi_ref, kappa_ref, disp_ref, stiff_ref, cells_ref, loads_ref, up_ref, down_ref, low_ref,
-         low_up_ref, low_down_ref, own_ref, phi_lo, kap_lo, phi_hi, kap_hi, up, down, own,
+def pack(phi_ref, kappa_ref, after_ref, disp_ref, stiff_ref, cells_ref, loads_ref, up_ref, down_ref, low_ref,
+         low_up_ref, low_down_ref, own_ref, phi_lo, kap_lo, phi_hi, kap_hi, up, down, own, last,
          in_sems, out_sems):
     cx, cy, cz = phi_ref.shape
     sx, sy = disp_ref.shape
@@ -465,6 +468,10 @@
     extra = own.shape[0]
     copy_in, copy_out = starter(in_sems), starter(out_sems)
     depth = 8
+    lows = [
+        copy_in(phi_ref.at[pl.ds(cx - 4, 4)], last.at[pl.ds(0, 4)]),
+        copy_in(kappa_ref.at[pl.ds(cx - 3, 3)], last.at[pl.ds(4, 3)]),
+    ]
     groups = []
     for x in range(0, cx, depth):
         at = pl.ds(x, depth)
@@ -474,10 +481,7 @@
             copy_in(phi_ref.at[at, pl.ds(cy - 8, 8)], phi_hi.at[at]),
             copy_in(kappa_ref.at[at, pl.ds(cy - 8, 8)], kap_hi.at[at]),
         ])
-    outs = [
-        copy_out(phi_ref.at[pl.ds(cx - 4, 4)], low_ref.at[pl.ds(0, 4)]),
-        copy_out(kappa_ref.at[pl.ds(cx - 3, 3)], low_ref.at[pl.ds(4, 3)]),
-    ]
+    outs = []
     for n in range(2 * peers // 8):
         source = cells_ref if n < peers // 8 else loads_ref
         base = 8 * (n % (peers // 8))
@@ -511,6 +515,9 @@
     ]
     for e in range(extra):
         outs.append(copy_out(own.at[e], low_ref.at[7 + e // 4, pl.ds(8 * (e % 4), 8)]))
+    for made in lows:
+        made.wait()
+    outs.append(copy_out(last, low_ref.at[pl.ds(0, 7)]))
     upper = lax.broadcasted_iota(jnp.int32, (depth, 8, cz), 1) < 4
     for number, copies in enumerate(groups):
         for made in copies:
@@ -529,7 +536,7 @@
         made.wait()
 
 
-def packed(phi, kappa, displacement, stiffness, cells, loads):
+def packed(phi, kappa, after, displacement, stiffness, cells, loads):
     cx, cy, cz = phi.shape
     peers = cells.shape[0]
     extra = -(-2 * peers // 64) + 2
@@ -539,8 +546,8 @@
 
     return pl.pallas_call(
         pack,
-        in_specs=any_specs(2) + vmem_specs(4),
-        out_specs=any_specs(6),
+        in_specs=hbm_specs(3) + vmem_specs(4),
+        out_specs=hbm_specs(6),
         out_shape=[
             shape(cx + extra), shape(cx + extra), shape(7 + -(-extra // 4), cy),
             shape(4 + extra), shape(4 + extra), shape(extra),
@@ -548,15 +555,16 @@
         scratch_shapes=[pltpu.VMEM((cx, 8, cz), F32)] * 6
         + [
             pltpu.VMEM((extra, 8, cz), F32),
-            pltpu.SemaphoreType.DMA((cx // 2,)),
+            pltpu.VMEM((7, cy, cz), F32),
+            pltpu.SemaphoreType.DMA((cx // 2 + 2,)),
             pltpu.SemaphoreType.DMA((32,)),
         ],
         compiler_params=params(),
         name="pack",
-    )(phi, kappa, displacement, stiffness, cells, loads)
-
-
-def substep(src, kap, coef, dst, plane, advect, cy, cz):
+    )(phi, kappa, after, displacement, stiffness, cells, loads)
+
+
+def substep(src, kap, dst, plane, advect, cy, cz):
     wide = cy + 8
     chunks = cz // 128
     lane = lax.broadcasted_iota(jnp.int32, (wide, 128), 1)
@@ -565,203 +573,157 @@
     def take(ref, at, q):
         return ref[at, :, q * 128 : (q + 1) * 128]
 
-    zero = jnp.zeros((wide, 128), F32)
-    now = take(src, plane, 0)
-    back, back_before = pltpu.roll(now, 1, axis=1), zero
-    ahead = pltpu.roll(now, 127, axis=1)
     for q in range(chunks):
-        if q + 1 < chunks:
-            later = take(src, plane, q + 1)
-            ahead_later = pltpu.roll(later, 127, axis=1)
-        else:
-            later, ahead_later = None, zero
+        now = take(src, plane, q)
+        left = take(src, plane, q - 1) if q else 0.0
+        right = take(src, plane, q + 1) if q + 1 < chunks else 0.0
+        total = pltpu.roll(jnp.where(last, left, now), 1, axis=1) + pltpu.roll(
+            jnp.where(first, right, now), 127, axis=1
+        )
+        total = total + (pltpu.roll(now, 1, axis=0) + pltpu.roll(now, wide - 1, axis=0))
         before = take(src, plane - 1, q)
-        above = jnp.concatenate([now[8:], pltpu.roll(now[:8], 7, axis=0)], axis=0)
-        below = jnp.concatenate([pltpu.roll(now[wide - 8 :], 1, axis=0), now[: wide - 8]], axis=0)
-        total = (before + take(src, plane + 1, q)) + (above + below)
-        total = total + (jnp.where(first, back_before, back) + jnp.where(last, ahead_later, ahead))
+        total = total + (before + take(src, plane + 1, q))
         dst[plane, :, q * 128 : (q + 1) * 128] = (
-            take(coef, plane, q) * now + advect * before + take(kap, plane, q) * total
-        )
-        if later is not None:
-            back_before, back = back, pltpu.roll(later, 1, axis=1)
-            now, ahead = later, ahead_later
-
-
-def fluid(x0, x1, cx, cy, cz, with_wet, *refs):
+            now + advect * (before - now) + take(kap, plane - 1, q) * (total - 6.0 * now)
+        )
+
+
+def fluid(x0, x1, cx, cy, cz, kind, *refs):
     planes = x1 - x0 + 8
-    wide = cy + 8
-    chunks = cz // 128
-    names = ["phi", "kappa", "up", "down", "forced"]
-    names += ["low", "low_up", "low_down"] if x0 - 4 < 0 else []
-    names += ["high"] if x1 + 4 > cx else []
-    names += ["wet"] if with_wet else []
-    names += ["out"] + ([] if with_wet else ["send"])
-    names += ["nat", "knat", "a", "b", "kap", "coef", "upb", "downb", "sems", "out_sems"]
+    names = ["phi", "kappa", "up", "down"]
+    names += {"wet": ["forced", "low", "low_up", "low_down"], "middle": ["forced", "wet"],
+              "end": ["high", "whole"]}[kind]
+    names += {"wet": ["out", "send"]}.get(kind, ["out"])
+    names += ["a", "b", "kap", "upb", "downb", "sems", "out_sems"]
     r = dict(zip(names, refs))
-    nat, knat, a, b, kap, coef = (r[n] for n in ("nat", "knat", "a", "b", "kap", "coef"))
-    upb, downb = r["upb"], r["downb"]
+    a, b, kap, upb, downb = r["a"], r["b"], r["kap"], r["upb"], r["downb"]
     is_last = lax.axis_index("gx") == lax.axis_size("gx") - 1
     copy, copy_out = starter(r["sems"]), starter(r["out_sems"])
 
-    def chunked(src, s0, count, dst, d0, rows, start=copy):
-        return [
-            start(
-                src.at[pl.ds(s0, count), pl.ds(0, rows), pl.ds(q * 128, 128)],
-                dst.at[pl.ds(d0, count), q, pl.ds(0, rows)],
-            )
-            for q in range(chunks)
-        ]
-
-    def unchunked(src, s0, count, dst, d0, rows):
-        return [
-            copy_out(
-                src.at[pl.ds(s0, count), q, pl.ds(0, rows)],
-                dst.at[pl.ds(d0, count), pl.ds(0, rows), pl.ds(q * 128, 128)],
-            )
-            for q in range(chunks)
-        ]
-
-    outs = []
+    own0, own1 = max(0, x0 - 4), min(cx, x1 + 4)
     groups = []
-    if x0 - 4 < 0:
-        groups.append((0, 4, True, chunked(r["low"], 0, 4, nat, 0, cy)
-                       + chunked(r["low"], 4, 3, knat, 1, cy) + [
+    if kind == "wet":
+        groups.append((0, 4, [
+            copy(r["low"].at[pl.ds(0, 4)], a.at[pl.ds(0, 4), pl.ds(0, cy)]),
+            copy(r["low"].at[pl.ds(4, 3)], kap.at[pl.ds(0, 3), pl.ds(0, cy)]),
             copy(r["low_up"].at[pl.ds(0, 4)], upb.at[pl.ds(0, 4)]),
             copy(r["low_down"].at[pl.ds(0, 4)], downb.at[pl.ds(0, 4)]),
         ]))
-    own0, own1 = max(0, x0 - 4), min(cx, x1 + 4)
-    start = own0
-    while start < own1:
-        count = min(8, own1 - start)
+    for start in range(own0, own1, 4):
         i = start - (x0 - 4)
-        groups.append((i, i + count, True, chunked(r["phi"], start, count, nat, i, cy)
-                       + chunked(r["kappa"], start, count, knat, i, cy) + [
-            copy(r["up"].at[pl.ds(start, count)], upb.at[pl.ds(i, count)]),
-            copy(r["down"].at[pl.ds(start, count)], downb.at[pl.ds(i, count)]),
+        k0, k1 = max(start, x0 - 3), min(start + 4, x1 + 3)
+        groups.append((i, i + 4, [
+            copy(r["phi"].at[pl.ds(start, 4)], a.at[pl.ds(i, 4), pl.ds(0, cy)]),
+            copy(r["up"].at[pl.ds(start, 4)], upb.at[pl.ds(i, 4)]),
+            copy(r["down"].at[pl.ds(start, 4)], downb.at[pl.ds(i, 4)]),
+            copy(r["kappa"].at[pl.ds(k0, k1 - k0)],
+                 kap.at[pl.ds(k0 - (x0 - 3), k1 - k0), pl.ds(0, cy)]),
         ]))
-        start += count
-    if x1 + 4 > cx:
+    if kind == "end":
         i = cx - (x0 - 4)
-        groups.append((i, i + 4, False, chunked(r["high"], 0, 4, nat, i, wide)
-                       + chunked(r["high"], 4, 3, knat, i, wide)))
-    if with_wet:
+        groups.append((i, i + 4, [
+            copy(r["high"].at[pl.ds(0, 4)], a.at[pl.ds(i, 4)]),
+            copy(r["high"].at[pl.ds(4, 3)], kap.at[pl.ds(i - 1, 3)]),
+        ]))
+    outs = []
+    if kind == "middle":
         outs.append(copy_out(r["wet"], r["out"].at[pl.ds(0, x0)]))
 
     upper = lax.broadcasted_iota(jnp.int32, (8, cz), 0) < 4
-    tiles = wide // 8
-
-    def prepare(i, halo, wet):
-        if halo:
+
+    def assemble(i0, i1):
+        for i in range(i0, i1):
+            x = x0 - 4 + i
+            if x >= cx:
+                continue
             up, down = upb[i], downb[i]
-            edge = jnp.where(upper, up, down)
-            kedge = pltpu.roll(jnp.where(upper, down, up), 4, axis=0)
-            for q in range(chunks):
-                nat[i, q, cy:wide, :] = edge[:, q * 128 : (q + 1) * 128]
-                knat[i, q, cy:wide, :] = kedge[:, q * 128 : (q + 1) * 128]
-        for q in range(chunks):
-            at = slice(q * 128, (q + 1) * 128)
-            if wet:
-                nat[i, q] = nat[i, q] + r["forced"][i + (x0 - 4), :, at]
-            for j in range(tiles):
-                rows = slice(8 * j, 8 * j + 8)
-                a[i, rows, at] = nat[i, q, pl.ds(j, 8, stride=tiles), :]
-                k = knat[i, q, pl.ds(j, 8, stride=tiles), :]
-                kap[i, rows, at] = k
-                coef[i, rows, at] = 0.75 - 6.0 * k
-
-    def step(src, dst, i):
-        outside = jnp.logical_and(is_last, i + (x0 - 4) >= cx)
-        substep(src, kap, coef, dst, i, jnp.where(outside, 0.0, 0.25), cy, cz)
-
-    def loop(lo, hi, *work):
+            a[i, cy : cy + 8, :] = jnp.where(upper, up, down)
+            if 1 <= i < planes - 1:
+                kap[i - 1, cy : cy + 8, :] = pltpu.roll(jnp.where(upper, down, up), 4, axis=0)
+            if "forced" in r and 0 <= x < r["forced"].shape[0]:
+                a[i] = a[i] + r["forced"][x]
+
+    def run(src, dst, lo, hi):
         def body(i, carry):
-            for one in work:
-                one(i)
+            advect = 0.25
+            if kind == "end":
+                outside = jnp.logical_and(is_last, i + (x0 - 4) >= cx)
+                advect = jnp.where(outside, 0.0, 0.25)
+            substep(src, kap, dst, i, advect, cy, cz)
             return carry
 
-        if hi > lo:
-            lax.fori_loop(lo, hi, body, 0)
-
-    wet_lo, wet_hi = 4 - x0, 4 - x0 + r["forced"].shape[0]
-    for i0, i1, halo, copies in groups:
+        lax.fori_loop(lo, hi, body, 0)
+
+    done = 1
+    for i0, i1, copies in groups:
         for made in copies:
             made.wait()
-        edges = sorted({i0, i1, min(max(2, i0), i1), min(max(wet_lo, i0), i1), min(max(wet_hi, i0), i1)})
-        for lo, hi in zip(edges[:-1], edges[1:]):
-            wet = wet_lo <= lo < wet_hi
-            work = [lambda i: prepare(i, halo, wet)]
-            if lo >= 2:
-                work.append(lambda i: step(a, b, i - 1))
-            loop(lo, hi, *work)
-        if not with_wet and i0 == 4:
-            outs += unchunked(nat, 4, 4, r["send"], 0, wide)
-            outs += unchunked(knat, 4, 3, r["send"], 4, wide)
-    loop(2, planes - 2, lambda i: step(b, a, i))
-    loop(3, planes - 3, lambda i: step(a, b, i))
-
-    def finish(i):
-        step(b, a, i)
-        for q in range(chunks):
-            for j in range(tiles):
-                rows = slice(8 * j, 8 * j + 8)
-                done[i, q, pl.ds(j, 8, stride=tiles), :] = a[i, rows, q * 128 : (q + 1) * 128]
-
-    done = nat if with_wet else knat
-    if not with_wet:
+        assemble(i0, i1)
+        if kind == "wet" and i0 == 4:
+            outs.append(copy_out(a.at[pl.ds(4, 4)], r["send"].at[pl.ds(0, 4)]))
+            outs.append(copy_out(kap.at[pl.ds(3, 3)], r["send"].at[pl.ds(4, 3)]))
+        ready = i1 - 1
+        if ready > done:
+            run(a, b, done, ready)
+            done = ready
+    if kind == "wet":
         for made in outs:
             made.wait()
         outs = []
-    start = 4
-    while start < planes - 4:
-        count = min(8, planes - 4 - start)
-        loop(start, start + count, finish)
-        x = x0 + start - 4
-        outs += unchunked(done, start, count, r["out"], x if with_wet else x - x0, cy)
-        start += count
+    run(b, a, 2, planes - 2)
+    run(a, b, 3, planes - 3)
+    for start in range(4, planes - 4, 4):
+        run(b, a, start, start + 4)
+        if kind == "wet":
+            for i in range(start, start + 4):
+                r["out"][i - 4] = a[i, 0:cy, :]
+        else:
+            x = x0 + start - 4
+            outs.append(
+                copy_out(a.at[pl.ds(start, 4), pl.ds(0, cy)], r["out"].at[pl.ds(x, 4)])
+            )
     for made in outs:
         made.wait()
 
 
-def fluid_call(x0, x1, phi, kappa, up, down, forced, low=None, high=None, wet=None):
+def fluid_call(kind, x0, x1, phi, kappa, up, down, *more):
     cx, cy, cz = phi.shape
     planes = x1 - x0 + 8
-    args = [phi, kappa, up, down, forced]
-    specs = any_specs(4) + vmem_specs(1)
-    if low is not None:
-        args += list(low)
-        specs += any_specs(3)
-    if high is not None:
-        args.append(high)
-        specs += any_specs(1)
-    if wet is not None:
-        args.append(wet)
-        specs += any_specs(1)
-        out_shape = jax.ShapeDtypeStruct((cx, cy, cz), F32)
-        out_specs = pl.BlockSpec(memory_space=pl.ANY)
-    else:
+    field = jax.ShapeDtypeStruct((cx, cy, cz), F32)
+    whole = hbm_specs(1)[0]
+    if kind == "wet":
+        specs = vmem_specs(1) + hbm_specs(3)
         out_shape = [
             jax.ShapeDtypeStruct((x1 - x0, cy, cz), F32),
             jax.ShapeDtypeStruct((7, cy + 8, cz), F32),
         ]
-        out_specs = any_specs(2)
+        out_specs = vmem_specs(1) + hbm_specs(1)
+    elif kind == "middle":
+        specs, out_shape, out_specs = vmem_specs(2), field, whole
+    else:
+        specs, out_shape, out_specs = hbm_specs(2), field, whole
     cells = planes * (cy + 8) * cz
-    natural = pltpu.VMEM((planes, cz // 128, cy + 8, 128), F32)
-    stored = pltpu.VMEM((planes, cy + 8, cz), F32)
     return pl.pallas_call(
-        functools.partial(fluid, x0, x1, cx, cy, cz, wet is not None),
-        in_specs=specs,
+        functools.partial(fluid, x0, x1, cx, cy, cz, kind),
+        in_specs=hbm_specs(4) + specs,
         out_specs=out_specs,
         out_shape=out_shape,
-        scratch_shapes=[natural, natural, stored, stored, stored, stored]
-        + [pltpu.VMEM((planes, 8, cz), F32)] * 2
-        + [pltpu.SemaphoreType.DMA((128,)), pltpu.SemaphoreType.DMA((64,))],
+        scratch_shapes=[
+            pltpu.VMEM((planes, cy + 8, cz), F32),
+            pltpu.VMEM((planes, cy + 8, cz), F32),
+            pltpu.VMEM((planes - 2, cy + 8, cz), F32),
+            pltpu.VMEM((planes, 8, cz), F32),
+            pltpu.VMEM((planes, 8, cz), F32),
+            pltpu.SemaphoreType.DMA((48,)),
+            pltpu.SemaphoreType.DMA((12,)),
+        ],
+        input_output_aliases={5: 0} if kind == "end" else {},
         compiler_params=params(),
         cost_estimate=pl.CostEstimate(
             flops=48 * cells, bytes_accessed=12 * cells, transcendentals=0
         ),
-        name="fluid_wet" if wet is None else "fluid_rest",
-    )(*args)
+        name="fluid_" + kind,
+    )(phi, kappa, up, down, *more)
 
 
 def shifted_pairs(n_gx, n_gy, dx, dy):
@@ -806,8 +768,13 @@
     def f32(*shape):
         return jax.ShapeDtypeStruct(shape, F32)
 
+    sent = call(
+        functools.partial(gather_disp, n_gy), f32(peers, 1, 3 * blk),
+        [pltpu.VMEM((peers, blk), F32)], "gather_disp", vmem_specs(2), displacement, ldof,
+    )
+    disp = exchange(sent)
     up_send, down_send, low_send, low_up_send, low_down_send, own = packed(
-        phi, kappa, displacement, stiffness, fcell, ldof
+        phi, kappa, disp, displacement, stiffness, fcell, ldof
     )
     extra = own.shape[0]
     low = shift(low_send, 1, 0)
@@ -817,25 +784,23 @@
     low_down = shift(low_down_send, 1, 1)
     near = shift(jnp.concatenate([own, up[cx:], down[cx:]], axis=0), -1, 0)
 
-    sent = call(
-        functools.partial(gather_disp, n_gy), f32(peers, 1, 3 * blk),
-        [pltpu.VMEM((peers, blk), F32)], "gather_disp", vmem_specs(2), displacement, ldof,
-    )
-    disp = exchange(sent)
-    chunks = cz // 256
+    chunks = cz // 128
     forced = call(
         functools.partial(scatter_disp, cx, cy, cz), f32(wet_planes, cy + 8, cz),
         [
-            pltpu.VMEM((wet_planes * cy * chunks, 512), F32),
-            pltpu.VMEM((wet_planes * 8 * chunks, 512), F32),
+            pltpu.VMEM((wet_planes * cy * chunks, 256), F32),
+            pltpu.VMEM((512, wet_planes * 4 * chunks), F32),
             pltpu.VMEM((2, (extra - 2) // 2 + (extra - 2) % 2, 8, cz), F32),
             pltpu.SemaphoreType.DMA((2,)),
         ],
-        "scatter_disp", vmem_specs(2) + any_specs(2), disp, fcell, up, down,
+        "scatter_disp", vmem_specs(2) + hbm_specs(2), disp, fcell, up, down,
     )
     wet, send = fluid_call(
-        0, wet_planes, phi, kappa, up, down, forced, low=(low, low_up, low_down)
-    )
+        "wet", 0, wet_planes, phi, kappa, up, down, forced, low, low_up, low_down
+    )
+    high = shift(send, -1, 0)
+    middle = fluid_call("middle", wet_planes, cx - 4, phi, kappa, up, down, forced, wet)
+    field = fluid_call("end", cx - 4, cx, phi, kappa, up, down, high, middle)
     size = 8 * hist
     gram = call(
         gram_rows, f32(peers, 128),
@@ -845,14 +810,14 @@
             pltpu.VMEM((max(128, peers, 2 * peers if peers < hist else 0), 128), F32),
             pltpu.SemaphoreType.DMA((sx // 8,)),
         ],
-        "gram_rows", any_specs(1), v_hist,
+        "gram_rows", hbm_specs(1), v_hist,
     )
     press = call(
         functools.partial(gather_press, n_gx, n_gy), f32(peers, 1, (len(NEAR) + 1) * blk),
-        [pltpu.VMEM((peers, blk), F32)], "gather_press", vmem_specs(3), wet, fcell, gram,
+        [pltpu.VMEM((peers, blk), F32)], "gather_press", vmem_specs(3) + hbm_specs(1),
+        wet, fcell, gram, middle,
     )
     loads = exchange(press)
-    high = shift(send, -1, 0)
     resp, late = call(
         shell, [f32(sx, sy), f32(peers, 1, 256)],
         [
@@ -867,15 +832,14 @@
             pltpu.SemaphoreType.DMA((7 + extra,)),
             pltpu.SemaphoreType.DMA((1,)),
         ],
-        "shell", vmem_specs(5) + any_specs(7),
+        "shell", vmem_specs(5) + hbm_specs(7),
         loads, ldof, displacement, stiffness, r_prev, v_hist, up, down, low, low_up, low_down, near,
     )
     x_next = call(
         solve, f32(sx, sy),
         [pltpu.VMEM((hist, sx, sy), F32), pltpu.SemaphoreType.DMA((1,))],
-        "solve", vmem_specs(3) + any_specs(1), exchange(late), resp, w_prev, w_hist,
-    )
-    field = fluid_call(wet_planes, cx, phi, kappa, up, down, forced, high=high, wet=wet)
+        "solve", vmem_specs(3) + hbm_specs(1), exchange(late), resp, w_prev, w_hist,
+    )
     return (field, x_next)
 
 

time: 198 us -> 166 us (0.84)
  Pallas kernels: 108 us -> 82.9 us
  blocking collectives: 38.5 us -> 26.7 us
  waiting for transfers between devices: 13.4 us -> 23.2 us
  starting transfers between devices: 30.9 us -> 24.9 us
    pallas_call x3 -> x4, Pallas kernels: 67.5 us -> 42.4 us  [the longest x3 36.7 us: fluid_call(): pl.pallas_call(functools.partial(fluid, x0, x1, cx, cy, cz, kind), in_spe...]
    ppermute x7, waiting for transfers between devices: 11.2 us -> 23.2 us  [shift(): return lax.ppermute(value, axes, shifted_pairs(n_gx, n_gy, dx, dy))]
    all_to_all x2, blocking collectives: 38.5 us -> 26.7 us  [exchange(): return lax.all_to_all(value, axes, split_axis=0, concat_axis=0, tiled=True)]
    ppermute x7, starting transfers between devices: 18.8 us -> 15.5 us  [shift(): return lax.ppermute(value, axes, shifted_pairs(n_gx, n_gy, dx, dy))]
    all_to_all x1, starting transfers between devices: 12 us -> 9.45 us  [exchange(): return lax.all_to_all(value, axes, split_axis=0, concat_axis=0, tiled=True)]
    all_to_all x1, waiting for transfers between devices: 2.28 us -> 0.01 us  [exchange(): return lax.all_to_all(value, axes, split_axis=0, concat_axis=0, tiled=True)]
  transfers between devices with their start and end apart: 8 -> 8, of which waited for: 2 -> 2; matrix products, arithmetic and copies ran while one was open for 0% -> 0% of each run, Pallas kernels for 21% -> 36%
where the time goes in v1:
time: 166 us; the launch traced here: 165 us
  Pallas kernels  82.9 us (50%)
  blocking collectives  26.7 us (16%)
  starting transfers between devices  24.9 us (15%)
  waiting for transfers between devices  23.2 us (14%)
  local copies, waits for them, and re-layouts  6.16 us (4%)
    pallas_call x6, Pallas kernels, call(): pl.pallas_call(body, in_specs=specs, out_specs=vmem_specs(len(out_shape))...  40.6 us
    pallas_call x3, Pallas kernels, fluid_call(): pl.pallas_call(functools.partial(fluid, x0, x1, cx, cy, cz, kind), in_spe...  36.7 us
    all_to_all x2, blocking collectives, exchange(): return lax.all_to_all(value, axes, split_axis=0, concat_axis=0, tiled=True)  26.7 us
    ppermute x7, waiting for transfers between devices, shift(): return lax.ppermute(value, axes, shifted_pairs(n_gx, n_gy, dx, dy))  23.2 us
    ppermute x7, starting transfers between devices, shift(): return lax.ppermute(value, axes, shifted_pairs(n_gx, n_gy, dx, dy))  15.5 us
    all_to_all x1, starting transfers between devices, exchange(): return lax.all_to_all(value, axes, split_axis=0, concat_axis=0, tiled=True)  9.45 us
    unnamed x18, local copies, waits for them, and re-layouts  6.15 us
    pallas_call x1, Pallas kernels, packed(): pl.pallas_call(pack, in_specs=hbm_specs(3) + vmem_specs(4), out_specs=hbm...  5.66 us
  transfers between devices with their start and end apart: 8, of which 2 were waited for; matrix products, arithmetic and copies ran while one was open for 0% of the time, Pallas kernels for 36%

profile of v1, /device:TPU:0, one launch (start us, length us, event | category | flops | bytes accessed | tf_op | source)
XLA Modules:
  0.0 165.0 jit_solution(11600617400316096132)
XLA Ops:
  0.6 3.0 %gather_disp.1 = f32[32,1,384]{2,1,0:T(1,128)} custom-call(f32[64,512]{1,0:T(8,128)} %disp_ref.5, s32[32,128]{1,0:T(8,128)} %bitcast.5), custom_call_target="tpu_custom_call" | custom-call | tf_op jit(solution)/shard_map/gather_disp/pallas_call | solution.py:758
  3.6 14.7 %all_to_all.15.after_ref.disp_ref = f32[32,1,384]{2,1,0:T(1,128)} all-to-all(f32[32,1,384]{2,1,0:T(1,128)} %gather_disp.1), channel_id=1, replica_groups=mesh['gx'=8,'gy'=4] {'gx','gy'}, dimensions={0} | all-to-all | bytes 98304 | tf_op jit(solution)/shard_map/all_to_all | solution.py:754
  18.4 5.7 %pack.1 = (f32[35,8,1024]{2,1,0:T(8,128)}, f32[35,8,1024]{2,1,0:T(8,128)}, f32[8,32,1024]{2,1,0:T(8,128)}, f32[7,8,1024]{2,1,0:T(8,128)}, f32[7,8,1024]{2,1,0:T(8,128)}, /*index=5*/f32[3,8,1024]{2,1,0:T(8,128)}) custom-call(f32[32,32,1024]{2,1,0:T(8,128)} %refs_0_.5, f32[32,32,1024]{2,1,0:T(8,128)} %refs_1_.5, f32[32,1,384]{2,1,0:T(1,128)} %all_to_all.15.after_ref.disp_ref, ...), custom_call_target="tpu_custom_call" | custom-call | tf_op jit(solution)/shard_map/pack/pallas_call | solution.py:547
  24.0 1.3 collective-permute-start
  25.3 3.1 %collective-permute-start.1 = (f32[35,8,1024]{2,1,0:T(8,128)}, f32[35,8,1024]{2,1,0:T(8,128)S(1)}, u32[]{:S(2)}, u32[]{:S(2)}) collective-permute-start(f32[35,8,1024]{2,1,0:T(8,128)} %get-tuple-element.13), channel_id=1, source_target_pairs={{0,1},{1,2},{2,3},{4,5},{5,6},{6,7},{8,9},{9,10},{10,11},{12,13},{... | collective-permute-start | bytes 3440648 | tf_op jit(solution)/shard_map/ppermute | solution.py:751
  28.4 2.5 %collective-permute-start.2 = (f32[8,32,1024]{2,1,0:T(8,128)}, f32[8,32,1024]{2,1,0:T(8,128)S(1)}, u32[]{:S(2)}, u32[]{:S(2)}) collective-permute-start(f32[8,32,1024]{2,1,0:T(8,128)} %get-tuple-element.14), channel_id=1, source_target_pairs={{0,4},{1,5},{2,6},{3,7},{4,8},{5,9},{6,10},{7,11},{8,12},{9,13},{1... | collective-permute-start | bytes 3145736 | tf_op jit(solution)/shard_map/ppermute | solution.py:751
  31.7 4.9 %collective-permute-start.4 = (f32[7,8,1024]{2,1,0:T(8,128)}, f32[7,8,1024]{2,1,0:T(8,128)S(1)}, u32[]{:S(2)}, u32[]{:S(2)}) collective-permute-start(f32[7,8,1024]{2,1,0:T(8,128)} %get-tuple-element.16), channel_id=1, source_target_pairs={{0,5},{1,6},{2,7},{4,9},{5,10},{6,11},{8,13},{9,14},{10,15},{12,17... | collective-permute-start | bytes 688136 | tf_op jit(solution)/shard_map/ppermute | solution.py:751
  36.6 1.0 copy-done
  38.6 10.7 %scatter_disp.1.refs_4_ = f32[4,40,1024]{2,1,0:T(8,128)} custom-call(f32[32,1,384]{2,1,0:T(1,128)} %all_to_all.15.after_ref.disp_ref, s32[32,128]{1,0:T(8,128)} %bitcast.3, f32[35,8,1024]{2,1,0:T(8,128)} %copy-done, f32[35,8,1024]{2,1,0:T(8,128)} %copy-done.1), custom_call_target="tpu_custom_call" | custom-call | tf_op jit(solution)/shard_map/scatter_disp/pallas_call | solution.py:758
  49.3 12.6 %collective-permute-done.4.refs_7_.low_down_ref = f32[7,8,1024]{2,1,0:T(8,128)S(1)} collective-permute-done((f32[7,8,1024]{2,1,0:T(8,128)}, f32[7,8,1024]{2,1,0:T(8,128)S(1)}, u32[]{:S(2)}, u32[]{:S(2)}) %collective-permute-start.4) | collective-permute-done | bytes 229408 | tf_op jit(solution)/shard_map/ppermute | solution.py:751
  62.6 1.0 copy-done.2
  63.6 8.3 %fluid_wet.1 = (f32[4,32,1024]{2,1,0:T(8,128)}, f32[7,40,1024]{2,1,0:T(8,128)}) custom-call(f32[32,32,1024]{2,1,0:T(8,128)} %refs_0_.5, f32[32,32,1024]{2,1,0:T(8,128)} %refs_1_.5, f32[35,8,1024]{2,1,0:T(8,128)} %copy-done, f32[35,8,1024]{2,1,0:T(8,128)} %copy-done.1, f32[4,40,1024]{2,1,0:T(8,128)} %scatter_disp.1.refs_4_, f32[8,32,1024]{2,1,0:T(8,128)} %copy-done.2, ...), custom_call_target="tpu_custom_call" | custom-call | flops 23592960 | bytes 5898240 | tf_op jit(solution)/shard_map/fluid_wet/pallas_call | solution.py:706
  71.9 1.5 collective-permute-start.5
  73.4 7.9 %gram_rows.1.gram_ref = f32[32,128]{1,0:T(8,128)} custom-call(f32[40,64,512]{2,1,0:T(8,128)} %v_ref.3), custom_call_target="tpu_custom_call" | custom-call | tf_op jit(solution)/shard_map/gram_rows/pallas_call | solution.py:758
  81.3 21.3 %fluid_middle.1.refs_5_.after_ref = f32[32,32,1024]{2,1,0:T(8,128)} custom-call(f32[32,32,1024]{2,1,0:T(8,128)} %refs_0_.5, f32[32,32,1024]{2,1,0:T(8,128)} %refs_1_.5, f32[35,8,1024]{2,1,0:T(8,128)} %copy-done, f32[35,8,1024]{2,1,0:T(8,128)} %copy-done.1, f32[4,40,1024]{2,1,0:T(8,128)} %scatter_disp.1.refs_4_, f32[4,32,1024]{2,1,0:T(8,128)} %get-tuple-element.18.refs_5_.wet_ref), custom_call_target="tpu_custom_call" | custom-call | flops 62914560 | bytes 15728640 | tf_op jit(solution)/shard_map/fluid_middle/pallas_call | solution.py:706
  102.6 4.4 %gather_press.1 = f32[32,1,1280]{2,1,0:T(1,128)} custom-call(f32[4,32,1024]{2,1,0:T(8,128)} %get-tuple-element.18.refs_5_.wet_ref, s32[32,128]{1,0:T(8,128)} %bitcast.4, f32[32,128]{1,0:T(8,128)} %gram_rows.1.gram_ref, f32[32,32,1024]{2,1,0:T(8,128)} %fluid_middle.1.refs_5_.after_ref), custom_call_target="tpu_custom_call" | custom-call | tf_op jit(solution)/shard_map/gather_press/pallas_call | solution.py:758
  107.0 9.5 %all-to-all-start.1 = ((f32[32,1,1280]{2,1,0:T(1,128)}), f32[32,1,1280]{2,1,0:T(1,128)S(1)}, u32[]{:S(2)}, u32[]{:S(2)}) async-start(f32[32,1,1280]{2,1,0:T(1,128)} %gather_press.1), calls=%async_computation.1 | async-start | bytes 327680 | tf_op jit(solution)/shard_map/all_to_all | solution.py:754
  116.6 1.5 collective-permute-start.6
  118.1 10.6 %collective-permute-done.6.high_ref = f32[9,8,1024]{2,1,0:T(8,128)S(1)} collective-permute-done((f32[9,8,1024]{2,1,0:T(8,128)S(1)}, f32[9,8,1024]{2,1,0:T(8,128)S(1)}, u32[]{:S(2)}, u32[]{:S(2)}) %collective-permute-start.6) | collective-permute-done | bytes 294944 | tf_op jit(solution)/shard_map/ppermute | solution.py:751
  130.1 8.9 %shell.1 = (f32[64,512]{1,0:T(8,128)}, f32[32,1,256]{2,1,0:T(1,128)}) custom-call(f32[32,1,1280]{2,1,0:T(1,128)} %copy-done.6, s32[32,128]{1,0:T(8,128)} %bitcast.7, f32[64,512]{1,0:T(8,128)} %disp_ref.5, f32[64,512]{1,0:T(8,128)} %stiff_ref.3, f32[64,512]{1,0:T(8,128)} %prev_ref.2, f32[40,64,512]{2,1,0:T(8,128)} %v_ref.3, f32[35,8,1024]{2,1,0:T(8,128)} %copy-done, ...), custom_call_target="tpu_custom_call" | custom-call | tf_op jit(solution)/shard_map/shell/pallas_call | solution.py:758
  139.0 12.0 %all_to_all.16.recv_ref = f32[32,1,256]{2,1,0:T(1,128)} all-to-all(f32[32,1,256]{2,1,0:T(1,128)} %get-tuple-element.20), channel_id=1, replica_groups=mesh['gx'=8,'gy'=4] {'gx','gy'}, dimensions={0} | all-to-all | bytes 65536 | tf_op jit(solution)/shard_map/all_to_all | solution.py:754
  151.0 5.6 %solve.1 = f32[64,512]{1,0:T(8,128)} custom-call(f32[32,1,256]{2,1,0:T(1,128)} %all_to_all.16.recv_ref, f32[64,512]{1,0:T(8,128)} %get-tuple-element.21.resp_ref, f32[64,512]{1,0:T(8,128)} %prev_ref.3, f32[40,64,512]{2,1,0:T(8,128)} %w_ref.1), custom_call_target="tpu_custom_call" | custom-call | tf_op jit(solution)/shard_map/solve/pallas_call | solution.py:758
  156.7 1.0 copy-done.3
  157.7 7.1 %fluid_end.1 = f32[32,32,1024]{2,1,0:T(8,128)} custom-call(f32[32,32,1024]{2,1,0:T(8,128)} %refs_0_.5, f32[32,32,1024]{2,1,0:T(8,128)} %refs_1_.5, f32[35,8,1024]{2,1,0:T(8,128)} %copy-done, f32[35,8,1024]{2,1,0:T(8,128)} %copy-done.1, f32[7,40,1024]{2,1,0:T(8,128)} %copy-done.3, ...), custom_call_target="tpu_custom_call", output_to_operand_aliasing={{}: (5, {})} | custom-call | flops 23592960 | bytes 5898240 | tf_op jit(solution)/shard_map/fluid_end/pallas_call | solution.py:706
  (27 shorter events, 3.8 us)
Async XLA Ops:
  24.0 12.5 %collective-permute-start = (f32[35,8,1024]{2,1,0:T(8,128)}, f32[35,8,1024]{2,1,0:T(8,128)S(1)}, u32[]{:S(2)}, u32[]{:S(2)}) collective-permute-start(f32[35,8,1024]{2,1,0:T(8,128)} %get-tuple-element.12), channel_id=1, source_target_pairs={{1,0},{2,1},{3,2},{5,4},{6,5},{7,6},{9,8},{10,9},{11,10},{13,12},{... | collective-permute-start | bytes 3440648 | tf_op jit(solution)/shard_map/ppermute | solution.py:751
  25.3 11.2 %collective-permute-start.1 = (f32[35,8,1024]{2,1,0:T(8,128)}, f32[35,8,1024]{2,1,0:T(8,128)S(1)}, u32[]{:S(2)}, u32[]{:S(2)}) collective-permute-start(f32[35,8,1024]{2,1,0:T(8,128)} %get-tuple-element.13), channel_id=1, source_target_pairs={{0,1},{1,2},{2,3},{4,5},{5,6},{6,7},{8,9},{9,10},{10,11},{12,13},{... | collective-permute-start | bytes 3440648 | tf_op jit(solution)/shard_map/ppermute | solution.py:751
  28.4 33.5 %collective-permute-start.2 = (f32[8,32,1024]{2,1,0:T(8,128)}, f32[8,32,1024]{2,1,0:T(8,128)S(1)}, u32[]{:S(2)}, u32[]{:S(2)}) collective-permute-start(f32[8,32,1024]{2,1,0:T(8,128)} %get-tuple-element.14), channel_id=1, source_target_pairs={{0,4},{1,5},{2,6},{3,7},{4,8},{5,9},{6,10},{7,11},{8,12},{9,13},{1... | collective-permute-start | bytes 3145736 | tf_op jit(solution)/shard_map/ppermute | solution.py:751
  31.0 18.3 %collective-permute-start.3 = (f32[7,8,1024]{2,1,0:T(8,128)}, f32[7,8,1024]{2,1,0:T(8,128)S(1)}, u32[]{:S(2)}, u32[]{:S(2)}) collective-permute-start(f32[7,8,1024]{2,1,0:T(8,128)} %get-tuple-element.15), channel_id=1, source_target_pairs={{1,4},{2,5},{3,6},{5,8},{6,9},{7,10},{9,12},{10,13},{11,14},{13,16... | collective-permute-start | bytes 688136 | tf_op jit(solution)/shard_map/ppermute | solution.py:751
  31.7 30.2 %collective-permute-start.4 = (f32[7,8,1024]{2,1,0:T(8,128)}, f32[7,8,1024]{2,1,0:T(8,128)S(1)}, u32[]{:S(2)}, u32[]{:S(2)}) collective-permute-start(f32[7,8,1024]{2,1,0:T(8,128)} %get-tuple-element.16), channel_id=1, source_target_pairs={{0,5},{1,6},{2,7},{4,9},{5,10},{6,11},{8,13},{9,14},{10,15},{12,17... | collective-permute-start | bytes 688136 | tf_op jit(solution)/shard_map/ppermute | solution.py:751
  36.6 1.0 copy-start
  37.6 1.0 copy-start.1
  49.3 12.6 %copy-start.4 = (f32[7,8,1024]{2,1,0:T(8,128)}, f32[7,8,1024]{2,1,0:T(8,128)S(1)}, u32[]{:S(2)}) copy-start(f32[7,8,1024]{2,1,0:T(8,128)S(1)} %collective-permute-done.3.refs_6_.low_up_ref) | copy-start | bytes 688132
  61.9 0.7 copy-start.5
  62.6 1.0 copy-start.2
  71.9 84.7 %collective-permute-start.5 = (f32[7,40,1024]{2,1,0:T(8,128)}, f32[7,40,1024]{2,1,0:T(8,128)S(1)}, u32[]{:S(2)}, u32[]{:S(2)}) collective-permute-start(f32[7,40,1024]{2,1,0:T(8,128)} %get-tuple-element.17), channel_id=1, source_target_pairs={{4,0},{5,1},{6,2},{7,3},{8,4},{9,5},{10,6},{11,7},{12,8},{13,9},{1... | collective-permute-start | bytes 3440648 | tf_op jit(solution)/shard_map/ppermute | solution.py:751
  102.6 13.9 %slice-start = ((f32[35,8,1024]{2,1,0:T(8,128)}), f32[3,8,1024]{2,1,0:T(8,128)S(1)}, s32[]{:S(2)}) async-start(f32[35,8,1024]{2,1,0:T(8,128)} %copy-done), calls=%async_computation.3 | async-start | bytes 196608 | tf_op jit(solution)/shard_map/slice | solution.py:785
  102.6 13.9 %slice-start.1 = ((f32[35,8,1024]{2,1,0:T(8,128)}), f32[3,8,1024]{2,1,0:T(8,128)S(1)}, s32[]{:S(2)}) async-start(f32[35,8,1024]{2,1,0:T(8,128)} %copy-done.1), calls=%async_computation.4 | async-start | bytes 196608 | tf_op jit(solution)/shard_map/slice | solution.py:785
  102.6 13.9 %copy-start.8 = (f32[3,8,1024]{2,1,0:T(8,128)S(1)}, f32[3,8,1024]{2,1,0:T(8,128)}, u32[]{:S(2)}) copy-start(f32[3,8,1024]{2,1,0:T(8,128)} %get-tuple-element.19) | copy-start | bytes 294916
  107.0 21.6 %all-to-all-start.1 = ((f32[32,1,1280]{2,1,0:T(1,128)}), f32[32,1,1280]{2,1,0:T(1,128)S(1)}, u32[]{:S(2)}, u32[]{:S(2)}) async-start(f32[32,1,1280]{2,1,0:T(1,128)} %gather_press.1), calls=%async_computation.1 | async-start | bytes 327680 | tf_op jit(solution)/shard_map/all_to_all | solution.py:754
  116.6 12.1 %collective-permute-start.6 = (f32[9,8,1024]{2,1,0:T(8,128)S(1)}, f32[9,8,1024]{2,1,0:T(8,128)S(1)}, u32[]{:S(2)}, u32[]{:S(2)}) collective-permute-start(f32[9,8,1024]{2,1,0:T(8,128)S(1)} %pad_maximum_fusion), channel_id=1, source_target_pairs={{4,0},{5,1},{6,2},{7,3},{8,4},{9,5},{10,6},{11,7},{12,8},{13,9},{1... | collective-permute-start | bytes 884744 | tf_op jit(solution)/shard_map/ppermute | solution.py:751
  128.7 0.7 copy-start.7
  129.4 0.7 copy-start.6
  156.7 1.0 copy-start.3

commit v2 on v1

--- a/solution.py
+++ b/solution.py
@@ -10,7 +10,7 @@
 NSUB = 4
 SWEEPS = 3
 HIST = 40
-VMEM_BYTES = 56 * 1024 * 1024
+VMEM_BYTES = 32 * 1024 * 1024
 F32 = jnp.float32
 BF16 = jnp.bfloat16
 
@@ -21,6 +21,10 @@
 
 def vmem_specs(count):
     return [pl.BlockSpec(memory_space=pltpu.VMEM)] * count
+
+
+def any_specs(count):
+    return [pl.BlockSpec(memory_space=pl.ANY)] * count
 
 
 def hbm_specs(count):
@@ -40,9 +44,23 @@
     return jnp.concatenate([block[i : i + 1] for i in range(block.shape[0])], axis=1)
 
 
+def both_rows(row):
+    return jnp.broadcast_to(row, (16, row.shape[1])).astype(BF16)
+
+
+def matches(keys, rows):
+    ids = lax.broadcasted_iota(jnp.int32, (16, keys.shape[1]), 0).astype(F32).astype(BF16)
+    found = []
+    for base in range(0, rows, 256):
+        key = both_rows((keys - base).astype(F32))
+        for start in range(0, min(256, rows - base), 16):
+            found.append(key == ids + jnp.bfloat16(start))
+    return found
+
+
 def one_hot(keys, rows):
-    ids = lax.broadcasted_iota(jnp.int32, (rows, keys.shape[1]), 0)
-    return jnp.where(ids == keys, 1.0, 0.0).astype(BF16)
+    one, zero = jnp.bfloat16(1), jnp.bfloat16(0)
+    return jnp.concatenate([jnp.where(m, one, zero) for m in matches(keys, rows)], axis=0)
 
 
 def select_sum(table, lane, group, rows, parts):
@@ -69,12 +87,13 @@
 
 
 def spread_values(values, lane, lanes, parts):
-    ids = lax.broadcasted_iota(jnp.int32, (lanes, lane.shape[1]), 0)
-    match = ids == lane
-    return jnp.concatenate(
-        [jnp.where(match, part.astype(F32), 0.0).astype(BF16) for part in pieces(values, parts)],
-        axis=0,
-    )
+    zero = jnp.bfloat16(0)
+    found = matches(lane, lanes)
+    spread = []
+    for part in pieces(values, parts):
+        part = both_rows(part.astype(F32))
+        spread += [jnp.where(m, part, zero) for m in found]
+    return jnp.concatenate(spread, axis=0)
 
 
 NEAR = ((0, 0), (1, 0), (-1, 0), (0, 1), (0, -1), (1, 1), (1, -1), (-1, 1), (-1, -1))
@@ -120,20 +139,13 @@
     out_ref[:, 0, 2 * blk : 3 * blk] = jnp.where(beside == 0, 0.0, pltpu.roll(own, 1, axis=0))
 
 
-def scatter_disp(cx, cy, cz, disp_ref, cells_ref, up_ref, down_ref, out_ref, acc_ref, side_ref, near_ref, sems):
+def scatter_disp(cx, cy, cz, disp_ref, cells_ref, up_ref, down_ref, out_ref, acc_ref, side_ref):
     planes = out_ref.shape[0]
     peers, blk = cells_ref.shape
     rows = planes * cy
     chunks = cz // 128
     row_bits = cz.bit_length() - 1
     step = 8
-    extra = near_ref.shape[1]
-    copy = starter(sems)
-    copies = [
-        copy(ref.at[pl.ds(cx, extra)], near_ref.at[side])
-        for side, ref in enumerate((up_ref, down_ref))
-    ]
-
     def accumulate(target, first, left, right):
         added = lax.dot_general(
             left, right, (((1,), (1,)), ((), ())), preferred_element_type=F32
@@ -151,11 +163,9 @@
             acc_ref, base == 0, one_hot(keys, rows * chunks),
             spread_values(values, index & 127, 128, 2),
         )
-    for made in copies:
-        made.wait()
     for base in range(0, peers, step):
         for side in range(2):
-            index = as_row(tile_of(near_ref.at[side], 0, base // step).astype(jnp.int32))
+            index = as_row(tile_of(up_ref if side == 0 else down_ref, cx, base // step).astype(jnp.int32))
             values = 0.5 * as_row(
                 disp_ref[base : base + step, 0, (side + 1) * blk : (side + 2) * blk]
             )
@@ -252,35 +262,28 @@
         out_ref[...] = wide[0:peers, :] + pltpu.roll(wide[peers : 2 * peers, :], 64, axis=1)
 
 
-def shell(recv_ref, index_ref, disp_ref, stiff_ref, prev_ref, v_ref, up_ref, down_ref, low_ref,
-          low_up_ref, low_down_ref, high_ref, resp_ref, late_ref, v, packs, acc, rows_acc, cols_acc,
-          corner_acc, ext, dots, sems, v_sem):
+def shell(recv_ref, index_ref, disp_ref, stiff_ref, prev_ref, up_ref, down_ref, low_ref,
+          low_up_ref, low_down_ref, high_ref, v_ref, after_ref, resp_ref, late_ref, v, acc, rows_acc,
+          cols_acc, corner_acc, ext, dots, v_sem):
     sx, sy = disp_ref.shape
     peers, blk = index_ref.shape
-    extra = packs.shape[1]
-    index_planes = extra - 2
     load_tiles = peers // 8
+    index_planes = -(-2 * load_tiles // 8)
+    corner_planes = -(-(load_tiles + 4) // 8)
     chunks = sy // 128
     hist = v_ref.shape[0]
     v_copy = pltpu.make_async_copy(v_ref, v, v_sem.at[0])
     v_copy.start()
-    copy = starter(sems)
-    top = up_ref.shape[0] - extra
-    corner = low_up_ref.shape[0] - extra
-    low_planes = low_ref.shape[0] - (-(-extra // 4))
-    copies = [
-        copy(high_ref.at[pl.ds(0, extra)], packs.at[0]),
-        copy(up_ref.at[pl.ds(top, extra)], packs.at[2]),
-        copy(down_ref.at[pl.ds(top, extra)], packs.at[3]),
-        copy(high_ref.at[pl.ds(extra, extra)], packs.at[4]),
-        copy(high_ref.at[pl.ds(2 * extra, extra)], packs.at[5]),
-        copy(low_up_ref.at[pl.ds(corner, extra)], packs.at[6]),
-        copy(low_down_ref.at[pl.ds(corner, extra)], packs.at[7]),
+    top = up_ref.shape[0] - (index_planes + 2 + corner_planes)
+    low_top = low_ref.shape[0] - (index_planes + 1)
+    corner_top = low_up_ref.shape[0] - corner_planes
+    near_top = index_planes + 1
+    load_at = [
+        (high_ref, 0, load_tiles), (low_ref, low_top, load_tiles), (up_ref, top, load_tiles),
+        (down_ref, top, load_tiles), (high_ref, near_top, 0),
+        (high_ref, near_top + corner_planes, 0), (low_up_ref, corner_top, 0),
+        (low_down_ref, corner_top, 0),
     ]
-    for e in range(extra):
-        copies.append(
-            copy(low_ref.at[low_planes + e // 4, pl.ds(8 * (e % 4), 8)], packs.at[1, e])
-        )
 
     def accumulate(target, first, keys, height, lane, lanes, values):
         added = lax.dot_general(
@@ -299,14 +302,12 @@
         index = as_row(index_ref[base : base + 8, :])
         keys = ((index >> 7) & (chunks - 1)) * sx + index // sy
         accumulate(acc, base == 0, keys, sx * chunks, index & 127, 128, values_of(0, base))
-    for made in copies:
-        made.wait()
     for k, (dx, dy) in enumerate(NEAR):
         if k == 0:
             continue
         for base in range(0, peers, 8):
-            number = load_tiles + base // 8
-            index = as_row(tile_of(packs.at[k - 1], 0, number).astype(jnp.int32))
+            ref, plane, number = load_at[k - 1]
+            index = as_row(tile_of(ref, plane, number + base // 8).astype(jnp.int32))
             row = index // sy
             lane = index & (sy - 1)
             if dx == 1:
@@ -324,16 +325,16 @@
                     rows_acc, k == 1 and base == 0, keys, 8 * chunks, lane & 127, 128, values
                 )
             elif dx == 0:
-                accumulate(cols_acc, k == 3 and base == 0, row, sx, lane8, 8, values)
+                accumulate(cols_acc, k == 3 and base == 0, row, sx, lane8, 16, values)
             else:
-                accumulate(corner_acc, k == 5 and base == 0, row8, 8, lane8, 8, values)
-
-    ids = lax.broadcasted_iota(jnp.int32, (8, 128), 0)
-    lanes = lax.broadcasted_iota(jnp.int32, (8, 128), 1)
-    placed = (jnp.where(ids < 4, ids, ids + 120) == lanes).astype(F32)
+                accumulate(corner_acc, k == 5 and base == 0, row8, 16, lane8, 16, values)
+
+    ids = lax.broadcasted_iota(jnp.int32, (16, 128), 0)
+    lanes = lax.broadcasted_iota(jnp.int32, (16, 128), 1)
+    placed = (jnp.where(ids < 4, ids, jnp.where(ids < 8, ids + 120, -1)) == lanes).astype(F32)
 
     def widened(ref):
-        both = ref[:, 0:8] + ref[:, 8:16]
+        both = ref[:, 0:16] + ref[:, 16:32]
         return jnp.dot(both, placed, precision=lax.Precision.HIGHEST, preferred_element_type=F32)
 
     force, disp, stiff = ext.at[0], ext.at[1], ext.at[2]
@@ -345,38 +346,42 @@
         force[sx : sx + 8, at] = part[:, 0:128] + part[:, 128:256]
     side = slice(sy, sy + 128)
     force[0:sx, side] = widened(cols_acc)
-    force[sx : sx + 8, side] = widened(corner_acc)
+    force[sx : sx + 8, side] = widened(corner_acc)[0:8]
     sub = lax.broadcasted_iota(jnp.int32, (8, sy), 0) < 4
     sub1 = lax.broadcasted_iota(jnp.int32, (8, 128), 0) < 4
     lane = lax.broadcasted_iota(jnp.int32, (sx, 128), 1)
     lane1 = lax.broadcasted_iota(jnp.int32, (8, 128), 1)
     for kind, (target, own) in enumerate(((disp, disp_ref), (stiff, stiff_ref))):
 
-        def row_tile(pack, start, size):
-            at = kind * sy + start
-            return packs[pack, index_planes, :, at : at + size]
-
-        def col_tile(pack):
-            return jnp.concatenate(
-                [tile_of(packs.at[pack], index_planes + 1, m) for m in range(sx // 8)], axis=0
-            )
+        def row_tile(ref, plane):
+            return ref[plane, :, kind * sy : (kind + 1) * sy]
+
+        def col_tile(ref):
+            plane = top + index_planes + 1
+            return jnp.concatenate([tile_of(ref, plane, m) for m in range(sx // 8)], axis=0)
 
         target[0:sx, 0:sy] = own[...]
-        target[sx : sx + 8, 0:sy] = jnp.where(sub, row_tile(0, 0, sy), row_tile(1, 0, sy))
-        ahead, behind = col_tile(2), col_tile(3)
+        target[sx : sx + 8, 0:sy] = jnp.where(
+            sub, row_tile(high_ref, index_planes), row_tile(low_ref, low_top + index_planes)
+        )
+        ahead, behind = col_tile(up_ref), col_tile(down_ref)
         if kind == 0:
             behind = pltpu.roll(behind, 64, axis=1)
         else:
             ahead = pltpu.roll(ahead, 64, axis=1)
         target[0:sx, side] = jnp.where(lane < 32, ahead, jnp.where(lane >= 96, behind, 0.0))
 
-        def corner_tile(pack_ahead, pack_behind):
+        def corner_tile(ahead, ahead_plane, behind, behind_plane):
+            number = load_tiles + 2 * kind
             return jnp.where(
-                lane1 < 32, row_tile(pack_ahead, 0, 128),
-                jnp.where(lane1 >= 96, row_tile(pack_behind, sy - 128, 128), 0.0),
+                lane1 < 32, tile_of(ahead, ahead_plane, number),
+                jnp.where(lane1 >= 96, tile_of(behind, behind_plane, number + 1), 0.0),
             )
 
-        target[sx : sx + 8, side] = jnp.where(sub1, corner_tile(4, 5), corner_tile(6, 7))
+        target[sx : sx + 8, side] = jnp.where(
+            sub1, corner_tile(high_ref, near_top, high_ref, near_top + corner_planes),
+            corner_tile(low_up_ref, corner_top, low_down_ref, corner_top),
+        )
 
     load = force[...]
     k = stiff[...]
@@ -459,19 +464,23 @@
     out_ref[...] = total
 
 
-def pack(phi_ref, kappa_ref, after_ref, disp_ref, stiff_ref, cells_ref, loads_ref, up_ref, down_ref, low_ref,
-         low_up_ref, low_down_ref, own_ref, phi_lo, kap_lo, phi_hi, kap_hi, up, down, own, last,
-         in_sems, out_sems):
+def pack(phi_ref, kappa_ref, after_ref, gram_ref, disp_ref, stiff_ref, cells_ref, loads_ref,
+         up_ref, down_ref, low_ref, low_up_ref, low_down_ref, own_ref, phi_lo, kap_lo, phi_hi,
+         kap_hi, in_sems):
     cx, cy, cz = phi_ref.shape
     sx, sy = disp_ref.shape
     peers = cells_ref.shape[0]
-    extra = own.shape[0]
-    copy_in, copy_out = starter(in_sems), starter(out_sems)
+    tiles = peers // 8
+    index_planes = -(-2 * tiles // 8)
+    corner_planes = -(-(tiles + 4) // 8)
+    copy_in = starter(in_sems)
     depth = 8
-    lows = [
-        copy_in(phi_ref.at[pl.ds(cx - 4, 4)], last.at[pl.ds(0, 4)]),
-        copy_in(kappa_ref.at[pl.ds(cx - 3, 3)], last.at[pl.ds(4, 3)]),
-    ]
+    lows = []
+    for n, (ref, x) in enumerate(
+        [(phi_ref, x) for x in range(cx - 4, cx)] + [(kappa_ref, x) for x in range(cx - 3, cx)]
+    ):
+        for t in range(cy // 8):
+            lows.append(copy_in(ref.at[x, pl.ds(8 * t, 8)], low_ref.at[n * (cy // 8) + t]))
     groups = []
     for x in range(0, cx, depth):
         at = pl.ds(x, depth)
@@ -481,20 +490,23 @@
             copy_in(phi_ref.at[at, pl.ds(cy - 8, 8)], phi_hi.at[at]),
             copy_in(kappa_ref.at[at, pl.ds(cy - 8, 8)], kap_hi.at[at]),
         ])
-    outs = []
-    for n in range(2 * peers // 8):
-        source = cells_ref if n < peers // 8 else loads_ref
-        base = 8 * (n % (peers // 8))
-        own[n // 8, :, (n % 8) * 128 : (n % 8 + 1) * 128] = source[base : base + 8, :].astype(F32)
-    if 2 * peers % 64:
-        own[2 * peers // 64, :, 2 * peers % 64 * 16 :] = jnp.zeros(
-            (8, 1024 - 2 * peers % 64 * 16), F32
-        )
+    own_ref[...] = jnp.zeros_like(own_ref)
+
+    def put(plane, number, tile):
+        own_ref[plane + number // 8, :, (number % 8) * 128 : (number % 8 + 1) * 128] = tile
+
+    corner = index_planes + 2
+    for n in range(tiles):
+        put(0, n, cells_ref[8 * n : 8 * n + 8, :].astype(F32))
+        loads = loads_ref[8 * n : 8 * n + 8, :].astype(F32)
+        put(0, tiles + n, loads)
+        put(corner, n, loads)
     sub = lax.broadcasted_iota(jnp.int32, (8, sy), 0) < 4
     for kind, ref in enumerate((disp_ref, stiff_ref)):
-        own[extra - 2, :, kind * sy : (kind + 1) * sy] = jnp.where(
-            sub, ref[0:8, :], ref[sx - 8 : sx, :]
-        )
+        edge = jnp.where(sub, ref[0:8, :], ref[sx - 8 : sx, :])
+        own_ref[index_planes, :, kind * sy : (kind + 1) * sy] = edge
+        put(corner, tiles + 2 * kind, edge[:, 0:128])
+        put(corner, tiles + 2 * kind + 1, edge[:, sy - 128 : sy])
     lane = lax.broadcasted_iota(jnp.int32, (sx, 128), 1)
     first, final = slice(0, 128), slice(sy - 128, sy)
     columns = jnp.where(
@@ -505,63 +517,53 @@
         ),
     )
     for m in range(sx // 8):
-        own[extra - 1, :, m * 128 : (m + 1) * 128] = columns[8 * m : 8 * m + 8, :]
-    outs += [
-        copy_out(own, own_ref),
-        copy_out(own, up_ref.at[pl.ds(cx, extra)]),
-        copy_out(own, down_ref.at[pl.ds(cx, extra)]),
-        copy_out(own, low_up_ref.at[pl.ds(4, extra)]),
-        copy_out(own, low_down_ref.at[pl.ds(4, extra)]),
-    ]
-    for e in range(extra):
-        outs.append(copy_out(own.at[e], low_ref.at[7 + e // 4, pl.ds(8 * (e % 4), 8)]))
-    for made in lows:
-        made.wait()
-    outs.append(copy_out(last, low_ref.at[pl.ds(0, 7)]))
+        put(index_planes + 1, m, columns[8 * m : 8 * m + 8, :])
+    own = own_ref[...]
+    up_ref[cx:] = own
+    down_ref[cx:] = own
+    low_ref[7 * (cy // 8) :] = own[: index_planes + 1]
+    low_up_ref[3:] = own[corner:]
+    low_down_ref[3:] = own[corner:]
     upper = lax.broadcasted_iota(jnp.int32, (depth, 8, cz), 1) < 4
     for number, copies in enumerate(groups):
         for made in copies:
             made.wait()
-        x = number * depth
-        at = slice(x, x + depth)
-        up[at] = jnp.where(upper, phi_lo[at], pltpu.roll(kap_lo[at], 4, axis=1))
-        down[at] = jnp.where(upper, pltpu.roll(kap_hi[at], 4, axis=1), phi_hi[at])
-        at = pl.ds(x, depth)
-        outs.append(copy_out(up.at[at], up_ref.at[at]))
-        outs.append(copy_out(down.at[at], down_ref.at[at]))
-    at = pl.ds(cx - 4, 4)
-    outs.append(copy_out(up.at[at], low_up_ref.at[pl.ds(0, 4)]))
-    outs.append(copy_out(down.at[at], low_down_ref.at[pl.ds(0, 4)]))
-    for made in outs:
+        at = slice(number * depth, (number + 1) * depth)
+        up = jnp.where(upper, phi_lo[at], pltpu.roll(kap_lo[at], 4, axis=1))
+        down = jnp.where(upper, pltpu.roll(kap_hi[at], 4, axis=1), phi_hi[at])
+        up_ref[at] = up
+        down_ref[at] = down
+        if (number + 1) * depth == cx:
+            low_up_ref[0:3] = up[depth - 3 :]
+            low_down_ref[0:3] = down[depth - 3 :]
+    for made in lows:
         made.wait()
 
 
-def packed(phi, kappa, after, displacement, stiffness, cells, loads):
+def packed(phi, kappa, after, gram, displacement, stiffness, cells, loads):
     cx, cy, cz = phi.shape
-    peers = cells.shape[0]
-    extra = -(-2 * peers // 64) + 2
-
-    def shape(planes, rows=8):
-        return jax.ShapeDtypeStruct((planes, rows, cz), F32)
+    tiles = cells.shape[0] // 8
+    index_planes = -(-2 * tiles // 8)
+    corner_planes = -(-(tiles + 4) // 8)
+    extra = index_planes + 2 + corner_planes
+    low_planes = 7 * (cy // 8)
+
+    def shape(planes):
+        return jax.ShapeDtypeStruct((planes, 8, cz), F32)
 
     return pl.pallas_call(
         pack,
-        in_specs=hbm_specs(3) + vmem_specs(4),
-        out_specs=hbm_specs(6),
+        in_specs=hbm_specs(2) + any_specs(2) + vmem_specs(4),
+        out_specs=vmem_specs(6),
         out_shape=[
-            shape(cx + extra), shape(cx + extra), shape(7 + -(-extra // 4), cy),
-            shape(4 + extra), shape(4 + extra), shape(extra),
+            shape(cx + extra), shape(cx + extra), shape(low_planes + index_planes + 1),
+            shape(3 + corner_planes), shape(3 + corner_planes), shape(extra),
         ],
-        scratch_shapes=[pltpu.VMEM((cx, 8, cz), F32)] * 6
-        + [
-            pltpu.VMEM((extra, 8, cz), F32),
-            pltpu.VMEM((7, cy, cz), F32),
-            pltpu.SemaphoreType.DMA((cx // 2 + 2,)),
-            pltpu.SemaphoreType.DMA((32,)),
-        ],
+        scratch_shapes=[pltpu.VMEM((cx, 8, cz), F32)] * 4
+        + [pltpu.SemaphoreType.DMA((cx // 2 + low_planes,))],
         compiler_params=params(),
         name="pack",
-    )(phi, kappa, after, displacement, stiffness, cells, loads)
+    )(phi, kappa, after, gram, displacement, stiffness, cells, loads)
 
 
 def substep(src, kap, dst, plane, advect, cy, cz):
@@ -570,78 +572,108 @@
     lane = lax.broadcasted_iota(jnp.int32, (wide, 128), 1)
     first, last = lane == 0, lane == 127
 
-    def take(ref, at, q):
-        return ref[at, :, q * 128 : (q + 1) * 128]
+    def take(at, q, start=8):
+        return src[at, q, pl.ds(start, wide), :]
 
     for q in range(chunks):
-        now = take(src, plane, q)
-        left = take(src, plane, q - 1) if q else 0.0
-        right = take(src, plane, q + 1) if q + 1 < chunks else 0.0
+        now = take(plane, q)
+        left = take(plane, q - 1) if q else 0.0
+        right = take(plane, q + 1) if q + 1 < chunks else 0.0
         total = pltpu.roll(jnp.where(last, left, now), 1, axis=1) + pltpu.roll(
             jnp.where(first, right, now), 127, axis=1
         )
-        total = total + (pltpu.roll(now, 1, axis=0) + pltpu.roll(now, wide - 1, axis=0))
-        before = take(src, plane - 1, q)
-        total = total + (before + take(src, plane + 1, q))
-        dst[plane, :, q * 128 : (q + 1) * 128] = (
-            now + advect * (before - now) + take(kap, plane - 1, q) * (total - 6.0 * now)
-        )
+        total = total + (take(plane, q, 7) + take(plane, q, 9))
+        before = take(plane - 1, q)
+        total = total + (before + take(plane + 1, q))
+        new = now + advect * (before - now) + kap[plane - 1, q] * (total - 6.0 * now)
+        dst[plane, q, 8 : 8 + wide, :] = new
+        dst[plane, q, 7:8, :] = new[wide - 1 :]
+        dst[plane, q, 8 + wide : 9 + wide, :] = new[0:1]
 
 
 def fluid(x0, x1, cx, cy, cz, kind, *refs):
     planes = x1 - x0 + 8
+    wide = cy + 8
+    chunks = cz // 128
     names = ["phi", "kappa", "up", "down"]
-    names += {"wet": ["forced", "low", "low_up", "low_down"], "middle": ["forced", "wet"],
-              "end": ["high", "whole"]}[kind]
+    names += {"wet": ["forced", "low", "low_up", "low_down"],
+              "middle": ["forced", "wet", "near"], "end": ["high", "whole"]}[kind]
     names += {"wet": ["out", "send"]}.get(kind, ["out"])
-    names += ["a", "b", "kap", "upb", "downb", "sems", "out_sems"]
+    names += ["a", "b", "kap", "sems", "out_sems"]
     r = dict(zip(names, refs))
-    a, b, kap, upb, downb = r["a"], r["b"], r["kap"], r["upb"], r["downb"]
+    a, b, kap = r["a"], r["b"], r["kap"]
     is_last = lax.axis_index("gx") == lax.axis_size("gx") - 1
     copy, copy_out = starter(r["sems"]), starter(r["out_sems"])
 
+    def chunked(src, s0, count, dst, d0, row):
+        return [
+            copy(
+                src.at[pl.ds(s0, count), :, pl.ds(q * 128, 128)],
+                dst.at[pl.ds(d0, count), q, pl.ds(row, cy)],
+            )
+            for q in range(chunks)
+        ]
+
+    def unchunked(src, s0, count, row, rows, dst, d0):
+        return [
+            copy_out(
+                src.at[pl.ds(s0, count), q, pl.ds(row, rows)],
+                dst.at[pl.ds(d0, count), :, pl.ds(q * 128, 128)],
+            )
+            for q in range(chunks)
+        ]
+
     own0, own1 = max(0, x0 - 4), min(cx, x1 + 4)
     groups = []
-    if kind == "wet":
-        groups.append((0, 4, [
-            copy(r["low"].at[pl.ds(0, 4)], a.at[pl.ds(0, 4), pl.ds(0, cy)]),
-            copy(r["low"].at[pl.ds(4, 3)], kap.at[pl.ds(0, 3), pl.ds(0, cy)]),
-            copy(r["low_up"].at[pl.ds(0, 4)], upb.at[pl.ds(0, 4)]),
-            copy(r["low_down"].at[pl.ds(0, 4)], downb.at[pl.ds(0, 4)]),
-        ]))
-    for start in range(own0, own1, 4):
+    start = own0
+    while start < own1:
+        count = min(8, own1 - start)
         i = start - (x0 - 4)
-        k0, k1 = max(start, x0 - 3), min(start + 4, x1 + 3)
-        groups.append((i, i + 4, [
-            copy(r["phi"].at[pl.ds(start, 4)], a.at[pl.ds(i, 4), pl.ds(0, cy)]),
-            copy(r["up"].at[pl.ds(start, 4)], upb.at[pl.ds(i, 4)]),
-            copy(r["down"].at[pl.ds(start, 4)], downb.at[pl.ds(i, 4)]),
-            copy(r["kappa"].at[pl.ds(k0, k1 - k0)],
-                 kap.at[pl.ds(k0 - (x0 - 3), k1 - k0), pl.ds(0, cy)]),
-        ]))
-    if kind == "end":
-        i = cx - (x0 - 4)
-        groups.append((i, i + 4, [
-            copy(r["high"].at[pl.ds(0, 4)], a.at[pl.ds(i, 4)]),
-            copy(r["high"].at[pl.ds(4, 3)], kap.at[pl.ds(i - 1, 3)]),
-        ]))
+        k0, k1 = max(start, x0 - 3), min(start + count, x1 + 3)
+        groups.append((i, i + count, chunked(r["phi"], start, count, a, i, 8)
+                       + chunked(r["kappa"], k0, k1 - k0, kap, k0 - (x0 - 3), 0)))
+        start += count
     outs = []
     if kind == "middle":
         outs.append(copy_out(r["wet"], r["out"].at[pl.ds(0, x0)]))
 
     upper = lax.broadcasted_iota(jnp.int32, (8, cz), 0) < 4
 
-    def assemble(i0, i1):
-        for i in range(i0, i1):
-            x = x0 - 4 + i
-            if x >= cx:
-                continue
-            up, down = upb[i], downb[i]
-            a[i, cy : cy + 8, :] = jnp.where(upper, up, down)
-            if 1 <= i < planes - 1:
-                kap[i - 1, cy : cy + 8, :] = pltpu.roll(jnp.where(upper, down, up), 4, axis=0)
-            if "forced" in r and 0 <= x < r["forced"].shape[0]:
-                a[i] = a[i] + r["forced"][x]
+    def assemble(i):
+        x = x0 - 4 + i
+        inner = 1 <= i < planes - 1
+        if x >= cx:
+            for q in range(chunks):
+                at = slice(q * 128, (q + 1) * 128)
+                a[i, q, 8 : 8 + wide, :] = r["high"][x - cx, :, at]
+                if inner:
+                    kap[i - 1, q] = r["high"][4 + x - cx, :, at]
+        else:
+            if x >= 0:
+                up, down = r["up"][x], r["down"][x]
+            elif x > -4:
+                up, down = r["low_up"][x + 3], r["low_down"][x + 3]
+            else:
+                up = down = jnp.zeros((8, cz), F32)
+            edge = jnp.where(upper, up, down)
+            kedge = pltpu.roll(jnp.where(upper, down, up), 4, axis=0)
+            for q in range(chunks):
+                at = slice(q * 128, (q + 1) * 128)
+                if x < 0:
+                    for t in range(cy // 8):
+                        a[i, q, 8 + 8 * t : 16 + 8 * t, :] = r["low"][(x + 4) * (cy // 8) + t, :, at]
+                        if inner:
+                            kap[i - 1, q, 8 * t : 8 * t + 8, :] = r["low"][
+                                (x + 7) * (cy // 8) + t, :, at
+                            ]
+                a[i, q, 8 + cy : 8 + wide, :] = edge[:, at]
+                if inner:
+                    kap[i - 1, q, cy:wide, :] = kedge[:, at]
+                if "forced" in r and 0 <= x < r["forced"].shape[0]:
+                    a[i, q, 8 : 8 + wide, :] = a[i, q, 8 : 8 + wide, :] + r["forced"][x, :, at]
+        for q in range(chunks):
+            a[i, q, 7:8, :] = a[i, q, 7 + wide : 8 + wide, :]
+            a[i, q, 8 + wide : 9 + wide, :] = a[i, q, 8:9, :]
 
     def run(src, dst, lo, hi):
         def body(i, carry):
@@ -652,36 +684,41 @@
             substep(src, kap, dst, i, advect, cy, cz)
             return carry
 
-        lax.fori_loop(lo, hi, body, 0)
-
+        if hi > lo:
+            lax.fori_loop(lo, hi, body, 0)
+
+    if kind == "wet":
+        for i in range(4):
+            assemble(i)
     done = 1
     for i0, i1, copies in groups:
         for made in copies:
             made.wait()
-        assemble(i0, i1)
-        if kind == "wet" and i0 == 4:
-            outs.append(copy_out(a.at[pl.ds(4, 4)], r["send"].at[pl.ds(0, 4)]))
-            outs.append(copy_out(kap.at[pl.ds(3, 3)], r["send"].at[pl.ds(4, 3)]))
-        ready = i1 - 1
-        if ready > done:
-            run(a, b, done, ready)
-            done = ready
-    if kind == "wet":
-        for made in outs:
-            made.wait()
-        outs = []
+        for i in range(i0, i1):
+            assemble(i)
+        if kind == "wet":
+            for i in range(4, 8):
+                for q in range(chunks):
+                    at = slice(q * 128, (q + 1) * 128)
+                    r["send"][i - 4, :, at] = a[i, q, 8 : 8 + wide, :]
+                    if i < 7:
+                        r["send"][i, :, at] = kap[i - 1, q]
+        run(a, b, done, i1 - 1)
+        done = i1 - 1
+    if kind == "end":
+        for i in range(planes - 4, planes):
+            assemble(i)
+        run(a, b, done, planes - 1)
     run(b, a, 2, planes - 2)
     run(a, b, 3, planes - 3)
     for start in range(4, planes - 4, 4):
         run(b, a, start, start + 4)
         if kind == "wet":
             for i in range(start, start + 4):
-                r["out"][i - 4] = a[i, 0:cy, :]
+                for q in range(chunks):
+                    r["out"][i - 4, :, q * 128 : (q + 1) * 128] = a[i, q, 8 : 8 + cy, :]
         else:
-            x = x0 + start - 4
-            outs.append(
-                copy_out(a.at[pl.ds(start, 4), pl.ds(0, cy)], r["out"].at[pl.ds(x, 4)])
-            )
+            outs += unchunked(a, start, 4, 8, cy, r["out"], x0 + start - 4)
     for made in outs:
         made.wait()
 
@@ -692,30 +729,28 @@
     field = jax.ShapeDtypeStruct((cx, cy, cz), F32)
     whole = hbm_specs(1)[0]
     if kind == "wet":
-        specs = vmem_specs(1) + hbm_specs(3)
+        specs = vmem_specs(4)
         out_shape = [
             jax.ShapeDtypeStruct((x1 - x0, cy, cz), F32),
             jax.ShapeDtypeStruct((7, cy + 8, cz), F32),
         ]
-        out_specs = vmem_specs(1) + hbm_specs(1)
+        out_specs = vmem_specs(2)
     elif kind == "middle":
-        specs, out_shape, out_specs = vmem_specs(2), field, whole
+        specs, out_shape, out_specs = vmem_specs(2) + any_specs(1), field, whole
     else:
-        specs, out_shape, out_specs = hbm_specs(2), field, whole
+        specs, out_shape, out_specs = vmem_specs(1) + hbm_specs(1), field, whole
     cells = planes * (cy + 8) * cz
     return pl.pallas_call(
         functools.partial(fluid, x0, x1, cx, cy, cz, kind),
-        in_specs=hbm_specs(4) + specs,
+        in_specs=hbm_specs(2) + vmem_specs(2) + specs,
         out_specs=out_specs,
         out_shape=out_shape,
         scratch_shapes=[
-            pltpu.VMEM((planes, cy + 8, cz), F32),
-            pltpu.VMEM((planes, cy + 8, cz), F32),
-            pltpu.VMEM((planes - 2, cy + 8, cz), F32),
-            pltpu.VMEM((planes, 8, cz), F32),
-            pltpu.VMEM((planes, 8, cz), F32),
-            pltpu.SemaphoreType.DMA((48,)),
-            pltpu.SemaphoreType.DMA((12,)),
+            pltpu.VMEM((planes, cz // 128, cy + 24, 128), F32),
+            pltpu.VMEM((planes, cz // 128, cy + 24, 128), F32),
+            pltpu.VMEM((planes - 2, cz // 128, cy + 8, 128), F32),
+            pltpu.SemaphoreType.DMA((80,)),
+            pltpu.SemaphoreType.DMA((80,)),
         ],
         input_output_aliases={5: 0} if kind == "end" else {},
         compiler_params=params(),
@@ -773,34 +808,6 @@
         [pltpu.VMEM((peers, blk), F32)], "gather_disp", vmem_specs(2), displacement, ldof,
     )
     disp = exchange(sent)
-    up_send, down_send, low_send, low_up_send, low_down_send, own = packed(
-        phi, kappa, disp, displacement, stiffness, fcell, ldof
-    )
-    extra = own.shape[0]
-    low = shift(low_send, 1, 0)
-    up = shift(up_send, 0, -1)
-    down = shift(down_send, 0, 1)
-    low_up = shift(low_up_send, 1, -1)
-    low_down = shift(low_down_send, 1, 1)
-    near = shift(jnp.concatenate([own, up[cx:], down[cx:]], axis=0), -1, 0)
-
-    chunks = cz // 128
-    forced = call(
-        functools.partial(scatter_disp, cx, cy, cz), f32(wet_planes, cy + 8, cz),
-        [
-            pltpu.VMEM((wet_planes * cy * chunks, 256), F32),
-            pltpu.VMEM((512, wet_planes * 4 * chunks), F32),
-            pltpu.VMEM((2, (extra - 2) // 2 + (extra - 2) % 2, 8, cz), F32),
-            pltpu.SemaphoreType.DMA((2,)),
-        ],
-        "scatter_disp", vmem_specs(2) + hbm_specs(2), disp, fcell, up, down,
-    )
-    wet, send = fluid_call(
-        "wet", 0, wet_planes, phi, kappa, up, down, forced, low, low_up, low_down
-    )
-    high = shift(send, -1, 0)
-    middle = fluid_call("middle", wet_planes, cx - 4, phi, kappa, up, down, forced, wet)
-    field = fluid_call("end", cx - 4, cx, phi, kappa, up, down, high, middle)
     size = 8 * hist
     gram = call(
         gram_rows, f32(peers, 128),
@@ -812,6 +819,35 @@
         ],
         "gram_rows", hbm_specs(1), v_hist,
     )
+    up_send, down_send, low_send, low_up_send, low_down_send, own = packed(
+        phi, kappa, disp, gram, displacement, stiffness, fcell, ldof
+    )
+    index_planes = -(-2 * (peers // 8) // 8)
+    low = shift(low_send, 1, 0)
+    up = shift(up_send, 0, -1)
+    down = shift(down_send, 0, 1)
+    low_up = shift(low_up_send, 1, -1)
+    low_down = shift(low_down_send, 1, 1)
+    corner = cx + index_planes + 2
+    near = shift(
+        jnp.concatenate([own[: index_planes + 1], up[corner:], down[corner:]], axis=0), -1, 0
+    )
+
+    chunks = cz // 128
+    forced = call(
+        functools.partial(scatter_disp, cx, cy, cz), f32(wet_planes, cy + 8, cz),
+        [
+            pltpu.VMEM((wet_planes * cy * chunks, 256), F32),
+            pltpu.VMEM((512, wet_planes * 4 * chunks), F32),
+        ],
+        "scatter_disp", vmem_specs(4), disp, fcell, up, down,
+    )
+    wet, send = fluid_call(
+        "wet", 0, wet_planes, phi, kappa, up, down, forced, low, low_up, low_down
+    )
+    high = shift(send, -1, 0)
+    middle = fluid_call("middle", wet_planes, cx - 4, phi, kappa, up, down, forced, wet, near)
+    field = fluid_call("end", cx - 4, cx, phi, kappa, up, down, high, middle)
     press = call(
         functools.partial(gather_press, n_gx, n_gy), f32(peers, 1, (len(NEAR) + 1) * blk),
         [pltpu.VMEM((peers, blk), F32)], "gather_press", vmem_specs(3) + hbm_specs(1),
@@ -822,18 +858,17 @@
         shell, [f32(sx, sy), f32(peers, 1, 256)],
         [
             pltpu.VMEM((hist, sx, sy), F32),
-            pltpu.VMEM((8, extra, 8, cz), F32),
             pltpu.VMEM((sx * (sy // 128), 256), F32),
             pltpu.VMEM((8 * (sy // 128), 256), F32),
-            pltpu.VMEM((sx, 16), F32),
-            pltpu.VMEM((8, 16), F32),
+            pltpu.VMEM((sx, 32), F32),
+            pltpu.VMEM((16, 32), F32),
             pltpu.VMEM((3, sx + 8, sy + 128), F32),
             pltpu.VMEM((128, 128), F32),
-            pltpu.SemaphoreType.DMA((7 + extra,)),
             pltpu.SemaphoreType.DMA((1,)),
         ],
-        "shell", vmem_specs(5) + hbm_specs(7),
-        loads, ldof, displacement, stiffness, r_prev, v_hist, up, down, low, low_up, low_down, near,
+        "shell", vmem_specs(11) + hbm_specs(2),
+        loads, ldof, displacement, stiffness, r_prev, up, down, low, low_up, low_down, near,
+        v_hist, field,
     )
     x_next = call(
         solve, f32(sx, sy),

time: 166 us -> 183 us (1.10)
  waiting for transfers between devices: 23.2 us -> 45.5 us
  local copies, waits for them, and re-layouts: 6.16 us -> 27.4 us
  Pallas kernels: 82.9 us -> 65.6 us
  blocking collectives: 26.7 us -> 12.6 us
  starting transfers between devices: 24.9 us -> 29.9 us
    ppermute x7, waiting for transfers between devices: 23.2 us -> 45.5 us  [shift(): return lax.ppermute(value, axes, shifted_pairs(n_gx, n_gy, dx, dy))]
    unnamed x18 -> x56, local copies, waits for them, and re-layouts: 6.15 us -> 27.4 us
    pallas_call x6, Pallas kernels: 40.6 us -> 26.4 us  [call(): pl.pallas_call(body, in_specs=specs, out_specs=vmem_specs(len(out_shape))...]
    all_to_all x2 -> x1, blocking collectives: 26.7 us -> 12.6 us  [exchange(): return lax.all_to_all(value, axes, split_axis=0, concat_axis=0, tiled=True)]
    pallas_call x1, Pallas kernels: 5.66 us -> 2.27 us  [packed(): pl.pallas_call(pack, in_specs=hbm_specs(2) + any_specs(2) + vmem_specs(4)...]
    all_to_all x1 -> x2, starting transfers between devices: 9.45 us -> 12.5 us  [exchange(): return lax.all_to_all(value, axes, split_axis=0, concat_axis=0, tiled=True)]
    ppermute x7, starting transfers between devices: 15.5 us -> 17.4 us  [shift(): return lax.ppermute(value, axes, shifted_pairs(n_gx, n_gy, dx, dy))]
  transfers between devices with their start and end apart: 8 -> 9, of which waited for: 2 -> 2; matrix products, arithmetic and copies ran while one was open for 0% -> 0% of each run, Pallas kernels for 36% -> 24%
where the time goes in v2:
time: 183 us; the launch traced here: 182 us
  Pallas kernels  65.6 us (36%)
  waiting for transfers between devices  45.5 us (25%)
  starting transfers between devices  29.9 us (16%)
  local copies, waits for them, and re-layouts  27.4 us (15%)
  blocking collectives  12.6 us (7%)
    ppermute x7, waiting for transfers between devices, shift(): return lax.ppermute(value, axes, shifted_pairs(n_gx, n_gy, dx, dy))  45.5 us
    pallas_call x3, Pallas kernels, fluid_call(): pl.pallas_call(functools.partial(fluid, x0, x1, cx, cy, cz, kind), in_spe...  37 us
    unnamed x56, local copies, waits for them, and re-layouts  27.4 us
    pallas_call x6, Pallas kernels, call(): pl.pallas_call(body, in_specs=specs, out_specs=vmem_specs(len(out_shape))...  26.4 us
    ppermute x7, starting transfers between devices, shift(): return lax.ppermute(value, axes, shifted_pairs(n_gx, n_gy, dx, dy))  17.4 us
    all_to_all x1, blocking collectives, exchange(): return lax.all_to_all(value, axes, split_axis=0, concat_axis=0, tiled=True)  12.6 us
    all_to_all x2, starting transfers between devices, exchange(): return lax.all_to_all(value, axes, split_axis=0, concat_axis=0, tiled=True)  12.5 us
  transfers between devices with their start and end apart: 9, of which 2 were waited for; matrix products, arithmetic and copies ran while one was open for 0% of the time, Pallas kernels for 24%

profile of v2, /device:TPU:0, one launch (start us, length us, event | category | flops | bytes accessed | tf_op | source)
XLA Modules:
  0.0 182.2 jit_solution(336493179667783810)
XLA Ops:
  4.1 7.3 %all-to-all-start = ((f32[32,1,384]{2,1,0:T(1,128)}), f32[32,1,384]{2,1,0:T(1,128)S(1)}, u32[]{:S(2)}, u32[]{:S(2)}) async-start(f32[32,1,384]{2,1,0:T(1,128)} %gather_disp.1), calls=%async_computation | async-start | bytes 98304 | tf_op jit(solution)/shard_map/all_to_all | solution.py:789
  11.4 2.5 %copy-done.8 = f32[40,64,512]{2,1,0:T(8,128)S(1)} copy-done((f32[40,64,512]{2,1,0:T(8,128)S(1)}, f32[40,64,512]{2,1,0:T(8,128)}, u32[]{:S(2)}) %copy-start.8) | copy-done | bytes 5242904
  13.9 6.7 %gram_rows.1.gram_ref = f32[32,128]{1,0:T(8,128)S(1)} custom-call(f32[40,64,512]{2,1,0:T(8,128)S(1)} %copy-done.8), custom_call_target="tpu_custom_call" | custom-call | tf_op jit(solution)/shard_map/gram_rows/pallas_call | solution.py:793
  20.6 2.2 %copy-done = f32[32,32,1024]{2,1,0:T(8,128)S(1)} copy-done((f32[32,32,1024]{2,1,0:T(8,128)S(1)}, f32[32,32,1024]{2,1,0:T(8,128)}, u32[]{:S(2)}) %copy-start) | copy-done | bytes 4194328
  22.8 2.2 %copy-done.3 = f32[32,32,1024]{2,1,0:T(8,128)S(1)} copy-done((f32[32,32,1024]{2,1,0:T(8,128)S(1)}, f32[32,32,1024]{2,1,0:T(8,128)}, u32[]{:S(2)}) %copy-start.3) | copy-done | bytes 4194328
  25.0 2.3 %pack.1 = (f32[36,8,1024]{2,1,0:T(8,128)S(1)}, f32[36,8,1024]{2,1,0:T(8,128)S(1)}, f32[30,8,1024]{2,1,0:T(8,128)S(1)}, f32[4,8,1024]{2,1,0:T(8,128)S(1)}, f32[4,...) custom-call(f32[32,32,1024]{2,1,0:T(8,128)S(1)} %copy-done, f32[32,32,1024]{2,1,0:T(8,128)S(1)} %copy-done.3, ...), custom_call_target="tpu_custom_call" | custom-call | tf_op jit(solution)/shard_map/pack/pallas_call | solution.py:554
  28.7 3.1 %collective-permute-start.1 = (f32[36,8,1024]{2,1,0:T(8,128)S(1)}, f32[36,8,1024]{2,1,0:T(8,128)S(1)}, u32[]{:S(2)}, u32[]{:S(2)}) collective-permute-start(f32[36,8,1024]{2,1,0:T(8,128)S(1)} %get-tuple-element.13), channel_id=1, source_target_pairs={{0,1},{1,2},{2,3},{4,5},{5,6},{6,7},{8,9},{9,10},{10,11},{12,13},{... | collective-permute-start | bytes 3538952 | tf_op jit(solution)/shard_map/ppermute | solution.py:786
  31.8 3.7 %collective-permute-start.2 = (f32[30,8,1024]{2,1,0:T(8,128)S(1)}, f32[30,8,1024]{2,1,0:T(8,128)S(1)}, u32[]{:S(2)}, u32[]{:S(2)}) collective-permute-start(f32[30,8,1024]{2,1,0:T(8,128)S(1)} %get-tuple-element.14), channel_id=1, source_target_pairs={{0,4},{1,5},{2,6},{3,7},{4,8},{5,9},{6,10},{7,11},{8,12},{9,13},{1... | collective-permute-start | bytes 2949128 | tf_op jit(solution)/shard_map/ppermute | solution.py:786
  36.2 5.9 %collective-permute-start.4 = (f32[4,8,1024]{2,1,0:T(8,128)S(1)}, f32[4,8,1024]{2,1,0:T(8,128)S(1)}, u32[]{:S(2)}, u32[]{:S(2)}) collective-permute-start(f32[4,8,1024]{2,1,0:T(8,128)S(1)} %get-tuple-element.16), channel_id=1, source_target_pairs={{0,5},{1,6},{2,7},{4,9},{5,10},{6,11},{8,13},{9,14},{10,15},{12,17... | collective-permute-start | bytes 393224 | tf_op jit(solution)/shard_map/ppermute | solution.py:786
  42.2 4.6 %scatter_disp.1.refs_4_ = f32[4,40,1024]{2,1,0:T(8,128)S(1)} custom-call(f32[32,1,384]{2,1,0:T(1,128)S(1)} %all-to-all-done.after_ref.disp_ref, s32[32,128]{1,0:T(8,128)S(1)} %bitcast.3, f32[36,8,1024]{2,1,0:T(8,128)S(1)} %collective-permute-done.up_ref.refs_2_, f32[36,8,1024]{2,1,0:T(8,128)S(1)} %collective-permute-done.1.down_ref.refs_3_), custom_call_target="tpu_custom_call" | custom-call | tf_op jit(solution)/shard_map/scatter_disp/pallas_call | solution.py:793
  46.8 14.7 %collective-permute-done.4.refs_7_.low_down_ref = f32[4,8,1024]{2,1,0:T(8,128)S(1)} collective-permute-done((f32[4,8,1024]{2,1,0:T(8,128)S(1)}, f32[4,8,1024]{2,1,0:T(8,128)S(1)}, u32[]{:S(2)}, u32[]{:S(2)}) %collective-permute-start.4) | collective-permute-done | bytes 131104 | tf_op jit(solution)/shard_map/ppermute | solution.py:786
  61.5 7.5 %fluid_wet.1 = (f32[4,32,1024]{2,1,0:T(8,128)S(1)}, f32[7,40,1024]{2,1,0:T(8,128)}) custom-call(f32[32,32,1024]{2,1,0:T(8,128)S(1)} %copy-done.1, f32[32,32,1024]{2,1,0:T(8,128)S(1)} %copy-done.4, f32[36,8,1024]{2,1,0:T(8,128)S(1)} %collective-permute-done.up_ref.refs_2_, f32[36,8,1024]{2,1,0:T(8,128)S(1)} %collective-permute-done.1.down_ref.refs_3_, ...), custom_call_target="tpu_custom_call" | custom-call | flops 23592960 | bytes 5898240 | tf_op jit(solution)/shard_map/fluid_wet/pallas_call | solution.py:743
  71.8 30.7 %collective-permute-done.6.refs_6_.high_ref = f32[4,8,1024]{2,1,0:T(8,128)S(1)} collective-permute-done((f32[4,8,1024]{2,1,0:T(8,128)S(1)}, f32[4,8,1024]{2,1,0:T(8,128)S(1)}, u32[]{:S(2)}, u32[]{:S(2)}) %collective-permute-start.6) | collective-permute-done | bytes 131104 | tf_op jit(solution)/shard_map/ppermute | solution.py:786
  102.5 21.1 %fluid_middle.1.refs_5_.after_ref = f32[32,32,1024]{2,1,0:T(8,128)} custom-call(f32[32,32,1024]{2,1,0:T(8,128)S(1)} %copy-done.1, f32[32,32,1024]{2,1,0:T(8,128)S(1)} %copy-done.4, f32[36,8,1024]{2,1,0:T(8,128)S(1)} %collective-permute-done.up_ref.refs_2_, f32[36,8,1024]{2,1,0:T(8,128)S(1)} %collective-permute-done.1.down_ref.refs_3_, ...), custom_call_target="tpu_custom_call" | custom-call | flops 62914560 | bytes 15728640 | tf_op jit(solution)/shard_map/fluid_middle/pallas_call | solution.py:743
  123.6 2.2 %copy-done.6 = f32[32,32,1024]{2,1,0:T(8,128)S(1)} copy-done((f32[32,32,1024]{2,1,0:T(8,128)S(1)}, f32[32,32,1024]{2,1,0:T(8,128)}, u32[]{:S(2)}) %copy-start.6) | copy-done | bytes 4194328
  125.8 2.5 %gather_press.1 = f32[32,1,1280]{2,1,0:T(1,128)S(1)} custom-call(f32[4,32,1024]{2,1,0:T(8,128)S(1)} %get-tuple-element.18.refs_5_.wet_ref, s32[32,128]{1,0:T(8,128)S(1)} %bitcast.4, f32[32,128]{1,0:T(8,128)S(1)} %gram_rows.1.gram_ref, f32[32,32,1024]{2,1,0:T(8,128)S(1)} %copy-done.6), custom_call_target="tpu_custom_call" | custom-call | tf_op jit(solution)/shard_map/gather_press/pallas_call | solution.py:793
  129.0 5.2 %all-to-all-start.1 = ((f32[32,1,1280]{2,1,0:T(1,128)}), f32[32,1,1280]{2,1,0:T(1,128)}, u32[]{:S(2)}, u32[]{:S(2)}) async-start(f32[32,1,1280]{2,1,0:T(1,128)} %copy-done.13), calls=%async_computation.1 | async-start | bytes 327680 | tf_op jit(solution)/shard_map/all_to_all | solution.py:789
  136.4 2.2 %copy-done.5 = f32[32,32,1024]{2,1,0:T(8,128)S(1)} copy-done((f32[32,32,1024]{2,1,0:T(8,128)S(1)}, f32[32,32,1024]{2,1,0:T(8,128)}, u32[]{:S(2)}) %copy-start.5) | copy-done | bytes 4194328
  138.5 8.4 %fluid_end.1.after_ref = f32[32,32,1024]{2,1,0:T(8,128)} custom-call(f32[32,32,1024]{2,1,0:T(8,128)S(1)} %copy-done.2, f32[32,32,1024]{2,1,0:T(8,128)S(1)} %copy-done.5, f32[36,8,1024]{2,1,0:T(8,128)S(1)} %collective-permute-done.up_ref.refs_2_, f32[36,8,1024]{2,1,0:T(8,128)S(1)} %collective-permute-done.1.down_ref.refs_3_, ...), custom_call_target="tpu_custom_call", output_to_operand_aliasing={{}: (5, {})} | custom-call | flops 23592960 | bytes 5898240 | tf_op jit(solution)/shard_map/fluid_end/pallas_call | solution.py:743
  149.2 2.5 %copy-done.9 = f32[40,64,512]{2,1,0:T(8,128)S(1)} copy-done((f32[40,64,512]{2,1,0:T(8,128)S(1)}, f32[40,64,512]{2,1,0:T(8,128)}, u32[]{:S(2)}) %copy-start.9) | copy-done | bytes 5242904
  156.2 5.8 %shell.1 = (f32[64,512]{1,0:T(8,128)S(1)}, f32[32,1,256]{2,1,0:T(1,128)S(1)}) custom-call(f32[32,1,1280]{2,1,0:T(1,128)} %all-to-all-done.1.recv_ref, s32[32,128]{1,0:T(8,128)S(1)} %bitcast.7, f32[64,512]{1,0:T(8,128)S(1)} %copy-done.12, f32[64,512]{1,0:T(8,128)S(1)} %copy-done.15, f32[64,512]{1,0:T(8,128)S(1)} %copy-done.26, ...), custom_call_target="tpu_custom_call" | custom-call | tf_op jit(solution)/shard_map/shell/pallas_call | solution.py:793
  161.9 12.6 %all_to_all.15.recv_ref = f32[32,1,256]{2,1,0:T(1,128)S(1)} all-to-all(f32[32,1,256]{2,1,0:T(1,128)S(1)} %get-tuple-element.20), channel_id=1, replica_groups=mesh['gx'=8,'gy'=4] {'gx','gy'}, dimensions={0} | all-to-all | bytes 65536 | tf_op jit(solution)/shard_map/all_to_all | solution.py:789
  174.6 2.5 %copy-done.10 = f32[40,64,512]{2,1,0:T(8,128)S(1)} copy-done((f32[40,64,512]{2,1,0:T(8,128)S(1)}, f32[40,64,512]{2,1,0:T(8,128)}, u32[]{:S(2)}) %copy-start.10) | copy-done | bytes 5242904
  177.1 5.0 %solve.1 = f32[64,512]{1,0:T(8,128)} custom-call(f32[32,1,256]{2,1,0:T(1,128)S(1)} %all_to_all.15.recv_ref, f32[64,512]{1,0:T(8,128)S(1)} %get-tuple-element.21.resp_ref, f32[64,512]{1,0:T(8,128)S(1)} %copy-done.27, f32[40,64,512]{2,1,0:T(8,128)S(1)} %copy-done.10), custom_call_target="tpu_custom_call" | custom-call | tf_op jit(solution)/shard_map/solve/pallas_call | solution.py:793
  (65 shorter events, 17.8 us)
Async XLA Ops:
  2.3 18.3 %copy-start.12 = (f32[64,512]{1,0:T(8,128)S(1)}, f32[64,512]{1,0:T(8,128)}, u32[]{:S(2)}) copy-start(f32[64,512]{1,0:T(8,128)} %disp_ref.5) | copy-start | bytes 393220
  2.3 18.3 %copy-start.14 = (f32[64,512]{1,0:T(8,128)S(1)}, f32[64,512]{1,0:T(8,128)}, u32[]{:S(2)}) copy-start(f32[64,512]{1,0:T(8,128)} %stiff_ref.3) | copy-start | bytes 393220
  2.3 18.4 %copy-start.22 = (s32[1,1,32,128]{3,2,1,0:T(8,128)S(1)}, s32[1,1,32,128]{3,2,1,0:T(8,128)}, u32[]{:S(2)}) copy-start(s32[1,1,32,128]{3,2,1,0:T(8,128)} %param.13) | copy-start | bytes 49156
  2.3 18.4 %copy-start.24 = (s32[1,1,32,128]{3,2,1,0:T(8,128)S(1)}, s32[1,1,32,128]{3,2,1,0:T(8,128)}, u32[]{:S(2)}) copy-start(s32[1,1,32,128]{3,2,1,0:T(8,128)} %param.14) | copy-start | bytes 49156
  4.1 16.5 %all-to-all-start = ((f32[32,1,384]{2,1,0:T(1,128)}), f32[32,1,384]{2,1,0:T(1,128)S(1)}, u32[]{:S(2)}, u32[]{:S(2)}) async-start(f32[32,1,384]{2,1,0:T(1,128)} %gather_disp.1), calls=%async_computation | async-start | bytes 98304 | tf_op jit(solution)/shard_map/all_to_all | solution.py:789
  11.4 2.5 %copy-start.8 = (f32[40,64,512]{2,1,0:T(8,128)S(1)}, f32[40,64,512]{2,1,0:T(8,128)}, u32[]{:S(2)}) copy-start(f32[40,64,512]{2,1,0:T(8,128)} %v_ref.3) | copy-start | bytes 15728644
  20.6 2.2 %copy-start = (f32[32,32,1024]{2,1,0:T(8,128)S(1)}, f32[32,32,1024]{2,1,0:T(8,128)}, u32[]{:S(2)}) copy-start(f32[32,32,1024]{2,1,0:T(8,128)} %refs_0_.5) | copy-start | bytes 12582916
  25.0 36.5 %copy-start.1 = (f32[32,32,1024]{2,1,0:T(8,128)S(1)}, f32[32,32,1024]{2,1,0:T(8,128)}, u32[]{:S(2)}) copy-start(f32[32,32,1024]{2,1,0:T(8,128)} %refs_0_.5) | copy-start | bytes 12582916
  25.0 36.5 %copy-start.4 = (f32[32,32,1024]{2,1,0:T(8,128)S(1)}, f32[32,32,1024]{2,1,0:T(8,128)}, u32[]{:S(2)}) copy-start(f32[32,32,1024]{2,1,0:T(8,128)} %refs_1_.5) | copy-start | bytes 12582916
  27.3 14.9 %collective-permute-start = (f32[36,8,1024]{2,1,0:T(8,128)S(1)}, f32[36,8,1024]{2,1,0:T(8,128)S(1)}, u32[]{:S(2)}, u32[]{:S(2)}) collective-permute-start(f32[36,8,1024]{2,1,0:T(8,128)S(1)} %get-tuple-element.12), channel_id=1, source_target_pairs={{1,0},{2,1},{3,2},{5,4},{6,5},{7,6},{9,8},{10,9},{11,10},{13,12},{... | collective-permute-start | bytes 3538952 | tf_op jit(solution)/shard_map/ppermute | solution.py:786
  28.7 13.5 %collective-permute-start.1 = (f32[36,8,1024]{2,1,0:T(8,128)S(1)}, f32[36,8,1024]{2,1,0:T(8,128)S(1)}, u32[]{:S(2)}, u32[]{:S(2)}) collective-permute-start(f32[36,8,1024]{2,1,0:T(8,128)S(1)} %get-tuple-element.13), channel_id=1, source_target_pairs={{0,1},{1,2},{2,3},{4,5},{5,6},{6,7},{8,9},{9,10},{10,11},{12,13},{... | collective-permute-start | bytes 3538952 | tf_op jit(solution)/shard_map/ppermute | solution.py:786
  31.8 29.7 %collective-permute-start.2 = (f32[30,8,1024]{2,1,0:T(8,128)S(1)}, f32[30,8,1024]{2,1,0:T(8,128)S(1)}, u32[]{:S(2)}, u32[]{:S(2)}) collective-permute-start(f32[30,8,1024]{2,1,0:T(8,128)S(1)} %get-tuple-element.14), channel_id=1, source_target_pairs={{0,4},{1,5},{2,6},{3,7},{4,8},{5,9},{6,10},{7,11},{8,12},{9,13},{1... | collective-permute-start | bytes 2949128 | tf_op jit(solution)/shard_map/ppermute | solution.py:786
  35.6 11.2 %collective-permute-start.3 = (f32[4,8,1024]{2,1,0:T(8,128)S(1)}, f32[4,8,1024]{2,1,0:T(8,128)S(1)}, u32[]{:S(2)}, u32[]{:S(2)}) collective-permute-start(f32[4,8,1024]{2,1,0:T(8,128)S(1)} %get-tuple-element.15), channel_id=1, source_target_pairs={{1,4},{2,5},{3,6},{5,8},{6,9},{7,10},{9,12},{10,13},{11,14},{13,16... | collective-permute-start | bytes 393224 | tf_op jit(solution)/shard_map/ppermute | solution.py:786
  36.2 25.3 %collective-permute-start.4 = (f32[4,8,1024]{2,1,0:T(8,128)S(1)}, f32[4,8,1024]{2,1,0:T(8,128)S(1)}, u32[]{:S(2)}, u32[]{:S(2)}) collective-permute-start(f32[4,8,1024]{2,1,0:T(8,128)S(1)} %get-tuple-element.16), channel_id=1, source_target_pairs={{0,5},{1,6},{2,7},{4,9},{5,10},{6,11},{8,13},{9,14},{10,15},{12,17... | collective-permute-start | bytes 393224 | tf_op jit(solution)/shard_map/ppermute | solution.py:786
  46.8 22.3 %copy-start.16 = (f32[4,8,1024]{2,1,0:T(8,128)}, f32[4,8,1024]{2,1,0:T(8,128)S(1)}, u32[]{:S(2)}) copy-start(f32[4,8,1024]{2,1,0:T(8,128)S(1)} %collective-permute-done.3.refs_6_.low_up_ref) | copy-start | bytes 393220
  61.5 7.6 %copy-start.18 = (f32[4,8,1024]{2,1,0:T(8,128)}, f32[4,8,1024]{2,1,0:T(8,128)S(1)}, u32[]{:S(2)}) copy-start(f32[4,8,1024]{2,1,0:T(8,128)S(1)} %collective-permute-done.4.refs_7_.low_down_ref) | copy-start | bytes 393220
  69.1 65.1 %collective-permute-start.5 = (f32[7,40,1024]{2,1,0:T(8,128)}, f32[7,40,1024]{2,1,0:T(8,128)}, u32[]{:S(2)}, u32[]{:S(2)}) collective-permute-start(f32[7,40,1024]{2,1,0:T(8,128)} %get-tuple-element.17), channel_id=1, source_target_pairs={{4,0},{5,1},{6,2},{7,3},{8,4},{9,5},{10,6},{11,7},{12,8},{13,9},{1... | collective-permute-start | bytes 3440648 | tf_op jit(solution)/shard_map/ppermute | solution.py:786
  70.5 32.0 %collective-permute-start.6 = (f32[4,8,1024]{2,1,0:T(8,128)S(1)}, f32[4,8,1024]{2,1,0:T(8,128)S(1)}, u32[]{:S(2)}, u32[]{:S(2)}) collective-permute-start(f32[4,8,1024]{2,1,0:T(8,128)S(1)} %pad_maximum_fusion), channel_id=1, source_target_pairs={{4,0},{5,1},{6,2},{7,3},{8,4},{9,5},{10,6},{11,7},{12,8},{13,9},{1... | collective-permute-start | bytes 393224 | tf_op jit(solution)/shard_map/ppermute | solution.py:786
  102.5 21.1 %copy-start.20 = (f32[4,8,1024]{2,1,0:T(8,128)}, f32[4,8,1024]{2,1,0:T(8,128)S(1)}, u32[]{:S(2)}) copy-start(f32[4,8,1024]{2,1,0:T(8,128)S(1)} %collective-permute-done.6.refs_6_.high_ref) | copy-start | bytes 393220
  129.0 18.0 %all-to-all-start.1 = ((f32[32,1,1280]{2,1,0:T(1,128)}), f32[32,1,1280]{2,1,0:T(1,128)}, u32[]{:S(2)}, u32[]{:S(2)}) async-start(f32[32,1,1280]{2,1,0:T(1,128)} %copy-done.13), calls=%async_computation.1 | async-start | bytes 327680 | tf_op jit(solution)/shard_map/all_to_all | solution.py:789
  138.5 8.4 %copy-start.25 = (s32[1,1,32,128]{3,2,1,0:T(8,128)S(1)}, s32[1,1,32,128]{3,2,1,0:T(8,128)}, u32[]{:S(2)}) copy-start(s32[1,1,32,128]{3,2,1,0:T(8,128)} %param.14) | copy-start | bytes 49156
  149.2 2.5 %copy-start.9 = (f32[40,64,512]{2,1,0:T(8,128)S(1)}, f32[40,64,512]{2,1,0:T(8,128)}, u32[]{:S(2)}) copy-start(f32[40,64,512]{2,1,0:T(8,128)} %v_ref.3) | copy-start | bytes 15728644
  156.2 18.4 %copy-start.27 = (f32[64,512]{1,0:T(8,128)S(1)}, f32[64,512]{1,0:T(8,128)}, u32[]{:S(2)}) copy-start(f32[64,512]{1,0:T(8,128)} %prev_ref.3) | copy-start | bytes 393220
  174.6 2.5 %copy-start.10 = (f32[40,64,512]{2,1,0:T(8,128)S(1)}, f32[40,64,512]{2,1,0:T(8,128)}, u32[]{:S(2)}) copy-start(f32[40,64,512]{2,1,0:T(8,128)} %w_ref.1) | copy-start | bytes 15728644
  (13 other events, 17.8 us)

commit v3 on v2

--- a/solution.py
+++ b/solution.py
@@ -10,7 +10,7 @@
 NSUB = 4
 SWEEPS = 3
 HIST = 40
-VMEM_BYTES = 32 * 1024 * 1024
+VMEM_BYTES = 50 * 1024 * 1024
 F32 = jnp.float32
 BF16 = jnp.bfloat16
 
@@ -464,7 +464,7 @@
     out_ref[...] = total
 
 
-def pack(phi_ref, kappa_ref, after_ref, gram_ref, disp_ref, stiff_ref, cells_ref, loads_ref,
+def pack(phi_ref, kappa_ref, after_ref, disp_ref, stiff_ref, cells_ref, loads_ref,
          up_ref, down_ref, low_ref, low_up_ref, low_down_ref, own_ref, phi_lo, kap_lo, phi_hi,
          kap_hi, in_sems):
     cx, cy, cz = phi_ref.shape
@@ -540,7 +540,7 @@
         made.wait()
 
 
-def packed(phi, kappa, after, gram, displacement, stiffness, cells, loads):
+def packed(phi, kappa, after, displacement, stiffness, cells, loads):
     cx, cy, cz = phi.shape
     tiles = cells.shape[0] // 8
     index_planes = -(-2 * tiles // 8)
@@ -553,7 +553,7 @@
 
     return pl.pallas_call(
         pack,
-        in_specs=hbm_specs(2) + any_specs(2) + vmem_specs(4),
+        in_specs=hbm_specs(2) + any_specs(1) + vmem_specs(4),
         out_specs=vmem_specs(6),
         out_shape=[
             shape(cx + extra), shape(cx + extra), shape(low_planes + index_planes + 1),
@@ -563,7 +563,7 @@
         + [pltpu.SemaphoreType.DMA((cx // 2 + low_planes,))],
         compiler_params=params(),
         name="pack",
-    )(phi, kappa, after, gram, displacement, stiffness, cells, loads)
+    )(phi, kappa, after, displacement, stiffness, cells, loads)
 
 
 def substep(src, kap, dst, plane, advect, cy, cz):
@@ -596,8 +596,8 @@
     wide = cy + 8
     chunks = cz // 128
     names = ["phi", "kappa", "up", "down"]
-    names += {"wet": ["forced", "low", "low_up", "low_down"],
-              "middle": ["forced", "wet", "near"], "end": ["high", "whole"]}[kind]
+    names += {"wet": ["forced", "low", "low_up", "low_down", "near", "gram"],
+              "middle": ["forced", "wet"], "end": ["high", "whole"]}[kind]
     names += {"wet": ["out", "send"]}.get(kind, ["out"])
     names += ["a", "b", "kap", "sems", "out_sems"]
     r = dict(zip(names, refs))
@@ -729,14 +729,14 @@
     field = jax.ShapeDtypeStruct((cx, cy, cz), F32)
     whole = hbm_specs(1)[0]
     if kind == "wet":
-        specs = vmem_specs(4)
+        specs = vmem_specs(4) + any_specs(2)
         out_shape = [
             jax.ShapeDtypeStruct((x1 - x0, cy, cz), F32),
             jax.ShapeDtypeStruct((7, cy + 8, cz), F32),
         ]
         out_specs = vmem_specs(2)
     elif kind == "middle":
-        specs, out_shape, out_specs = vmem_specs(2) + any_specs(1), field, whole
+        specs, out_shape, out_specs = vmem_specs(2), field, whole
     else:
         specs, out_shape, out_specs = vmem_specs(1) + hbm_specs(1), field, whole
     cells = planes * (cy + 8) * cz
@@ -820,7 +820,7 @@
         "gram_rows", hbm_specs(1), v_hist,
     )
     up_send, down_send, low_send, low_up_send, low_down_send, own = packed(
-        phi, kappa, disp, gram, displacement, stiffness, fcell, ldof
+        phi, kappa, disp, displacement, stiffness, fcell, ldof
     )
     index_planes = -(-2 * (peers // 8) // 8)
     low = shift(low_send, 1, 0)
@@ -843,10 +843,10 @@
         "scatter_disp", vmem_specs(4), disp, fcell, up, down,
     )
     wet, send = fluid_call(
-        "wet", 0, wet_planes, phi, kappa, up, down, forced, low, low_up, low_down
+        "wet", 0, wet_planes, phi, kappa, up, down, forced, low, low_up, low_down, near, gram
     )
     high = shift(send, -1, 0)
-    middle = fluid_call("middle", wet_planes, cx - 4, phi, kappa, up, down, forced, wet, near)
+    middle = fluid_call("middle", wet_planes, cx - 4, phi, kappa, up, down, forced, wet)
     field = fluid_call("end", cx - 4, cx, phi, kappa, up, down, high, middle)
     press = call(
         functools.partial(gather_press, n_gx, n_gy), f32(peers, 1, (len(NEAR) + 1) * blk),

time: 183 us -> 141 us (0.77)
  waiting for transfers between devices: 45.5 us -> 9.77 us
  local copies, waits for them, and re-layouts: 27.4 us -> 7.82 us
  blocking collectives: 12.6 us -> 27.3 us
  starting transfers between devices: 29.9 us -> 22.4 us
  Pallas kernels: 65.6 us -> 71.5 us
    ppermute x7, waiting for transfers between devices: 45.5 us -> 9.77 us  [shift(): return lax.ppermute(value, axes, shifted_pairs(n_gx, n_gy, dx, dy))]
    unnamed x56 -> x40, local copies, waits for them, and re-layouts: 27.4 us -> 7.81 us
    all_to_all x1 -> x2, blocking collectives: 12.6 us -> 27.3 us  [exchange(): return lax.all_to_all(value, axes, split_axis=0, concat_axis=0, tiled=True)]
    all_to_all x2 -> x1, starting transfers between devices: 12.5 us -> 6.89 us  [exchange(): return lax.all_to_all(value, axes, split_axis=0, concat_axis=0, tiled=True)]
    pallas_call x3, Pallas kernels: 37 us -> 41.7 us  [fluid_call(): pl.pallas_call(functools.partial(fluid, x0, x1, cx, cy, cz, kind), in_spe...]
    ppermute x7, starting transfers between devices: 17.4 us -> 15.5 us  [shift(): return lax.ppermute(value, axes, shifted_pairs(n_gx, n_gy, dx, dy))]
  transfers between devices with their start and end apart: 9 -> 8, of which waited for: 2 -> 1; matrix products, arithmetic and copies ran while one was open for 0% -> 0% of each run, Pallas kernels for 24% -> 33%
where the time goes in v3:
time: 141 us; the launch traced here: 140 us
  Pallas kernels  71.5 us (51%)
  blocking collectives  27.3 us (19%)
  starting transfers between devices  22.4 us (16%)
  waiting for transfers between devices  9.77 us (7%)
  local copies, waits for them, and re-layouts  7.82 us (6%)
    pallas_call x3, Pallas kernels, fluid_call(): pl.pallas_call(functools.partial(fluid, x0, x1, cx, cy, cz, kind), in_spe...  41.7 us
    all_to_all x2, blocking collectives, exchange(): return lax.all_to_all(value, axes, split_axis=0, concat_axis=0, tiled=True)  27.3 us
    pallas_call x6, Pallas kernels, call(): pl.pallas_call(body, in_specs=specs, out_specs=vmem_specs(len(out_shape))...  26.7 us
    ppermute x7, starting transfers between devices, shift(): return lax.ppermute(value, axes, shifted_pairs(n_gx, n_gy, dx, dy))  15.5 us
    ppermute x7, waiting for transfers between devices, shift(): return lax.ppermute(value, axes, shifted_pairs(n_gx, n_gy, dx, dy))  9.77 us
    unnamed x40, local copies, waits for them, and re-layouts  7.81 us
    all_to_all x1, starting transfers between devices, exchange(): return lax.all_to_all(value, axes, split_axis=0, concat_axis=0, tiled=True)  6.89 us
    pallas_call x1, Pallas kernels, packed(): pl.pallas_call(pack, in_specs=hbm_specs(2) + any_specs(1) + vmem_specs(4)...  3.04 us
  transfers between devices with their start and end apart: 8, of which 1 were waited for; matrix products, arithmetic and copies ran while one was open for 0% of the time, Pallas kernels for 33%

profile of v3, /device:TPU:0, one launch (start us, length us, event | category | flops | bytes accessed | tf_op | source)
XLA Modules:
  0.0 139.9 jit_solution(5818570808173615232)
XLA Ops:
  2.3 1.2 gather_disp.1
  3.5 14.4 %all_to_all.15.after_ref.disp_ref = f32[32,1,384]{2,1,0:T(1,128)S(1)} all-to-all(f32[32,1,384]{2,1,0:T(1,128)S(1)} %gather_disp.1), channel_id=1, replica_groups=mesh['gx'=8,'gy'=4] {'gx','gy'}, dimensions={0} | all-to-all | bytes 98304 | tf_op jit(solution)/shard_map/all_to_all | solution.py:789
  17.9 0.9 copy-done.6
  19.5 3.0 %pack.1 = (f32[36,8,1024]{2,1,0:T(8,128)S(1)}, f32[36,8,1024]{2,1,0:T(8,128)S(1)}, f32[30,8,1024]{2,1,0:T(8,128)S(1)}, f32[4,8,1024]{2,1,0:T(8,128)S(1)}, f32[4,...) custom-call(f32[32,32,1024]{2,1,0:T(8,128)} %refs_0_.5, f32[32,32,1024]{2,1,0:T(8,128)} %refs_1_.5, ...), custom_call_target="tpu_custom_call" | custom-call | tf_op jit(solution)/shard_map/pack/pallas_call | solution.py:554
  22.6 1.3 collective-permute-start
  23.9 3.1 %collective-permute-start.1 = (f32[36,8,1024]{2,1,0:T(8,128)S(1)}, f32[36,8,1024]{2,1,0:T(8,128)S(1)}, u32[]{:S(2)}, u32[]{:S(2)}) collective-permute-start(f32[36,8,1024]{2,1,0:T(8,128)S(1)} %get-tuple-element.13), channel_id=1, source_target_pairs={{0,1},{1,2},{2,3},{4,5},{5,6},{6,7},{8,9},{9,10},{10,11},{12,13},{... | collective-permute-start | bytes 3538952 | tf_op jit(solution)/shard_map/ppermute | solution.py:786
  27.0 2.5 %collective-permute-start.2 = (f32[30,8,1024]{2,1,0:T(8,128)S(1)}, f32[30,8,1024]{2,1,0:T(8,128)S(1)}, u32[]{:S(2)}, u32[]{:S(2)}) collective-permute-start(f32[30,8,1024]{2,1,0:T(8,128)S(1)} %get-tuple-element.14), channel_id=1, source_target_pairs={{0,4},{1,5},{2,6},{3,7},{4,8},{5,9},{6,10},{7,11},{8,12},{9,13},{1... | collective-permute-start | bytes 2949128 | tf_op jit(solution)/shard_map/ppermute | solution.py:786
  30.2 4.9 %collective-permute-start.4 = (f32[4,8,1024]{2,1,0:T(8,128)S(1)}, f32[4,8,1024]{2,1,0:T(8,128)S(1)}, u32[]{:S(2)}, u32[]{:S(2)}) collective-permute-start(f32[4,8,1024]{2,1,0:T(8,128)S(1)} %get-tuple-element.16), channel_id=1, source_target_pairs={{0,5},{1,6},{2,7},{4,9},{5,10},{6,11},{8,13},{9,14},{10,15},{12,17... | collective-permute-start | bytes 393224 | tf_op jit(solution)/shard_map/ppermute | solution.py:786
  35.2 1.5 %collective-permute-start.5 = (f32[4,8,1024]{2,1,0:T(8,128)S(1)}, f32[4,8,1024]{2,1,0:T(8,128)S(1)}, u32[]{:S(2)}, u32[]{:S(2)}) collective-permute-start(f32[4,8,1024]{2,1,0:T(8,128)S(1)} %pad_maximum_fusion), channel_id=1, source_target_pairs={{4,0},{5,1},{6,2},{7,3},{8,4},{9,5},{10,6},{11,7},{12,8},{13,9},{1... | collective-permute-start | bytes 393224 | tf_op jit(solution)/shard_map/ppermute | solution.py:786
  36.7 7.3 %gram_rows.1.refs_9_.gram_ref = f32[32,128]{1,0:T(8,128)S(1)} custom-call(f32[40,64,512]{2,1,0:T(8,128)} %v_ref.3), custom_call_target="tpu_custom_call" | custom-call | tf_op jit(solution)/shard_map/gram_rows/pallas_call | solution.py:793
  44.0 4.6 %scatter_disp.1.refs_4_ = f32[4,40,1024]{2,1,0:T(8,128)S(1)} custom-call(f32[32,1,384]{2,1,0:T(1,128)S(1)} %all_to_all.15.after_ref.disp_ref, s32[32,128]{1,0:T(8,128)S(1)} %bitcast.3, f32[36,8,1024]{2,1,0:T(8,128)S(1)} %collective-permute-done.up_ref.refs_2_, f32[36,8,1024]{2,1,0:T(8,128)S(1)} %collective-permute-done.1.down_ref.refs_3_), custom_call_target="tpu_custom_call" | custom-call | tf_op jit(solution)/shard_map/scatter_disp/pallas_call | solution.py:793
  48.6 9.8 %collective-permute-done.4.refs_7_.low_down_ref = f32[4,8,1024]{2,1,0:T(8,128)S(1)} collective-permute-done((f32[4,8,1024]{2,1,0:T(8,128)S(1)}, f32[4,8,1024]{2,1,0:T(8,128)S(1)}, u32[]{:S(2)}, u32[]{:S(2)}) %collective-permute-start.4) | collective-permute-done | bytes 131104 | tf_op jit(solution)/shard_map/ppermute | solution.py:786
  58.4 10.3 %fluid_wet.1 = (f32[4,32,1024]{2,1,0:T(8,128)S(1)}, f32[7,40,1024]{2,1,0:T(8,128)}) custom-call(f32[32,32,1024]{2,1,0:T(8,128)} %refs_0_.5, f32[32,32,1024]{2,1,0:T(8,128)} %refs_1_.5, f32[36,8,1024]{2,1,0:T(8,128)} %copy-done, f32[36,8,1024]{2,1,0:T(8,128)} %copy-done.2, f32[4,40,1024]{2,1,0:T(8,128)S(1)} %scatter_disp.1.refs_4_, ...), custom_call_target="tpu_custom_call" | custom-call | flops 23592960 | bytes 5898240 | tf_op jit(solution)/shard_map/fluid_wet/pallas_call | solution.py:743
  68.7 1.5 %collective-permute-start.6 = (f32[7,40,1024]{2,1,0:T(8,128)}, f32[7,40,1024]{2,1,0:T(8,128)}, u32[]{:S(2)}, u32[]{:S(2)}) collective-permute-start(f32[7,40,1024]{2,1,0:T(8,128)} %get-tuple-element.18), channel_id=1, source_target_pairs={{4,0},{5,1},{6,2},{7,3},{8,4},{9,5},{10,6},{11,7},{12,8},{13,9},{1... | collective-permute-start | bytes 3440648 | tf_op jit(solution)/shard_map/ppermute | solution.py:786
  70.2 21.7 %fluid_middle.1.refs_5_.after_ref = f32[32,32,1024]{2,1,0:T(8,128)} custom-call(f32[32,32,1024]{2,1,0:T(8,128)} %refs_0_.5, f32[32,32,1024]{2,1,0:T(8,128)} %refs_1_.5, f32[36,8,1024]{2,1,0:T(8,128)S(1)} %copy-done.1, f32[36,8,1024]{2,1,0:T(8,128)S(1)} %copy-done.3, f32[4,40,1024]{2,1,0:T(8,128)S(1)} %scatter_disp.1.refs_4_, ...), custom_call_target="tpu_custom_call" | custom-call | flops 62914560 | bytes 15728640 | tf_op jit(solution)/shard_map/fluid_middle/pallas_call | solution.py:743
  92.0 3.2 %gather_press.1 = f32[32,1,1280]{2,1,0:T(1,128)} custom-call(f32[4,32,1024]{2,1,0:T(8,128)S(1)} %get-tuple-element.19.refs_5_.wet_ref, s32[32,128]{1,0:T(8,128)S(1)} %bitcast.4, f32[32,128]{1,0:T(8,128)S(1)} %gram_rows.1.refs_9_.gram_ref, f32[32,32,1024]{2,1,0:T(8,128)} %fluid_middle.1.refs_5_.after_ref), custom_call_target="tpu_custom_call" | custom-call | tf_op jit(solution)/shard_map/gather_press/pallas_call | solution.py:793
  95.1 6.9 %all-to-all-start.1 = ((f32[32,1,1280]{2,1,0:T(1,128)}), f32[32,1,1280]{2,1,0:T(1,128)}, u32[]{:S(2)}, u32[]{:S(2)}) async-start(f32[32,1,1280]{2,1,0:T(1,128)} %gather_press.1), calls=%async_computation.1 | async-start | bytes 327680 | tf_op jit(solution)/shard_map/all_to_all | solution.py:789
  102.1 9.7 %fluid_end.1.after_ref = f32[32,32,1024]{2,1,0:T(8,128)} custom-call(f32[32,32,1024]{2,1,0:T(8,128)} %refs_0_.5, f32[32,32,1024]{2,1,0:T(8,128)} %refs_1_.5, f32[36,8,1024]{2,1,0:T(8,128)S(1)} %copy-done.1, f32[36,8,1024]{2,1,0:T(8,128)S(1)} %copy-done.3, f32[7,40,1024]{2,1,0:T(8,128)} %collective-permute-done.6.refs_4_, ...), custom_call_target="tpu_custom_call", output_to_operand_aliasing={{}: (5, {})} | custom-call | flops 23592960 | bytes 5898240 | tf_op jit(solution)/shard_map/fluid_end/pallas_call | solution.py:743
  112.7 0.9 copy-done.9
  113.6 0.9 copy-done.11
  115.5 0.9 copy-done.18
  116.4 5.9 %shell.1 = (f32[64,512]{1,0:T(8,128)S(1)}, f32[32,1,256]{2,1,0:T(1,128)S(1)}) custom-call(f32[32,1,1280]{2,1,0:T(1,128)} %all-to-all-done.1.recv_ref, s32[32,128]{1,0:T(8,128)S(1)} %bitcast.7, f32[64,512]{1,0:T(8,128)S(1)} %copy-done.5, f32[64,512]{1,0:T(8,128)S(1)} %copy-done.7, f32[64,512]{1,0:T(8,128)S(1)} %copy-done.18, f32[36,8,1024]{2,1,0:T(8,128)S(1)} %copy-done.1, ...), custom_call_target="tpu_custom_call" | custom-call | tf_op jit(solution)/shard_map/shell/pallas_call | solution.py:793
  122.2 12.8 %all_to_all.16.recv_ref = f32[32,1,256]{2,1,0:T(1,128)S(1)} all-to-all(f32[32,1,256]{2,1,0:T(1,128)S(1)} %get-tuple-element.20), channel_id=1, replica_groups=mesh['gx'=8,'gy'=4] {'gx','gy'}, dimensions={0} | all-to-all | bytes 65536 | tf_op jit(solution)/shard_map/all_to_all | solution.py:789
  135.1 4.7 %solve.1 = f32[64,512]{1,0:T(8,128)} custom-call(f32[32,1,256]{2,1,0:T(1,128)S(1)} %all_to_all.16.recv_ref, f32[64,512]{1,0:T(8,128)S(1)} %get-tuple-element.21.resp_ref, f32[64,512]{1,0:T(8,128)S(1)} %copy-done.19, f32[40,64,512]{2,1,0:T(8,128)} %w_ref.1), custom_call_target="tpu_custom_call" | custom-call | tf_op jit(solution)/shard_map/solve/pallas_call | solution.py:793
  (48 shorter events, 4.9 us)
Async XLA Ops:
  0.6 0.9 copy-start.4
  17.9 0.9 copy-start.6
  22.6 21.4 %copy-start.15 = (s32[1,1,32,128]{3,2,1,0:T(8,128)S(1)}, s32[1,1,32,128]{3,2,1,0:T(8,128)}, u32[]{:S(2)}) copy-start(s32[1,1,32,128]{3,2,1,0:T(8,128)} %param.13) | copy-start | bytes 49156
  22.6 12.5 %collective-permute-start = (f32[36,8,1024]{2,1,0:T(8,128)S(1)}, f32[36,8,1024]{2,1,0:T(8,128)S(1)}, u32[]{:S(2)}, u32[]{:S(2)}) collective-permute-start(f32[36,8,1024]{2,1,0:T(8,128)S(1)} %get-tuple-element.12), channel_id=1, source_target_pairs={{1,0},{2,1},{3,2},{5,4},{6,5},{7,6},{9,8},{10,9},{11,10},{13,12},{... | collective-permute-start | bytes 3538952 | tf_op jit(solution)/shard_map/ppermute | solution.py:786
  23.9 11.3 %collective-permute-start.1 = (f32[36,8,1024]{2,1,0:T(8,128)S(1)}, f32[36,8,1024]{2,1,0:T(8,128)S(1)}, u32[]{:S(2)}, u32[]{:S(2)}) collective-permute-start(f32[36,8,1024]{2,1,0:T(8,128)S(1)} %get-tuple-element.13), channel_id=1, source_target_pairs={{0,1},{1,2},{2,3},{4,5},{5,6},{6,7},{8,9},{9,10},{10,11},{12,13},{... | collective-permute-start | bytes 3538952 | tf_op jit(solution)/shard_map/ppermute | solution.py:786
  27.0 31.4 %collective-permute-start.2 = (f32[30,8,1024]{2,1,0:T(8,128)S(1)}, f32[30,8,1024]{2,1,0:T(8,128)S(1)}, u32[]{:S(2)}, u32[]{:S(2)}) collective-permute-start(f32[30,8,1024]{2,1,0:T(8,128)S(1)} %get-tuple-element.14), channel_id=1, source_target_pairs={{0,4},{1,5},{2,6},{3,7},{4,8},{5,9},{6,10},{7,11},{8,12},{9,13},{1... | collective-permute-start | bytes 2949128 | tf_op jit(solution)/shard_map/ppermute | solution.py:786
  29.6 19.0 %collective-permute-start.3 = (f32[4,8,1024]{2,1,0:T(8,128)S(1)}, f32[4,8,1024]{2,1,0:T(8,128)S(1)}, u32[]{:S(2)}, u32[]{:S(2)}) collective-permute-start(f32[4,8,1024]{2,1,0:T(8,128)S(1)} %get-tuple-element.15), channel_id=1, source_target_pairs={{1,4},{2,5},{3,6},{5,8},{6,9},{7,10},{9,12},{10,13},{11,14},{13,16... | collective-permute-start | bytes 393224 | tf_op jit(solution)/shard_map/ppermute | solution.py:786
  30.2 28.1 %collective-permute-start.4 = (f32[4,8,1024]{2,1,0:T(8,128)S(1)}, f32[4,8,1024]{2,1,0:T(8,128)S(1)}, u32[]{:S(2)}, u32[]{:S(2)}) collective-permute-start(f32[4,8,1024]{2,1,0:T(8,128)S(1)} %get-tuple-element.16), channel_id=1, source_target_pairs={{0,5},{1,6},{2,7},{4,9},{5,10},{6,11},{8,13},{9,14},{10,15},{12,17... | collective-permute-start | bytes 393224 | tf_op jit(solution)/shard_map/ppermute | solution.py:786
  35.1 13.4 %copy-start = (f32[36,8,1024]{2,1,0:T(8,128)}, f32[36,8,1024]{2,1,0:T(8,128)S(1)}, u32[]{:S(2)}) copy-start(f32[36,8,1024]{2,1,0:T(8,128)S(1)} %collective-permute-done.up_ref.refs_2_) | copy-start | bytes 3538948
  35.2 13.4 %copy-start.2 = (f32[36,8,1024]{2,1,0:T(8,128)}, f32[36,8,1024]{2,1,0:T(8,128)S(1)}, u32[]{:S(2)}) copy-start(f32[36,8,1024]{2,1,0:T(8,128)S(1)} %collective-permute-done.1.down_ref.refs_3_) | copy-start | bytes 3538948
  35.2 23.2 %collective-permute-start.5 = (f32[4,8,1024]{2,1,0:T(8,128)S(1)}, f32[4,8,1024]{2,1,0:T(8,128)S(1)}, u32[]{:S(2)}, u32[]{:S(2)}) collective-permute-start(f32[4,8,1024]{2,1,0:T(8,128)S(1)} %pad_maximum_fusion), channel_id=1, source_target_pairs={{4,0},{5,1},{6,2},{7,3},{8,4},{9,5},{10,6},{11,7},{12,8},{13,9},{1... | collective-permute-start | bytes 393224 | tf_op jit(solution)/shard_map/ppermute | solution.py:786
  48.6 20.1 %copy-start.8 = (f32[4,8,1024]{2,1,0:T(8,128)}, f32[4,8,1024]{2,1,0:T(8,128)S(1)}, u32[]{:S(2)}) copy-start(f32[4,8,1024]{2,1,0:T(8,128)S(1)} %collective-permute-done.3.refs_6_.low_up_ref) | copy-start | bytes 393220
  48.6 21.6 %copy-start.1 = (f32[36,8,1024]{2,1,0:T(8,128)S(1)}, f32[36,8,1024]{2,1,0:T(8,128)}, u32[]{:S(2)}) copy-start(f32[36,8,1024]{2,1,0:T(8,128)} %copy-done) | copy-start | bytes 3538948
  48.6 21.6 %copy-start.3 = (f32[36,8,1024]{2,1,0:T(8,128)S(1)}, f32[36,8,1024]{2,1,0:T(8,128)}, u32[]{:S(2)}) copy-start(f32[36,8,1024]{2,1,0:T(8,128)} %copy-done.2) | copy-start | bytes 3538948
  58.4 10.3 %copy-start.10 = (f32[4,8,1024]{2,1,0:T(8,128)}, f32[4,8,1024]{2,1,0:T(8,128)S(1)}, u32[]{:S(2)}) copy-start(f32[4,8,1024]{2,1,0:T(8,128)S(1)} %collective-permute-done.4.refs_7_.low_down_ref) | copy-start | bytes 393220
  58.4 10.3 %copy-start.12 = (f32[4,8,1024]{2,1,0:T(8,128)}, f32[4,8,1024]{2,1,0:T(8,128)S(1)}, u32[]{:S(2)}) copy-start(f32[4,8,1024]{2,1,0:T(8,128)S(1)} %collective-permute-done.5.refs_8_.high_ref) | copy-start | bytes 393220
  68.7 33.4 %collective-permute-start.6 = (f32[7,40,1024]{2,1,0:T(8,128)}, f32[7,40,1024]{2,1,0:T(8,128)}, u32[]{:S(2)}, u32[]{:S(2)}) collective-permute-start(f32[7,40,1024]{2,1,0:T(8,128)} %get-tuple-element.18), channel_id=1, source_target_pairs={{4,0},{5,1},{6,2},{7,3},{8,4},{9,5},{10,6},{11,7},{12,8},{13,9},{1... | collective-permute-start | bytes 3440648 | tf_op jit(solution)/shard_map/ppermute | solution.py:786
  95.1 16.7 %all-to-all-start.1 = ((f32[32,1,1280]{2,1,0:T(1,128)}), f32[32,1,1280]{2,1,0:T(1,128)}, u32[]{:S(2)}, u32[]{:S(2)}) async-start(f32[32,1,1280]{2,1,0:T(1,128)} %gather_press.1), calls=%async_computation.1 | async-start | bytes 327680 | tf_op jit(solution)/shard_map/all_to_all | solution.py:789
  102.0 9.8 %copy-start.5 = (f32[64,512]{1,0:T(8,128)S(1)}, f32[64,512]{1,0:T(8,128)}, u32[]{:S(2)}) copy-start(f32[64,512]{1,0:T(8,128)} %disp_ref.5) | copy-start | bytes 393220
  102.1 9.8 %copy-start.17 = (s32[1,1,32,128]{3,2,1,0:T(8,128)S(1)}, s32[1,1,32,128]{3,2,1,0:T(8,128)}, u32[]{:S(2)}) copy-start(s32[1,1,32,128]{3,2,1,0:T(8,128)} %param.14) | copy-start | bytes 49156
  111.8 0.9 copy-start.7
  114.6 0.9 copy-start.13
  115.5 0.9 copy-start.18
  116.4 18.7 %copy-start.19 = (f32[64,512]{1,0:T(8,128)S(1)}, f32[64,512]{1,0:T(8,128)}, u32[]{:S(2)}) copy-start(f32[64,512]{1,0:T(8,128)} %prev_ref.3) | copy-start | bytes 393220
  (4 other events, 3.2 us)

commit v4 on v3

--- a/solution.py
+++ b/solution.py
@@ -116,9 +116,11 @@
     return copy
 
 
-def gather_disp(n_gy, disp_ref, index_ref, out_ref, own_ref):
+def gather_disp(n_gy, small_ref, numbers_ref, out_ref, own_ref):
+    disp_ref = small_ref.at[0]
+    peers, blk = own_ref.shape
+    index_ref = numbers_ref.at[pl.ds(peers, peers)]
     sx, sy = disp_ref.shape
-    peers, blk = index_ref.shape
     chunk_bits = (sy // 128).bit_length() - 1
     columns = []
     for q in range(sy // 128):
@@ -139,9 +141,10 @@
     out_ref[:, 0, 2 * blk : 3 * blk] = jnp.where(beside == 0, 0.0, pltpu.roll(own, 1, axis=0))
 
 
-def scatter_disp(cx, cy, cz, disp_ref, cells_ref, up_ref, down_ref, out_ref, acc_ref, side_ref):
+def scatter_disp(cx, cy, cz, disp_ref, numbers_ref, up_ref, down_ref, out_ref, acc_ref, side_ref):
     planes = out_ref.shape[0]
-    peers, blk = cells_ref.shape
+    peers, blk = disp_ref.shape[0], numbers_ref.shape[1]
+    cells_ref = numbers_ref.at[pl.ds(0, peers)]
     rows = planes * cy
     chunks = cz // 128
     row_bits = cz.bit_length() - 1
@@ -191,9 +194,10 @@
         out_ref[:, cy : cy + 8, q * 256 : (q + 1) * 256] = part.reshape(planes, 8, 256)
 
 
-def gather_press(n_gx, n_gy, wet_ref, index_ref, gram_ref, after_ref, out_ref, own_ref):
+def gather_press(n_gx, n_gy, wet_ref, numbers_ref, gram_ref, after_ref, out_ref, own_ref):
+    index_ref = numbers_ref.at[pl.ds(0, own_ref.shape[0])]
     planes, cy, cz = wet_ref.shape
-    peers, blk = index_ref.shape
+    peers, blk = own_ref.shape
     rows = planes * cy
     chunks = cz // 256
     columns = []
@@ -262,11 +266,13 @@
         out_ref[...] = wide[0:peers, :] + pltpu.roll(wide[peers : 2 * peers, :], 64, axis=1)
 
 
-def shell(recv_ref, index_ref, disp_ref, stiff_ref, prev_ref, up_ref, down_ref, low_ref,
+def shell(recv_ref, numbers_ref, small_ref, up_ref, down_ref, low_ref,
           low_up_ref, low_down_ref, high_ref, v_ref, after_ref, resp_ref, late_ref, v, acc, rows_acc,
           cols_acc, corner_acc, ext, dots, v_sem):
+    disp_ref, stiff_ref, prev_ref = small_ref.at[0], small_ref.at[1], small_ref.at[2]
     sx, sy = disp_ref.shape
-    peers, blk = index_ref.shape
+    peers, blk = recv_ref.shape[0], numbers_ref.shape[1]
+    index_ref = numbers_ref.at[pl.ds(peers, peers)]
     load_tiles = peers // 8
     index_planes = -(-2 * load_tiles // 8)
     corner_planes = -(-(load_tiles + 4) // 8)
@@ -426,9 +432,10 @@
     late_ref[:, 0, 128:256] = jnp.broadcast_to(gram, (peers, 128))
 
 
-def solve(recv_ref, resp_ref, prev_ref, w_ref, out_ref, w, sems):
+def solve(recv_ref, resp_ref, small_ref, w_ref, out_ref, w, sems):
     peers = recv_ref.shape[0]
     hist = w_ref.shape[0]
+    prev_ref = small_ref.at[3]
     sx, sy = resp_ref.shape
     w_copy = pltpu.make_async_copy(w_ref, w, sems.at[0])
     w_copy.start()
@@ -464,12 +471,13 @@
     out_ref[...] = total
 
 
-def pack(phi_ref, kappa_ref, after_ref, disp_ref, stiff_ref, cells_ref, loads_ref,
-         up_ref, down_ref, low_ref, low_up_ref, low_down_ref, own_ref, phi_lo, kap_lo, phi_hi,
+def pack(phi_ref, kappa_ref, after_ref, small_ref, numbers_ref, up_ref, down_ref, low_ref, low_up_ref, low_down_ref, own_ref, phi_lo, kap_lo, phi_hi,
          kap_hi, in_sems):
     cx, cy, cz = phi_ref.shape
+    disp_ref, stiff_ref = small_ref.at[0], small_ref.at[1]
     sx, sy = disp_ref.shape
-    peers = cells_ref.shape[0]
+    peers = numbers_ref.shape[0] // 2
+    cells_ref, loads_ref = numbers_ref.at[pl.ds(0, peers)], numbers_ref.at[pl.ds(peers, peers)]
     tiles = peers // 8
     index_planes = -(-2 * tiles // 8)
     corner_planes = -(-(tiles + 4) // 8)
@@ -540,9 +548,9 @@
         made.wait()
 
 
-def packed(phi, kappa, after, displacement, stiffness, cells, loads):
+def packed(phi, kappa, after, small, numbers):
     cx, cy, cz = phi.shape
-    tiles = cells.shape[0] // 8
+    tiles = numbers.shape[0] // 16
     index_planes = -(-2 * tiles // 8)
     corner_planes = -(-(tiles + 4) // 8)
     extra = index_planes + 2 + corner_planes
@@ -553,7 +561,7 @@
 
     return pl.pallas_call(
         pack,
-        in_specs=hbm_specs(2) + any_specs(1) + vmem_specs(4),
+        in_specs=hbm_specs(2) + any_specs(1) + vmem_specs(2),
         out_specs=vmem_specs(6),
         out_shape=[
             shape(cx + extra), shape(cx + extra), shape(low_planes + index_planes + 1),
@@ -563,32 +571,52 @@
         + [pltpu.SemaphoreType.DMA((cx // 2 + low_planes,))],
         compiler_params=params(),
         name="pack",
-    )(phi, kappa, after, displacement, stiffness, cells, loads)
-
-
-def substep(src, kap, dst, plane, advect, cy, cz):
+    )(phi, kappa, after, small, numbers)
+
+
+def band(ref):
+    row = lax.broadcasted_iota(jnp.int32, (256, 256), 0)
+    column = lax.broadcasted_iota(jnp.int32, (256, 256), 1)
+    inner = jnp.where(jnp.abs(row - column) == 1, 1.0, 0.0).astype(BF16)
+    row, column = row[0:128], column[0:128]
+    target = jnp.where(row == 0, 255, jnp.where(row == 127, 0, -1))
+    outer = jnp.where(column == target, 1.0, 0.0).astype(BF16)
+    ref[...] = jnp.concatenate([inner, inner, outer, outer], axis=0)
+
+
+def substeps(src, kap, dst, near, plane, count, advect, cy, cz):
     wide = cy + 8
     chunks = cz // 128
-    lane = lax.broadcasted_iota(jnp.int32, (wide, 128), 1)
-    first, last = lane == 0, lane == 127
+    ahead = lax.broadcasted_iota(jnp.int32, (wide, 128), 1) < 64
 
     def take(at, q, start=8):
         return src[at, q, pl.ds(start, wide), :]
 
-    for q in range(chunks):
-        now = take(plane, q)
-        left = take(plane, q - 1) if q else 0.0
-        right = take(plane, q + 1) if q + 1 < chunks else 0.0
-        total = pltpu.roll(jnp.where(last, left, now), 1, axis=1) + pltpu.roll(
-            jnp.where(first, right, now), 127, axis=1
-        )
-        total = total + (take(plane, q, 7) + take(plane, q, 9))
-        before = take(plane - 1, q)
-        total = total + (before + take(plane + 1, q))
-        new = now + advect * (before - now) + kap[plane - 1, q] * (total - 6.0 * now)
-        dst[plane, q, 8 : 8 + wide, :] = new
-        dst[plane, q, 7:8, :] = new[wide - 1 :]
-        dst[plane, q, 8 + wide : 9 + wide, :] = new[0:1]
+    own, edge = [], []
+    zero = jnp.zeros((wide, 128), F32)
+    for p in range(count):
+        for q in range(0, chunks, 2):
+            own.append(jnp.concatenate([take(plane + p, q), take(plane + p, q + 1)], axis=1))
+            before = take(plane + p, q - 1) if q else zero
+            after = take(plane + p, q + 2) if q + 2 < chunks else zero
+            edge.append(jnp.where(ahead, after, before))
+    parts = pieces(jnp.concatenate(own, axis=0), 2) + pieces(jnp.concatenate(edge, axis=0), 2)
+    beside = jnp.dot(jnp.concatenate(parts, axis=1), near[...], preferred_element_type=F32)
+    for p in range(count):
+        at = plane + p
+        for q in range(chunks):
+            now = take(at, q)
+            row = (p * chunks + q) // 2 * wide
+            lane = q % 2 * 128
+            total = beside[row : row + wide, lane : lane + 128]
+            total = total + (take(at, q, 7) + take(at, q, 9))
+            before = take(at - 1, q)
+            total = total + (before + take(at + 1, q))
+            k = kap[at - 1, :, q * 128 : (q + 1) * 128]
+            new = now + advect(at) * (before - now) + k * (total - 6.0 * now)
+            dst[at, q, 8 : 8 + wide, :] = new
+            dst[at, q, 7:8, :] = new[wide - 1 :]
+            dst[at, q, 8 + wide : 9 + wide, :] = new[0:1]
 
 
 def fluid(x0, x1, cx, cy, cz, kind, *refs):
@@ -599,20 +627,11 @@
     names += {"wet": ["forced", "low", "low_up", "low_down", "near", "gram"],
               "middle": ["forced", "wet"], "end": ["high", "whole"]}[kind]
     names += {"wet": ["out", "send"]}.get(kind, ["out"])
-    names += ["a", "b", "kap", "sems", "out_sems"]
+    names += ["a", "b", "kap", "stage", "near_lanes", "sems", "out_sems"]
     r = dict(zip(names, refs))
-    a, b, kap = r["a"], r["b"], r["kap"]
+    a, b, kap, stage = r["a"], r["b"], r["kap"], r["stage"]
     is_last = lax.axis_index("gx") == lax.axis_size("gx") - 1
     copy, copy_out = starter(r["sems"]), starter(r["out_sems"])
-
-    def chunked(src, s0, count, dst, d0, row):
-        return [
-            copy(
-                src.at[pl.ds(s0, count), :, pl.ds(q * 128, 128)],
-                dst.at[pl.ds(d0, count), q, pl.ds(row, cy)],
-            )
-            for q in range(chunks)
-        ]
 
     def unchunked(src, s0, count, row, rows, dst, d0):
         return [
@@ -627,11 +646,14 @@
     groups = []
     start = own0
     while start < own1:
-        count = min(8, own1 - start)
+        count = min(4, own1 - start)
         i = start - (x0 - 4)
         k0, k1 = max(start, x0 - 3), min(start + count, x1 + 3)
-        groups.append((i, i + count, chunked(r["phi"], start, count, a, i, 8)
-                       + chunked(r["kappa"], k0, k1 - k0, kap, k0 - (x0 - 3), 0)))
+        groups.append((i, i + count, [
+            copy(r["phi"].at[pl.ds(start, count)], stage.at[pl.ds(start - own0, count)]),
+            copy(r["kappa"].at[pl.ds(k0, k1 - k0)],
+                 kap.at[pl.ds(k0 - (x0 - 3), k1 - k0), pl.ds(0, cy)]),
+        ]))
         start += count
     outs = []
     if kind == "middle":
@@ -647,7 +669,7 @@
                 at = slice(q * 128, (q + 1) * 128)
                 a[i, q, 8 : 8 + wide, :] = r["high"][x - cx, :, at]
                 if inner:
-                    kap[i - 1, q] = r["high"][4 + x - cx, :, at]
+                    kap[i - 1, :, at] = r["high"][4 + x - cx, :, at]
         else:
             if x >= 0:
                 up, down = r["up"][x], r["down"][x]
@@ -663,29 +685,34 @@
                     for t in range(cy // 8):
                         a[i, q, 8 + 8 * t : 16 + 8 * t, :] = r["low"][(x + 4) * (cy // 8) + t, :, at]
                         if inner:
-                            kap[i - 1, q, 8 * t : 8 * t + 8, :] = r["low"][
+                            kap[i - 1, 8 * t : 8 * t + 8, at] = r["low"][
                                 (x + 7) * (cy // 8) + t, :, at
                             ]
+                else:
+                    a[i, q, 8 : 8 + cy, :] = stage[x - own0, :, at]
                 a[i, q, 8 + cy : 8 + wide, :] = edge[:, at]
                 if inner:
-                    kap[i - 1, q, cy:wide, :] = kedge[:, at]
+                    kap[i - 1, cy:wide, at] = kedge[:, at]
                 if "forced" in r and 0 <= x < r["forced"].shape[0]:
                     a[i, q, 8 : 8 + wide, :] = a[i, q, 8 : 8 + wide, :] + r["forced"][x, :, at]
         for q in range(chunks):
             a[i, q, 7:8, :] = a[i, q, 7 + wide : 8 + wide, :]
             a[i, q, 8 + wide : 9 + wide, :] = a[i, q, 8:9, :]
 
+    band(r["near_lanes"])
+
+    def advect(i):
+        if kind != "end":
+            return 0.25
+        return jnp.where(jnp.logical_and(is_last, i + (x0 - 4) >= cx), 0.0, 0.25)
+
     def run(src, dst, lo, hi):
-        def body(i, carry):
-            advect = 0.25
-            if kind == "end":
-                outside = jnp.logical_and(is_last, i + (x0 - 4) >= cx)
-                advect = jnp.where(outside, 0.0, 0.25)
-            substep(src, kap, dst, i, advect, cy, cz)
+        def body(n, carry):
+            substeps(src, kap, dst, r["near_lanes"], lo + 2 * n, 2, advect, cy, cz)
             return carry
 
         if hi > lo:
-            lax.fori_loop(lo, hi, body, 0)
+            lax.fori_loop(0, (hi - lo) // 2, body, 0)
 
     if kind == "wet":
         for i in range(4):
@@ -702,9 +729,10 @@
                     at = slice(q * 128, (q + 1) * 128)
                     r["send"][i - 4, :, at] = a[i, q, 8 : 8 + wide, :]
                     if i < 7:
-                        r["send"][i, :, at] = kap[i - 1, q]
-        run(a, b, done, i1 - 1)
-        done = i1 - 1
+                        r["send"][i, :, at] = kap[i - 1, :, at]
+        ready = done + (i1 - 1 - done) // 2 * 2
+        run(a, b, done, ready)
+        done = ready
     if kind == "end":
         for i in range(planes - 4, planes):
             assemble(i)
@@ -748,7 +776,9 @@
         scratch_shapes=[
             pltpu.VMEM((planes, cz // 128, cy + 24, 128), F32),
             pltpu.VMEM((planes, cz // 128, cy + 24, 128), F32),
-            pltpu.VMEM((planes - 2, cz // 128, cy + 8, 128), F32),
+            pltpu.VMEM((planes - 2, cy + 8, cz), F32),
+            pltpu.VMEM((min(cx, x1 + 4) - max(0, x0 - 4), cy, cz), F32),
+            pltpu.VMEM((768, 256), BF16),
             pltpu.SemaphoreType.DMA((80,)),
             pltpu.SemaphoreType.DMA((80,)),
         ],
@@ -759,6 +789,20 @@
         ),
         name="fluid_" + kind,
     )(phi, kappa, up, down, *more)
+
+
+def held_for(awaited, *arrays):
+    def nothing(*refs):
+        pass
+
+    return pl.pallas_call(
+        nothing,
+        in_specs=any_specs(1 + len(arrays)),
+        out_specs=any_specs(len(arrays)),
+        out_shape=[jax.ShapeDtypeStruct(a.shape, a.dtype) for a in arrays],
+        input_output_aliases={i + 1: i for i in range(len(arrays))},
+        name="held",
+    )(awaited, *arrays)
 
 
 def shifted_pairs(n_gx, n_gy, dx, dy):
@@ -803,9 +847,11 @@
     def f32(*shape):
         return jax.ShapeDtypeStruct(shape, F32)
 
+    small = jnp.stack([displacement, stiffness, r_prev, w_prev])
+    numbers = jnp.concatenate([fcell, ldof], axis=0)
     sent = call(
         functools.partial(gather_disp, n_gy), f32(peers, 1, 3 * blk),
-        [pltpu.VMEM((peers, blk), F32)], "gather_disp", vmem_specs(2), displacement, ldof,
+        [pltpu.VMEM((peers, blk), F32)], "gather_disp", vmem_specs(2), small, numbers,
     )
     disp = exchange(sent)
     size = 8 * hist
@@ -820,9 +866,12 @@
         "gram_rows", hbm_specs(1), v_hist,
     )
     up_send, down_send, low_send, low_up_send, low_down_send, own = packed(
-        phi, kappa, disp, displacement, stiffness, fcell, ldof
+        phi, kappa, sent, small, numbers
     )
     index_planes = -(-2 * (peers // 8) // 8)
+    up_send, down_send, low_send, low_up_send, low_down_send = held_for(
+        disp, up_send, down_send, low_send, low_up_send, low_down_send
+    )
     low = shift(low_send, 1, 0)
     up = shift(up_send, 0, -1)
     down = shift(down_send, 0, 1)
@@ -840,7 +889,7 @@
             pltpu.VMEM((wet_planes * cy * chunks, 256), F32),
             pltpu.VMEM((512, wet_planes * 4 * chunks), F32),
         ],
-        "scatter_disp", vmem_specs(4), disp, fcell, up, down,
+        "scatter_disp", vmem_specs(4), disp, numbers, up, down,
     )
     wet, send = fluid_call(
         "wet", 0, wet_planes, phi, kappa, up, down, forced, low, low_up, low_down, near, gram
@@ -851,7 +900,7 @@
     press = call(
         functools.partial(gather_press, n_gx, n_gy), f32(peers, 1, (len(NEAR) + 1) * blk),
         [pltpu.VMEM((peers, blk), F32)], "gather_press", vmem_specs(3) + hbm_specs(1),
-        wet, fcell, gram, middle,
+        wet, numbers, gram, middle,
     )
     loads = exchange(press)
     resp, late = call(
@@ -866,14 +915,14 @@
             pltpu.VMEM((128, 128), F32),
             pltpu.SemaphoreType.DMA((1,)),
         ],
-        "shell", vmem_specs(11) + hbm_specs(2),
-        loads, ldof, displacement, stiffness, r_prev, up, down, low, low_up, low_down, near,
+        "shell", vmem_specs(9) + hbm_specs(2),
+        loads, numbers, small, up, down, low, low_up, low_down, near,
         v_hist, field,
     )
     x_next = call(
         solve, f32(sx, sy),
         [pltpu.VMEM((hist, sx, sy), F32), pltpu.SemaphoreType.DMA((1,))],
-        "solve", vmem_specs(3) + hbm_specs(1), exchange(late), resp, w_prev, w_hist,
+        "solve", vmem_specs(3) + hbm_specs(1), exchange(late), resp, small, w_hist,
     )
     return (field, x_next)
 

time: 141 us -> 138 us (0.979)
  blocking collectives: 27.3 us -> 12.6 us
  starting transfers between devices: 22.4 us -> 33.4 us
  local copies, waits for them, and re-layouts: 7.82 us -> 5.17 us
  Pallas kernels: 71.5 us -> 74.1 us
  other arithmetic: 0.01 us -> 1.88 us
    all_to_all x2 -> x1, blocking collectives: 27.3 us -> 12.6 us  [exchange(): return lax.all_to_all(value, axes, split_axis=0, concat_axis=0, tiled=True)]
    all_to_all x1 -> x2, starting transfers between devices: 6.89 us -> 15.8 us  [exchange(): return lax.all_to_all(value, axes, split_axis=0, concat_axis=0, tiled=True)]
    unnamed x40 -> x24, local copies, waits for them, and re-layouts: 7.81 us -> 5.15 us
    ppermute x7, starting transfers between devices: 15.5 us -> 17.6 us  [shift(): return lax.ppermute(value, axes, shifted_pairs(n_gx, n_gy, dx, dy))]
    pallas_call x1 -> x2, Pallas kernels: 3.04 us -> 4.06 us  [the longest x1 4.06 us: packed(): pl.pallas_call(pack, in_specs=hbm_specs(2) + any_specs(1) + vmem_specs(2)...]
  transfers between devices with their start and end apart: 8 -> 9, of which waited for: 1 -> 1; matrix products, arithmetic and copies ran while one was open for 0% -> 0% of each run, Pallas kernels for 33% -> 37%
where the time goes in v4:
time: 138 us; the launch traced here: 137 us
  Pallas kernels  74.1 us (54%)
  starting transfers between devices  33.4 us (24%)
  blocking collectives  12.6 us (9%)
  waiting for transfers between devices  9.02 us (7%)
  local copies, waits for them, and re-layouts  5.17 us (4%)
  other arithmetic  1.88 us (1%)
    pallas_call x3, Pallas kernels, fluid_call(): pl.pallas_call(functools.partial(fluid, x0, x1, cx, cy, cz, kind), in_spe...  42.8 us
    pallas_call x6, Pallas kernels, call(): pl.pallas_call(body, in_specs=specs, out_specs=vmem_specs(len(out_shape))...  27.3 us
    ppermute x7, starting transfers between devices, shift(): return lax.ppermute(value, axes, shifted_pairs(n_gx, n_gy, dx, dy))  17.6 us
    all_to_all x2, starting transfers between devices, exchange(): return lax.all_to_all(value, axes, split_axis=0, concat_axis=0, tiled=True)  15.8 us
    all_to_all x1, blocking collectives, exchange(): return lax.all_to_all(value, axes, split_axis=0, concat_axis=0, tiled=True)  12.6 us
    ppermute x7, waiting for transfers between devices, shift(): return lax.ppermute(value, axes, shifted_pairs(n_gx, n_gy, dx, dy))  9.01 us
    unnamed x24, local copies, waits for them, and re-layouts  5.15 us
    pallas_call x1, Pallas kernels, packed(): pl.pallas_call(pack, in_specs=hbm_specs(2) + any_specs(1) + vmem_specs(2)...  4.06 us
  transfers between devices with their start and end apart: 9, of which 1 were waited for; matrix products, arithmetic and copies ran while one was open for 0% of the time, Pallas kernels for 37%

profile of v4, /device:TPU:0, one launch (start us, length us, event | category | flops | bytes accessed | tf_op | source)
XLA Modules:
  0.0 137.4 jit_solution(15741777779647563270)
XLA Ops:
  1.4 1.1 pad_maximum_fusion.small_ref
  2.5 1.8 %gather_disp.1.after_ref = f32[32,1,384]{2,1,0:T(1,128)} custom-call(f32[4,64,512]{2,1,0:T(8,128)S(1)} %pad_maximum_fusion.small_ref, s32[64,128]{1,0:T(8,128)S(1)} %pad_add_fusion.numbers_ref), custom_call_target="tpu_custom_call" | custom-call | tf_op jit(solution)/shard_map/gather_disp/pallas_call | solution.py:837
  4.3 7.3 %all-to-all-start = ((f32[32,1,384]{2,1,0:T(1,128)}), f32[32,1,384]{2,1,0:T(1,128)S(1)}, u32[]{:S(2)}, u32[]{:S(2)}) async-start(f32[32,1,384]{2,1,0:T(1,128)} %gather_disp.1.after_ref), calls=%async_computation | async-start | bytes 98304 | tf_op jit(solution)/shard_map/all_to_all | solution.py:833
  11.6 4.1 %pack.1 = (f32[36,8,1024]{2,1,0:T(8,128)S(1)}, f32[36,8,1024]{2,1,0:T(8,128)}, f32[30,8,1024]{2,1,0:T(8,128)S(1)}, f32[4,8,1024]{2,1,0:T(8,128)S(1)}, f32[4,8,10...) custom-call(f32[32,32,1024]{2,1,0:T(8,128)} %refs_0_.5, f32[32,32,1024]{2,1,0:T(8,128)} %refs_1_.5, ...), custom_call_target="tpu_custom_call" | custom-call | tf_op jit(solution)/shard_map/pack/pallas_call | solution.py:562
  15.7 1.0 copy-done.6
  16.7 1.0 copy-done.7
  19.6 1.3 collective-permute-start
  20.9 3.1 %collective-permute-start.1 = (f32[36,8,1024]{2,1,0:T(8,128)}, f32[36,8,1024]{2,1,0:T(8,128)S(1)}, u32[]{:S(2)}, u32[]{:S(2)}) collective-permute-start(f32[36,8,1024]{2,1,0:T(8,128)} %get-tuple-element.23), channel_id=1, source_target_pairs={{0,1},{1,2},{2,3},{4,5},{5,6},{6,7},{8,9},{9,10},{10,11},{12,13},{... | collective-permute-start | bytes 3538952 | tf_op jit(solution)/shard_map/ppermute | solution.py:830
  24.0 3.7 %collective-permute-start.2 = (f32[30,8,1024]{2,1,0:T(8,128)}, f32[30,8,1024]{2,1,0:T(8,128)S(1)}, u32[]{:S(2)}, u32[]{:S(2)}) collective-permute-start(f32[30,8,1024]{2,1,0:T(8,128)} %get-tuple-element.24), channel_id=1, source_target_pairs={{0,4},{1,5},{2,6},{3,7},{4,8},{5,9},{6,10},{7,11},{8,12},{9,13},{1... | collective-permute-start | bytes 2949128 | tf_op jit(solution)/shard_map/ppermute | solution.py:830
  28.5 5.7 %collective-permute-start.4 = (f32[4,8,1024]{2,1,0:T(8,128)}, f32[4,8,1024]{2,1,0:T(8,128)S(1)}, u32[]{:S(2)}, u32[]{:S(2)}) collective-permute-start(f32[4,8,1024]{2,1,0:T(8,128)} %get-tuple-element.26), channel_id=1, source_target_pairs={{0,5},{1,6},{2,7},{4,9},{5,10},{6,11},{8,13},{9,14},{10,15},{12,17... | collective-permute-start | bytes 393224 | tf_op jit(solution)/shard_map/ppermute | solution.py:830
  34.3 1.6 %collective-permute-start.5 = (f32[4,8,1024]{2,1,0:T(8,128)S(1)}, f32[4,8,1024]{2,1,0:T(8,128)S(1)}, u32[]{:S(2)}, u32[]{:S(2)}) collective-permute-start(f32[4,8,1024]{2,1,0:T(8,128)S(1)} %pad_maximum_fusion.1), channel_id=1, source_target_pairs={{4,0},{5,1},{6,2},{7,3},{8,4},{9,5},{10,6},{11,7},{12,8},{13,9},{1... | collective-permute-start | bytes 393224 | tf_op jit(solution)/shard_map/ppermute | solution.py:830
  35.9 7.3 %gram_rows.1.refs_9_.gram_ref = f32[32,128]{1,0:T(8,128)S(1)} custom-call(f32[40,64,512]{2,1,0:T(8,128)} %v_ref.3), custom_call_target="tpu_custom_call" | custom-call | tf_op jit(solution)/shard_map/gram_rows/pallas_call | solution.py:837
  43.3 4.6 %scatter_disp.1.refs_4_ = f32[4,40,1024]{2,1,0:T(8,128)S(1)} custom-call(f32[32,1,384]{2,1,0:T(1,128)S(1)} %copy-done.9, s32[64,128]{1,0:T(8,128)S(1)} %pad_add_fusion.numbers_ref, f32[36,8,1024]{2,1,0:T(8,128)S(1)} %collective-permute-done.up_ref.refs_2_, f32[36,8,1024]{2,1,0:T(8,128)S(1)} %collective-permute-done.1.down_ref.refs_3_), custom_call_target="tpu_custom_call" | custom-call | tf_op jit(solution)/shard_map/scatter_disp/pallas_call | solution.py:837
  47.8 9.0 %collective-permute-done.4.refs_7_.low_down_ref = f32[4,8,1024]{2,1,0:T(8,128)S(1)} collective-permute-done((f32[4,8,1024]{2,1,0:T(8,128)}, f32[4,8,1024]{2,1,0:T(8,128)S(1)}, u32[]{:S(2)}, u32[]{:S(2)}) %collective-permute-start.4) | collective-permute-done | bytes 131104 | tf_op jit(solution)/shard_map/ppermute | solution.py:830
  56.8 10.4 %fluid_wet.1 = (f32[4,32,1024]{2,1,0:T(8,128)S(1)}, f32[7,40,1024]{2,1,0:T(8,128)}) custom-call(f32[32,32,1024]{2,1,0:T(8,128)} %refs_0_.5, f32[32,32,1024]{2,1,0:T(8,128)} %refs_1_.5, f32[36,8,1024]{2,1,0:T(8,128)} %copy-done, f32[36,8,1024]{2,1,0:T(8,128)} %copy-done.2, f32[4,40,1024]{2,1,0:T(8,128)S(1)} %scatter_disp.1.refs_4_, ...), custom_call_target="tpu_custom_call" | custom-call | flops 23592960 | bytes 5898240 | tf_op jit(solution)/shard_map/fluid_wet/pallas_call | solution.py:771
  67.3 1.5 %collective-permute-start.6 = (f32[7,40,1024]{2,1,0:T(8,128)}, f32[7,40,1024]{2,1,0:T(8,128)}, u32[]{:S(2)}, u32[]{:S(2)}) collective-permute-start(f32[7,40,1024]{2,1,0:T(8,128)} %get-tuple-element.28), channel_id=1, source_target_pairs={{4,0},{5,1},{6,2},{7,3},{8,4},{9,5},{10,6},{11,7},{12,8},{13,9},{1... | collective-permute-start | bytes 3440648 | tf_op jit(solution)/shard_map/ppermute | solution.py:830
  68.8 22.8 %fluid_middle.1.refs_5_.after_ref = f32[32,32,1024]{2,1,0:T(8,128)} custom-call(f32[32,32,1024]{2,1,0:T(8,128)} %refs_0_.5, f32[32,32,1024]{2,1,0:T(8,128)} %refs_1_.5, f32[36,8,1024]{2,1,0:T(8,128)S(1)} %copy-done.1, f32[36,8,1024]{2,1,0:T(8,128)S(1)} %copy-done.3, f32[4,40,1024]{2,1,0:T(8,128)S(1)} %scatter_disp.1.refs_4_, ...), custom_call_target="tpu_custom_call" | custom-call | flops 62914560 | bytes 15728640 | tf_op jit(solution)/shard_map/fluid_middle/pallas_call | solution.py:771
  91.6 3.2 %gather_press.1 = f32[32,1,1280]{2,1,0:T(1,128)} custom-call(f32[4,32,1024]{2,1,0:T(8,128)S(1)} %get-tuple-element.29.refs_5_.wet_ref, s32[64,128]{1,0:T(8,128)S(1)} %pad_add_fusion.numbers_ref, f32[32,128]{1,0:T(8,128)S(1)} %gram_rows.1.refs_9_.gram_ref, f32[32,32,1024]{2,1,0:T(8,128)} %fluid_middle.1.refs_5_.after_ref), custom_call_target="tpu_custom_call" | custom-call | tf_op jit(solution)/shard_map/gather_press/pallas_call | solution.py:837
  94.8 8.5 %all-to-all-start.1 = ((f32[32,1,1280]{2,1,0:T(1,128)}), f32[32,1,1280]{2,1,0:T(1,128)S(1)}, u32[]{:S(2)}, u32[]{:S(2)}) async-start(f32[32,1,1280]{2,1,0:T(1,128)} %gather_press.1), calls=%async_computation.1 | async-start | bytes 327680 | tf_op jit(solution)/shard_map/all_to_all | solution.py:833
  103.3 9.6 %fluid_end.1.after_ref = f32[32,32,1024]{2,1,0:T(8,128)} custom-call(f32[32,32,1024]{2,1,0:T(8,128)} %refs_0_.5, f32[32,32,1024]{2,1,0:T(8,128)} %refs_1_.5, f32[36,8,1024]{2,1,0:T(8,128)S(1)} %copy-done.1, f32[36,8,1024]{2,1,0:T(8,128)S(1)} %copy-done.3, f32[7,40,1024]{2,1,0:T(8,128)} %collective-permute-done.6.refs_4_, ...), custom_call_target="tpu_custom_call", output_to_operand_aliasing={{}: (5, {})} | custom-call | flops 23592960 | bytes 5898240 | tf_op jit(solution)/shard_map/fluid_end/pallas_call | solution.py:771
  113.0 1.2 copy-done.5
  114.2 5.7 %shell.1 = (f32[64,512]{1,0:T(8,128)S(1)}, f32[32,1,256]{2,1,0:T(1,128)S(1)}) custom-call(f32[32,1,1280]{2,1,0:T(1,128)S(1)} %all-to-all-done.1.recv_ref, s32[64,128]{1,0:T(8,128)S(1)} %pad_add_fusion.numbers_ref, f32[4,64,512]{2,1,0:T(8,128)S(1)} %pad_maximum_fusion.small_ref, f32[36,8,1024]{2,1,0:T(8,128)S(1)} %copy-done.1, f32[36,8,1024]{2,1,0:T(8,128)} %copy-done.2, ...), custom_call_target="tpu_custom_call" | custom-call | tf_op jit(solution)/shard_map/shell/pallas_call | solution.py:837
  119.9 12.6 %all_to_all.15.recv_ref = f32[32,1,256]{2,1,0:T(1,128)S(1)} all-to-all(f32[32,1,256]{2,1,0:T(1,128)S(1)} %get-tuple-element.30), channel_id=1, replica_groups=mesh['gx'=8,'gy'=4] {'gx','gy'}, dimensions={0} | all-to-all | bytes 65536 | tf_op jit(solution)/shard_map/all_to_all | solution.py:833
  132.5 4.7 %solve.1 = f32[64,512]{1,0:T(8,128)} custom-call(f32[32,1,256]{2,1,0:T(1,128)S(1)} %all_to_all.15.recv_ref, f32[64,512]{1,0:T(8,128)S(1)} %get-tuple-element.31.resp_ref, f32[4,64,512]{2,1,0:T(8,128)S(1)} %pad_maximum_fusion.small_ref, f32[40,64,512]{2,1,0:T(8,128)} %w_ref.1), custom_call_target="tpu_custom_call" | custom-call | tf_op jit(solution)/shard_map/solve/pallas_call | solution.py:837
  (36 shorter events, 3.4 us)
Async XLA Ops:
  4.3 14.7 %all-to-all-start = ((f32[32,1,384]{2,1,0:T(1,128)}), f32[32,1,384]{2,1,0:T(1,128)S(1)}, u32[]{:S(2)}, u32[]{:S(2)}) async-start(f32[32,1,384]{2,1,0:T(1,128)} %gather_disp.1.after_ref), calls=%async_computation | async-start | bytes 98304 | tf_op jit(solution)/shard_map/all_to_all | solution.py:833
  15.7 1.1 copy-start.6
  16.7 1.0 copy-start.7
  17.7 0.7 copy-start.10
  18.4 0.6 copy-start.11
  19.0 0.6 copy-start.8
  19.6 14.6 %collective-permute-start = (f32[36,8,1024]{2,1,0:T(8,128)}, f32[36,8,1024]{2,1,0:T(8,128)S(1)}, u32[]{:S(2)}, u32[]{:S(2)}) collective-permute-start(f32[36,8,1024]{2,1,0:T(8,128)} %get-tuple-element.22), channel_id=1, source_target_pairs={{1,0},{2,1},{3,2},{5,4},{6,5},{7,6},{9,8},{10,9},{11,10},{13,12},{... | collective-permute-start | bytes 3538952 | tf_op jit(solution)/shard_map/ppermute | solution.py:830
  20.9 13.3 %collective-permute-start.1 = (f32[36,8,1024]{2,1,0:T(8,128)}, f32[36,8,1024]{2,1,0:T(8,128)S(1)}, u32[]{:S(2)}, u32[]{:S(2)}) collective-permute-start(f32[36,8,1024]{2,1,0:T(8,128)} %get-tuple-element.23), channel_id=1, source_target_pairs={{0,1},{1,2},{2,3},{4,5},{5,6},{6,7},{8,9},{9,10},{10,11},{12,13},{... | collective-permute-start | bytes 3538952 | tf_op jit(solution)/shard_map/ppermute | solution.py:830
  24.0 32.8 %collective-permute-start.2 = (f32[30,8,1024]{2,1,0:T(8,128)}, f32[30,8,1024]{2,1,0:T(8,128)S(1)}, u32[]{:S(2)}, u32[]{:S(2)}) collective-permute-start(f32[30,8,1024]{2,1,0:T(8,128)} %get-tuple-element.24), channel_id=1, source_target_pairs={{0,4},{1,5},{2,6},{3,7},{4,8},{5,9},{6,10},{7,11},{8,12},{9,13},{1... | collective-permute-start | bytes 2949128 | tf_op jit(solution)/shard_map/ppermute | solution.py:830
  27.8 20.0 %collective-permute-start.3 = (f32[4,8,1024]{2,1,0:T(8,128)}, f32[4,8,1024]{2,1,0:T(8,128)S(1)}, u32[]{:S(2)}, u32[]{:S(2)}) collective-permute-start(f32[4,8,1024]{2,1,0:T(8,128)} %get-tuple-element.25), channel_id=1, source_target_pairs={{1,4},{2,5},{3,6},{5,8},{6,9},{7,10},{9,12},{10,13},{11,14},{13,16... | collective-permute-start | bytes 393224 | tf_op jit(solution)/shard_map/ppermute | solution.py:830
  28.5 28.4 %collective-permute-start.4 = (f32[4,8,1024]{2,1,0:T(8,128)}, f32[4,8,1024]{2,1,0:T(8,128)S(1)}, u32[]{:S(2)}, u32[]{:S(2)}) collective-permute-start(f32[4,8,1024]{2,1,0:T(8,128)} %get-tuple-element.26), channel_id=1, source_target_pairs={{0,5},{1,6},{2,7},{4,9},{5,10},{6,11},{8,13},{9,14},{10,15},{12,17... | collective-permute-start | bytes 393224 | tf_op jit(solution)/shard_map/ppermute | solution.py:830
  34.2 9.0 %copy-start = (f32[36,8,1024]{2,1,0:T(8,128)}, f32[36,8,1024]{2,1,0:T(8,128)S(1)}, u32[]{:S(2)}) copy-start(f32[36,8,1024]{2,1,0:T(8,128)S(1)} %collective-permute-done.up_ref.refs_2_) | copy-start | bytes 3538948
  34.3 9.0 %copy-start.2 = (f32[36,8,1024]{2,1,0:T(8,128)}, f32[36,8,1024]{2,1,0:T(8,128)S(1)}, u32[]{:S(2)}) copy-start(f32[36,8,1024]{2,1,0:T(8,128)S(1)} %collective-permute-done.1.down_ref.refs_3_) | copy-start | bytes 3538948
  34.3 8.9 %copy-start.9 = (f32[32,1,384]{2,1,0:T(1,128)S(1)}, f32[32,1,384]{2,1,0:T(1,128)}, u32[]{:S(2)}) copy-start(f32[32,1,384]{2,1,0:T(1,128)} %copy-done.8) | copy-start | bytes 147460
  34.3 22.5 %collective-permute-start.5 = (f32[4,8,1024]{2,1,0:T(8,128)S(1)}, f32[4,8,1024]{2,1,0:T(8,128)S(1)}, u32[]{:S(2)}, u32[]{:S(2)}) collective-permute-start(f32[4,8,1024]{2,1,0:T(8,128)S(1)} %pad_maximum_fusion.1), channel_id=1, source_target_pairs={{4,0},{5,1},{6,2},{7,3},{8,4},{9,5},{10,6},{11,7},{12,8},{13,9},{1... | collective-permute-start | bytes 393224 | tf_op jit(solution)/shard_map/ppermute | solution.py:830
  47.8 21.0 %copy-start.1 = (f32[36,8,1024]{2,1,0:T(8,128)S(1)}, f32[36,8,1024]{2,1,0:T(8,128)}, u32[]{:S(2)}) copy-start(f32[36,8,1024]{2,1,0:T(8,128)} %copy-done) | copy-start | bytes 3538948
  47.8 21.0 %copy-start.3 = (f32[36,8,1024]{2,1,0:T(8,128)S(1)}, f32[36,8,1024]{2,1,0:T(8,128)}, u32[]{:S(2)}) copy-start(f32[36,8,1024]{2,1,0:T(8,128)} %copy-done.2) | copy-start | bytes 3538948
  56.8 10.4 %copy-start.4 = (f32[30,8,1024]{2,1,0:T(8,128)}, f32[30,8,1024]{2,1,0:T(8,128)S(1)}, u32[]{:S(2)}) copy-start(f32[30,8,1024]{2,1,0:T(8,128)S(1)} %collective-permute-done.2.refs_5_.low_ref) | copy-start | bytes 2949124
  67.3 36.0 %collective-permute-start.6 = (f32[7,40,1024]{2,1,0:T(8,128)}, f32[7,40,1024]{2,1,0:T(8,128)}, u32[]{:S(2)}, u32[]{:S(2)}) collective-permute-start(f32[7,40,1024]{2,1,0:T(8,128)} %get-tuple-element.28), channel_id=1, source_target_pairs={{4,0},{5,1},{6,2},{7,3},{8,4},{9,5},{10,6},{11,7},{12,8},{13,9},{1... | collective-permute-start | bytes 3440648 | tf_op jit(solution)/shard_map/ppermute | solution.py:830
  94.8 18.1 %all-to-all-start.1 = ((f32[32,1,1280]{2,1,0:T(1,128)}), f32[32,1,1280]{2,1,0:T(1,128)S(1)}, u32[]{:S(2)}, u32[]{:S(2)}) async-start(f32[32,1,1280]{2,1,0:T(1,128)} %gather_press.1), calls=%async_computation.1 | async-start | bytes 327680 | tf_op jit(solution)/shard_map/all_to_all | solution.py:833
  113.0 1.2 copy-start.5

commit v5 on v3

--- a/solution.py
+++ b/solution.py
@@ -116,9 +116,11 @@
     return copy
 
 
-def gather_disp(n_gy, disp_ref, index_ref, out_ref, own_ref):
+def gather_disp(n_gy, small_ref, numbers_ref, out_ref, own_ref):
+    disp_ref = small_ref.at[0]
+    peers, blk = own_ref.shape
+    index_ref = numbers_ref.at[pl.ds(peers, peers)]
     sx, sy = disp_ref.shape
-    peers, blk = index_ref.shape
     chunk_bits = (sy // 128).bit_length() - 1
     columns = []
     for q in range(sy // 128):
@@ -139,9 +141,16 @@
     out_ref[:, 0, 2 * blk : 3 * blk] = jnp.where(beside == 0, 0.0, pltpu.roll(own, 1, axis=0))
 
 
-def scatter_disp(cx, cy, cz, disp_ref, cells_ref, up_ref, down_ref, out_ref, acc_ref, side_ref):
-    planes = out_ref.shape[0]
-    peers, blk = cells_ref.shape
+def scatter_disp(cx, cy, cz, disp_ref, numbers_ref, up_ref, down_ref, phi_ref, kappa_ref, out_ref,
+                 acc_ref, side_ref, stage, kstage, sems):
+    planes = stage.shape[0]
+    copy = starter(sems)
+    copies = [
+        copy(phi_ref.at[pl.ds(0, planes)], stage),
+        copy(kappa_ref.at[pl.ds(0, planes - 1)], kstage),
+    ]
+    peers, blk = disp_ref.shape[0], numbers_ref.shape[1]
+    cells_ref = numbers_ref.at[pl.ds(0, peers)]
     rows = planes * cy
     chunks = cz // 128
     row_bits = cz.bit_length() - 1
@@ -180,20 +189,36 @@
                 side_ref, base == 0 and side == 0, spread_values(values, index & 255, 256, 2),
                 one_hot(keys, planes * 4 * chunks),
             )
+    for made in copies:
+        made.wait()
+    upper = lax.broadcasted_iota(jnp.int32, (8, cz), 0) < 4
+    for x in range(planes):
+        up, down = up_ref[x], down_ref[x]
+        out_ref[x, cy : cy + 8, :] = jnp.where(upper, up, down)
+        if x < planes - 1:
+            out_ref[planes + x, 0:cy, :] = kstage[x]
+            out_ref[planes + x, cy : cy + 8, :] = pltpu.roll(
+                jnp.where(upper, down, up), 4, axis=0
+            )
     for q in range(chunks):
         part = acc_ref[q * rows : (q + 1) * rows, :]
-        out_ref[:, 0:cy, q * 128 : (q + 1) * 128] = (part[:, :128] + part[:, 128:]).reshape(
+        at = slice(q * 128, (q + 1) * 128)
+        out_ref[0:planes, 0:cy, at] = stage[:, :, at] + (part[:, :128] + part[:, 128:]).reshape(
             planes, cy, 128
         )
     both = jnp.transpose(side_ref[0:256, :] + side_ref[256:512, :])
     for q in range(chunks // 2):
         part = both[q * planes * 8 : (q + 1) * planes * 8, :]
-        out_ref[:, cy : cy + 8, q * 256 : (q + 1) * 256] = part.reshape(planes, 8, 256)
-
-
-def gather_press(n_gx, n_gy, wet_ref, index_ref, gram_ref, after_ref, out_ref, own_ref):
+        at = slice(q * 256, (q + 1) * 256)
+        out_ref[0:planes, cy : cy + 8, at] = out_ref[0:planes, cy : cy + 8, at] + part.reshape(
+            planes, 8, 256
+        )
+
+
+def gather_press(n_gx, n_gy, wet_ref, numbers_ref, gram_ref, out_ref, own_ref):
+    index_ref = numbers_ref.at[pl.ds(0, own_ref.shape[0])]
     planes, cy, cz = wet_ref.shape
-    peers, blk = index_ref.shape
+    peers, blk = own_ref.shape
     rows = planes * cy
     chunks = cz // 256
     columns = []
@@ -262,11 +287,13 @@
         out_ref[...] = wide[0:peers, :] + pltpu.roll(wide[peers : 2 * peers, :], 64, axis=1)
 
 
-def shell(recv_ref, index_ref, disp_ref, stiff_ref, prev_ref, up_ref, down_ref, low_ref,
+def shell(recv_ref, numbers_ref, small_ref, up_ref, down_ref, low_ref,
           low_up_ref, low_down_ref, high_ref, v_ref, after_ref, resp_ref, late_ref, v, acc, rows_acc,
           cols_acc, corner_acc, ext, dots, v_sem):
+    disp_ref, stiff_ref, prev_ref = small_ref.at[0], small_ref.at[1], small_ref.at[2]
     sx, sy = disp_ref.shape
-    peers, blk = index_ref.shape
+    peers, blk = recv_ref.shape[0], numbers_ref.shape[1]
+    index_ref = numbers_ref.at[pl.ds(peers, peers)]
     load_tiles = peers // 8
     index_planes = -(-2 * load_tiles // 8)
     corner_planes = -(-(load_tiles + 4) // 8)
@@ -426,9 +453,10 @@
     late_ref[:, 0, 128:256] = jnp.broadcast_to(gram, (peers, 128))
 
 
-def solve(recv_ref, resp_ref, prev_ref, w_ref, out_ref, w, sems):
+def solve(recv_ref, resp_ref, small_ref, w_ref, after_ref, out_ref, w, sems):
     peers = recv_ref.shape[0]
     hist = w_ref.shape[0]
+    prev_ref = small_ref.at[3]
     sx, sy = resp_ref.shape
     w_copy = pltpu.make_async_copy(w_ref, w, sems.at[0])
     w_copy.start()
@@ -464,12 +492,13 @@
     out_ref[...] = total
 
 
-def pack(phi_ref, kappa_ref, after_ref, disp_ref, stiff_ref, cells_ref, loads_ref,
-         up_ref, down_ref, low_ref, low_up_ref, low_down_ref, own_ref, phi_lo, kap_lo, phi_hi,
+def pack(phi_ref, kappa_ref, after_ref, small_ref, numbers_ref, up_ref, down_ref, low_ref, low_up_ref, low_down_ref, own_ref, phi_lo, kap_lo, phi_hi,
          kap_hi, in_sems):
     cx, cy, cz = phi_ref.shape
+    disp_ref, stiff_ref = small_ref.at[0], small_ref.at[1]
     sx, sy = disp_ref.shape
-    peers = cells_ref.shape[0]
+    peers = numbers_ref.shape[0] // 2
+    cells_ref, loads_ref = numbers_ref.at[pl.ds(0, peers)], numbers_ref.at[pl.ds(peers, peers)]
     tiles = peers // 8
     index_planes = -(-2 * tiles // 8)
     corner_planes = -(-(tiles + 4) // 8)
@@ -540,9 +569,9 @@
         made.wait()
 
 
-def packed(phi, kappa, after, displacement, stiffness, cells, loads):
+def packed(phi, kappa, after, small, numbers):
     cx, cy, cz = phi.shape
-    tiles = cells.shape[0] // 8
+    tiles = numbers.shape[0] // 16
     index_planes = -(-2 * tiles // 8)
     corner_planes = -(-(tiles + 4) // 8)
     extra = index_planes + 2 + corner_planes
@@ -553,7 +582,7 @@
 
     return pl.pallas_call(
         pack,
-        in_specs=hbm_specs(2) + any_specs(1) + vmem_specs(4),
+        in_specs=hbm_specs(2) + any_specs(1) + vmem_specs(2),
         out_specs=vmem_specs(6),
         out_shape=[
             shape(cx + extra), shape(cx + extra), shape(low_planes + index_planes + 1),
@@ -563,7 +592,7 @@
         + [pltpu.SemaphoreType.DMA((cx // 2 + low_planes,))],
         compiler_params=params(),
         name="pack",
-    )(phi, kappa, after, displacement, stiffness, cells, loads)
+    )(phi, kappa, after, small, numbers)
 
 
 def substep(src, kap, dst, plane, advect, cy, cz):
@@ -575,6 +604,7 @@
     def take(at, q, start=8):
         return src[at, q, pl.ds(start, wide), :]
 
+    result = []
     for q in range(chunks):
         now = take(plane, q)
         left = take(plane, q - 1) if q else 0.0
@@ -585,7 +615,9 @@
         total = total + (take(plane, q, 7) + take(plane, q, 9))
         before = take(plane - 1, q)
         total = total + (before + take(plane + 1, q))
-        new = now + advect * (before - now) + kap[plane - 1, q] * (total - 6.0 * now)
+        k = kap[plane - 1, :, q * 128 : (q + 1) * 128]
+        result.append(now + advect * (before - now) + k * (total - 6.0 * now))
+    for q, new in enumerate(result):
         dst[plane, q, 8 : 8 + wide, :] = new
         dst[plane, q, 7:8, :] = new[wide - 1 :]
         dst[plane, q, 8 + wide : 9 + wide, :] = new[0:1]
@@ -596,23 +628,13 @@
     wide = cy + 8
     chunks = cz // 128
     names = ["phi", "kappa", "up", "down"]
-    names += {"wet": ["forced", "low", "low_up", "low_down", "near", "gram"],
-              "middle": ["forced", "wet"], "end": ["high", "whole"]}[kind]
-    names += {"wet": ["out", "send"]}.get(kind, ["out"])
-    names += ["a", "b", "kap", "sems", "out_sems"]
+    names += {"wet": ["forced", "low", "low_up", "low_down", "gram"],
+              "middle": ["forced", "wet", "press"], "end": ["high", "whole", "late"]}[kind]
+    names += ["out", "a", "b", "kap", "stage", "sems", "out_sems"]
     r = dict(zip(names, refs))
-    a, b, kap = r["a"], r["b"], r["kap"]
+    a, b, kap, stage = r["a"], r["b"], r["kap"], r["stage"]
     is_last = lax.axis_index("gx") == lax.axis_size("gx") - 1
     copy, copy_out = starter(r["sems"]), starter(r["out_sems"])
-
-    def chunked(src, s0, count, dst, d0, row):
-        return [
-            copy(
-                src.at[pl.ds(s0, count), :, pl.ds(q * 128, 128)],
-                dst.at[pl.ds(d0, count), q, pl.ds(row, cy)],
-            )
-            for q in range(chunks)
-        ]
 
     def unchunked(src, s0, count, row, rows, dst, d0):
         return [
@@ -627,11 +649,18 @@
     groups = []
     start = own0
     while start < own1:
-        count = min(8, own1 - start)
+        count = min(4, own1 - start)
         i = start - (x0 - 4)
         k0, k1 = max(start, x0 - 3), min(start + count, x1 + 3)
-        groups.append((i, i + count, chunked(r["phi"], start, count, a, i, 8)
-                       + chunked(r["kappa"], k0, k1 - k0, kap, k0 - (x0 - 3), 0)))
+        copies = [
+            copy(r["kappa"].at[pl.ds(k0, k1 - k0)],
+                 kap.at[pl.ds(k0 - (x0 - 3), k1 - k0), pl.ds(0, cy)]),
+        ]
+        if "forced" not in r or start >= 4:
+            copies.append(
+                copy(r["phi"].at[pl.ds(start, count)], stage.at[pl.ds(start - own0, count)])
+            )
+        groups.append((i, i + count, copies))
         start += count
     outs = []
     if kind == "middle":
@@ -647,7 +676,7 @@
                 at = slice(q * 128, (q + 1) * 128)
                 a[i, q, 8 : 8 + wide, :] = r["high"][x - cx, :, at]
                 if inner:
-                    kap[i - 1, q] = r["high"][4 + x - cx, :, at]
+                    kap[i - 1, :, at] = r["high"][4 + x - cx, :, at]
         else:
             if x >= 0:
                 up, down = r["up"][x], r["down"][x]
@@ -663,14 +692,17 @@
                     for t in range(cy // 8):
                         a[i, q, 8 + 8 * t : 16 + 8 * t, :] = r["low"][(x + 4) * (cy // 8) + t, :, at]
                         if inner:
-                            kap[i - 1, q, 8 * t : 8 * t + 8, :] = r["low"][
+                            kap[i - 1, 8 * t : 8 * t + 8, at] = r["low"][
                                 (x + 7) * (cy // 8) + t, :, at
                             ]
-                a[i, q, 8 + cy : 8 + wide, :] = edge[:, at]
+                if "forced" in r and 0 <= x < 4:
+                    a[i, q, 8 : 8 + wide, :] = r["forced"][x, :, at]
+                else:
+                    if x >= 0:
+                        a[i, q, 8 : 8 + cy, :] = stage[x - own0, :, at]
+                    a[i, q, 8 + cy : 8 + wide, :] = edge[:, at]
                 if inner:
-                    kap[i - 1, q, cy:wide, :] = kedge[:, at]
-                if "forced" in r and 0 <= x < r["forced"].shape[0]:
-                    a[i, q, 8 : 8 + wide, :] = a[i, q, 8 : 8 + wide, :] + r["forced"][x, :, at]
+                    kap[i - 1, cy:wide, at] = kedge[:, at]
         for q in range(chunks):
             a[i, q, 7:8, :] = a[i, q, 7 + wide : 8 + wide, :]
             a[i, q, 8 + wide : 9 + wide, :] = a[i, q, 8:9, :]
@@ -696,13 +728,6 @@
             made.wait()
         for i in range(i0, i1):
             assemble(i)
-        if kind == "wet":
-            for i in range(4, 8):
-                for q in range(chunks):
-                    at = slice(q * 128, (q + 1) * 128)
-                    r["send"][i - 4, :, at] = a[i, q, 8 : 8 + wide, :]
-                    if i < 7:
-                        r["send"][i, :, at] = kap[i - 1, q]
         run(a, b, done, i1 - 1)
         done = i1 - 1
     if kind == "end":
@@ -729,16 +754,13 @@
     field = jax.ShapeDtypeStruct((cx, cy, cz), F32)
     whole = hbm_specs(1)[0]
     if kind == "wet":
-        specs = vmem_specs(4) + any_specs(2)
-        out_shape = [
-            jax.ShapeDtypeStruct((x1 - x0, cy, cz), F32),
-            jax.ShapeDtypeStruct((7, cy + 8, cz), F32),
-        ]
-        out_specs = vmem_specs(2)
+        specs = vmem_specs(4) + any_specs(1)
+        out_shape, out_specs = jax.ShapeDtypeStruct((x1 - x0, cy, cz), F32), vmem_specs(1)[0]
     elif kind == "middle":
-        specs, out_shape, out_specs = vmem_specs(2), field, whole
+        specs, out_shape, out_specs = vmem_specs(2) + any_specs(1), field, whole
     else:
-        specs, out_shape, out_specs = vmem_specs(1) + hbm_specs(1), field, whole
+        specs = vmem_specs(1) + hbm_specs(1) + any_specs(1)
+        out_shape, out_specs = field, whole
     cells = planes * (cy + 8) * cz
     return pl.pallas_call(
         functools.partial(fluid, x0, x1, cx, cy, cz, kind),
@@ -748,7 +770,8 @@
         scratch_shapes=[
             pltpu.VMEM((planes, cz // 128, cy + 24, 128), F32),
             pltpu.VMEM((planes, cz // 128, cy + 24, 128), F32),
-            pltpu.VMEM((planes - 2, cz // 128, cy + 8, 128), F32),
+            pltpu.VMEM((planes - 2, cy + 8, cz), F32),
+            pltpu.VMEM((min(cx, x1 + 4) - max(0, x0 - 4), cy, cz), F32),
             pltpu.SemaphoreType.DMA((80,)),
             pltpu.SemaphoreType.DMA((80,)),
         ],
@@ -803,9 +826,11 @@
     def f32(*shape):
         return jax.ShapeDtypeStruct(shape, F32)
 
+    small = jnp.stack([displacement, stiffness, r_prev, w_prev])
+    numbers = jnp.concatenate([fcell, ldof], axis=0)
     sent = call(
         functools.partial(gather_disp, n_gy), f32(peers, 1, 3 * blk),
-        [pltpu.VMEM((peers, blk), F32)], "gather_disp", vmem_specs(2), displacement, ldof,
+        [pltpu.VMEM((peers, blk), F32)], "gather_disp", vmem_specs(2), small, numbers,
     )
     disp = exchange(sent)
     size = 8 * hist
@@ -820,7 +845,7 @@
         "gram_rows", hbm_specs(1), v_hist,
     )
     up_send, down_send, low_send, low_up_send, low_down_send, own = packed(
-        phi, kappa, disp, displacement, stiffness, fcell, ldof
+        phi, kappa, sent, small, numbers
     )
     index_planes = -(-2 * (peers // 8) // 8)
     low = shift(low_send, 1, 0)
@@ -835,25 +860,26 @@
 
     chunks = cz // 128
     forced = call(
-        functools.partial(scatter_disp, cx, cy, cz), f32(wet_planes, cy + 8, cz),
+        functools.partial(scatter_disp, cx, cy, cz), f32(2 * wet_planes - 1, cy + 8, cz),
         [
             pltpu.VMEM((wet_planes * cy * chunks, 256), F32),
             pltpu.VMEM((512, wet_planes * 4 * chunks), F32),
+            pltpu.VMEM((wet_planes, cy, cz), F32),
+            pltpu.VMEM((wet_planes - 1, cy, cz), F32),
+            pltpu.SemaphoreType.DMA((2,)),
         ],
-        "scatter_disp", vmem_specs(4), disp, fcell, up, down,
-    )
-    wet, send = fluid_call(
-        "wet", 0, wet_planes, phi, kappa, up, down, forced, low, low_up, low_down, near, gram
-    )
-    high = shift(send, -1, 0)
-    middle = fluid_call("middle", wet_planes, cx - 4, phi, kappa, up, down, forced, wet)
-    field = fluid_call("end", cx - 4, cx, phi, kappa, up, down, high, middle)
+        "scatter_disp", vmem_specs(4) + hbm_specs(2), disp, numbers, up, down, phi, kappa,
+    )
+    high = shift(forced, -1, 0)
+    wet = fluid_call(
+        "wet", 0, wet_planes, phi, kappa, up, down, forced, low, low_up, low_down, gram
+    )
     press = call(
         functools.partial(gather_press, n_gx, n_gy), f32(peers, 1, (len(NEAR) + 1) * blk),
-        [pltpu.VMEM((peers, blk), F32)], "gather_press", vmem_specs(3) + hbm_specs(1),
-        wet, fcell, gram, middle,
+        [pltpu.VMEM((peers, blk), F32)], "gather_press", vmem_specs(3), wet, numbers, gram,
     )
     loads = exchange(press)
+    middle = fluid_call("middle", wet_planes, cx - 4, phi, kappa, up, down, forced, wet, press)
     resp, late = call(
         shell, [f32(sx, sy), f32(peers, 1, 256)],
         [
@@ -866,14 +892,15 @@
             pltpu.VMEM((128, 128), F32),
             pltpu.SemaphoreType.DMA((1,)),
         ],
-        "shell", vmem_specs(11) + hbm_specs(2),
-        loads, ldof, displacement, stiffness, r_prev, up, down, low, low_up, low_down, near,
-        v_hist, field,
-    )
+        "shell", vmem_specs(9) + hbm_specs(2),
+        loads, numbers, small, up, down, low, low_up, low_down, near,
+        v_hist, middle,
+    )
+    field = fluid_call("end", cx - 4, cx, phi, kappa, up, down, high, middle, late)
     x_next = call(
         solve, f32(sx, sy),
         [pltpu.VMEM((hist, sx, sy), F32), pltpu.SemaphoreType.DMA((1,))],
-        "solve", vmem_specs(3) + hbm_specs(1), exchange(late), resp, w_prev, w_hist,
+        "solve", vmem_specs(3) + hbm_specs(2), exchange(late), resp, small, w_hist, field,
     )
     return (field, x_next)
 

time: 141 us -> 155 us (1.099)
  starting transfers between devices: 22.4 us -> 35.4 us
  waiting for transfers between devices: 9.77 us -> 15.9 us
  blocking collectives: 27.3 us -> 22.5 us
  local copies, waits for them, and re-layouts: 7.82 us -> 3.73 us
  Pallas kernels: 71.5 us -> 74.2 us
  other arithmetic: 0.01 us -> 1.88 us
    ppermute x7, starting transfers between devices: 15.5 us -> 22.1 us  [shift(): return lax.ppermute(value, axes, shifted_pairs(n_gx, n_gy, dx, dy))]
    all_to_all x1 -> x2, starting transfers between devices: 6.89 us -> 13.3 us  [exchange(): return lax.all_to_all(value, axes, split_axis=0, concat_axis=0, tiled=True)]
    ppermute x7, waiting for transfers between devices: 9.77 us -> 15.9 us  [shift(): return lax.ppermute(value, axes, shifted_pairs(n_gx, n_gy, dx, dy))]
    all_to_all x2 -> x1, blocking collectives: 27.3 us -> 22.5 us  [exchange(): return lax.all_to_all(value, axes, split_axis=0, concat_axis=0, tiled=True)]
    unnamed x40 -> x12, local copies, waits for them, and re-layouts: 7.81 us -> 3.71 us
    pallas_call x6, Pallas kernels: 26.7 us -> 29.2 us  [call(): pl.pallas_call(body, in_specs=specs, out_specs=vmem_specs(len(out_shape))...]
  transfers between devices with their start and end apart: 8 -> 9, of which waited for: 1 -> 1; matrix products, arithmetic and copies ran while one was open for 0% -> 0% of each run, Pallas kernels for 33% -> 42%
where the time goes in v5:
time: 155 us
  Pallas kernels  74.2 us (48%)
  starting transfers between devices  35.4 us (23%)
  blocking collectives  22.5 us (15%)
  waiting for transfers between devices  15.9 us (10%)
  local copies, waits for them, and re-layouts  3.73 us (2%)
  other arithmetic  1.88 us (1%)
    pallas_call x3, Pallas kernels, fluid_call(): pl.pallas_call(functools.partial(fluid, x0, x1, cx, cy, cz, kind), in_spe...  40.9 us
    pallas_call x6, Pallas kernels, call(): pl.pallas_call(body, in_specs=specs, out_specs=vmem_specs(len(out_shape))...  29.2 us
    all_to_all x1, blocking collectives, exchange(): return lax.all_to_all(value, axes, split_axis=0, concat_axis=0, tiled=True)  22.5 us
    ppermute x7, starting transfers between devices, shift(): return lax.ppermute(value, axes, shifted_pairs(n_gx, n_gy, dx, dy))  22.1 us
    ppermute x7, waiting for transfers between devices, shift(): return lax.ppermute(value, axes, shifted_pairs(n_gx, n_gy, dx, dy))  15.9 us
    all_to_all x2, starting transfers between devices, exchange(): return lax.all_to_all(value, axes, split_axis=0, concat_axis=0, tiled=True)  13.3 us
    pallas_call x1, Pallas kernels, packed(): pl.pallas_call(pack, in_specs=hbm_specs(2) + any_specs(1) + vmem_specs(2)...  4.06 us
    unnamed x12, local copies, waits for them, and re-layouts  3.71 us
  transfers between devices with their start and end apart: 9, of which 1 were waited for; matrix products, arithmetic and copies ran while one was open for 0% of the time, Pallas kernels for 42%

profile of v5, /device:TPU:0, one launch (start us, length us, event | category | flops | bytes accessed | tf_op | source)
XLA Modules:
  0.0 154.7 jit_solution(871947295143714768)
XLA Ops:
  1.4 1.1 pad_maximum_fusion.small_ref
  2.5 1.2 gather_disp.1.after_ref
  3.7 4.1 %pack.1 = (f32[36,8,1024]{2,1,0:T(8,128)S(1)}, f32[36,8,1024]{2,1,0:T(8,128)}, f32[30,8,1024]{2,1,0:T(8,128)S(1)}, f32[4,8,1024]{2,1,0:T(8,128)S(1)}, f32[4,8,10...) custom-call(f32[32,32,1024]{2,1,0:T(8,128)} %refs_0_.5, f32[32,32,1024]{2,1,0:T(8,128)} %refs_1_.5, ...), custom_call_target="tpu_custom_call" | custom-call | tf_op jit(solution)/shard_map/pack/pallas_call | solution.py:583
  7.8 1.3 collective-permute-start
  9.1 3.1 %collective-permute-start.1 = (f32[36,8,1024]{2,1,0:T(8,128)}, f32[36,8,1024]{2,1,0:T(8,128)S(1)}, u32[]{:S(2)}, u32[]{:S(2)}) collective-permute-start(f32[36,8,1024]{2,1,0:T(8,128)} %get-tuple-element.11), channel_id=1, source_target_pairs={{0,1},{1,2},{2,3},{4,5},{5,6},{6,7},{8,9},{9,10},{10,11},{12,13},{... | collective-permute-start | bytes 3538952 | tf_op jit(solution)/shard_map/ppermute | solution.py:809
  12.2 4.9 %collective-permute-start.3 = (f32[30,8,1024]{2,1,0:T(8,128)S(1)}, f32[30,8,1024]{2,1,0:T(8,128)S(1)}, u32[]{:S(2)}, u32[]{:S(2)}) collective-permute-start(f32[30,8,1024]{2,1,0:T(8,128)S(1)} %get-tuple-element.12), channel_id=1, source_target_pairs={{0,4},{1,5},{2,6},{3,7},{4,8},{5,9},{6,10},{7,11},{8,12},{9,13},{1... | collective-permute-start | bytes 2949128 | tf_op jit(solution)/shard_map/ppermute | solution.py:809
  17.1 22.5 %all_to_all.15.disp_ref = f32[32,1,384]{2,1,0:T(1,128)S(1)} all-to-all(f32[32,1,384]{2,1,0:T(1,128)S(1)} %gather_disp.1.after_ref), channel_id=1, replica_groups=mesh['gx'=8,'gy'=4] {'gx','gy'}, dimensions={0} | all-to-all | bytes 98304 | tf_op jit(solution)/shard_map/all_to_all | solution.py:812
  39.7 6.5 %scatter_disp.1.refs_4_ = f32[7,40,1024]{2,1,0:T(8,128)} custom-call(f32[32,1,384]{2,1,0:T(1,128)S(1)} %all_to_all.15.disp_ref, s32[64,128]{1,0:T(8,128)S(1)} %pad_add_fusion.numbers_ref, f32[36,8,1024]{2,1,0:T(8,128)S(1)} %collective-permute-done.up_ref.refs_2_, f32[36,8,1024]{2,1,0:T(8,128)S(1)} %collective-permute-done.1.down_ref.refs_3_, ...), custom_call_target="tpu_custom_call" | custom-call | tf_op jit(solution)/shard_map/scatter_disp/pallas_call | solution.py:816
  46.2 1.3 collective-permute-start.2
  48.2 9.3 %collective-permute-start.5 = (f32[4,8,1024]{2,1,0:T(8,128)S(1)}, f32[4,8,1024]{2,1,0:T(8,128)S(1)}, u32[]{:S(2)}, u32[]{:S(2)}) collective-permute-start(f32[4,8,1024]{2,1,0:T(8,128)S(1)} %get-tuple-element.14), channel_id=1, source_target_pairs={{0,5},{1,6},{2,7},{4,9},{5,10},{6,11},{8,13},{9,14},{10,15},{12,17... | collective-permute-start | bytes 393224 | tf_op jit(solution)/shard_map/ppermute | solution.py:809
  57.5 7.3 %gram_rows.1.refs_8_.gram_ref = f32[32,128]{1,0:T(8,128)S(1)} custom-call(f32[40,64,512]{2,1,0:T(8,128)} %v_ref.3), custom_call_target="tpu_custom_call" | custom-call | tf_op jit(solution)/shard_map/gram_rows/pallas_call | solution.py:816
  64.8 15.9 %collective-permute-done.5.refs_7_.low_down_ref = f32[4,8,1024]{2,1,0:T(8,128)S(1)} collective-permute-done((f32[4,8,1024]{2,1,0:T(8,128)S(1)}, f32[4,8,1024]{2,1,0:T(8,128)S(1)}, u32[]{:S(2)}, u32[]{:S(2)}) %collective-permute-start.5) | collective-permute-done | bytes 131104 | tf_op jit(solution)/shard_map/ppermute | solution.py:809
  80.7 8.7 %fluid_wet.1.wet_ref.refs_5_ = f32[4,32,1024]{2,1,0:T(8,128)S(1)} custom-call(f32[32,32,1024]{2,1,0:T(8,128)} %refs_0_.5, f32[32,32,1024]{2,1,0:T(8,128)} %refs_1_.5, f32[36,8,1024]{2,1,0:T(8,128)S(1)} %collective-permute-done.up_ref.refs_2_, f32[36,8,1024]{2,1,0:T(8,128)} %copy-done, f32[7,40,1024]{2,1,0:T(8,128)} %scatter_disp.1.refs_4_, ...), custom_call_target="tpu_custom_call" | custom-call | flops 23592960 | bytes 5898240 | tf_op jit(solution)/shard_map/fluid_wet/pallas_call | solution.py:765
  89.5 0.9 copy-done.2
  90.4 3.2 %gather_press.1.refs_6_ = f32[32,1,1280]{2,1,0:T(1,128)} custom-call(f32[4,32,1024]{2,1,0:T(8,128)S(1)} %fluid_wet.1.wet_ref.refs_5_, s32[64,128]{1,0:T(8,128)S(1)} %pad_add_fusion.numbers_ref, f32[32,128]{1,0:T(8,128)S(1)} %gram_rows.1.refs_8_.gram_ref), custom_call_target="tpu_custom_call" | custom-call | tf_op jit(solution)/shard_map/gather_press/pallas_call | solution.py:816
  93.6 6.3 %all-to-all-start.1 = ((f32[32,1,1280]{2,1,0:T(1,128)}), f32[32,1,1280]{2,1,0:T(1,128)S(1)}, u32[]{:S(2)}, u32[]{:S(2)}) async-start(f32[32,1,1280]{2,1,0:T(1,128)} %gather_press.1.refs_6_), calls=%async_computation.1 | async-start | bytes 327680 | tf_op jit(solution)/shard_map/all_to_all | solution.py:812
  99.9 1.5 collective-permute-start.6
  101.5 22.9 %fluid_middle.1.after_ref.refs_5_ = f32[32,32,1024]{2,1,0:T(8,128)} custom-call(f32[32,32,1024]{2,1,0:T(8,128)} %refs_0_.5, f32[32,32,1024]{2,1,0:T(8,128)} %refs_1_.5, f32[36,8,1024]{2,1,0:T(8,128)S(1)} %collective-permute-done.up_ref.refs_2_, f32[36,8,1024]{2,1,0:T(8,128)} %copy-done, f32[7,40,1024]{2,1,0:T(8,128)} %scatter_disp.1.refs_4_, ...), custom_call_target="tpu_custom_call" | custom-call | flops 62914560 | bytes 15728640 | tf_op jit(solution)/shard_map/fluid_middle/pallas_call | solution.py:765
  125.0 1.2 copy-done.3
  126.2 0.9 copy-done.5
  127.1 6.3 %shell.1 = (f32[64,512]{1,0:T(8,128)S(1)}, f32[32,1,256]{2,1,0:T(1,128)}) custom-call(f32[32,1,1280]{2,1,0:T(1,128)S(1)} %all-to-all-done.1.recv_ref, s32[64,128]{1,0:T(8,128)S(1)} %pad_add_fusion.numbers_ref, f32[4,64,512]{2,1,0:T(8,128)S(1)} %pad_maximum_fusion.small_ref, f32[36,8,1024]{2,1,0:T(8,128)S(1)} %collective-permute-done.up_ref.refs_2_, ...), custom_call_target="tpu_custom_call" | custom-call | tf_op jit(solution)/shard_map/shell/pallas_call | solution.py:816
  133.5 7.0 %all-to-all-start.2 = ((f32[32,1,256]{2,1,0:T(1,128)}), f32[32,1,256]{2,1,0:T(1,128)S(1)}, u32[]{:S(2)}, u32[]{:S(2)}) async-start(f32[32,1,256]{2,1,0:T(1,128)} %get-tuple-element.16.refs_6_), calls=%async_computation.2 | async-start | bytes 65536 | tf_op jit(solution)/shard_map/all_to_all | solution.py:812
  140.5 9.3 %fluid_end.1.after_ref = f32[32,32,1024]{2,1,0:T(8,128)} custom-call(f32[32,32,1024]{2,1,0:T(8,128)} %refs_0_.5, f32[32,32,1024]{2,1,0:T(8,128)} %refs_1_.5, f32[36,8,1024]{2,1,0:T(8,128)S(1)} %collective-permute-done.up_ref.refs_2_, f32[36,8,1024]{2,1,0:T(8,128)S(1)} %copy-done.1, ...), custom_call_target="tpu_custom_call", output_to_operand_aliasing={{}: (5, {})} | custom-call | flops 23592960 | bytes 5898240 | tf_op jit(solution)/shard_map/fluid_end/pallas_call | solution.py:765
  149.8 4.7 %solve.1 = f32[64,512]{1,0:T(8,128)} custom-call(f32[32,1,256]{2,1,0:T(1,128)S(1)} %all-to-all-done.2.recv_ref, f32[64,512]{1,0:T(8,128)S(1)} %get-tuple-element.17.resp_ref, f32[4,64,512]{2,1,0:T(8,128)S(1)} %pad_maximum_fusion.small_ref, f32[40,64,512]{2,1,0:T(8,128)} %w_ref.1, f32[32,32,1024]{2,1,0:T(8,128)} %fluid_end.1.after_ref), custom_call_target="tpu_custom_call" | custom-call | tf_op jit(solution)/shard_map/solve/pallas_call | solution.py:816
  (24 shorter events, 2.1 us)
Async XLA Ops:
  7.8 31.9 %collective-permute-start = (f32[36,8,1024]{2,1,0:T(8,128)S(1)}, f32[36,8,1024]{2,1,0:T(8,128)S(1)}, u32[]{:S(2)}, u32[]{:S(2)}) collective-permute-start(f32[36,8,1024]{2,1,0:T(8,128)S(1)} %get-tuple-element.10), channel_id=1, source_target_pairs={{1,0},{2,1},{3,2},{5,4},{6,5},{7,6},{9,8},{10,9},{11,10},{13,12},{... | collective-permute-start | bytes 3538952 | tf_op jit(solution)/shard_map/ppermute | solution.py:809
  9.1 30.6 %collective-permute-start.1 = (f32[36,8,1024]{2,1,0:T(8,128)}, f32[36,8,1024]{2,1,0:T(8,128)S(1)}, u32[]{:S(2)}, u32[]{:S(2)}) collective-permute-start(f32[36,8,1024]{2,1,0:T(8,128)} %get-tuple-element.11), channel_id=1, source_target_pairs={{0,1},{1,2},{2,3},{4,5},{5,6},{6,7},{8,9},{9,10},{10,11},{12,13},{... | collective-permute-start | bytes 3538952 | tf_op jit(solution)/shard_map/ppermute | solution.py:809
  12.2 68.5 %collective-permute-start.3 = (f32[30,8,1024]{2,1,0:T(8,128)S(1)}, f32[30,8,1024]{2,1,0:T(8,128)S(1)}, u32[]{:S(2)}, u32[]{:S(2)}) collective-permute-start(f32[30,8,1024]{2,1,0:T(8,128)S(1)} %get-tuple-element.12), channel_id=1, source_target_pairs={{0,4},{1,5},{2,6},{3,7},{4,8},{5,9},{6,10},{7,11},{8,12},{9,13},{1... | collective-permute-start | bytes 2949128 | tf_op jit(solution)/shard_map/ppermute | solution.py:809
  39.7 6.6 %copy-start = (f32[36,8,1024]{2,1,0:T(8,128)}, f32[36,8,1024]{2,1,0:T(8,128)S(1)}, u32[]{:S(2)}) copy-start(f32[36,8,1024]{2,1,0:T(8,128)S(1)} %collective-permute-done.1.down_ref.refs_3_) | copy-start | bytes 3538948
  46.2 94.2 %collective-permute-start.2 = (f32[7,40,1024]{2,1,0:T(8,128)}, f32[7,40,1024]{2,1,0:T(8,128)}, u32[]{:S(2)}, u32[]{:S(2)}) collective-permute-start(f32[7,40,1024]{2,1,0:T(8,128)} %scatter_disp.1.refs_4_), channel_id=1, source_target_pairs={{4,0},{5,1},{6,2},{7,3},{8,4},{9,5},{10,6},{11,7},{12,8},{13,9},{1... | collective-permute-start | bytes 3440648 | tf_op jit(solution)/shard_map/ppermute | solution.py:809
  47.5 17.3 %collective-permute-start.4 = (f32[4,8,1024]{2,1,0:T(8,128)S(1)}, f32[4,8,1024]{2,1,0:T(8,128)S(1)}, u32[]{:S(2)}, u32[]{:S(2)}) collective-permute-start(f32[4,8,1024]{2,1,0:T(8,128)S(1)} %get-tuple-element.13), channel_id=1, source_target_pairs={{1,4},{2,5},{3,6},{5,8},{6,9},{7,10},{9,12},{10,13},{11,14},{13,16... | collective-permute-start | bytes 393224 | tf_op jit(solution)/shard_map/ppermute | solution.py:809
  48.2 32.5 %collective-permute-start.5 = (f32[4,8,1024]{2,1,0:T(8,128)S(1)}, f32[4,8,1024]{2,1,0:T(8,128)S(1)}, u32[]{:S(2)}, u32[]{:S(2)}) collective-permute-start(f32[4,8,1024]{2,1,0:T(8,128)S(1)} %get-tuple-element.14), channel_id=1, source_target_pairs={{0,5},{1,6},{2,7},{4,9},{5,10},{6,11},{8,13},{9,14},{10,15},{12,17... | collective-permute-start | bytes 393224 | tf_op jit(solution)/shard_map/ppermute | solution.py:809
  64.8 35.1 %slice-start = ((f32[36,8,1024]{2,1,0:T(8,128)}), f32[1,8,1024]{2,1,0:T(8,128)S(1)}, s32[]{:S(2)}) async-start(f32[36,8,1024]{2,1,0:T(8,128)} %copy-done), calls=%async_computation.3 | async-start | bytes 65536 | tf_op jit(solution)/shard_map/slice | solution.py:858
  89.4 1.0 copy-start.2
  93.6 31.5 %all-to-all-start.1 = ((f32[32,1,1280]{2,1,0:T(1,128)}), f32[32,1,1280]{2,1,0:T(1,128)S(1)}, u32[]{:S(2)}, u32[]{:S(2)}) async-start(f32[32,1,1280]{2,1,0:T(1,128)} %gather_press.1.refs_6_), calls=%async_computation.1 | async-start | bytes 327680 | tf_op jit(solution)/shard_map/all_to_all | solution.py:812
  99.9 24.4 %collective-permute-start.6 = (f32[4,8,1024]{2,1,0:T(8,128)S(1)}, f32[4,8,1024]{2,1,0:T(8,128)S(1)}, u32[]{:S(2)}, u32[]{:S(2)}) collective-permute-start(f32[4,8,1024]{2,1,0:T(8,128)S(1)} %pad_maximum_fusion.1), channel_id=1, source_target_pairs={{4,0},{5,1},{6,2},{7,3},{8,4},{9,5},{10,6},{11,7},{12,8},{13,9},{1... | collective-permute-start | bytes 393224 | tf_op jit(solution)/shard_map/ppermute | solution.py:809
  124.4 16.1 %copy-start.1 = (f32[36,8,1024]{2,1,0:T(8,128)S(1)}, f32[36,8,1024]{2,1,0:T(8,128)}, u32[]{:S(2)}) copy-start(f32[36,8,1024]{2,1,0:T(8,128)} %copy-done) | copy-start | bytes 3538948
  124.4 0.7 copy-start.4
  125.0 1.2 copy-start.3
  126.2 0.9 copy-start.5
  133.5 16.4 %all-to-all-start.2 = ((f32[32,1,256]{2,1,0:T(1,128)}), f32[32,1,256]{2,1,0:T(1,128)S(1)}, u32[]{:S(2)}, u32[]{:S(2)}) async-start(f32[32,1,256]{2,1,0:T(1,128)} %get-tuple-element.16.refs_6_), calls=%async_computation.2 | async-start | bytes 65536 | tf_op jit(solution)/shard_map/all_to_all | solution.py:812

commit v6 on v5

--- a/solution.py
+++ b/solution.py
@@ -215,7 +215,7 @@
         )
 
 
-def gather_press(n_gx, n_gy, wet_ref, numbers_ref, gram_ref, out_ref, own_ref):
+def gather_press(n_gx, n_gy, wet_ref, numbers_ref, gram_ref, after_ref, out_ref, own_ref):
     index_ref = numbers_ref.at[pl.ds(0, own_ref.shape[0])]
     planes, cy, cz = wet_ref.shape
     peers, blk = own_ref.shape
@@ -453,7 +453,7 @@
     late_ref[:, 0, 128:256] = jnp.broadcast_to(gram, (peers, 128))
 
 
-def solve(recv_ref, resp_ref, small_ref, w_ref, after_ref, out_ref, w, sems):
+def solve(recv_ref, resp_ref, small_ref, w_ref, out_ref, w, sems):
     peers = recv_ref.shape[0]
     hist = w_ref.shape[0]
     prev_ref = small_ref.at[3]
@@ -595,16 +595,15 @@
     )(phi, kappa, after, small, numbers)
 
 
-def substep(src, kap, dst, plane, advect, cy, cz):
-    wide = cy + 8
+def substep(src, kap, coef, dst, plane, advect, rows, cz):
     chunks = cz // 128
-    lane = lax.broadcasted_iota(jnp.int32, (wide, 128), 1)
+    wide = kap.shape[1]
+    lane = lax.broadcasted_iota(jnp.int32, (rows, 128), 1)
     first, last = lane == 0, lane == 127
 
     def take(at, q, start=8):
-        return src[at, q, pl.ds(start, wide), :]
-
-    result = []
+        return src[at, q, pl.ds(start, rows), :]
+
     for q in range(chunks):
         now = take(plane, q)
         left = take(plane, q - 1) if q else 0.0
@@ -615,12 +614,14 @@
         total = total + (take(plane, q, 7) + take(plane, q, 9))
         before = take(plane - 1, q)
         total = total + (before + take(plane + 1, q))
-        k = kap[plane - 1, :, q * 128 : (q + 1) * 128]
-        result.append(now + advect * (before - now) + k * (total - 6.0 * now))
-    for q, new in enumerate(result):
-        dst[plane, q, 8 : 8 + wide, :] = new
-        dst[plane, q, 7:8, :] = new[wide - 1 :]
-        dst[plane, q, 8 + wide : 9 + wide, :] = new[0:1]
+        at = slice(q * 128, (q + 1) * 128)
+        new = (coef[plane - 1, 0:rows, at] * now + advect * before) + kap[
+            plane - 1, 0:rows, at
+        ] * total
+        dst[plane, q, 8 : 8 + rows, :] = new
+        if rows == wide:
+            dst[plane, q, 7:8, :] = new[wide - 1 :]
+            dst[plane, q, 8 + wide : 9 + wide, :] = new[0:1]
 
 
 def fluid(x0, x1, cx, cy, cz, kind, *refs):
@@ -628,11 +629,15 @@
     wide = cy + 8
     chunks = cz // 128
     names = ["phi", "kappa", "up", "down"]
-    names += {"wet": ["forced", "low", "low_up", "low_down", "gram"],
-              "middle": ["forced", "wet", "press"], "end": ["high", "whole", "late"]}[kind]
-    names += ["out", "a", "b", "kap", "stage", "sems", "out_sems"]
+    names += {"wet": ["forced", "low", "low_up", "low_down", "near", "gram"],
+              "middle": ["state_a", "state_b", "wet"],
+              "end": ["state_a", "state_b", "high", "whole"]}[kind]
+    names += {"wet": ["out", "next_a", "next_b", "send"], "middle": ["out", "next_a", "next_b"],
+              "end": ["out"]}[kind]
+    names += ["a", "b", "kap", "coef", "stage", "sems", "out_sems"]
     r = dict(zip(names, refs))
-    a, b, kap, stage = r["a"], r["b"], r["kap"], r["stage"]
+    a, b, kap, coef, stage = r["a"], r["b"], r["kap"], r["coef"], r["stage"]
+    carried = kind != "wet"
     is_last = lax.axis_index("gx") == lax.axis_size("gx") - 1
     copy, copy_out = starter(r["sems"]), starter(r["out_sems"])
 
@@ -645,18 +650,21 @@
             for q in range(chunks)
         ]
 
-    own0, own1 = max(0, x0 - 4), min(cx, x1 + 4)
+    own0, own1 = x0 + 4 if carried else x0, min(cx, x1 + 4)
+    kap0 = x0 if carried else x0 - 3
     groups = []
+    if carried:
+        kappa_first = copy(r["kappa"].at[pl.ds(x0, 4)], kap.at[pl.ds(3, 4), pl.ds(0, cy)])
     start = own0
     while start < own1:
         count = min(4, own1 - start)
         i = start - (x0 - 4)
-        k0, k1 = max(start, x0 - 3), min(start + count, x1 + 3)
-        copies = [
+        k0, k1 = start, min(start + count, x1 + 3)
+        copies = [] if k1 <= k0 else [
             copy(r["kappa"].at[pl.ds(k0, k1 - k0)],
                  kap.at[pl.ds(k0 - (x0 - 3), k1 - k0), pl.ds(0, cy)]),
         ]
-        if "forced" not in r or start >= 4:
+        if carried or start >= 4:
             copies.append(
                 copy(r["phi"].at[pl.ds(start, count)], stage.at[pl.ds(start - own0, count)])
             )
@@ -668,15 +676,13 @@
 
     upper = lax.broadcasted_iota(jnp.int32, (8, cz), 0) < 4
 
-    def assemble(i):
+    def assemble(i, only_kappa=False):
         x = x0 - 4 + i
         inner = 1 <= i < planes - 1
+        whole = slice(8, 8 + wide)
         if x >= cx:
-            for q in range(chunks):
-                at = slice(q * 128, (q + 1) * 128)
-                a[i, q, 8 : 8 + wide, :] = r["high"][x - cx, :, at]
-                if inner:
-                    kap[i - 1, :, at] = r["high"][4 + x - cx, :, at]
+            if inner:
+                kap[i - 1] = r["high"][4 + x - cx]
         else:
             if x >= 0:
                 up, down = r["up"][x], r["down"][x]
@@ -685,35 +691,38 @@
             else:
                 up = down = jnp.zeros((8, cz), F32)
             edge = jnp.where(upper, up, down)
-            kedge = pltpu.roll(jnp.where(upper, down, up), 4, axis=0)
-            for q in range(chunks):
-                at = slice(q * 128, (q + 1) * 128)
+            if inner:
+                if x < 0:
+                    for t in range(cy // 8):
+                        kap[i - 1, 8 * t : 8 * t + 8, :] = r["low"][(x + 7) * (cy // 8) + t]
+                kap[i - 1, cy:wide, :] = pltpu.roll(jnp.where(upper, down, up), 4, axis=0)
+        if inner:
+            coef[i - 1] = 0.75 - 6.0 * kap[i - 1]
+        if only_kappa:
+            return
+        for q in range(chunks):
+            at = slice(q * 128, (q + 1) * 128)
+            if x >= cx:
+                a[i, q, whole, :] = r["high"][x - cx, :, at]
+            elif kind == "wet" and 0 <= x < 4:
+                a[i, q, whole, :] = r["forced"][x, :, at]
+            else:
                 if x < 0:
                     for t in range(cy // 8):
                         a[i, q, 8 + 8 * t : 16 + 8 * t, :] = r["low"][(x + 4) * (cy // 8) + t, :, at]
-                        if inner:
-                            kap[i - 1, 8 * t : 8 * t + 8, at] = r["low"][
-                                (x + 7) * (cy // 8) + t, :, at
-                            ]
-                if "forced" in r and 0 <= x < 4:
-                    a[i, q, 8 : 8 + wide, :] = r["forced"][x, :, at]
                 else:
-                    if x >= 0:
-                        a[i, q, 8 : 8 + cy, :] = stage[x - own0, :, at]
-                    a[i, q, 8 + cy : 8 + wide, :] = edge[:, at]
-                if inner:
-                    kap[i - 1, cy:wide, at] = kedge[:, at]
-        for q in range(chunks):
+                    a[i, q, 8 : 8 + cy, :] = stage[x - own0, :, at]
+                a[i, q, 8 + cy : 8 + wide, :] = edge[:, at]
             a[i, q, 7:8, :] = a[i, q, 7 + wide : 8 + wide, :]
             a[i, q, 8 + wide : 9 + wide, :] = a[i, q, 8:9, :]
 
-    def run(src, dst, lo, hi):
+    def run(src, dst, lo, hi, rows=wide):
         def body(i, carry):
             advect = 0.25
             if kind == "end":
                 outside = jnp.logical_and(is_last, i + (x0 - 4) >= cx)
                 advect = jnp.where(outside, 0.0, 0.25)
-            substep(src, kap, dst, i, advect, cy, cz)
+            substep(src, kap, coef, dst, i, advect, rows, cz)
             return carry
 
         if hi > lo:
@@ -722,7 +731,14 @@
     if kind == "wet":
         for i in range(4):
             assemble(i)
-    done = 1
+        done = 1
+    else:
+        a[4:8] = r["state_a"][...]
+        b[3:7] = r["state_b"][...]
+        kappa_first.wait()
+        for i in range(4, 8):
+            assemble(i, True)
+        done = 7
     for i0, i1, copies in groups:
         for made in copies:
             made.wait()
@@ -734,16 +750,21 @@
         for i in range(planes - 4, planes):
             assemble(i)
         run(a, b, done, planes - 1)
-    run(b, a, 2, planes - 2)
-    run(a, b, 3, planes - 3)
+    run(b, a, 6 if carried else 2, planes - 2)
+    run(a, b, 5 if carried else 3, planes - 3)
+    if kind == "wet":
+        r["send"][...] = r["forced"][...]
     for start in range(4, planes - 4, 4):
-        run(b, a, start, start + 4)
+        run(b, a, start, start + 4, cy)
         if kind == "wet":
             for i in range(start, start + 4):
                 for q in range(chunks):
                     r["out"][i - 4, :, q * 128 : (q + 1) * 128] = a[i, q, 8 : 8 + cy, :]
         else:
             outs += unchunked(a, start, 4, 8, cy, r["out"], x0 + start - 4)
+    if kind != "end":
+        r["next_a"][...] = a[planes - 4 : planes]
+        r["next_b"][...] = b[planes - 5 : planes - 1]
     for made in outs:
         made.wait()
 
@@ -752,15 +773,20 @@
     cx, cy, cz = phi.shape
     planes = x1 - x0 + 8
     field = jax.ShapeDtypeStruct((cx, cy, cz), F32)
-    whole = hbm_specs(1)[0]
+    state = [jax.ShapeDtypeStruct((4, cz // 128, cy + 24, 128), F32)] * 2
     if kind == "wet":
-        specs = vmem_specs(4) + any_specs(1)
-        out_shape, out_specs = jax.ShapeDtypeStruct((x1 - x0, cy, cz), F32), vmem_specs(1)[0]
+        specs = vmem_specs(4) + any_specs(2)
+        out_shape = [
+            jax.ShapeDtypeStruct((x1 - x0, cy, cz), F32), *state,
+            jax.ShapeDtypeStruct((7, cy + 8, cz), F32),
+        ]
+        out_specs = vmem_specs(4)
     elif kind == "middle":
-        specs, out_shape, out_specs = vmem_specs(2) + any_specs(1), field, whole
+        specs = vmem_specs(3)
+        out_shape, out_specs = [field, *state], hbm_specs(1) + vmem_specs(2)
     else:
-        specs = vmem_specs(1) + hbm_specs(1) + any_specs(1)
-        out_shape, out_specs = field, whole
+        specs = vmem_specs(3) + hbm_specs(1)
+        out_shape, out_specs = field, hbm_specs(1)[0]
     cells = planes * (cy + 8) * cz
     return pl.pallas_call(
         functools.partial(fluid, x0, x1, cx, cy, cz, kind),
@@ -771,11 +797,12 @@
             pltpu.VMEM((planes, cz // 128, cy + 24, 128), F32),
             pltpu.VMEM((planes, cz // 128, cy + 24, 128), F32),
             pltpu.VMEM((planes - 2, cy + 8, cz), F32),
-            pltpu.VMEM((min(cx, x1 + 4) - max(0, x0 - 4), cy, cz), F32),
+            pltpu.VMEM((planes - 2, cy + 8, cz), F32),
+            pltpu.VMEM((max(min(cx, x1 + 4) - (x0 if kind == "wet" else x0 + 4), 1), cy, cz), F32),
             pltpu.SemaphoreType.DMA((80,)),
             pltpu.SemaphoreType.DMA((80,)),
         ],
-        input_output_aliases={5: 0} if kind == "end" else {},
+        input_output_aliases={7: 0} if kind == "end" else {},
         compiler_params=params(),
         cost_estimate=pl.CostEstimate(
             flops=48 * cells, bytes_accessed=12 * cells, transcendentals=0
@@ -845,7 +872,7 @@
         "gram_rows", hbm_specs(1), v_hist,
     )
     up_send, down_send, low_send, low_up_send, low_down_send, own = packed(
-        phi, kappa, sent, small, numbers
+        phi, kappa, disp, small, numbers
     )
     index_planes = -(-2 * (peers // 8) // 8)
     low = shift(low_send, 1, 0)
@@ -870,16 +897,22 @@
         ],
         "scatter_disp", vmem_specs(4) + hbm_specs(2), disp, numbers, up, down, phi, kappa,
     )
-    high = shift(forced, -1, 0)
-    wet = fluid_call(
-        "wet", 0, wet_planes, phi, kappa, up, down, forced, low, low_up, low_down, gram
+    wet, state_a, state_b, send = fluid_call(
+        "wet", 0, wet_planes, phi, kappa, up, down, forced, low, low_up, low_down, near, gram
+    )
+    high = shift(send, -1, 0)
+    middle, state_a, state_b = fluid_call(
+        "middle", wet_planes, cx - 4, phi, kappa, up, down, state_a, state_b, wet
+    )
+    field = fluid_call(
+        "end", cx - 4, cx, phi, kappa, up, down, state_a, state_b, high, middle
     )
     press = call(
         functools.partial(gather_press, n_gx, n_gy), f32(peers, 1, (len(NEAR) + 1) * blk),
-        [pltpu.VMEM((peers, blk), F32)], "gather_press", vmem_specs(3), wet, numbers, gram,
+        [pltpu.VMEM((peers, blk), F32)], "gather_press", vmem_specs(3) + any_specs(1),
+        wet, numbers, gram, middle,
     )
     loads = exchange(press)
-    middle = fluid_call("middle", wet_planes, cx - 4, phi, kappa, up, down, forced, wet, press)
     resp, late = call(
         shell, [f32(sx, sy), f32(peers, 1, 256)],
         [
@@ -894,13 +927,12 @@
         ],
         "shell", vmem_specs(9) + hbm_specs(2),
         loads, numbers, small, up, down, low, low_up, low_down, near,
-        v_hist, middle,
-    )
-    field = fluid_call("end", cx - 4, cx, phi, kappa, up, down, high, middle, late)
+        v_hist, field,
+    )
     x_next = call(
         solve, f32(sx, sy),
         [pltpu.VMEM((hist, sx, sy), F32), pltpu.SemaphoreType.DMA((1,))],
-        "solve", vmem_specs(3) + hbm_specs(2), exchange(late), resp, small, w_hist, field,
+        "solve", vmem_specs(3) + hbm_specs(1), exchange(late), resp, small, w_hist,
     )
     return (field, x_next)
 

time: 155 us -> 139 us (0.90)
  starting transfers between devices: 35.4 us -> 21.2 us
  waiting for transfers between devices: 15.9 us -> 7.85 us
  blocking collectives: 22.5 us -> 27.3 us
  local copies, waits for them, and re-layouts: 3.73 us -> 7.61 us
  Pallas kernels: 74.2 us -> 71.3 us
    ppermute x7, waiting for transfers between devices: 15.9 us -> 7.85 us  [shift(): return lax.ppermute(value, axes, shifted_pairs(n_gx, n_gy, dx, dy))]
    all_to_all x2 -> x1, starting transfers between devices: 13.3 us -> 5.79 us  [exchange(): return lax.all_to_all(value, axes, split_axis=0, concat_axis=0, tiled=True)]
    ppermute x7, starting transfers between devices: 22.1 us -> 15.5 us  [shift(): return lax.ppermute(value, axes, shifted_pairs(n_gx, n_gy, dx, dy))]
    all_to_all x1 -> x2, blocking collectives: 22.5 us -> 27.3 us  [exchange(): return lax.all_to_all(value, axes, split_axis=0, concat_axis=0, tiled=True)]
    unnamed x12 -> x26, local copies, waits for them, and re-layouts: 3.71 us -> 7.59 us
    pallas_call x6, Pallas kernels: 29.2 us -> 27.6 us  [call(): pl.pallas_call(body, in_specs=specs, out_specs=vmem_specs(len(out_shape))...]
  transfers between devices with their start and end apart: 9 -> 8, of which waited for: 1 -> 1; matrix products, arithmetic and copies ran while one was open for 0% -> 0% of each run, Pallas kernels for 42% -> 33%
where the time goes in v6:
time: 139 us; the launch traced here: 138 us
  Pallas kernels  71.3 us (51%)
  blocking collectives  27.3 us (20%)
  starting transfers between devices  21.2 us (15%)
  waiting for transfers between devices  7.85 us (6%)
  local copies, waits for them, and re-layouts  7.61 us (5%)
  other arithmetic  1.88 us (1%)
    pallas_call x3, Pallas kernels, fluid_call(): pl.pallas_call(functools.partial(fluid, x0, x1, cx, cy, cz, kind), in_spe...  39.6 us
    pallas_call x6, Pallas kernels, call(): pl.pallas_call(body, in_specs=specs, out_specs=vmem_specs(len(out_shape))...  27.6 us
    all_to_all x2, blocking collectives, exchange(): return lax.all_to_all(value, axes, split_axis=0, concat_axis=0, tiled=True)  27.3 us
    ppermute x7, starting transfers between devices, shift(): return lax.ppermute(value, axes, shifted_pairs(n_gx, n_gy, dx, dy))  15.5 us
    ppermute x7, waiting for transfers between devices, shift(): return lax.ppermute(value, axes, shifted_pairs(n_gx, n_gy, dx, dy))  7.85 us
    unnamed x26, local copies, waits for them, and re-layouts  7.59 us
    all_to_all x1, starting transfers between devices, exchange(): return lax.all_to_all(value, axes, split_axis=0, concat_axis=0, tiled=True)  5.79 us
    pallas_call x1, Pallas kernels, packed(): pl.pallas_call(pack, in_specs=hbm_specs(2) + any_specs(1) + vmem_specs(2)...  4.05 us
  transfers between devices with their start and end apart: 8, of which 1 were waited for; matrix products, arithmetic and copies ran while one was open for 0% of the time, Pallas kernels for 33%

profile of v6, /device:TPU:0, one launch (start us, length us, event | category | flops | bytes accessed | tf_op | source)
XLA Modules:
  0.0 138.3 jit_solution(15058470689810455324)
XLA Ops:
  1.4 1.1 pad_maximum_fusion.small_ref
  2.5 1.2 gather_disp.1
  3.7 14.4 %all_to_all.15.after_ref.disp_ref = f32[32,1,384]{2,1,0:T(1,128)S(1)} all-to-all(f32[32,1,384]{2,1,0:T(1,128)S(1)} %gather_disp.1), channel_id=1, replica_groups=mesh['gx'=8,'gy'=4] {'gx','gy'}, dimensions={0} | all-to-all | bytes 98304 | tf_op jit(solution)/shard_map/all_to_all | solution.py:839
  18.1 4.0 %pack.1 = (f32[36,8,1024]{2,1,0:T(8,128)S(1)}, f32[36,8,1024]{2,1,0:T(8,128)}, f32[30,8,1024]{2,1,0:T(8,128)S(1)}, f32[4,8,1024]{2,1,0:T(8,128)S(1)}, f32[4,8,10...) custom-call(f32[32,32,1024]{2,1,0:T(8,128)} %refs_0_.5, f32[32,32,1024]{2,1,0:T(8,128)} %refs_1_.5, ...), custom_call_target="tpu_custom_call" | custom-call | tf_op jit(solution)/shard_map/pack/pallas_call | solution.py:583
  22.2 1.3 collective-permute-start
  23.5 3.1 %collective-permute-start.1 = (f32[36,8,1024]{2,1,0:T(8,128)}, f32[36,8,1024]{2,1,0:T(8,128)S(1)}, u32[]{:S(2)}, u32[]{:S(2)}) collective-permute-start(f32[36,8,1024]{2,1,0:T(8,128)} %get-tuple-element.18), channel_id=1, source_target_pairs={{0,1},{1,2},{2,3},{4,5},{5,6},{6,7},{8,9},{9,10},{10,11},{12,13},{... | collective-permute-start | bytes 3538952 | tf_op jit(solution)/shard_map/ppermute | solution.py:836
  26.6 2.5 %collective-permute-start.2 = (f32[30,8,1024]{2,1,0:T(8,128)S(1)}, f32[30,8,1024]{2,1,0:T(8,128)S(1)}, u32[]{:S(2)}, u32[]{:S(2)}) collective-permute-start(f32[30,8,1024]{2,1,0:T(8,128)S(1)} %get-tuple-element.19), channel_id=1, source_target_pairs={{0,4},{1,5},{2,6},{3,7},{4,8},{5,9},{6,10},{7,11},{8,12},{9,13},{1... | collective-permute-start | bytes 2949128 | tf_op jit(solution)/shard_map/ppermute | solution.py:836
  29.9 4.9 %collective-permute-start.4 = (f32[4,8,1024]{2,1,0:T(8,128)S(1)}, f32[4,8,1024]{2,1,0:T(8,128)S(1)}, u32[]{:S(2)}, u32[]{:S(2)}) collective-permute-start(f32[4,8,1024]{2,1,0:T(8,128)S(1)} %get-tuple-element.21), channel_id=1, source_target_pairs={{0,5},{1,6},{2,7},{4,9},{5,10},{6,11},{8,13},{9,14},{10,15},{12,17... | collective-permute-start | bytes 393224 | tf_op jit(solution)/shard_map/ppermute | solution.py:836
  34.8 1.5 %collective-permute-start.5 = (f32[4,8,1024]{2,1,0:T(8,128)S(1)}, f32[4,8,1024]{2,1,0:T(8,128)S(1)}, u32[]{:S(2)}, u32[]{:S(2)}) collective-permute-start(f32[4,8,1024]{2,1,0:T(8,128)S(1)} %pad_maximum_fusion.1), channel_id=1, source_target_pairs={{4,0},{5,1},{6,2},{7,3},{8,4},{9,5},{10,6},{11,7},{12,8},{13,9},{1... | collective-permute-start | bytes 393224 | tf_op jit(solution)/shard_map/ppermute | solution.py:836
  36.3 7.3 %gram_rows.1.refs_9_.gram_ref = f32[32,128]{1,0:T(8,128)S(1)} custom-call(f32[40,64,512]{2,1,0:T(8,128)} %v_ref.3), custom_call_target="tpu_custom_call" | custom-call | tf_op jit(solution)/shard_map/gram_rows/pallas_call | solution.py:843
  43.6 5.5 %scatter_disp.1.refs_4_ = f32[7,40,1024]{2,1,0:T(8,128)S(1)} custom-call(f32[32,1,384]{2,1,0:T(1,128)S(1)} %all_to_all.15.after_ref.disp_ref, s32[64,128]{1,0:T(8,128)S(1)} %pad_add_fusion.numbers_ref, f32[36,8,1024]{2,1,0:T(8,128)S(1)} %collective-permute-done.up_ref.refs_2_, f32[36,8,1024]{2,1,0:T(8,128)S(1)} %collective-permute-done.1.down_ref.refs_3_, ...), custom_call_target="tpu_custom_call" | custom-call | tf_op jit(solution)/shard_map/scatter_disp/pallas_call | solution.py:843
  50.2 7.8 %collective-permute-done.4.refs_7_.low_down_ref = f32[4,8,1024]{2,1,0:T(8,128)S(1)} collective-permute-done((f32[4,8,1024]{2,1,0:T(8,128)S(1)}, f32[4,8,1024]{2,1,0:T(8,128)S(1)}, u32[]{:S(2)}, u32[]{:S(2)}) %collective-permute-start.4) | collective-permute-done | bytes 131104 | tf_op jit(solution)/shard_map/ppermute | solution.py:836
  58.0 10.5 %fluid_wet.1 = (f32[4,32,1024]{2,1,0:T(8,128)S(1)}, f32[4,8,56,128]{3,2,1,0:T(8,128)S(1)}, f32[4,8,56,128]{3,2,1,0:T(8,128)S(1)}, f32[7,40,1024]{2,1,0:T(8,128)}) custom-call(f32[32,32,1024]{2,1,0:T(8,128)} %refs_0_.5, f32[32,32,1024]{2,1,0:T(8,128)} %refs_1_.5, f32[36,8,1024]{2,1,0:T(8,128)} %copy-done, f32[36,8,1024]{2,1,0:T(8,128)} %copy-done.2, ...), custom_call_target="tpu_custom_call" | custom-call | flops 23592960 | bytes 5898240 | tf_op jit(solution)/shard_map/fluid_wet/pallas_call | solution.py:791
  69.5 1.5 %collective-permute-start.6 = (f32[7,40,1024]{2,1,0:T(8,128)}, f32[7,40,1024]{2,1,0:T(8,128)S(1)}, u32[]{:S(2)}, u32[]{:S(2)}) collective-permute-start(f32[7,40,1024]{2,1,0:T(8,128)} %get-tuple-element.28), channel_id=1, source_target_pairs={{4,0},{5,1},{6,2},{7,3},{8,4},{9,5},{10,6},{11,7},{12,8},{13,9},{1... | collective-permute-start | bytes 3440648 | tf_op jit(solution)/shard_map/ppermute | solution.py:836
  71.0 21.4 %fluid_middle.1 = (f32[32,32,1024]{2,1,0:T(8,128)}, f32[4,8,56,128]{3,2,1,0:T(8,128)S(1)}, f32[4,8,56,128]{3,2,1,0:T(8,128)S(1)}) custom-call(f32[32,32,1024]{2,1,0:T(8,128)} %refs_0_.5, f32[32,32,1024]{2,1,0:T(8,128)} %refs_1_.5, f32[36,8,1024]{2,1,0:T(8,128)} %copy-done, f32[36,8,1024]{2,1,0:T(8,128)} %copy-done.2, ...), custom_call_target="tpu_custom_call" | custom-call | flops 62914560 | bytes 15728640 | tf_op jit(solution)/shard_map/fluid_middle/pallas_call | solution.py:791
  93.4 3.2 %gather_press.1 = f32[32,1,1280]{2,1,0:T(1,128)} custom-call(f32[4,32,1024]{2,1,0:T(8,128)S(1)} %get-tuple-element.25.refs_6_.wet_ref, s32[64,128]{1,0:T(8,128)S(1)} %pad_add_fusion.numbers_ref, f32[32,128]{1,0:T(8,128)S(1)} %gram_rows.1.refs_9_.gram_ref, f32[32,32,1024]{2,1,0:T(8,128)} %get-tuple-element.29.refs_7_.after_ref), custom_call_target="tpu_custom_call" | custom-call | tf_op jit(solution)/shard_map/gather_press/pallas_call | solution.py:843
  96.6 5.8 %all-to-all-start.1 = ((f32[32,1,1280]{2,1,0:T(1,128)}), f32[32,1,1280]{2,1,0:T(1,128)S(1)}, u32[]{:S(2)}, u32[]{:S(2)}) async-start(f32[32,1,1280]{2,1,0:T(1,128)} %gather_press.1), calls=%async_computation.1 | async-start | bytes 327680 | tf_op jit(solution)/shard_map/all_to_all | solution.py:839
  103.5 1.3 copy-done.7
  104.7 1.2 copy-done.10
  105.9 1.2 copy-done.12
  107.1 7.7 %fluid_end.1.after_ref = f32[32,32,1024]{2,1,0:T(8,128)} custom-call(f32[32,32,1024]{2,1,0:T(8,128)} %refs_0_.5, f32[32,32,1024]{2,1,0:T(8,128)} %refs_1_.5, f32[36,8,1024]{2,1,0:T(8,128)} %copy-done, f32[36,8,1024]{2,1,0:T(8,128)} %copy-done.2, f32[4,8,56,128]{3,2,1,0:T(8,128)S(1)} %copy-done.10, ...), custom_call_target="tpu_custom_call", output_to_operand_aliasing={{}: (7, {})} | custom-call | flops 23592960 | bytes 5898240 | tf_op jit(solution)/shard_map/fluid_end/pallas_call | solution.py:791
  114.8 5.7 %shell.1 = (f32[64,512]{1,0:T(8,128)S(1)}, f32[32,1,256]{2,1,0:T(1,128)S(1)}) custom-call(f32[32,1,1280]{2,1,0:T(1,128)S(1)} %all-to-all-done.1.recv_ref, s32[64,128]{1,0:T(8,128)S(1)} %pad_add_fusion.numbers_ref, f32[4,64,512]{2,1,0:T(8,128)S(1)} %pad_maximum_fusion.small_ref, f32[36,8,1024]{2,1,0:T(8,128)S(1)} %copy-done.1, f32[36,8,1024]{2,1,0:T(8,128)} %copy-done.2, ...), custom_call_target="tpu_custom_call" | custom-call | tf_op jit(solution)/shard_map/shell/pallas_call | solution.py:843
  120.6 12.9 %all_to_all.16.recv_ref = f32[32,1,256]{2,1,0:T(1,128)S(1)} all-to-all(f32[32,1,256]{2,1,0:T(1,128)S(1)} %get-tuple-element.30), channel_id=1, replica_groups=mesh['gx'=8,'gy'=4] {'gx','gy'}, dimensions={0} | all-to-all | bytes 65536 | tf_op jit(solution)/shard_map/all_to_all | solution.py:839
  133.5 4.7 %solve.1 = f32[64,512]{1,0:T(8,128)} custom-call(f32[32,1,256]{2,1,0:T(1,128)S(1)} %all_to_all.16.recv_ref, f32[64,512]{1,0:T(8,128)S(1)} %get-tuple-element.31.resp_ref, f32[4,64,512]{2,1,0:T(8,128)S(1)} %pad_maximum_fusion.small_ref, f32[40,64,512]{2,1,0:T(8,128)} %w_ref.1), custom_call_target="tpu_custom_call" | custom-call | tf_op jit(solution)/shard_map/solve/pallas_call | solution.py:843
  (36 shorter events, 5.4 us)
Async XLA Ops:
  22.2 12.5 %collective-permute-start = (f32[36,8,1024]{2,1,0:T(8,128)S(1)}, f32[36,8,1024]{2,1,0:T(8,128)S(1)}, u32[]{:S(2)}, u32[]{:S(2)}) collective-permute-start(f32[36,8,1024]{2,1,0:T(8,128)S(1)} %get-tuple-element.17), channel_id=1, source_target_pairs={{1,0},{2,1},{3,2},{5,4},{6,5},{7,6},{9,8},{10,9},{11,10},{13,12},{... | collective-permute-start | bytes 3538952 | tf_op jit(solution)/shard_map/ppermute | solution.py:836
  23.5 11.3 %collective-permute-start.1 = (f32[36,8,1024]{2,1,0:T(8,128)}, f32[36,8,1024]{2,1,0:T(8,128)S(1)}, u32[]{:S(2)}, u32[]{:S(2)}) collective-permute-start(f32[36,8,1024]{2,1,0:T(8,128)} %get-tuple-element.18), channel_id=1, source_target_pairs={{0,1},{1,2},{2,3},{4,5},{5,6},{6,7},{8,9},{9,10},{10,11},{12,13},{... | collective-permute-start | bytes 3538952 | tf_op jit(solution)/shard_map/ppermute | solution.py:836
  26.6 31.4 %collective-permute-start.2 = (f32[30,8,1024]{2,1,0:T(8,128)S(1)}, f32[30,8,1024]{2,1,0:T(8,128)S(1)}, u32[]{:S(2)}, u32[]{:S(2)}) collective-permute-start(f32[30,8,1024]{2,1,0:T(8,128)S(1)} %get-tuple-element.19), channel_id=1, source_target_pairs={{0,4},{1,5},{2,6},{3,7},{4,8},{5,9},{6,10},{7,11},{8,12},{9,13},{1... | collective-permute-start | bytes 2949128 | tf_op jit(solution)/shard_map/ppermute | solution.py:836
  29.2 21.0 %collective-permute-start.3 = (f32[4,8,1024]{2,1,0:T(8,128)S(1)}, f32[4,8,1024]{2,1,0:T(8,128)S(1)}, u32[]{:S(2)}, u32[]{:S(2)}) collective-permute-start(f32[4,8,1024]{2,1,0:T(8,128)S(1)} %get-tuple-element.20), channel_id=1, source_target_pairs={{1,4},{2,5},{3,6},{5,8},{6,9},{7,10},{9,12},{10,13},{11,14},{13,16... | collective-permute-start | bytes 393224 | tf_op jit(solution)/shard_map/ppermute | solution.py:836
  29.9 28.1 %collective-permute-start.4 = (f32[4,8,1024]{2,1,0:T(8,128)S(1)}, f32[4,8,1024]{2,1,0:T(8,128)S(1)}, u32[]{:S(2)}, u32[]{:S(2)}) collective-permute-start(f32[4,8,1024]{2,1,0:T(8,128)S(1)} %get-tuple-element.21), channel_id=1, source_target_pairs={{0,5},{1,6},{2,7},{4,9},{5,10},{6,11},{8,13},{9,14},{10,15},{12,17... | collective-permute-start | bytes 393224 | tf_op jit(solution)/shard_map/ppermute | solution.py:836
  34.8 8.9 %copy-start = (f32[36,8,1024]{2,1,0:T(8,128)}, f32[36,8,1024]{2,1,0:T(8,128)S(1)}, u32[]{:S(2)}) copy-start(f32[36,8,1024]{2,1,0:T(8,128)S(1)} %collective-permute-done.up_ref.refs_2_) | copy-start | bytes 3538948
  34.8 8.8 %copy-start.2 = (f32[36,8,1024]{2,1,0:T(8,128)}, f32[36,8,1024]{2,1,0:T(8,128)S(1)}, u32[]{:S(2)}) copy-start(f32[36,8,1024]{2,1,0:T(8,128)S(1)} %collective-permute-done.1.down_ref.refs_3_) | copy-start | bytes 3538948
  34.8 23.2 %collective-permute-start.5 = (f32[4,8,1024]{2,1,0:T(8,128)S(1)}, f32[4,8,1024]{2,1,0:T(8,128)S(1)}, u32[]{:S(2)}, u32[]{:S(2)}) collective-permute-start(f32[4,8,1024]{2,1,0:T(8,128)S(1)} %pad_maximum_fusion.1), channel_id=1, source_target_pairs={{4,0},{5,1},{6,2},{7,3},{8,4},{9,5},{10,6},{11,7},{12,8},{13,9},{1... | collective-permute-start | bytes 393224 | tf_op jit(solution)/shard_map/ppermute | solution.py:836
  49.2 1.0 copy-start.3
  58.0 10.5 %copy-start.4 = (f32[30,8,1024]{2,1,0:T(8,128)}, f32[30,8,1024]{2,1,0:T(8,128)S(1)}, u32[]{:S(2)}) copy-start(f32[30,8,1024]{2,1,0:T(8,128)S(1)} %collective-permute-done.2.refs_5_.low_ref) | copy-start | bytes 2949124
  68.6 1.0 copy-start.8
  69.5 32.9 %collective-permute-start.6 = (f32[7,40,1024]{2,1,0:T(8,128)}, f32[7,40,1024]{2,1,0:T(8,128)S(1)}, u32[]{:S(2)}, u32[]{:S(2)}) collective-permute-start(f32[7,40,1024]{2,1,0:T(8,128)} %get-tuple-element.28), channel_id=1, source_target_pairs={{4,0},{5,1},{6,2},{7,3},{8,4},{9,5},{10,6},{11,7},{12,8},{13,9},{1... | collective-permute-start | bytes 3440648 | tf_op jit(solution)/shard_map/ppermute | solution.py:836
  92.5 1.0 copy-start.11
  93.4 3.2 %copy-start.9 = (f32[4,8,56,128]{3,2,1,0:T(8,128)}, f32[4,8,56,128]{3,2,1,0:T(8,128)S(1)}, u32[]{:S(2)}) copy-start(f32[4,8,56,128]{3,2,1,0:T(8,128)S(1)} %get-tuple-element.26.refs_4_) | copy-start | bytes 2752516
  96.6 18.2 %all-to-all-start.1 = ((f32[32,1,1280]{2,1,0:T(1,128)}), f32[32,1,1280]{2,1,0:T(1,128)S(1)}, u32[]{:S(2)}, u32[]{:S(2)}) async-start(f32[32,1,1280]{2,1,0:T(1,128)} %gather_press.1), calls=%async_computation.1 | async-start | bytes 327680 | tf_op jit(solution)/shard_map/all_to_all | solution.py:839
  102.4 1.0 copy-start.6
  103.5 1.3 copy-start.7
  104.7 1.2 copy-start.10
  105.9 1.2 copy-start.12
  107.1 7.7 %copy-start.1 = (f32[36,8,1024]{2,1,0:T(8,128)S(1)}, f32[36,8,1024]{2,1,0:T(8,128)}, u32[]{:S(2)}) copy-start(f32[36,8,1024]{2,1,0:T(8,128)} %copy-done) | copy-start | bytes 3538948
  107.1 7.8 %copy-start.5 = (f32[30,8,1024]{2,1,0:T(8,128)S(1)}, f32[30,8,1024]{2,1,0:T(8,128)}, u32[]{:S(2)}) copy-start(f32[30,8,1024]{2,1,0:T(8,128)} %copy-done.4) | copy-start | bytes 2949124

commit v7 on v6

--- a/solution.py
+++ b/solution.py
@@ -595,9 +595,8 @@
     )(phi, kappa, after, small, numbers)
 
 
-def substep(src, kap, coef, dst, plane, advect, rows, cz):
-    chunks = cz // 128
-    wide = kap.shape[1]
+def substep(src, kap, coef, write, plane, advect, rows):
+    chunks = src.shape[1]
     lane = lax.broadcasted_iota(jnp.int32, (rows, 128), 1)
     first, last = lane == 0, lane == 127
 
@@ -615,158 +614,177 @@
         before = take(plane - 1, q)
         total = total + (before + take(plane + 1, q))
         at = slice(q * 128, (q + 1) * 128)
-        new = (coef[plane - 1, 0:rows, at] * now + advect * before) + kap[
-            plane - 1, 0:rows, at
-        ] * total
-        dst[plane, q, 8 : 8 + rows, :] = new
-        if rows == wide:
-            dst[plane, q, 7:8, :] = new[wide - 1 :]
-            dst[plane, q, 8 + wide : 9 + wide, :] = new[0:1]
+        write(q, (coef[plane, 0:rows, at] * now + advect * before) + kap[
+            plane, 0:rows, at
+        ] * total)
 
 
 def fluid(x0, x1, cx, cy, cz, kind, *refs):
     planes = x1 - x0 + 8
     wide = cy + 8
     chunks = cz // 128
+    tiles = cy // 8
     names = ["phi", "kappa", "up", "down"]
     names += {"wet": ["forced", "low", "low_up", "low_down", "near", "gram"],
               "middle": ["state_a", "state_b", "wet"],
               "end": ["state_a", "state_b", "high", "whole"]}[kind]
     names += {"wet": ["out", "next_a", "next_b", "send"], "middle": ["out", "next_a", "next_b"],
               "end": ["out"]}[kind]
-    names += ["a", "b", "kap", "coef", "stage", "sems", "out_sems"]
+    names += ["a", "b", "kap", "coef", "stage", "done", "sems", "kap_sems", "out_sems", "more_sems"]
     r = dict(zip(names, refs))
     a, b, kap, coef, stage = r["a"], r["b"], r["kap"], r["coef"], r["stage"]
     carried = kind != "wet"
     is_last = lax.axis_index("gx") == lax.axis_size("gx") - 1
-    copy, copy_out = starter(r["sems"]), starter(r["out_sems"])
-
-    def unchunked(src, s0, count, row, rows, dst, d0):
-        return [
-            copy_out(
-                src.at[pl.ds(s0, count), q, pl.ds(row, rows)],
-                dst.at[pl.ds(d0, count), :, pl.ds(q * 128, 128)],
-            )
-            for q in range(chunks)
-        ]
-
-    own0, own1 = x0 + 4 if carried else x0, min(cx, x1 + 4)
-    kap0 = x0 if carried else x0 - 3
-    groups = []
+    copy = starter(r["more_sems"])
+    phi0, own1 = x0 + 4, min(cx, x1 + 4)
+
+    def loop(lo, hi, body):
+        def run(i, carry):
+            body(i)
+            return carry
+
+        if hi > lo:
+            lax.fori_loop(lo, hi, run, 0)
+
+    def phi_copy(x):
+        return pltpu.make_async_copy(r["phi"].at[x], stage.at[x - phi0], r["sems"].at[x - phi0])
+
+    def kappa_copy(x):
+        return pltpu.make_async_copy(
+            r["kappa"].at[x], kap.at[x - (x0 - 4), pl.ds(0, cy)], r["kap_sems"].at[x - x0]
+        )
+
+    states = []
     if carried:
-        kappa_first = copy(r["kappa"].at[pl.ds(x0, 4)], kap.at[pl.ds(3, 4), pl.ds(0, cy)])
-    start = own0
-    while start < own1:
-        count = min(4, own1 - start)
-        i = start - (x0 - 4)
-        k0, k1 = start, min(start + count, x1 + 3)
-        copies = [] if k1 <= k0 else [
-            copy(r["kappa"].at[pl.ds(k0, k1 - k0)],
-                 kap.at[pl.ds(k0 - (x0 - 3), k1 - k0), pl.ds(0, cy)]),
-        ]
-        if carried or start >= 4:
-            copies.append(
-                copy(r["phi"].at[pl.ds(start, count)], stage.at[pl.ds(start - own0, count)])
-            )
-        groups.append((i, i + count, copies))
-        start += count
+        states = [copy(r["state_a"], a.at[pl.ds(4, 4)]), copy(r["state_b"], b.at[pl.ds(3, 4)])]
+    loop(x0, min(x0 + 4, own1), lambda x: kappa_copy(x).start())
+
+    def start_own(x):
+        phi_copy(x).start()
+        kappa_copy(x).start()
+
+    loop(phi0, own1, start_own)
     outs = []
     if kind == "middle":
-        outs.append(copy_out(r["wet"], r["out"].at[pl.ds(0, x0)]))
-
+        outs.append(copy(r["wet"], r["out"].at[pl.ds(0, x0)]))
     upper = lax.broadcasted_iota(jnp.int32, (8, cz), 0) < 4
 
-    def assemble(i, only_kappa=False):
-        x = x0 - 4 + i
-        inner = 1 <= i < planes - 1
-        whole = slice(8, 8 + wide)
-        if x >= cx:
-            if inner:
-                kap[i - 1] = r["high"][4 + x - cx]
-        else:
-            if x >= 0:
-                up, down = r["up"][x], r["down"][x]
-            elif x > -4:
-                up, down = r["low_up"][x + 3], r["low_down"][x + 3]
-            else:
-                up = down = jnp.zeros((8, cz), F32)
-            edge = jnp.where(upper, up, down)
-            if inner:
-                if x < 0:
-                    for t in range(cy // 8):
-                        kap[i - 1, 8 * t : 8 * t + 8, :] = r["low"][(x + 7) * (cy // 8) + t]
-                kap[i - 1, cy:wide, :] = pltpu.roll(jnp.where(upper, down, up), 4, axis=0)
-        if inner:
-            coef[i - 1] = 0.75 - 6.0 * kap[i - 1]
-        if only_kappa:
-            return
+    def set_kappa_edge(i, up, down):
+        kap[i, cy:wide, :] = pltpu.roll(jnp.where(upper, down, up), 4, axis=0)
+
+    def set_coef(i):
+        coef[i] = 0.75 - 6.0 * kap[i]
+
+    def repeat_rows(i, q):
+        a[i, q, 7:8, :] = a[i, q, 7 + wide : 8 + wide, :]
+        a[i, q, 8 + wide : 9 + wide, :] = a[i, q, 8:9, :]
+
+    def lanes(q):
+        return slice(q * 128, (q + 1) * 128)
+
+    def set_low(i):
+        from_tiles = jnp.maximum(i - 1, 0)
+        up, down = r["low_up"][from_tiles], r["low_down"][from_tiles]
+        edge = jnp.where(upper, up, down)
+        for t in range(tiles):
+            rows = r["low"][i * tiles + t]
+            kap[i, 8 * t : 8 * t + 8, :] = r["low"][(i + 3) * tiles + t]
+            for q in range(chunks):
+                a[i, q, 8 + 8 * t : 16 + 8 * t, :] = rows[:, lanes(q)]
+        set_kappa_edge(i, up, down)
+        set_coef(i)
         for q in range(chunks):
-            at = slice(q * 128, (q + 1) * 128)
-            if x >= cx:
-                a[i, q, whole, :] = r["high"][x - cx, :, at]
-            elif kind == "wet" and 0 <= x < 4:
-                a[i, q, whole, :] = r["forced"][x, :, at]
-            else:
-                if x < 0:
-                    for t in range(cy // 8):
-                        a[i, q, 8 + 8 * t : 16 + 8 * t, :] = r["low"][(x + 4) * (cy // 8) + t, :, at]
-                else:
-                    a[i, q, 8 : 8 + cy, :] = stage[x - own0, :, at]
-                a[i, q, 8 + cy : 8 + wide, :] = edge[:, at]
-            a[i, q, 7:8, :] = a[i, q, 7 + wide : 8 + wide, :]
-            a[i, q, 8 + wide : 9 + wide, :] = a[i, q, 8:9, :]
-
-    def run(src, dst, lo, hi, rows=wide):
-        def body(i, carry):
-            advect = 0.25
-            if kind == "end":
-                outside = jnp.logical_and(is_last, i + (x0 - 4) >= cx)
-                advect = jnp.where(outside, 0.0, 0.25)
-            substep(src, kap, coef, dst, i, advect, rows, cz)
-            return carry
-
-        if hi > lo:
-            lax.fori_loop(lo, hi, body, 0)
+            a[i, q, 8 + cy : 8 + wide, :] = edge[:, lanes(q)]
+            repeat_rows(i, q)
+
+    def set_first(i):
+        x = i + (x0 - 4)
+        kappa_copy(x).wait()
+        set_kappa_edge(i, r["up"][x], r["down"][x])
+        set_coef(i)
+        if kind == "wet":
+            for q in range(chunks):
+                a[i, q, 8 : 8 + wide, :] = r["forced"][x, :, lanes(q)]
+                repeat_rows(i, q)
+
+    def set_own(i):
+        x = i + (x0 - 4)
+        phi_copy(x).wait()
+        kappa_copy(x).wait()
+        up, down = r["up"][x], r["down"][x]
+        edge = jnp.where(upper, up, down)
+        set_kappa_edge(i, up, down)
+        set_coef(i)
+        for q in range(chunks):
+            a[i, q, 8 : 8 + cy, :] = stage[x - phi0, :, lanes(q)]
+            a[i, q, 8 + cy : 8 + wide, :] = edge[:, lanes(q)]
+            repeat_rows(i, q)
+
+    def set_high(i):
+        x = i + (x0 - 4) - cx
+        kap[i] = r["high"][jnp.minimum(x + 4, 6)]
+        set_coef(i)
+        for q in range(chunks):
+            a[i, q, 8 : 8 + wide, :] = r["high"][x, :, lanes(q)]
+            repeat_rows(i, q)
+
+    def step(src, dst, i):
+        advect = 0.25
+        if kind == "end":
+            advect = jnp.where(jnp.logical_and(is_last, i + (x0 - 4) >= cx), 0.0, 0.25)
+
+        def write(q, new):
+            dst[i, q, 8 : 8 + wide, :] = new
+            dst[i, q, 7:8, :] = new[wide - 1 :]
+            dst[i, q, 8 + wide : 9 + wide, :] = new[0:1]
+
+        substep(src, kap, coef, write, i, advect, wide)
+
+    def out_copy(i):
+        return pltpu.make_async_copy(
+            r["done"].at[i - 4], r["out"].at[x0 + i - 4], r["out_sems"].at[i - 4]
+        )
+
+    def final(i):
+        target = r["out"] if kind == "wet" else r["done"]
+
+        def write(q, new):
+            target[i - 4, :, lanes(q)] = new
+
+        substep(b, kap, coef, write, i, 0.25, cy)
+        if kind != "wet":
+            out_copy(i).start()
 
     if kind == "wet":
-        for i in range(4):
-            assemble(i)
-        done = 1
+        loop(0, 4, set_low)
+    loop(4, 8, set_first)
+    for made in states:
+        made.wait()
+    if kind == "wet":
+        loop(8, planes, set_own)
+        loop(1, planes - 1, lambda i: step(a, b, i))
+    elif kind == "middle":
+
+        def first_level(i):
+            set_own(i + 1)
+            step(a, b, i)
+
+        loop(7, planes - 1, first_level)
     else:
-        a[4:8] = r["state_a"][...]
-        b[3:7] = r["state_b"][...]
-        kappa_first.wait()
-        for i in range(4, 8):
-            assemble(i, True)
-        done = 7
-    for i0, i1, copies in groups:
-        for made in copies:
-            made.wait()
-        for i in range(i0, i1):
-            assemble(i)
-        run(a, b, done, i1 - 1)
-        done = i1 - 1
-    if kind == "end":
-        for i in range(planes - 4, planes):
-            assemble(i)
-        run(a, b, done, planes - 1)
-    run(b, a, 6 if carried else 2, planes - 2)
-    run(a, b, 5 if carried else 3, planes - 3)
+        loop(8, planes, set_high)
+        loop(7, planes - 1, lambda i: step(a, b, i))
+    loop(6 if carried else 2, planes - 2, lambda i: step(b, a, i))
+    loop(5 if carried else 3, planes - 3, lambda i: step(a, b, i))
+    if kind != "end":
+        outs.append(copy(a.at[pl.ds(planes - 4, 4)], r["next_a"]))
+        outs.append(copy(b.at[pl.ds(planes - 5, 4)], r["next_b"]))
     if kind == "wet":
-        r["send"][...] = r["forced"][...]
-    for start in range(4, planes - 4, 4):
-        run(b, a, start, start + 4, cy)
-        if kind == "wet":
-            for i in range(start, start + 4):
-                for q in range(chunks):
-                    r["out"][i - 4, :, q * 128 : (q + 1) * 128] = a[i, q, 8 : 8 + cy, :]
-        else:
-            outs += unchunked(a, start, 4, 8, cy, r["out"], x0 + start - 4)
-    if kind != "end":
-        r["next_a"][...] = a[planes - 4 : planes]
-        r["next_b"][...] = b[planes - 5 : planes - 1]
+        outs.append(copy(r["forced"], r["send"]))
+    loop(4, planes - 4, final)
     for made in outs:
         made.wait()
+    if kind != "wet":
+        loop(4, planes - 4, lambda i: out_copy(i).wait())
 
 
 def fluid_call(kind, x0, x1, phi, kappa, up, down, *more):
@@ -780,27 +798,27 @@
             jax.ShapeDtypeStruct((x1 - x0, cy, cz), F32), *state,
             jax.ShapeDtypeStruct((7, cy + 8, cz), F32),
         ]
-        out_specs = vmem_specs(4)
+        out_specs = vmem_specs(1) + any_specs(3)
     elif kind == "middle":
-        specs = vmem_specs(3)
-        out_shape, out_specs = [field, *state], hbm_specs(1) + vmem_specs(2)
+        specs = any_specs(2) + vmem_specs(1)
+        out_shape, out_specs = [field, *state], hbm_specs(1) + any_specs(2)
     else:
-        specs = vmem_specs(3) + hbm_specs(1)
+        specs = any_specs(2) + vmem_specs(1) + hbm_specs(1)
         out_shape, out_specs = field, hbm_specs(1)[0]
     cells = planes * (cy + 8) * cz
+    stepped = pltpu.VMEM((planes, cz // 128, cy + 24, 128), F32)
+    wide = pltpu.VMEM((planes, cy + 8, cz), F32)
+    sems = pltpu.SemaphoreType.DMA((planes,))
     return pl.pallas_call(
         functools.partial(fluid, x0, x1, cx, cy, cz, kind),
         in_specs=hbm_specs(2) + vmem_specs(2) + specs,
         out_specs=out_specs,
         out_shape=out_shape,
         scratch_shapes=[
-            pltpu.VMEM((planes, cz // 128, cy + 24, 128), F32),
-            pltpu.VMEM((planes, cz // 128, cy + 24, 128), F32),
-            pltpu.VMEM((planes - 2, cy + 8, cz), F32),
-            pltpu.VMEM((planes - 2, cy + 8, cz), F32),
-            pltpu.VMEM((max(min(cx, x1 + 4) - (x0 if kind == "wet" else x0 + 4), 1), cy, cz), F32),
-            pltpu.SemaphoreType.DMA((80,)),
-            pltpu.SemaphoreType.DMA((80,)),
+            stepped, stepped, wide, wide,
+            pltpu.VMEM((max(min(cx, x1 + 4) - x0 - 4, 1), cy, cz), F32),
+            pltpu.VMEM((1 if kind == "wet" else x1 - x0, cy, cz), F32),
+            sems, sems, sems, pltpu.SemaphoreType.DMA((8,)),
         ],
         input_output_aliases={7: 0} if kind == "end" else {},
         compiler_params=params(),

time: 139 us -> 137 us (0.986)
  Pallas kernels: 71.3 us -> 69.1 us
    pallas_call x3, Pallas kernels: 39.6 us -> 37.5 us  [fluid_call(): pl.pallas_call(functools.partial(fluid, x0, x1, cx, cy, cz, kind), in_spe...]
  transfers between devices with their start and end apart: 8 -> 8, of which waited for: 1 -> 1; matrix products, arithmetic and copies ran while one was open for 0% -> 0% of each run, Pallas kernels for 33% -> 32%
where the time goes in v7:
time: 137 us; the launch traced here: 136 us
  Pallas kernels  69.1 us (50%)
  blocking collectives  27.3 us (20%)
  starting transfers between devices  21.3 us (16%)
  waiting for transfers between devices  7.85 us (6%)
  local copies, waits for them, and re-layouts  7.61 us (6%)
  other arithmetic  1.88 us (1%)
    pallas_call x3, Pallas kernels, fluid_call(): pl.pallas_call(functools.partial(fluid, x0, x1, cx, cy, cz, kind), in_spe...  37.5 us
    pallas_call x6, Pallas kernels, call(): pl.pallas_call(body, in_specs=specs, out_specs=vmem_specs(len(out_shape))...  27.6 us
    all_to_all x2, blocking collectives, exchange(): return lax.all_to_all(value, axes, split_axis=0, concat_axis=0, tiled=True)  27.3 us
    ppermute x7, starting transfers between devices, shift(): return lax.ppermute(value, axes, shifted_pairs(n_gx, n_gy, dx, dy))  15.5 us
    ppermute x7, waiting for transfers between devices, shift(): return lax.ppermute(value, axes, shifted_pairs(n_gx, n_gy, dx, dy))  7.85 us
    unnamed x26, local copies, waits for them, and re-layouts  7.59 us
    all_to_all x1, starting transfers between devices, exchange(): return lax.all_to_all(value, axes, split_axis=0, concat_axis=0, tiled=True)  5.8 us
    pallas_call x1, Pallas kernels, packed(): pl.pallas_call(pack, in_specs=hbm_specs(2) + any_specs(1) + vmem_specs(2)...  4.05 us
  transfers between devices with their start and end apart: 8, of which 1 were waited for; matrix products, arithmetic and copies ran while one was open for 0% of the time, Pallas kernels for 32%

profile of v7, /device:TPU:0, one launch (start us, length us, event | category | flops | bytes accessed | tf_op | source)
XLA Modules:
  0.0 136.2 jit_solution(12524387701272412600)
XLA Ops:
  1.4 1.1 pad_maximum_fusion.small_ref
  2.5 1.2 gather_disp.1
  3.7 14.4 %all_to_all.15.after_ref.disp_ref = f32[32,1,384]{2,1,0:T(1,128)S(1)} all-to-all(f32[32,1,384]{2,1,0:T(1,128)S(1)} %gather_disp.1), channel_id=1, replica_groups=mesh['gx'=8,'gy'=4] {'gx','gy'}, dimensions={0} | all-to-all | bytes 98304 | tf_op jit(solution)/shard_map/all_to_all | solution.py:857
  18.1 4.0 %pack.1 = (f32[36,8,1024]{2,1,0:T(8,128)S(1)}, f32[36,8,1024]{2,1,0:T(8,128)}, f32[30,8,1024]{2,1,0:T(8,128)S(1)}, f32[4,8,1024]{2,1,0:T(8,128)S(1)}, f32[4,8,10...) custom-call(f32[32,32,1024]{2,1,0:T(8,128)} %refs_0_.5, f32[32,32,1024]{2,1,0:T(8,128)} %refs_1_.5, ...), custom_call_target="tpu_custom_call" | custom-call | tf_op jit(solution)/shard_map/pack/pallas_call | solution.py:583
  22.2 1.3 collective-permute-start
  23.5 3.1 %collective-permute-start.1 = (f32[36,8,1024]{2,1,0:T(8,128)}, f32[36,8,1024]{2,1,0:T(8,128)S(1)}, u32[]{:S(2)}, u32[]{:S(2)}) collective-permute-start(f32[36,8,1024]{2,1,0:T(8,128)} %get-tuple-element.18), channel_id=1, source_target_pairs={{0,1},{1,2},{2,3},{4,5},{5,6},{6,7},{8,9},{9,10},{10,11},{12,13},{... | collective-permute-start | bytes 3538952 | tf_op jit(solution)/shard_map/ppermute | solution.py:854
  26.6 2.5 %collective-permute-start.2 = (f32[30,8,1024]{2,1,0:T(8,128)S(1)}, f32[30,8,1024]{2,1,0:T(8,128)S(1)}, u32[]{:S(2)}, u32[]{:S(2)}) collective-permute-start(f32[30,8,1024]{2,1,0:T(8,128)S(1)} %get-tuple-element.19), channel_id=1, source_target_pairs={{0,4},{1,5},{2,6},{3,7},{4,8},{5,9},{6,10},{7,11},{8,12},{9,13},{1... | collective-permute-start | bytes 2949128 | tf_op jit(solution)/shard_map/ppermute | solution.py:854
  29.9 4.9 %collective-permute-start.4 = (f32[4,8,1024]{2,1,0:T(8,128)S(1)}, f32[4,8,1024]{2,1,0:T(8,128)S(1)}, u32[]{:S(2)}, u32[]{:S(2)}) collective-permute-start(f32[4,8,1024]{2,1,0:T(8,128)S(1)} %get-tuple-element.21), channel_id=1, source_target_pairs={{0,5},{1,6},{2,7},{4,9},{5,10},{6,11},{8,13},{9,14},{10,15},{12,17... | collective-permute-start | bytes 393224 | tf_op jit(solution)/shard_map/ppermute | solution.py:854
  34.8 1.5 %collective-permute-start.5 = (f32[4,8,1024]{2,1,0:T(8,128)S(1)}, f32[4,8,1024]{2,1,0:T(8,128)S(1)}, u32[]{:S(2)}, u32[]{:S(2)}) collective-permute-start(f32[4,8,1024]{2,1,0:T(8,128)S(1)} %pad_maximum_fusion.1), channel_id=1, source_target_pairs={{4,0},{5,1},{6,2},{7,3},{8,4},{9,5},{10,6},{11,7},{12,8},{13,9},{1... | collective-permute-start | bytes 393224 | tf_op jit(solution)/shard_map/ppermute | solution.py:854
  36.3 7.3 %gram_rows.1.refs_9_.gram_ref = f32[32,128]{1,0:T(8,128)S(1)} custom-call(f32[40,64,512]{2,1,0:T(8,128)} %v_ref.3), custom_call_target="tpu_custom_call" | custom-call | tf_op jit(solution)/shard_map/gram_rows/pallas_call | solution.py:861
  43.6 5.5 %scatter_disp.1.refs_4_ = f32[7,40,1024]{2,1,0:T(8,128)S(1)} custom-call(f32[32,1,384]{2,1,0:T(1,128)S(1)} %all_to_all.15.after_ref.disp_ref, s32[64,128]{1,0:T(8,128)S(1)} %pad_add_fusion.numbers_ref, f32[36,8,1024]{2,1,0:T(8,128)S(1)} %collective-permute-done.up_ref.refs_2_, f32[36,8,1024]{2,1,0:T(8,128)S(1)} %collective-permute-done.1.down_ref.refs_3_, ...), custom_call_target="tpu_custom_call" | custom-call | tf_op jit(solution)/shard_map/scatter_disp/pallas_call | solution.py:861
  50.2 7.8 %collective-permute-done.4.refs_7_.low_down_ref = f32[4,8,1024]{2,1,0:T(8,128)S(1)} collective-permute-done((f32[4,8,1024]{2,1,0:T(8,128)S(1)}, f32[4,8,1024]{2,1,0:T(8,128)S(1)}, u32[]{:S(2)}, u32[]{:S(2)}) %collective-permute-start.4) | collective-permute-done | bytes 131104 | tf_op jit(solution)/shard_map/ppermute | solution.py:854
  58.0 9.5 %fluid_wet.1 = (f32[4,32,1024]{2,1,0:T(8,128)S(1)}, f32[4,8,56,128]{3,2,1,0:T(8,128)S(1)}, f32[4,8,56,128]{3,2,1,0:T(8,128)S(1)}, f32[7,40,1024]{2,1,0:T(8,128)}) custom-call(f32[32,32,1024]{2,1,0:T(8,128)} %refs_0_.5, f32[32,32,1024]{2,1,0:T(8,128)} %refs_1_.5, f32[36,8,1024]{2,1,0:T(8,128)} %copy-done, f32[36,8,1024]{2,1,0:T(8,128)} %copy-done.2, ...), custom_call_target="tpu_custom_call" | custom-call | flops 23592960 | bytes 5898240 | tf_op jit(solution)/shard_map/fluid_wet/pallas_call | solution.py:812
  68.5 1.5 %collective-permute-start.6 = (f32[7,40,1024]{2,1,0:T(8,128)}, f32[7,40,1024]{2,1,0:T(8,128)S(1)}, u32[]{:S(2)}, u32[]{:S(2)}) collective-permute-start(f32[7,40,1024]{2,1,0:T(8,128)} %get-tuple-element.28), channel_id=1, source_target_pairs={{4,0},{5,1},{6,2},{7,3},{8,4},{9,5},{10,6},{11,7},{12,8},{13,9},{1... | collective-permute-start | bytes 3440648 | tf_op jit(solution)/shard_map/ppermute | solution.py:854
  70.0 21.0 %fluid_middle.1 = (f32[32,32,1024]{2,1,0:T(8,128)}, f32[4,8,56,128]{3,2,1,0:T(8,128)S(1)}, f32[4,8,56,128]{3,2,1,0:T(8,128)S(1)}) custom-call(f32[32,32,1024]{2,1,0:T(8,128)} %refs_0_.5, f32[32,32,1024]{2,1,0:T(8,128)} %refs_1_.5, f32[36,8,1024]{2,1,0:T(8,128)} %copy-done, f32[36,8,1024]{2,1,0:T(8,128)} %copy-done.2, ...), custom_call_target="tpu_custom_call" | custom-call | flops 62914560 | bytes 15728640 | tf_op jit(solution)/shard_map/fluid_middle/pallas_call | solution.py:812
  91.9 3.2 %gather_press.1 = f32[32,1,1280]{2,1,0:T(1,128)} custom-call(f32[4,32,1024]{2,1,0:T(8,128)S(1)} %get-tuple-element.25.refs_6_.wet_ref, s32[64,128]{1,0:T(8,128)S(1)} %pad_add_fusion.numbers_ref, f32[32,128]{1,0:T(8,128)S(1)} %gram_rows.1.refs_9_.gram_ref, f32[32,32,1024]{2,1,0:T(8,128)} %get-tuple-element.29.refs_7_.after_ref), custom_call_target="tpu_custom_call" | custom-call | tf_op jit(solution)/shard_map/gather_press/pallas_call | solution.py:861
  95.1 5.8 %all-to-all-start.1 = ((f32[32,1,1280]{2,1,0:T(1,128)}), f32[32,1,1280]{2,1,0:T(1,128)S(1)}, u32[]{:S(2)}, u32[]{:S(2)}) async-start(f32[32,1,1280]{2,1,0:T(1,128)} %gather_press.1), calls=%async_computation.1 | async-start | bytes 327680 | tf_op jit(solution)/shard_map/all_to_all | solution.py:857
  102.0 1.3 copy-done.7
  103.2 1.2 copy-done.10
  104.4 1.2 copy-done.12
  105.6 7.0 %fluid_end.1.after_ref = f32[32,32,1024]{2,1,0:T(8,128)} custom-call(f32[32,32,1024]{2,1,0:T(8,128)} %refs_0_.5, f32[32,32,1024]{2,1,0:T(8,128)} %refs_1_.5, f32[36,8,1024]{2,1,0:T(8,128)} %copy-done, f32[36,8,1024]{2,1,0:T(8,128)} %copy-done.2, f32[4,8,56,128]{3,2,1,0:T(8,128)S(1)} %copy-done.10, ...), custom_call_target="tpu_custom_call", output_to_operand_aliasing={{}: (7, {})} | custom-call | flops 23592960 | bytes 5898240 | tf_op jit(solution)/shard_map/fluid_end/pallas_call | solution.py:812
  112.7 5.7 %shell.1 = (f32[64,512]{1,0:T(8,128)S(1)}, f32[32,1,256]{2,1,0:T(1,128)S(1)}) custom-call(f32[32,1,1280]{2,1,0:T(1,128)S(1)} %all-to-all-done.1.recv_ref, s32[64,128]{1,0:T(8,128)S(1)} %pad_add_fusion.numbers_ref, f32[4,64,512]{2,1,0:T(8,128)S(1)} %pad_maximum_fusion.small_ref, f32[36,8,1024]{2,1,0:T(8,128)S(1)} %copy-done.1, f32[36,8,1024]{2,1,0:T(8,128)} %copy-done.2, ...), custom_call_target="tpu_custom_call" | custom-call | tf_op jit(solution)/shard_map/shell/pallas_call | solution.py:861
  118.4 12.9 %all_to_all.16.recv_ref = f32[32,1,256]{2,1,0:T(1,128)S(1)} all-to-all(f32[32,1,256]{2,1,0:T(1,128)S(1)} %get-tuple-element.30), channel_id=1, replica_groups=mesh['gx'=8,'gy'=4] {'gx','gy'}, dimensions={0} | all-to-all | bytes 65536 | tf_op jit(solution)/shard_map/all_to_all | solution.py:857
  131.3 4.7 %solve.1 = f32[64,512]{1,0:T(8,128)} custom-call(f32[32,1,256]{2,1,0:T(1,128)S(1)} %all_to_all.16.recv_ref, f32[64,512]{1,0:T(8,128)S(1)} %get-tuple-element.31.resp_ref, f32[4,64,512]{2,1,0:T(8,128)S(1)} %pad_maximum_fusion.small_ref, f32[40,64,512]{2,1,0:T(8,128)} %w_ref.1), custom_call_target="tpu_custom_call" | custom-call | tf_op jit(solution)/shard_map/solve/pallas_call | solution.py:861
  (36 shorter events, 5.4 us)
Async XLA Ops:
  22.2 12.5 %collective-permute-start = (f32[36,8,1024]{2,1,0:T(8,128)S(1)}, f32[36,8,1024]{2,1,0:T(8,128)S(1)}, u32[]{:S(2)}, u32[]{:S(2)}) collective-permute-start(f32[36,8,1024]{2,1,0:T(8,128)S(1)} %get-tuple-element.17), channel_id=1, source_target_pairs={{1,0},{2,1},{3,2},{5,4},{6,5},{7,6},{9,8},{10,9},{11,10},{13,12},{... | collective-permute-start | bytes 3538952 | tf_op jit(solution)/shard_map/ppermute | solution.py:854
  23.5 11.3 %collective-permute-start.1 = (f32[36,8,1024]{2,1,0:T(8,128)}, f32[36,8,1024]{2,1,0:T(8,128)S(1)}, u32[]{:S(2)}, u32[]{:S(2)}) collective-permute-start(f32[36,8,1024]{2,1,0:T(8,128)} %get-tuple-element.18), channel_id=1, source_target_pairs={{0,1},{1,2},{2,3},{4,5},{5,6},{6,7},{8,9},{9,10},{10,11},{12,13},{... | collective-permute-start | bytes 3538952 | tf_op jit(solution)/shard_map/ppermute | solution.py:854
  26.6 31.4 %collective-permute-start.2 = (f32[30,8,1024]{2,1,0:T(8,128)S(1)}, f32[30,8,1024]{2,1,0:T(8,128)S(1)}, u32[]{:S(2)}, u32[]{:S(2)}) collective-permute-start(f32[30,8,1024]{2,1,0:T(8,128)S(1)} %get-tuple-element.19), channel_id=1, source_target_pairs={{0,4},{1,5},{2,6},{3,7},{4,8},{5,9},{6,10},{7,11},{8,12},{9,13},{1... | collective-permute-start | bytes 2949128 | tf_op jit(solution)/shard_map/ppermute | solution.py:854
  29.2 21.0 %collective-permute-start.3 = (f32[4,8,1024]{2,1,0:T(8,128)S(1)}, f32[4,8,1024]{2,1,0:T(8,128)S(1)}, u32[]{:S(2)}, u32[]{:S(2)}) collective-permute-start(f32[4,8,1024]{2,1,0:T(8,128)S(1)} %get-tuple-element.20), channel_id=1, source_target_pairs={{1,4},{2,5},{3,6},{5,8},{6,9},{7,10},{9,12},{10,13},{11,14},{13,16... | collective-permute-start | bytes 393224 | tf_op jit(solution)/shard_map/ppermute | solution.py:854
  29.9 28.1 %collective-permute-start.4 = (f32[4,8,1024]{2,1,0:T(8,128)S(1)}, f32[4,8,1024]{2,1,0:T(8,128)S(1)}, u32[]{:S(2)}, u32[]{:S(2)}) collective-permute-start(f32[4,8,1024]{2,1,0:T(8,128)S(1)} %get-tuple-element.21), channel_id=1, source_target_pairs={{0,5},{1,6},{2,7},{4,9},{5,10},{6,11},{8,13},{9,14},{10,15},{12,17... | collective-permute-start | bytes 393224 | tf_op jit(solution)/shard_map/ppermute | solution.py:854
  34.8 8.9 %copy-start = (f32[36,8,1024]{2,1,0:T(8,128)}, f32[36,8,1024]{2,1,0:T(8,128)S(1)}, u32[]{:S(2)}) copy-start(f32[36,8,1024]{2,1,0:T(8,128)S(1)} %collective-permute-done.up_ref.refs_2_) | copy-start | bytes 3538948
  34.8 8.8 %copy-start.2 = (f32[36,8,1024]{2,1,0:T(8,128)}, f32[36,8,1024]{2,1,0:T(8,128)S(1)}, u32[]{:S(2)}) copy-start(f32[36,8,1024]{2,1,0:T(8,128)S(1)} %collective-permute-done.1.down_ref.refs_3_) | copy-start | bytes 3538948
  34.8 23.2 %collective-permute-start.5 = (f32[4,8,1024]{2,1,0:T(8,128)S(1)}, f32[4,8,1024]{2,1,0:T(8,128)S(1)}, u32[]{:S(2)}, u32[]{:S(2)}) collective-permute-start(f32[4,8,1024]{2,1,0:T(8,128)S(1)} %pad_maximum_fusion.1), channel_id=1, source_target_pairs={{4,0},{5,1},{6,2},{7,3},{8,4},{9,5},{10,6},{11,7},{12,8},{13,9},{1... | collective-permute-start | bytes 393224 | tf_op jit(solution)/shard_map/ppermute | solution.py:854
  49.2 1.0 copy-start.3
  58.0 9.5 %copy-start.4 = (f32[30,8,1024]{2,1,0:T(8,128)}, f32[30,8,1024]{2,1,0:T(8,128)S(1)}, u32[]{:S(2)}) copy-start(f32[30,8,1024]{2,1,0:T(8,128)S(1)} %collective-permute-done.2.refs_5_.low_ref) | copy-start | bytes 2949124
  67.5 1.0 copy-start.8
  68.5 32.5 %collective-permute-start.6 = (f32[7,40,1024]{2,1,0:T(8,128)}, f32[7,40,1024]{2,1,0:T(8,128)S(1)}, u32[]{:S(2)}, u32[]{:S(2)}) collective-permute-start(f32[7,40,1024]{2,1,0:T(8,128)} %get-tuple-element.28), channel_id=1, source_target_pairs={{4,0},{5,1},{6,2},{7,3},{8,4},{9,5},{10,6},{11,7},{12,8},{13,9},{1... | collective-permute-start | bytes 3440648 | tf_op jit(solution)/shard_map/ppermute | solution.py:854
  91.0 1.0 copy-start.11
  91.9 3.2 %copy-start.9 = (f32[4,8,56,128]{3,2,1,0:T(8,128)}, f32[4,8,56,128]{3,2,1,0:T(8,128)S(1)}, u32[]{:S(2)}) copy-start(f32[4,8,56,128]{3,2,1,0:T(8,128)S(1)} %get-tuple-element.26.refs_4_) | copy-start | bytes 2752516
  95.1 17.5 %all-to-all-start.1 = ((f32[32,1,1280]{2,1,0:T(1,128)}), f32[32,1,1280]{2,1,0:T(1,128)S(1)}, u32[]{:S(2)}, u32[]{:S(2)}) async-start(f32[32,1,1280]{2,1,0:T(1,128)} %gather_press.1), calls=%async_computation.1 | async-start | bytes 327680 | tf_op jit(solution)/shard_map/all_to_all | solution.py:857
  101.0 1.0 copy-start.6
  102.0 1.3 copy-start.7
  103.2 1.2 copy-start.10
  104.4 1.2 copy-start.12
  105.6 7.1 %copy-start.1 = (f32[36,8,1024]{2,1,0:T(8,128)S(1)}, f32[36,8,1024]{2,1,0:T(8,128)}, u32[]{:S(2)}) copy-start(f32[36,8,1024]{2,1,0:T(8,128)} %copy-done) | copy-start | bytes 3538948
  105.6 7.1 %copy-start.5 = (f32[30,8,1024]{2,1,0:T(8,128)S(1)}, f32[30,8,1024]{2,1,0:T(8,128)}, u32[]{:S(2)}) copy-start(f32[30,8,1024]{2,1,0:T(8,128)} %copy-done.4) | copy-start | bytes 2949124

commit v8 on v7

--- a/solution.py
+++ b/solution.py
@@ -10,7 +10,7 @@
 NSUB = 4
 SWEEPS = 3
 HIST = 40
-VMEM_BYTES = 50 * 1024 * 1024
+VMEM_BYTES = 46 * 1024 * 1024
 F32 = jnp.float32
 BF16 = jnp.bfloat16
 
@@ -215,7 +215,9 @@
         )
 
 
-def gather_press(n_gx, n_gy, wet_ref, numbers_ref, gram_ref, after_ref, out_ref, own_ref):
+def gather_press(n_gx, n_gy, wet_ref, numbers_ref, gram_ref, forced_ref, out_ref, send_ref,
+                 own_ref):
+    send_ref[...] = forced_ref[...]
     index_ref = numbers_ref.at[pl.ds(0, own_ref.shape[0])]
     planes, cy, cz = wet_ref.shape
     peers, blk = own_ref.shape
@@ -453,7 +455,7 @@
     late_ref[:, 0, 128:256] = jnp.broadcast_to(gram, (peers, 128))
 
 
-def solve(recv_ref, resp_ref, small_ref, w_ref, out_ref, w, sems):
+def solve(recv_ref, resp_ref, small_ref, w_ref, after_ref, out_ref, w, sems):
     peers = recv_ref.shape[0]
     hist = w_ref.shape[0]
     prev_ref = small_ref.at[3]
@@ -626,10 +628,10 @@
     tiles = cy // 8
     names = ["phi", "kappa", "up", "down"]
     names += {"wet": ["forced", "low", "low_up", "low_down", "near", "gram"],
-              "middle": ["state_a", "state_b", "wet"],
-              "end": ["state_a", "state_b", "high", "whole"]}[kind]
-    names += {"wet": ["out", "next_a", "next_b", "send"], "middle": ["out", "next_a", "next_b"],
-              "end": ["out"]}[kind]
+              "middle": ["state_a", "state_b", "wet", "press"],
+              "end": ["state_a", "state_b", "high", "whole", "late"]}[kind]
+    names += {"wet": ["out", "next_a", "next_b"], "middle": ["out", "next_a", "next_b"],
+              "end": ["out", "token"]}[kind]
     names += ["a", "b", "kap", "coef", "stage", "done", "sems", "kap_sems", "out_sems", "more_sems"]
     r = dict(zip(names, refs))
     a, b, kap, coef, stage = r["a"], r["b"], r["kap"], r["coef"], r["stage"]
@@ -778,8 +780,8 @@
     if kind != "end":
         outs.append(copy(a.at[pl.ds(planes - 4, 4)], r["next_a"]))
         outs.append(copy(b.at[pl.ds(planes - 5, 4)], r["next_b"]))
-    if kind == "wet":
-        outs.append(copy(r["forced"], r["send"]))
+    if kind == "end":
+        r["token"][...] = jnp.zeros((8, 128), F32)
     loop(4, planes - 4, final)
     for made in outs:
         made.wait()
@@ -796,15 +798,15 @@
         specs = vmem_specs(4) + any_specs(2)
         out_shape = [
             jax.ShapeDtypeStruct((x1 - x0, cy, cz), F32), *state,
-            jax.ShapeDtypeStruct((7, cy + 8, cz), F32),
         ]
-        out_specs = vmem_specs(1) + any_specs(3)
+        out_specs = vmem_specs(1) + any_specs(2)
     elif kind == "middle":
-        specs = any_specs(2) + vmem_specs(1)
+        specs = any_specs(2) + vmem_specs(1) + any_specs(1)
         out_shape, out_specs = [field, *state], hbm_specs(1) + any_specs(2)
     else:
-        specs = any_specs(2) + vmem_specs(1) + hbm_specs(1)
-        out_shape, out_specs = field, hbm_specs(1)[0]
+        specs = any_specs(2) + vmem_specs(1) + hbm_specs(1) + any_specs(1)
+        out_shape = [field, jax.ShapeDtypeStruct((8, 128), F32)]
+        out_specs = hbm_specs(1) + vmem_specs(1)
     cells = planes * (cy + 8) * cz
     stepped = pltpu.VMEM((planes, cz // 128, cy + 24, 128), F32)
     wide = pltpu.VMEM((planes, cy + 8, cz), F32)
@@ -915,22 +917,18 @@
         ],
         "scatter_disp", vmem_specs(4) + hbm_specs(2), disp, numbers, up, down, phi, kappa,
     )
-    wet, state_a, state_b, send = fluid_call(
+    wet, state_a, state_b = fluid_call(
         "wet", 0, wet_planes, phi, kappa, up, down, forced, low, low_up, low_down, near, gram
     )
+    press, send = call(
+        functools.partial(gather_press, n_gx, n_gy), [f32(peers, 1, (len(NEAR) + 1) * blk), f32(7, cy + 8, cz)],
+        [pltpu.VMEM((peers, blk), F32)], "gather_press", vmem_specs(4), wet, numbers, gram, forced,
+    )
+    loads = exchange(press)
     high = shift(send, -1, 0)
     middle, state_a, state_b = fluid_call(
-        "middle", wet_planes, cx - 4, phi, kappa, up, down, state_a, state_b, wet
-    )
-    field = fluid_call(
-        "end", cx - 4, cx, phi, kappa, up, down, state_a, state_b, high, middle
-    )
-    press = call(
-        functools.partial(gather_press, n_gx, n_gy), f32(peers, 1, (len(NEAR) + 1) * blk),
-        [pltpu.VMEM((peers, blk), F32)], "gather_press", vmem_specs(3) + any_specs(1),
-        wet, numbers, gram, middle,
-    )
-    loads = exchange(press)
+        "middle", wet_planes, cx - 4, phi, kappa, up, down, state_a, state_b, wet, press
+    )
     resp, late = call(
         shell, [f32(sx, sy), f32(peers, 1, 256)],
         [
@@ -943,14 +941,17 @@
             pltpu.VMEM((128, 128), F32),
             pltpu.SemaphoreType.DMA((1,)),
         ],
-        "shell", vmem_specs(9) + hbm_specs(2),
+        "shell", vmem_specs(9) + hbm_specs(1) + any_specs(1),
         loads, numbers, small, up, down, low, low_up, low_down, near,
-        v_hist, field,
+        v_hist, state_a,
+    )
+    field, token = fluid_call(
+        "end", cx - 4, cx, phi, kappa, up, down, state_a, state_b, high, middle, late
     )
     x_next = call(
         solve, f32(sx, sy),
         [pltpu.VMEM((hist, sx, sy), F32), pltpu.SemaphoreType.DMA((1,))],
-        "solve", vmem_specs(3) + hbm_specs(1), exchange(late), resp, small, w_hist,
+        "solve", vmem_specs(3) + hbm_specs(1) + any_specs(1), exchange(late), resp, small, w_hist, token,
     )
     return (field, x_next)
 

time: 137 us -> 137 us (level)
  blocking collectives: 27.3 us -> 14.4 us
  local copies, waits for them, and re-layouts: 7.61 us -> 19.2 us
  Pallas kernels: 69.1 us -> 64.1 us
  starting transfers between devices: 21.3 us -> 25.5 us
  waiting for transfers between devices: 7.85 us -> 9.81 us
    all_to_all x2 -> x1, blocking collectives: 27.3 us -> 14.4 us  [exchange(): return lax.all_to_all(value, axes, split_axis=0, concat_axis=0, tiled=True)]
    unnamed x26 -> x44, local copies, waits for them, and re-layouts: 7.59 us -> 19.2 us
    all_to_all x1 -> x2, starting transfers between devices: 5.8 us -> 10.3 us  [exchange(): return lax.all_to_all(value, axes, split_axis=0, concat_axis=0, tiled=True)]
    pallas_call x3, Pallas kernels: 37.5 us -> 33.3 us  [fluid_call(): pl.pallas_call(functools.partial(fluid, x0, x1, cx, cy, cz, kind), in_spe...]
    all_to_all x1 -> x2, waiting for transfers between devices: 0.01 us -> 2.72 us  [exchange(): return lax.all_to_all(value, axes, split_axis=0, concat_axis=0, tiled=True)]
  transfers between devices with their start and end apart: 8 -> 9, of which waited for: 1 -> 2; matrix products, arithmetic and copies ran while one was open for 0% -> 0% of each run, Pallas kernels for 32% -> 32%
where the time goes in v8:
time: 137 us; the launch traced here: 136 us
  Pallas kernels  64.1 us (47%)
  starting transfers between devices  25.5 us (19%)
  local copies, waits for them, and re-layouts  19.2 us (14%)
  blocking collectives  14.4 us (11%)
  waiting for transfers between devices  9.81 us (7%)
  other arithmetic  1.88 us (1%)
    pallas_call x3, Pallas kernels, fluid_call(): pl.pallas_call(functools.partial(fluid, x0, x1, cx, cy, cz, kind), in_spe...  33.3 us
    pallas_call x6, Pallas kernels, call(): pl.pallas_call(body, in_specs=specs, out_specs=vmem_specs(len(out_shape))...  27.8 us
    unnamed x44, local copies, waits for them, and re-layouts  19.2 us
    ppermute x7, starting transfers between devices, shift(): return lax.ppermute(value, axes, shifted_pairs(n_gx, n_gy, dx, dy))  15.2 us
    all_to_all x1, blocking collectives, exchange(): return lax.all_to_all(value, axes, split_axis=0, concat_axis=0, tiled=True)  14.4 us
    all_to_all x2, starting transfers between devices, exchange(): return lax.all_to_all(value, axes, split_axis=0, concat_axis=0, tiled=True)  10.3 us
    ppermute x7, waiting for transfers between devices, shift(): return lax.ppermute(value, axes, shifted_pairs(n_gx, n_gy, dx, dy))  7.09 us
    pallas_call x1, Pallas kernels, packed(): pl.pallas_call(pack, in_specs=hbm_specs(2) + any_specs(1) + vmem_specs(2)...  3.04 us
  transfers between devices with their start and end apart: 9, of which 2 were waited for; matrix products, arithmetic and copies ran while one was open for 0% of the time, Pallas kernels for 32%

profile of v8, /device:TPU:0, one launch (start us, length us, event | category | flops | bytes accessed | tf_op | source)
XLA Modules:
  0.0 136.1 jit_solution(17840839209726927242)
XLA Ops:
  2.5 1.2 gather_disp.1
  3.7 14.4 %all_to_all.15.after_ref.disp_ref = f32[32,1,384]{2,1,0:T(1,128)S(1)} all-to-all(f32[32,1,384]{2,1,0:T(1,128)S(1)} %gather_disp.1), channel_id=1, replica_groups=mesh['gx'=8,'gy'=4] {'gx','gy'}, dimensions={0} | all-to-all | bytes 98304 | tf_op jit(solution)/shard_map/all_to_all | solution.py:859
  18.1 3.0 %pack.1 = (f32[36,8,1024]{2,1,0:T(8,128)S(1)}, f32[36,8,1024]{2,1,0:T(8,128)S(1)}, f32[30,8,1024]{2,1,0:T(8,128)S(1)}, f32[4,8,1024]{2,1,0:T(8,128)S(1)}, f32[4,...) custom-call(f32[32,32,1024]{2,1,0:T(8,128)} %refs_0_.5, f32[32,32,1024]{2,1,0:T(8,128)} %refs_1_.5, ...), custom_call_target="tpu_custom_call" | custom-call | tf_op jit(solution)/shard_map/pack/pallas_call | solution.py:585
  21.2 1.3 collective-permute-start
  22.5 3.1 %collective-permute-start.1 = (f32[36,8,1024]{2,1,0:T(8,128)S(1)}, f32[36,8,1024]{2,1,0:T(8,128)S(1)}, u32[]{:S(2)}, u32[]{:S(2)}) collective-permute-start(f32[36,8,1024]{2,1,0:T(8,128)S(1)} %get-tuple-element.21), channel_id=1, source_target_pairs={{0,1},{1,2},{2,3},{4,5},{5,6},{6,7},{8,9},{9,10},{10,11},{12,13},{... | collective-permute-start | bytes 3538952 | tf_op jit(solution)/shard_map/ppermute | solution.py:856
  25.6 2.5 %collective-permute-start.2 = (f32[30,8,1024]{2,1,0:T(8,128)S(1)}, f32[30,8,1024]{2,1,0:T(8,128)S(1)}, u32[]{:S(2)}, u32[]{:S(2)}) collective-permute-start(f32[30,8,1024]{2,1,0:T(8,128)S(1)} %get-tuple-element.22), channel_id=1, source_target_pairs={{0,4},{1,5},{2,6},{3,7},{4,8},{5,9},{6,10},{7,11},{8,12},{9,13},{1... | collective-permute-start | bytes 2949128 | tf_op jit(solution)/shard_map/ppermute | solution.py:856
  28.9 4.9 %collective-permute-start.4 = (f32[4,8,1024]{2,1,0:T(8,128)S(1)}, f32[4,8,1024]{2,1,0:T(8,128)S(1)}, u32[]{:S(2)}, u32[]{:S(2)}) collective-permute-start(f32[4,8,1024]{2,1,0:T(8,128)S(1)} %get-tuple-element.24), channel_id=1, source_target_pairs={{0,5},{1,6},{2,7},{4,9},{5,10},{6,11},{8,13},{9,14},{10,15},{12,17... | collective-permute-start | bytes 393224 | tf_op jit(solution)/shard_map/ppermute | solution.py:856
  33.8 1.5 %collective-permute-start.5 = (f32[4,8,1024]{2,1,0:T(8,128)S(1)}, f32[4,8,1024]{2,1,0:T(8,128)S(1)}, u32[]{:S(2)}, u32[]{:S(2)}) collective-permute-start(f32[4,8,1024]{2,1,0:T(8,128)S(1)} %pad_maximum_fusion.1), channel_id=1, source_target_pairs={{4,0},{5,1},{6,2},{7,3},{8,4},{9,5},{10,6},{11,7},{12,8},{13,9},{1... | collective-permute-start | bytes 393224 | tf_op jit(solution)/shard_map/ppermute | solution.py:856
  35.3 2.5 %copy-done.1 = f32[40,64,512]{2,1,0:T(8,128)S(1)} copy-done((f32[40,64,512]{2,1,0:T(8,128)S(1)}, f32[40,64,512]{2,1,0:T(8,128)}, u32[]{:S(2)}) %copy-start.1) | copy-done | bytes 5242904
  37.8 6.7 %gram_rows.1.refs_9_.gram_ref = f32[32,128]{1,0:T(8,128)S(1)} custom-call(f32[40,64,512]{2,1,0:T(8,128)S(1)} %copy-done.1), custom_call_target="tpu_custom_call" | custom-call | tf_op jit(solution)/shard_map/gram_rows/pallas_call | solution.py:863
  44.5 5.4 %scatter_disp.1.refs_4_.forced_ref = f32[7,40,1024]{2,1,0:T(8,128)S(1)} custom-call(f32[32,1,384]{2,1,0:T(1,128)S(1)} %all_to_all.15.after_ref.disp_ref, s32[64,128]{1,0:T(8,128)S(1)} %pad_add_fusion.numbers_ref, f32[36,8,1024]{2,1,0:T(8,128)S(1)} %collective-permute-done.up_ref.refs_2_, f32[36,8,1024]{2,1,0:T(8,128)S(1)} %collective-permute-done.1.down_ref.refs_3_, ...), custom_call_target="tpu_custom_call" | custom-call | tf_op jit(solution)/shard_map/scatter_disp/pallas_call | solution.py:863
  49.9 7.1 %collective-permute-done.4.refs_7_.low_down_ref = f32[4,8,1024]{2,1,0:T(8,128)S(1)} collective-permute-done((f32[4,8,1024]{2,1,0:T(8,128)S(1)}, f32[4,8,1024]{2,1,0:T(8,128)S(1)}, u32[]{:S(2)}, u32[]{:S(2)}) %collective-permute-start.4) | collective-permute-done | bytes 131104 | tf_op jit(solution)/shard_map/ppermute | solution.py:856
  57.0 7.3 %fluid_wet.1 = (f32[4,32,1024]{2,1,0:T(8,128)S(1)}, f32[4,8,56,128]{3,2,1,0:T(8,128)S(1)}, f32[4,8,56,128]{3,2,1,0:T(8,128)S(1)}) custom-call(f32[32,32,1024]{2,1,0:T(8,128)} %refs_0_.5, f32[32,32,1024]{2,1,0:T(8,128)} %refs_1_.5, f32[36,8,1024]{2,1,0:T(8,128)S(1)} %collective-permute-done.up_ref.refs_2_, ...), custom_call_target="tpu_custom_call" | custom-call | flops 23592960 | bytes 5898240 | tf_op jit(solution)/shard_map/fluid_wet/pallas_call | solution.py:814
  65.3 3.6 %gather_press.1 = (f32[32,1,1280]{2,1,0:T(1,128)S(1)}, f32[7,40,1024]{2,1,0:T(8,128)}) custom-call(f32[4,32,1024]{2,1,0:T(8,128)S(1)} %get-tuple-element.28.wet_ref.refs_6_, s32[64,128]{1,0:T(8,128)S(1)} %pad_add_fusion.numbers_ref, f32[32,128]{1,0:T(8,128)S(1)} %gram_rows.1.refs_9_.gram_ref, f32[7,40,1024]{2,1,0:T(8,128)S(1)} %scatter_disp.1.refs_4_.forced_ref), custom_call_target="tpu_custom_call" | custom-call | tf_op jit(solution)/shard_map/gather_press/pallas_call | solution.py:863
  69.6 1.3 collective-permute-start.6
  70.9 7.2 %all-to-all-start.1 = ((f32[32,1,1280]{2,1,0:T(1,128)}), f32[32,1,1280]{2,1,0:T(1,128)}, u32[]{:S(2)}, u32[]{:S(2)}) async-start(f32[32,1,1280]{2,1,0:T(1,128)} %copy-done.14), calls=%async_computation.1 | async-start | bytes 327680 | tf_op jit(solution)/shard_map/all_to_all | solution.py:859
  81.4 19.4 %fluid_middle.1 = (f32[32,32,1024]{2,1,0:T(8,128)}, f32[4,8,56,128]{3,2,1,0:T(8,128)S(1)}, f32[4,8,56,128]{3,2,1,0:T(8,128)S(1)}) custom-call(f32[32,32,1024]{2,1,0:T(8,128)} %refs_0_.5, f32[32,32,1024]{2,1,0:T(8,128)} %refs_1_.5, f32[36,8,1024]{2,1,0:T(8,128)S(1)} %collective-permute-done.up_ref.refs_2_, ...), custom_call_target="tpu_custom_call" | custom-call | flops 62914560 | bytes 15728640 | tf_op jit(solution)/shard_map/fluid_middle/pallas_call | solution.py:814
  102.7 2.7 %all-to-all-done.1.recv_ref = f32[32,1,1280]{2,1,0:T(1,128)} async-done(((f32[32,1,1280]{2,1,0:T(1,128)}), f32[32,1,1280]{2,1,0:T(1,128)}, u32[]{:S(2)}, u32[]{:S(2)}) %all-to-all-start.1) | async-done | bytes 163872 | tf_op jit(solution)/shard_map/all_to_all | solution.py:859
  105.4 1.2 copy-done.4
  110.5 5.9 %shell.1 = (f32[64,512]{1,0:T(8,128)S(1)}, f32[32,1,256]{2,1,0:T(1,128)}) custom-call(f32[32,1,1280]{2,1,0:T(1,128)} %all-to-all-done.1.recv_ref, s32[64,128]{1,0:T(8,128)S(1)} %pad_add_fusion.numbers_ref, f32[4,64,512]{2,1,0:T(8,128)S(1)} %pad_maximum_fusion.small_ref, f32[36,8,1024]{2,1,0:T(8,128)S(1)} %collective-permute-done.up_ref.refs_2_, ...), custom_call_target="tpu_custom_call" | custom-call | tf_op jit(solution)/shard_map/shell/pallas_call | solution.py:863
  116.5 3.1 %all-to-all-start.2 = ((f32[32,1,256]{2,1,0:T(1,128)}), f32[32,1,256]{2,1,0:T(1,128)S(1)}, u32[]{:S(2)}, u32[]{:S(2)}) async-start(f32[32,1,256]{2,1,0:T(1,128)} %get-tuple-element.34.refs_8_), calls=%async_computation.2 | async-start | bytes 65536 | tf_op jit(solution)/shard_map/all_to_all | solution.py:859
  121.9 6.5 %fluid_end.1 = (f32[32,32,1024]{2,1,0:T(8,128)}, f32[8,128]{1,0:T(8,128)S(1)}) custom-call(f32[32,32,1024]{2,1,0:T(8,128)} %refs_0_.5, f32[32,32,1024]{2,1,0:T(8,128)} %refs_1_.5, f32[36,8,1024]{2,1,0:T(8,128)S(1)} %collective-permute-done.up_ref.refs_2_, ...), custom_call_target="tpu_custom_call", output_to_operand_aliasing={{0}: (7, {})} | custom-call | flops 23592960 | bytes 5898240 | tf_op jit(solution)/shard_map/fluid_end/pallas_call | solution.py:814
  128.5 2.5 %copy-done.2 = f32[40,64,512]{2,1,0:T(8,128)S(1)} copy-done((f32[40,64,512]{2,1,0:T(8,128)S(1)}, f32[40,64,512]{2,1,0:T(8,128)}, u32[]{:S(2)}) %copy-start.2) | copy-done | bytes 5242904
  131.0 5.0 %solve.1 = f32[64,512]{1,0:T(8,128)} custom-call(f32[32,1,256]{2,1,0:T(1,128)S(1)} %all-to-all-done.2.recv_ref, f32[64,512]{1,0:T(8,128)S(1)} %get-tuple-element.36.resp_ref, f32[4,64,512]{2,1,0:T(8,128)S(1)} %pad_maximum_fusion.small_ref, f32[40,64,512]{2,1,0:T(8,128)S(1)} %copy-done.2, f32[8,128]{1,0:T(8,128)S(1)} %get-tuple-element.37.after_ref), custom_call_target="tpu_custom_call" | custom-call | tf_op jit(solution)/shard_map/solve/pallas_call | solution.py:863
  (55 shorter events, 15.6 us)
Async XLA Ops:
  21.2 12.5 %collective-permute-start = (f32[36,8,1024]{2,1,0:T(8,128)S(1)}, f32[36,8,1024]{2,1,0:T(8,128)S(1)}, u32[]{:S(2)}, u32[]{:S(2)}) collective-permute-start(f32[36,8,1024]{2,1,0:T(8,128)S(1)} %get-tuple-element.20), channel_id=1, source_target_pairs={{1,0},{2,1},{3,2},{5,4},{6,5},{7,6},{9,8},{10,9},{11,10},{13,12},{... | collective-permute-start | bytes 3538952 | tf_op jit(solution)/shard_map/ppermute | solution.py:856
  22.5 11.3 %collective-permute-start.1 = (f32[36,8,1024]{2,1,0:T(8,128)S(1)}, f32[36,8,1024]{2,1,0:T(8,128)S(1)}, u32[]{:S(2)}, u32[]{:S(2)}) collective-permute-start(f32[36,8,1024]{2,1,0:T(8,128)S(1)} %get-tuple-element.21), channel_id=1, source_target_pairs={{0,1},{1,2},{2,3},{4,5},{5,6},{6,7},{8,9},{9,10},{10,11},{12,13},{... | collective-permute-start | bytes 3538952 | tf_op jit(solution)/shard_map/ppermute | solution.py:856
  25.6 31.4 %collective-permute-start.2 = (f32[30,8,1024]{2,1,0:T(8,128)S(1)}, f32[30,8,1024]{2,1,0:T(8,128)S(1)}, u32[]{:S(2)}, u32[]{:S(2)}) collective-permute-start(f32[30,8,1024]{2,1,0:T(8,128)S(1)} %get-tuple-element.22), channel_id=1, source_target_pairs={{0,4},{1,5},{2,6},{3,7},{4,8},{5,9},{6,10},{7,11},{8,12},{9,13},{1... | collective-permute-start | bytes 2949128 | tf_op jit(solution)/shard_map/ppermute | solution.py:856
  28.2 21.7 %collective-permute-start.3 = (f32[4,8,1024]{2,1,0:T(8,128)S(1)}, f32[4,8,1024]{2,1,0:T(8,128)S(1)}, u32[]{:S(2)}, u32[]{:S(2)}) collective-permute-start(f32[4,8,1024]{2,1,0:T(8,128)S(1)} %get-tuple-element.23), channel_id=1, source_target_pairs={{1,4},{2,5},{3,6},{5,8},{6,9},{7,10},{9,12},{10,13},{11,14},{13,16... | collective-permute-start | bytes 393224 | tf_op jit(solution)/shard_map/ppermute | solution.py:856
  28.9 28.1 %collective-permute-start.4 = (f32[4,8,1024]{2,1,0:T(8,128)S(1)}, f32[4,8,1024]{2,1,0:T(8,128)S(1)}, u32[]{:S(2)}, u32[]{:S(2)}) collective-permute-start(f32[4,8,1024]{2,1,0:T(8,128)S(1)} %get-tuple-element.24), channel_id=1, source_target_pairs={{0,5},{1,6},{2,7},{4,9},{5,10},{6,11},{8,13},{9,14},{10,15},{12,17... | collective-permute-start | bytes 393224 | tf_op jit(solution)/shard_map/ppermute | solution.py:856
  33.8 23.2 %collective-permute-start.5 = (f32[4,8,1024]{2,1,0:T(8,128)S(1)}, f32[4,8,1024]{2,1,0:T(8,128)S(1)}, u32[]{:S(2)}, u32[]{:S(2)}) collective-permute-start(f32[4,8,1024]{2,1,0:T(8,128)S(1)} %pad_maximum_fusion.1), channel_id=1, source_target_pairs={{4,0},{5,1},{6,2},{7,3},{8,4},{9,5},{10,6},{11,7},{12,8},{13,9},{1... | collective-permute-start | bytes 393224 | tf_op jit(solution)/shard_map/ppermute | solution.py:856
  35.3 2.5 %copy-start.1 = (f32[40,64,512]{2,1,0:T(8,128)S(1)}, f32[40,64,512]{2,1,0:T(8,128)}, u32[]{:S(2)}) copy-start(f32[40,64,512]{2,1,0:T(8,128)} %v_ref.3) | copy-start | bytes 15728644
  37.8 6.7 %copy-start = (f32[32,32,1024]{2,1,0:T(8,128)S(1)}, f32[32,32,1024]{2,1,0:T(8,128)}, u32[]{:S(2)}) copy-start(f32[32,32,1024]{2,1,0:T(8,128)} %refs_0_.5) | copy-start | bytes 12582916
  49.9 14.5 %copy-start.16 = (f32[4,8,1024]{2,1,0:T(8,128)}, f32[4,8,1024]{2,1,0:T(8,128)S(1)}, u32[]{:S(2)}) copy-start(f32[4,8,1024]{2,1,0:T(8,128)S(1)} %collective-permute-done.3.refs_6_.low_up_ref) | copy-start | bytes 393220
  57.0 7.4 %copy-start.18 = (f32[4,8,1024]{2,1,0:T(8,128)}, f32[4,8,1024]{2,1,0:T(8,128)S(1)}, u32[]{:S(2)}) copy-start(f32[4,8,1024]{2,1,0:T(8,128)S(1)} %collective-permute-done.4.refs_7_.low_down_ref) | copy-start | bytes 393220
  57.0 7.4 %copy-start.3 = (f32[30,8,1024]{2,1,0:T(8,128)}, f32[30,8,1024]{2,1,0:T(8,128)S(1)}, u32[]{:S(2)}) copy-start(f32[30,8,1024]{2,1,0:T(8,128)S(1)} %collective-permute-done.2.refs_5_.low_ref) | copy-start | bytes 2949124
  57.0 7.4 %copy-start.20 = (f32[4,8,1024]{2,1,0:T(8,128)}, f32[4,8,1024]{2,1,0:T(8,128)S(1)}, u32[]{:S(2)}) copy-start(f32[4,8,1024]{2,1,0:T(8,128)S(1)} %collective-permute-done.5.refs_8_.high_ref) | copy-start | bytes 393220
  65.3 3.6 %copy-start.8 = (f32[4,8,56,128]{3,2,1,0:T(8,128)}, f32[4,8,56,128]{3,2,1,0:T(8,128)S(1)}, u32[]{:S(2)}) copy-start(f32[4,8,56,128]{3,2,1,0:T(8,128)S(1)} %get-tuple-element.26.refs_4_) | copy-start | bytes 2752516
  69.6 50.0 %collective-permute-start.6 = (f32[7,40,1024]{2,1,0:T(8,128)}, f32[7,40,1024]{2,1,0:T(8,128)}, u32[]{:S(2)}, u32[]{:S(2)}) collective-permute-start(f32[7,40,1024]{2,1,0:T(8,128)} %get-tuple-element.32), channel_id=1, source_target_pairs={{4,0},{5,1},{6,2},{7,3},{8,4},{9,5},{10,6},{11,7},{12,8},{13,9},{1... | collective-permute-start | bytes 3440648 | tf_op jit(solution)/shard_map/ppermute | solution.py:856
  70.9 34.6 %all-to-all-start.1 = ((f32[32,1,1280]{2,1,0:T(1,128)}), f32[32,1,1280]{2,1,0:T(1,128)}, u32[]{:S(2)}, u32[]{:S(2)}) async-start(f32[32,1,1280]{2,1,0:T(1,128)} %copy-done.14), calls=%async_computation.1 | async-start | bytes 327680 | tf_op jit(solution)/shard_map/all_to_all | solution.py:859
  78.1 1.2 copy-start.9
  79.3 1.2 copy-start.11
  101.7 1.0 copy-start.12
  105.4 1.2 copy-start.4
  106.6 1.2 copy-start.6
  116.5 12.0 %all-to-all-start.2 = ((f32[32,1,256]{2,1,0:T(1,128)}), f32[32,1,256]{2,1,0:T(1,128)S(1)}, u32[]{:S(2)}, u32[]{:S(2)}) async-start(f32[32,1,256]{2,1,0:T(1,128)} %get-tuple-element.34.refs_8_), calls=%async_computation.2 | async-start | bytes 65536 | tf_op jit(solution)/shard_map/all_to_all | solution.py:859
  119.6 1.2 copy-start.7
  120.7 1.2 copy-start.13
  128.5 2.5 %copy-start.2 = (f32[40,64,512]{2,1,0:T(8,128)S(1)}, f32[40,64,512]{2,1,0:T(8,128)}, u32[]{:S(2)}) copy-start(f32[40,64,512]{2,1,0:T(8,128)} %w_ref.1) | copy-start | bytes 15728644
  (7 other events, 6.2 us)

commit v9 on v8

--- a/solution.py
+++ b/solution.py
@@ -11,12 +11,13 @@
 SWEEPS = 3
 HIST = 40
 VMEM_BYTES = 46 * 1024 * 1024
+ALONE_BYTES = 60 * 1024 * 1024
 F32 = jnp.float32
 BF16 = jnp.bfloat16
 
 
-def params():
-    return pltpu.CompilerParams(vmem_limit_bytes=VMEM_BYTES)
+def params(alone=False):
+    return pltpu.CompilerParams(vmem_limit_bytes=ALONE_BYTES if alone else VMEM_BYTES)
 
 
 def vmem_specs(count):
@@ -216,8 +217,9 @@
 
 
 def gather_press(n_gx, n_gy, wet_ref, numbers_ref, gram_ref, forced_ref, out_ref, send_ref,
-                 own_ref):
+                 token_ref, own_ref):
     send_ref[...] = forced_ref[...]
+    token_ref[...] = jnp.zeros((8, 128), F32)
     index_ref = numbers_ref.at[pl.ds(0, own_ref.shape[0])]
     planes, cy, cz = wet_ref.shape
     peers, blk = own_ref.shape
@@ -630,7 +632,7 @@
     names += {"wet": ["forced", "low", "low_up", "low_down", "near", "gram"],
               "middle": ["state_a", "state_b", "wet", "press"],
               "end": ["state_a", "state_b", "high", "whole", "late"]}[kind]
-    names += {"wet": ["out", "next_a", "next_b"], "middle": ["out", "next_a", "next_b"],
+    names += {"wet": ["out", "next_a", "next_b"], "middle": ["out", "next_a", "next_b", "token"],
               "end": ["out", "token"]}[kind]
     names += ["a", "b", "kap", "coef", "stage", "done", "sems", "kap_sems", "out_sems", "more_sems"]
     r = dict(zip(names, refs))
@@ -780,7 +782,7 @@
     if kind != "end":
         outs.append(copy(a.at[pl.ds(planes - 4, 4)], r["next_a"]))
         outs.append(copy(b.at[pl.ds(planes - 5, 4)], r["next_b"]))
-    if kind == "end":
+    if kind != "wet":
         r["token"][...] = jnp.zeros((8, 128), F32)
     loop(4, planes - 4, final)
     for made in outs:
@@ -799,12 +801,13 @@
         out_shape = [
             jax.ShapeDtypeStruct((x1 - x0, cy, cz), F32), *state,
         ]
-        out_specs = vmem_specs(1) + any_specs(2)
+        out_specs = vmem_specs(1) + hbm_specs(2)
     elif kind == "middle":
-        specs = any_specs(2) + vmem_specs(1) + any_specs(1)
-        out_shape, out_specs = [field, *state], hbm_specs(1) + any_specs(2)
+        specs = hbm_specs(2) + vmem_specs(1) + any_specs(1)
+        out_shape = [field, *state, jax.ShapeDtypeStruct((8, 128), F32)]
+        out_specs = hbm_specs(3) + vmem_specs(1)
     else:
-        specs = any_specs(2) + vmem_specs(1) + hbm_specs(1) + any_specs(1)
+        specs = hbm_specs(2) + vmem_specs(1) + hbm_specs(1) + any_specs(1)
         out_shape = [field, jax.ShapeDtypeStruct((8, 128), F32)]
         out_specs = hbm_specs(1) + vmem_specs(1)
     cells = planes * (cy + 8) * cz
@@ -823,7 +826,7 @@
             sems, sems, sems, pltpu.SemaphoreType.DMA((8,)),
         ],
         input_output_aliases={7: 0} if kind == "end" else {},
-        compiler_params=params(),
+        compiler_params=params(kind != "wet"),
         cost_estimate=pl.CostEstimate(
             flops=48 * cells, bytes_accessed=12 * cells, transcendentals=0
         ),
@@ -866,7 +869,7 @@
             out_specs=vmem_specs(len(out_shape)) if several else vmem_specs(1)[0],
             out_shape=out_shape,
             scratch_shapes=scratch,
-            compiler_params=params(),
+            compiler_params=params(name in ("shell", "solve")),
             name=name,
         )(*args)
 
@@ -920,14 +923,14 @@
     wet, state_a, state_b = fluid_call(
         "wet", 0, wet_planes, phi, kappa, up, down, forced, low, low_up, low_down, near, gram
     )
-    press, send = call(
-        functools.partial(gather_press, n_gx, n_gy), [f32(peers, 1, (len(NEAR) + 1) * blk), f32(7, cy + 8, cz)],
+    press, send, token = call(
+        functools.partial(gather_press, n_gx, n_gy), [f32(peers, 1, (len(NEAR) + 1) * blk), f32(7, cy + 8, cz), f32(8, 128)],
         [pltpu.VMEM((peers, blk), F32)], "gather_press", vmem_specs(4), wet, numbers, gram, forced,
     )
     loads = exchange(press)
     high = shift(send, -1, 0)
-    middle, state_a, state_b = fluid_call(
-        "middle", wet_planes, cx - 4, phi, kappa, up, down, state_a, state_b, wet, press
+    middle, state_a, state_b, token = fluid_call(
+        "middle", wet_planes, cx - 4, phi, kappa, up, down, state_a, state_b, wet, token
     )
     resp, late = call(
         shell, [f32(sx, sy), f32(peers, 1, 256)],
@@ -943,7 +946,7 @@
         ],
         "shell", vmem_specs(9) + hbm_specs(1) + any_specs(1),
         loads, numbers, small, up, down, low, low_up, low_down, near,
-        v_hist, state_a,
+        v_hist, token,
     )
     field, token = fluid_call(
         "end", cx - 4, cx, phi, kappa, up, down, state_a, state_b, high, middle, late

time: 137 us -> 133 us (0.971)
  local copies, waits for them, and re-layouts: 19.2 us -> 6.3 us
  Pallas kernels: 64.1 us -> 70.8 us
  waiting for transfers between devices: 9.81 us -> 13.8 us
  starting transfers between devices: 25.5 us -> 23.9 us
    unnamed x44 -> x34, local copies, waits for them, and re-layouts: 19.2 us -> 6.29 us
    all_to_all x2, waiting for transfers between devices: 2.72 us -> 6.71 us  [exchange(): return lax.all_to_all(value, axes, split_axis=0, concat_axis=0, tiled=True)]
    pallas_call x6, Pallas kernels: 27.8 us -> 31.3 us  [call(): pl.pallas_call(body, in_specs=specs, out_specs=vmem_specs(len(out_shape))...]
    pallas_call x3, Pallas kernels: 33.3 us -> 36.5 us  [fluid_call(): pl.pallas_call(functools.partial(fluid, x0, x1, cx, cy, cz, kind), in_spe...]
    all_to_all x2, starting transfers between devices: 10.3 us -> 8.7 us  [exchange(): return lax.all_to_all(value, axes, split_axis=0, concat_axis=0, tiled=True)]
  transfers between devices with their start and end apart: 9 -> 9, of which waited for: 2 -> 2; matrix products, arithmetic and copies ran while one was open for 0% -> 0% of each run, Pallas kernels for 32% -> 38%
where the time goes in v9:
time: 133 us; the launch traced here: 132 us
  Pallas kernels  70.8 us (53%)
  starting transfers between devices  23.9 us (18%)
  blocking collectives  14.4 us (11%)
  waiting for transfers between devices  13.8 us (10%)
  local copies, waits for them, and re-layouts  6.3 us (5%)
  other arithmetic  1.89 us (1%)
    pallas_call x3, Pallas kernels, fluid_call(): pl.pallas_call(functools.partial(fluid, x0, x1, cx, cy, cz, kind), in_spe...  36.5 us
    pallas_call x6, Pallas kernels, call(): pl.pallas_call(body, in_specs=specs, out_specs=vmem_specs(len(out_shape))...  31.3 us
    ppermute x7, starting transfers between devices, shift(): return lax.ppermute(value, axes, shifted_pairs(n_gx, n_gy, dx, dy))  15.2 us
    all_to_all x1, blocking collectives, exchange(): return lax.all_to_all(value, axes, split_axis=0, concat_axis=0, tiled=True)  14.4 us
    all_to_all x2, starting transfers between devices, exchange(): return lax.all_to_all(value, axes, split_axis=0, concat_axis=0, tiled=True)  8.7 us
    ppermute x7, waiting for transfers between devices, shift(): return lax.ppermute(value, axes, shifted_pairs(n_gx, n_gy, dx, dy))  7.09 us
    all_to_all x2, waiting for transfers between devices, exchange(): return lax.all_to_all(value, axes, split_axis=0, concat_axis=0, tiled=True)  6.71 us
    unnamed x34, local copies, waits for them, and re-layouts  6.29 us
  transfers between devices with their start and end apart: 9, of which 2 were waited for; matrix products, arithmetic and copies ran while one was open for 0% of the time, Pallas kernels for 38%

profile of v9, /device:TPU:0, one launch (start us, length us, event | category | flops | bytes accessed | tf_op | source)
XLA Modules:
  0.0 132.4 jit_solution(7734761459280633750)
XLA Ops:
  1.4 1.1 pad_maximum_fusion.small_ref
  2.5 1.2 gather_disp.1
  3.7 14.4 %all_to_all.15.after_ref.disp_ref = f32[32,1,384]{2,1,0:T(1,128)S(1)} all-to-all(f32[32,1,384]{2,1,0:T(1,128)S(1)} %gather_disp.1), channel_id=1, replica_groups=mesh['gx'=8,'gy'=4] {'gx','gy'}, dimensions={0} | all-to-all | bytes 98304 | tf_op jit(solution)/shard_map/all_to_all | solution.py:862
  18.2 3.0 %pack.1 = (f32[36,8,1024]{2,1,0:T(8,128)S(1)}, f32[36,8,1024]{2,1,0:T(8,128)S(1)}, f32[30,8,1024]{2,1,0:T(8,128)S(1)}, f32[4,8,1024]{2,1,0:T(8,128)S(1)}, f32[4,...) custom-call(f32[32,32,1024]{2,1,0:T(8,128)} %refs_0_.5, f32[32,32,1024]{2,1,0:T(8,128)} %refs_1_.5, ...), custom_call_target="tpu_custom_call" | custom-call | tf_op jit(solution)/shard_map/pack/pallas_call | solution.py:587
  21.2 1.3 collective-permute-start
  22.5 3.1 %collective-permute-start.1 = (f32[36,8,1024]{2,1,0:T(8,128)S(1)}, f32[36,8,1024]{2,1,0:T(8,128)S(1)}, u32[]{:S(2)}, u32[]{:S(2)}) collective-permute-start(f32[36,8,1024]{2,1,0:T(8,128)S(1)} %get-tuple-element.23), channel_id=1, source_target_pairs={{0,1},{1,2},{2,3},{4,5},{5,6},{6,7},{8,9},{9,10},{10,11},{12,13},{... | collective-permute-start | bytes 3538952 | tf_op jit(solution)/shard_map/ppermute | solution.py:859
  25.6 2.5 %collective-permute-start.2 = (f32[30,8,1024]{2,1,0:T(8,128)S(1)}, f32[30,8,1024]{2,1,0:T(8,128)S(1)}, u32[]{:S(2)}, u32[]{:S(2)}) collective-permute-start(f32[30,8,1024]{2,1,0:T(8,128)S(1)} %get-tuple-element.24), channel_id=1, source_target_pairs={{0,4},{1,5},{2,6},{3,7},{4,8},{5,9},{6,10},{7,11},{8,12},{9,13},{1... | collective-permute-start | bytes 2949128 | tf_op jit(solution)/shard_map/ppermute | solution.py:859
  28.9 4.9 %collective-permute-start.4 = (f32[4,8,1024]{2,1,0:T(8,128)S(1)}, f32[4,8,1024]{2,1,0:T(8,128)S(1)}, u32[]{:S(2)}, u32[]{:S(2)}) collective-permute-start(f32[4,8,1024]{2,1,0:T(8,128)S(1)} %get-tuple-element.26), channel_id=1, source_target_pairs={{0,5},{1,6},{2,7},{4,9},{5,10},{6,11},{8,13},{9,14},{10,15},{12,17... | collective-permute-start | bytes 393224 | tf_op jit(solution)/shard_map/ppermute | solution.py:859
  33.9 1.5 %collective-permute-start.5 = (f32[4,8,1024]{2,1,0:T(8,128)S(1)}, f32[4,8,1024]{2,1,0:T(8,128)S(1)}, u32[]{:S(2)}, u32[]{:S(2)}) collective-permute-start(f32[4,8,1024]{2,1,0:T(8,128)S(1)} %pad_maximum_fusion.1), channel_id=1, source_target_pairs={{4,0},{5,1},{6,2},{7,3},{8,4},{9,5},{10,6},{11,7},{12,8},{13,9},{1... | collective-permute-start | bytes 393224 | tf_op jit(solution)/shard_map/ppermute | solution.py:859
  35.3 2.5 %copy-done.3 = f32[40,64,512]{2,1,0:T(8,128)S(1)} copy-done((f32[40,64,512]{2,1,0:T(8,128)S(1)}, f32[40,64,512]{2,1,0:T(8,128)}, u32[]{:S(2)}) %copy-start.3) | copy-done | bytes 5242904
  37.8 6.7 %gram_rows.1.refs_9_.gram_ref = f32[32,128]{1,0:T(8,128)S(1)} custom-call(f32[40,64,512]{2,1,0:T(8,128)S(1)} %copy-done.3), custom_call_target="tpu_custom_call" | custom-call | tf_op jit(solution)/shard_map/gram_rows/pallas_call | solution.py:866
  44.5 5.4 %scatter_disp.1.refs_4_.forced_ref = f32[7,40,1024]{2,1,0:T(8,128)S(1)} custom-call(f32[32,1,384]{2,1,0:T(1,128)S(1)} %all_to_all.15.after_ref.disp_ref, s32[64,128]{1,0:T(8,128)S(1)} %pad_add_fusion.numbers_ref, f32[36,8,1024]{2,1,0:T(8,128)S(1)} %collective-permute-done.up_ref.refs_2_, f32[36,8,1024]{2,1,0:T(8,128)S(1)} %collective-permute-done.1.down_ref.refs_3_, ...), custom_call_target="tpu_custom_call" | custom-call | tf_op jit(solution)/shard_map/scatter_disp/pallas_call | solution.py:866
  50.0 7.1 %collective-permute-done.4.refs_7_.low_down_ref = f32[4,8,1024]{2,1,0:T(8,128)S(1)} collective-permute-done((f32[4,8,1024]{2,1,0:T(8,128)S(1)}, f32[4,8,1024]{2,1,0:T(8,128)S(1)}, u32[]{:S(2)}, u32[]{:S(2)}) %collective-permute-start.4) | collective-permute-done | bytes 131104 | tf_op jit(solution)/shard_map/ppermute | solution.py:859
  57.1 7.3 %fluid_wet.1 = (f32[4,32,1024]{2,1,0:T(8,128)S(1)}, f32[4,8,56,128]{3,2,1,0:T(8,128)S(1)}, f32[4,8,56,128]{3,2,1,0:T(8,128)S(1)}) custom-call(f32[32,32,1024]{2,1,0:T(8,128)} %refs_0_.5, f32[32,32,1024]{2,1,0:T(8,128)} %refs_1_.5, f32[36,8,1024]{2,1,0:T(8,128)S(1)} %collective-permute-done.up_ref.refs_2_, ...), custom_call_target="tpu_custom_call" | custom-call | flops 23592960 | bytes 5898240 | tf_op jit(solution)/shard_map/fluid_wet/pallas_call | solution.py:817
  65.4 3.2 %gather_press.1 = (f32[32,1,1280]{2,1,0:T(1,128)}, f32[7,40,1024]{2,1,0:T(8,128)S(1)}, f32[8,128]{1,0:T(8,128)S(1)}) custom-call(f32[4,32,1024]{2,1,0:T(8,128)S(1)} %get-tuple-element.30.wet_ref.refs_6_, s32[64,128]{1,0:T(8,128)S(1)} %pad_add_fusion.numbers_ref, f32[32,128]{1,0:T(8,128)S(1)} %gram_rows.1.refs_9_.gram_ref, ...), custom_call_target="tpu_custom_call" | custom-call | tf_op jit(solution)/shard_map/gather_press/pallas_call | solution.py:866
  69.2 1.3 collective-permute-start.6
  70.5 6.2 %all-to-all-start.1 = ((f32[32,1,1280]{2,1,0:T(1,128)}), f32[32,1,1280]{2,1,0:T(1,128)S(1)}, u32[]{:S(2)}, u32[]{:S(2)}) async-start(f32[32,1,1280]{2,1,0:T(1,128)} %get-tuple-element.36), calls=%async_computation.1 | async-start | bytes 327680 | tf_op jit(solution)/shard_map/all_to_all | solution.py:862
  76.7 21.3 %fluid_middle.1 = (f32[32,32,1024]{2,1,0:T(8,128)}, f32[4,8,56,128]{3,2,1,0:T(8,128)}, f32[4,8,56,128]{3,2,1,0:T(8,128)}, f32[8,128]{1,0:T(8,128)}) custom-call(f32[32,32,1024]{2,1,0:T(8,128)} %refs_0_.5, f32[32,32,1024]{2,1,0:T(8,128)} %refs_1_.5, f32[36,8,1024]{2,1,0:T(8,128)} %copy-done.1, f32[36,8,1024]{2,1,0:T(8,128)} %copy-done.2, ...), custom_call_target="tpu_custom_call" | custom-call | flops 62914560 | bytes 15728640 | tf_op jit(solution)/shard_map/fluid_middle/pallas_call | solution.py:817
  98.0 6.7 %all-to-all-done.1.recv_ref = f32[32,1,1280]{2,1,0:T(1,128)S(1)} async-done(((f32[32,1,1280]{2,1,0:T(1,128)}), f32[32,1,1280]{2,1,0:T(1,128)S(1)}, u32[]{:S(2)}, u32[]{:S(2)}) %all-to-all-start.1) | async-done | bytes 163872 | tf_op jit(solution)/shard_map/all_to_all | solution.py:862
  105.4 9.0 %shell.1 = (f32[64,512]{1,0:T(8,128)}, f32[32,1,256]{2,1,0:T(1,128)}) custom-call(f32[32,1,1280]{2,1,0:T(1,128)} %copy-done.15, s32[64,128]{1,0:T(8,128)} %copy-done.7, f32[4,64,512]{2,1,0:T(8,128)} %copy-done.4, f32[36,8,1024]{2,1,0:T(8,128)} %copy-done.1, f32[36,8,1024]{2,1,0:T(8,128)} %copy-done.2, f32[30,8,1024]{2,1,0:T(8,128)} %copy-done.5, ...), custom_call_target="tpu_custom_call" | custom-call | tf_op jit(solution)/shard_map/shell/pallas_call | solution.py:866
  114.4 2.5 %all-to-all-start.2 = ((f32[32,1,256]{2,1,0:T(1,128)}), f32[32,1,256]{2,1,0:T(1,128)S(1)}, u32[]{:S(2)}, u32[]{:S(2)}) async-start(f32[32,1,256]{2,1,0:T(1,128)} %get-tuple-element.38.refs_8_), calls=%async_computation.2 | async-start | bytes 65536 | tf_op jit(solution)/shard_map/all_to_all | solution.py:862
  116.9 1.0 copy-done.14
  117.9 7.9 %fluid_end.1 = (f32[32,32,1024]{2,1,0:T(8,128)}, f32[8,128]{1,0:T(8,128)}) custom-call(f32[32,32,1024]{2,1,0:T(8,128)} %refs_0_.5, f32[32,32,1024]{2,1,0:T(8,128)} %refs_1_.5, f32[36,8,1024]{2,1,0:T(8,128)} %copy-done.1, f32[36,8,1024]{2,1,0:T(8,128)} %copy-done.2, f32[4,8,56,128]{3,2,1,0:T(8,128)} %get-tuple-element.32.refs_4_, ...), custom_call_target="tpu_custom_call", output_to_operand_aliasing={{0}: (7, {})} | custom-call | flops 23592960 | bytes 5898240 | tf_op jit(solution)/shard_map/fluid_end/pallas_call | solution.py:817
  126.4 5.8 %solve.1 = f32[64,512]{1,0:T(8,128)} custom-call(f32[32,1,256]{2,1,0:T(1,128)} %copy-done.16, f32[64,512]{1,0:T(8,128)} %get-tuple-element.40.resp_ref, f32[4,64,512]{2,1,0:T(8,128)} %copy-done.4, f32[40,64,512]{2,1,0:T(8,128)} %w_ref.1, f32[8,128]{1,0:T(8,128)} %get-tuple-element.41.after_ref), custom_call_target="tpu_custom_call" | custom-call | tf_op jit(solution)/shard_map/solve/pallas_call | solution.py:866
  (45 shorter events, 4.3 us)
Async XLA Ops:
  1.4 64.0 %copy-start.7 = (s32[64,128]{1,0:T(8,128)}, s32[64,128]{1,0:T(8,128)S(1)}, u32[]{:S(2)}) copy-start(s32[64,128]{1,0:T(8,128)S(1)} %pad_add_fusion.numbers_ref) | copy-start | bytes 98308
  2.5 18.7 %copy-start.4 = (f32[4,64,512]{2,1,0:T(8,128)}, f32[4,64,512]{2,1,0:T(8,128)S(1)}, u32[]{:S(2)}) copy-start(f32[4,64,512]{2,1,0:T(8,128)S(1)} %pad_maximum_fusion.small_ref) | copy-start | bytes 1572868
  21.2 12.5 %collective-permute-start = (f32[36,8,1024]{2,1,0:T(8,128)S(1)}, f32[36,8,1024]{2,1,0:T(8,128)S(1)}, u32[]{:S(2)}, u32[]{:S(2)}) collective-permute-start(f32[36,8,1024]{2,1,0:T(8,128)S(1)} %get-tuple-element.22), channel_id=1, source_target_pairs={{1,0},{2,1},{3,2},{5,4},{6,5},{7,6},{9,8},{10,9},{11,10},{13,12},{... | collective-permute-start | bytes 3538952 | tf_op jit(solution)/shard_map/ppermute | solution.py:859
  22.5 11.3 %collective-permute-start.1 = (f32[36,8,1024]{2,1,0:T(8,128)S(1)}, f32[36,8,1024]{2,1,0:T(8,128)S(1)}, u32[]{:S(2)}, u32[]{:S(2)}) collective-permute-start(f32[36,8,1024]{2,1,0:T(8,128)S(1)} %get-tuple-element.23), channel_id=1, source_target_pairs={{0,1},{1,2},{2,3},{4,5},{5,6},{6,7},{8,9},{9,10},{10,11},{12,13},{... | collective-permute-start | bytes 3538952 | tf_op jit(solution)/shard_map/ppermute | solution.py:859
  25.6 31.4 %collective-permute-start.2 = (f32[30,8,1024]{2,1,0:T(8,128)S(1)}, f32[30,8,1024]{2,1,0:T(8,128)S(1)}, u32[]{:S(2)}, u32[]{:S(2)}) collective-permute-start(f32[30,8,1024]{2,1,0:T(8,128)S(1)} %get-tuple-element.24), channel_id=1, source_target_pairs={{0,4},{1,5},{2,6},{3,7},{4,8},{5,9},{6,10},{7,11},{8,12},{9,13},{1... | collective-permute-start | bytes 2949128 | tf_op jit(solution)/shard_map/ppermute | solution.py:859
  28.2 21.7 %collective-permute-start.3 = (f32[4,8,1024]{2,1,0:T(8,128)S(1)}, f32[4,8,1024]{2,1,0:T(8,128)S(1)}, u32[]{:S(2)}, u32[]{:S(2)}) collective-permute-start(f32[4,8,1024]{2,1,0:T(8,128)S(1)} %get-tuple-element.25), channel_id=1, source_target_pairs={{1,4},{2,5},{3,6},{5,8},{6,9},{7,10},{9,12},{10,13},{11,14},{13,16... | collective-permute-start | bytes 393224 | tf_op jit(solution)/shard_map/ppermute | solution.py:859
  28.9 28.1 %collective-permute-start.4 = (f32[4,8,1024]{2,1,0:T(8,128)S(1)}, f32[4,8,1024]{2,1,0:T(8,128)S(1)}, u32[]{:S(2)}, u32[]{:S(2)}) collective-permute-start(f32[4,8,1024]{2,1,0:T(8,128)S(1)} %get-tuple-element.26), channel_id=1, source_target_pairs={{0,5},{1,6},{2,7},{4,9},{5,10},{6,11},{8,13},{9,14},{10,15},{12,17... | collective-permute-start | bytes 393224 | tf_op jit(solution)/shard_map/ppermute | solution.py:859
  33.8 23.3 %copy-start.1 = (f32[36,8,1024]{2,1,0:T(8,128)}, f32[36,8,1024]{2,1,0:T(8,128)S(1)}, u32[]{:S(2)}) copy-start(f32[36,8,1024]{2,1,0:T(8,128)S(1)} %collective-permute-done.up_ref.refs_2_) | copy-start | bytes 3538948
  33.8 23.2 %copy-start.2 = (f32[36,8,1024]{2,1,0:T(8,128)}, f32[36,8,1024]{2,1,0:T(8,128)S(1)}, u32[]{:S(2)}) copy-start(f32[36,8,1024]{2,1,0:T(8,128)S(1)} %collective-permute-done.1.down_ref.refs_3_) | copy-start | bytes 3538948
  33.9 23.2 %collective-permute-start.5 = (f32[4,8,1024]{2,1,0:T(8,128)S(1)}, f32[4,8,1024]{2,1,0:T(8,128)S(1)}, u32[]{:S(2)}, u32[]{:S(2)}) collective-permute-start(f32[4,8,1024]{2,1,0:T(8,128)S(1)} %pad_maximum_fusion.1), channel_id=1, source_target_pairs={{4,0},{5,1},{6,2},{7,3},{8,4},{9,5},{10,6},{11,7},{12,8},{13,9},{1... | collective-permute-start | bytes 393224 | tf_op jit(solution)/shard_map/ppermute | solution.py:859
  35.3 2.5 %copy-start.3 = (f32[40,64,512]{2,1,0:T(8,128)S(1)}, f32[40,64,512]{2,1,0:T(8,128)}, u32[]{:S(2)}) copy-start(f32[40,64,512]{2,1,0:T(8,128)} %v_ref.3) | copy-start | bytes 15728644
  37.8 6.7 %copy-start = (f32[32,32,1024]{2,1,0:T(8,128)S(1)}, f32[32,32,1024]{2,1,0:T(8,128)}, u32[]{:S(2)}) copy-start(f32[32,32,1024]{2,1,0:T(8,128)} %refs_0_.5) | copy-start | bytes 12582916
  49.9 14.4 %copy-start.10 = (f32[4,8,1024]{2,1,0:T(8,128)}, f32[4,8,1024]{2,1,0:T(8,128)S(1)}, u32[]{:S(2)}) copy-start(f32[4,8,1024]{2,1,0:T(8,128)S(1)} %collective-permute-done.3.refs_6_.low_up_ref) | copy-start | bytes 393220
  57.0 7.4 %copy-start.11 = (f32[4,8,1024]{2,1,0:T(8,128)}, f32[4,8,1024]{2,1,0:T(8,128)S(1)}, u32[]{:S(2)}) copy-start(f32[4,8,1024]{2,1,0:T(8,128)S(1)} %collective-permute-done.4.refs_7_.low_down_ref) | copy-start | bytes 393220
  57.0 7.4 %copy-start.5 = (f32[30,8,1024]{2,1,0:T(8,128)}, f32[30,8,1024]{2,1,0:T(8,128)S(1)}, u32[]{:S(2)}) copy-start(f32[30,8,1024]{2,1,0:T(8,128)S(1)} %collective-permute-done.2.refs_5_.low_ref) | copy-start | bytes 2949124
  57.1 7.4 %copy-start.12 = (f32[4,8,1024]{2,1,0:T(8,128)}, f32[4,8,1024]{2,1,0:T(8,128)S(1)}, u32[]{:S(2)}) copy-start(f32[4,8,1024]{2,1,0:T(8,128)S(1)} %collective-permute-done.5.refs_8_.high_ref) | copy-start | bytes 393220
  64.4 0.9 copy-start.9
  65.4 3.2 %copy-start.6 = (f32[4,32,1024]{2,1,0:T(8,128)}, f32[4,32,1024]{2,1,0:T(8,128)S(1)}, u32[]{:S(2)}) copy-start(f32[4,32,1024]{2,1,0:T(8,128)S(1)} %get-tuple-element.30.wet_ref.refs_6_) | copy-start | bytes 1572868
  65.4 3.8 %copy-start.8 = (f32[4,8,56,128]{3,2,1,0:T(8,128)}, f32[4,8,56,128]{3,2,1,0:T(8,128)S(1)}, u32[]{:S(2)}) copy-start(f32[4,8,56,128]{3,2,1,0:T(8,128)S(1)} %get-tuple-element.28.refs_4_) | copy-start | bytes 2752516
  69.2 47.7 %collective-permute-start.6 = (f32[7,40,1024]{2,1,0:T(8,128)S(1)}, f32[7,40,1024]{2,1,0:T(8,128)S(1)}, u32[]{:S(2)}, u32[]{:S(2)}) collective-permute-start(f32[7,40,1024]{2,1,0:T(8,128)S(1)} %get-tuple-element.34), channel_id=1, source_target_pairs={{4,0},{5,1},{6,2},{7,3},{8,4},{9,5},{10,6},{11,7},{12,8},{13,9},{1... | collective-permute-start | bytes 3440648 | tf_op jit(solution)/shard_map/ppermute | solution.py:859
  70.5 34.2 %all-to-all-start.1 = ((f32[32,1,1280]{2,1,0:T(1,128)}), f32[32,1,1280]{2,1,0:T(1,128)S(1)}, u32[]{:S(2)}, u32[]{:S(2)}) async-start(f32[32,1,1280]{2,1,0:T(1,128)} %get-tuple-element.36), calls=%async_computation.1 | async-start | bytes 327680 | tf_op jit(solution)/shard_map/all_to_all | solution.py:862
  104.7 0.7 copy-start.15
  114.4 11.4 %all-to-all-start.2 = ((f32[32,1,256]{2,1,0:T(1,128)}), f32[32,1,256]{2,1,0:T(1,128)S(1)}, u32[]{:S(2)}, u32[]{:S(2)}) async-start(f32[32,1,256]{2,1,0:T(1,128)} %get-tuple-element.38.refs_8_), calls=%async_computation.2 | async-start | bytes 65536 | tf_op jit(solution)/shard_map/all_to_all | solution.py:862
  116.9 1.0 copy-start.14
  (2 other events, 1.2 us)

commit v10 on v9

--- a/solution.py
+++ b/solution.py
@@ -216,9 +216,7 @@
         )
 
 
-def gather_press(n_gx, n_gy, wet_ref, numbers_ref, gram_ref, forced_ref, out_ref, send_ref,
-                 token_ref, own_ref):
-    send_ref[...] = forced_ref[...]
+def gather_press(n_gx, n_gy, wet_ref, numbers_ref, gram_ref, out_ref, token_ref, own_ref):
     token_ref[...] = jnp.zeros((8, 128), F32)
     index_ref = numbers_ref.at[pl.ds(0, own_ref.shape[0])]
     planes, cy, cz = wet_ref.shape
@@ -632,7 +630,7 @@
     names += {"wet": ["forced", "low", "low_up", "low_down", "near", "gram"],
               "middle": ["state_a", "state_b", "wet", "press"],
               "end": ["state_a", "state_b", "high", "whole", "late"]}[kind]
-    names += {"wet": ["out", "next_a", "next_b"], "middle": ["out", "next_a", "next_b", "token"],
+    names += {"wet": ["out", "next_a", "next_b", "send"], "middle": ["out", "next_a", "next_b", "token"],
               "end": ["out", "token"]}[kind]
     names += ["a", "b", "kap", "coef", "stage", "done", "sems", "kap_sems", "out_sems", "more_sems"]
     r = dict(zip(names, refs))
@@ -782,7 +780,9 @@
     if kind != "end":
         outs.append(copy(a.at[pl.ds(planes - 4, 4)], r["next_a"]))
         outs.append(copy(b.at[pl.ds(planes - 5, 4)], r["next_b"]))
-    if kind != "wet":
+    if kind == "wet":
+        outs.append(copy(r["forced"], r["send"]))
+    else:
         r["token"][...] = jnp.zeros((8, 128), F32)
     loop(4, planes - 4, final)
     for made in outs:
@@ -800,8 +800,9 @@
         specs = vmem_specs(4) + any_specs(2)
         out_shape = [
             jax.ShapeDtypeStruct((x1 - x0, cy, cz), F32), *state,
+            jax.ShapeDtypeStruct((7, cy + 8, cz), F32),
         ]
-        out_specs = vmem_specs(1) + hbm_specs(2)
+        out_specs = vmem_specs(1) + hbm_specs(2) + any_specs(1)
     elif kind == "middle":
         specs = hbm_specs(2) + vmem_specs(1) + any_specs(1)
         out_shape = [field, *state, jax.ShapeDtypeStruct((8, 128), F32)]
@@ -920,12 +921,12 @@
         ],
         "scatter_disp", vmem_specs(4) + hbm_specs(2), disp, numbers, up, down, phi, kappa,
     )
-    wet, state_a, state_b = fluid_call(
+    wet, state_a, state_b, send = fluid_call(
         "wet", 0, wet_planes, phi, kappa, up, down, forced, low, low_up, low_down, near, gram
     )
-    press, send, token = call(
-        functools.partial(gather_press, n_gx, n_gy), [f32(peers, 1, (len(NEAR) + 1) * blk), f32(7, cy + 8, cz), f32(8, 128)],
-        [pltpu.VMEM((peers, blk), F32)], "gather_press", vmem_specs(4), wet, numbers, gram, forced,
+    press, token = call(
+        functools.partial(gather_press, n_gx, n_gy), [f32(peers, 1, (len(NEAR) + 1) * blk), f32(8, 128)],
+        [pltpu.VMEM((peers, blk), F32)], "gather_press", vmem_specs(3), wet, numbers, gram,
     )
     loads = exchange(press)
     high = shift(send, -1, 0)

time: 133 us -> 133 us (level)
  waiting for transfers between devices: 13.8 us -> 9.98 us
  Pallas kernels: 70.8 us -> 72.3 us
    all_to_all x2, waiting for transfers between devices: 6.71 us -> 2.91 us  [exchange(): return lax.all_to_all(value, axes, split_axis=0, concat_axis=0, tiled=True)]
    pallas_call x3, Pallas kernels: 36.5 us -> 38 us  [fluid_call(): pl.pallas_call(functools.partial(fluid, x0, x1, cx, cy, cz, kind), in_spe...]
  transfers between devices with their start and end apart: 9 -> 9, of which waited for: 2 -> 2; matrix products, arithmetic and copies ran while one was open for 0% -> 0% of each run, Pallas kernels for 38% -> 41%
where the time goes in v10:
time: 133 us; the launch traced here: 132 us
  Pallas kernels  72.3 us (54%)
  starting transfers between devices  24.6 us (18%)
  blocking collectives  14.4 us (11%)
  waiting for transfers between devices  9.98 us (8%)
  local copies, waits for them, and re-layouts  7.3 us (5%)
  other arithmetic  1.89 us (1%)
    pallas_call x3, Pallas kernels, fluid_call(): pl.pallas_call(functools.partial(fluid, x0, x1, cx, cy, cz, kind), in_spe...  38 us
    pallas_call x6, Pallas kernels, call(): pl.pallas_call(body, in_specs=specs, out_specs=vmem_specs(len(out_shape))...  31.3 us
    ppermute x7, starting transfers between devices, shift(): return lax.ppermute(value, axes, shifted_pairs(n_gx, n_gy, dx, dy))  15.5 us
    all_to_all x1, blocking collectives, exchange(): return lax.all_to_all(value, axes, split_axis=0, concat_axis=0, tiled=True)  14.4 us
    all_to_all x2, starting transfers between devices, exchange(): return lax.all_to_all(value, axes, split_axis=0, concat_axis=0, tiled=True)  9.14 us
    unnamed x34, local copies, waits for them, and re-layouts  7.29 us
    ppermute x7, waiting for transfers between devices, shift(): return lax.ppermute(value, axes, shifted_pairs(n_gx, n_gy, dx, dy))  7.08 us
    pallas_call x1, Pallas kernels, packed(): pl.pallas_call(pack, in_specs=hbm_specs(2) + any_specs(1) + vmem_specs(2)...  3.04 us
  transfers between devices with their start and end apart: 9, of which 2 were waited for; matrix products, arithmetic and copies ran while one was open for 0% of the time, Pallas kernels for 41%

profile of v10, /device:TPU:0, one launch (start us, length us, event | category | flops | bytes accessed | tf_op | source)
XLA Modules:
  0.0 131.7 jit_solution(12530788402446116881)
XLA Ops:
  1.4 1.1 pad_maximum_fusion.small_ref
  2.5 1.2 gather_disp.1
  3.7 14.4 %all_to_all.15.after_ref.disp_ref = f32[32,1,384]{2,1,0:T(1,128)S(1)} all-to-all(f32[32,1,384]{2,1,0:T(1,128)S(1)} %gather_disp.1), channel_id=1, replica_groups=mesh['gx'=8,'gy'=4] {'gx','gy'}, dimensions={0} | all-to-all | bytes 98304 | tf_op jit(solution)/shard_map/all_to_all | solution.py:863
  18.2 3.0 %pack.1 = (f32[36,8,1024]{2,1,0:T(8,128)S(1)}, f32[36,8,1024]{2,1,0:T(8,128)S(1)}, f32[30,8,1024]{2,1,0:T(8,128)S(1)}, f32[4,8,1024]{2,1,0:T(8,128)S(1)}, f32[4,...) custom-call(f32[32,32,1024]{2,1,0:T(8,128)} %refs_0_.5, f32[32,32,1024]{2,1,0:T(8,128)} %refs_1_.5, ...), custom_call_target="tpu_custom_call" | custom-call | tf_op jit(solution)/shard_map/pack/pallas_call | solution.py:585
  21.2 1.3 collective-permute-start
  22.5 3.1 %collective-permute-start.1 = (f32[36,8,1024]{2,1,0:T(8,128)S(1)}, f32[36,8,1024]{2,1,0:T(8,128)S(1)}, u32[]{:S(2)}, u32[]{:S(2)}) collective-permute-start(f32[36,8,1024]{2,1,0:T(8,128)S(1)} %get-tuple-element.23), channel_id=1, source_target_pairs={{0,1},{1,2},{2,3},{4,5},{5,6},{6,7},{8,9},{9,10},{10,11},{12,13},{... | collective-permute-start | bytes 3538952 | tf_op jit(solution)/shard_map/ppermute | solution.py:860
  25.6 2.5 %collective-permute-start.2 = (f32[30,8,1024]{2,1,0:T(8,128)S(1)}, f32[30,8,1024]{2,1,0:T(8,128)S(1)}, u32[]{:S(2)}, u32[]{:S(2)}) collective-permute-start(f32[30,8,1024]{2,1,0:T(8,128)S(1)} %get-tuple-element.24), channel_id=1, source_target_pairs={{0,4},{1,5},{2,6},{3,7},{4,8},{5,9},{6,10},{7,11},{8,12},{9,13},{1... | collective-permute-start | bytes 2949128 | tf_op jit(solution)/shard_map/ppermute | solution.py:860
  28.9 4.9 %collective-permute-start.4 = (f32[4,8,1024]{2,1,0:T(8,128)S(1)}, f32[4,8,1024]{2,1,0:T(8,128)S(1)}, u32[]{:S(2)}, u32[]{:S(2)}) collective-permute-start(f32[4,8,1024]{2,1,0:T(8,128)S(1)} %get-tuple-element.26), channel_id=1, source_target_pairs={{0,5},{1,6},{2,7},{4,9},{5,10},{6,11},{8,13},{9,14},{10,15},{12,17... | collective-permute-start | bytes 393224 | tf_op jit(solution)/shard_map/ppermute | solution.py:860
  33.9 1.5 %collective-permute-start.5 = (f32[4,8,1024]{2,1,0:T(8,128)S(1)}, f32[4,8,1024]{2,1,0:T(8,128)S(1)}, u32[]{:S(2)}, u32[]{:S(2)}) collective-permute-start(f32[4,8,1024]{2,1,0:T(8,128)S(1)} %pad_maximum_fusion.1), channel_id=1, source_target_pairs={{4,0},{5,1},{6,2},{7,3},{8,4},{9,5},{10,6},{11,7},{12,8},{13,9},{1... | collective-permute-start | bytes 393224 | tf_op jit(solution)/shard_map/ppermute | solution.py:860
  35.3 2.5 %copy-done.3 = f32[40,64,512]{2,1,0:T(8,128)S(1)} copy-done((f32[40,64,512]{2,1,0:T(8,128)S(1)}, f32[40,64,512]{2,1,0:T(8,128)}, u32[]{:S(2)}) %copy-start.3) | copy-done | bytes 5242904
  37.8 6.7 %gram_rows.1.refs_9_.gram_ref = f32[32,128]{1,0:T(8,128)S(1)} custom-call(f32[40,64,512]{2,1,0:T(8,128)S(1)} %copy-done.3), custom_call_target="tpu_custom_call" | custom-call | tf_op jit(solution)/shard_map/gram_rows/pallas_call | solution.py:867
  44.5 5.4 %scatter_disp.1.refs_4_ = f32[7,40,1024]{2,1,0:T(8,128)S(1)} custom-call(f32[32,1,384]{2,1,0:T(1,128)S(1)} %all_to_all.15.after_ref.disp_ref, s32[64,128]{1,0:T(8,128)S(1)} %pad_add_fusion.numbers_ref, f32[36,8,1024]{2,1,0:T(8,128)S(1)} %collective-permute-done.up_ref.refs_2_, f32[36,8,1024]{2,1,0:T(8,128)S(1)} %collective-permute-done.1.down_ref.refs_3_, ...), custom_call_target="tpu_custom_call" | custom-call | tf_op jit(solution)/shard_map/scatter_disp/pallas_call | solution.py:867
  50.0 7.1 %collective-permute-done.4.refs_7_.low_down_ref = f32[4,8,1024]{2,1,0:T(8,128)S(1)} collective-permute-done((f32[4,8,1024]{2,1,0:T(8,128)S(1)}, f32[4,8,1024]{2,1,0:T(8,128)S(1)}, u32[]{:S(2)}, u32[]{:S(2)}) %collective-permute-start.4) | collective-permute-done | bytes 131104 | tf_op jit(solution)/shard_map/ppermute | solution.py:860
  57.1 8.8 %fluid_wet.1 = (f32[4,32,1024]{2,1,0:T(8,128)S(1)}, f32[4,8,56,128]{3,2,1,0:T(8,128)S(1)}, f32[4,8,56,128]{3,2,1,0:T(8,128)S(1)}, f32[7,40,1024]{2,1,0:T(8,128)}) custom-call(f32[32,32,1024]{2,1,0:T(8,128)} %refs_0_.5, f32[32,32,1024]{2,1,0:T(8,128)} %refs_1_.5, f32[36,8,1024]{2,1,0:T(8,128)S(1)} %collective-permute-done.up_ref.refs_2_, ...), custom_call_target="tpu_custom_call" | custom-call | flops 23592960 | bytes 5898240 | tf_op jit(solution)/shard_map/fluid_wet/pallas_call | solution.py:818
  66.9 1.0 copy-done.9
  67.9 1.5 %collective-permute-start.6 = (f32[7,40,1024]{2,1,0:T(8,128)}, f32[7,40,1024]{2,1,0:T(8,128)S(1)}, u32[]{:S(2)}, u32[]{:S(2)}) collective-permute-start(f32[7,40,1024]{2,1,0:T(8,128)} %get-tuple-element.34), channel_id=1, source_target_pairs={{4,0},{5,1},{6,2},{7,3},{8,4},{9,5},{10,6},{11,7},{12,8},{13,9},{1... | collective-permute-start | bytes 3440648 | tf_op jit(solution)/shard_map/ppermute | solution.py:860
  69.4 3.2 %gather_press.1 = (f32[32,1,1280]{2,1,0:T(1,128)}, f32[8,128]{1,0:T(8,128)S(1)}) custom-call(f32[4,32,1024]{2,1,0:T(8,128)S(1)} %get-tuple-element.30.wet_ref.refs_6_, s32[64,128]{1,0:T(8,128)S(1)} %pad_add_fusion.numbers_ref, f32[32,128]{1,0:T(8,128)S(1)} %gram_rows.1.refs_9_.gram_ref), custom_call_target="tpu_custom_call" | custom-call | tf_op jit(solution)/shard_map/gather_press/pallas_call | solution.py:867
  73.2 6.2 %all-to-all-start.1 = ((f32[32,1,1280]{2,1,0:T(1,128)}), f32[32,1,1280]{2,1,0:T(1,128)S(1)}, u32[]{:S(2)}, u32[]{:S(2)}) async-start(f32[32,1,1280]{2,1,0:T(1,128)} %get-tuple-element.36), calls=%async_computation.1 | async-start | bytes 327680 | tf_op jit(solution)/shard_map/all_to_all | solution.py:863
  79.4 21.3 %fluid_middle.1 = (f32[32,32,1024]{2,1,0:T(8,128)}, f32[4,8,56,128]{3,2,1,0:T(8,128)}, f32[4,8,56,128]{3,2,1,0:T(8,128)}, f32[8,128]{1,0:T(8,128)}) custom-call(f32[32,32,1024]{2,1,0:T(8,128)} %refs_0_.5, f32[32,32,1024]{2,1,0:T(8,128)} %refs_1_.5, f32[36,8,1024]{2,1,0:T(8,128)} %copy-done.1, f32[36,8,1024]{2,1,0:T(8,128)} %copy-done.2, ...), custom_call_target="tpu_custom_call" | custom-call | flops 62914560 | bytes 15728640 | tf_op jit(solution)/shard_map/fluid_middle/pallas_call | solution.py:818
  100.7 2.9 %all-to-all-done.1.recv_ref = f32[32,1,1280]{2,1,0:T(1,128)S(1)} async-done(((f32[32,1,1280]{2,1,0:T(1,128)}), f32[32,1,1280]{2,1,0:T(1,128)S(1)}, u32[]{:S(2)}, u32[]{:S(2)}) %all-to-all-start.1) | async-done | bytes 163872 | tf_op jit(solution)/shard_map/all_to_all | solution.py:863
  104.3 9.0 %shell.1 = (f32[64,512]{1,0:T(8,128)}, f32[32,1,256]{2,1,0:T(1,128)}) custom-call(f32[32,1,1280]{2,1,0:T(1,128)} %copy-done.15, s32[64,128]{1,0:T(8,128)} %copy-done.7, f32[4,64,512]{2,1,0:T(8,128)} %copy-done.4, f32[36,8,1024]{2,1,0:T(8,128)} %copy-done.1, f32[36,8,1024]{2,1,0:T(8,128)} %copy-done.2, f32[30,8,1024]{2,1,0:T(8,128)} %copy-done.5, ...), custom_call_target="tpu_custom_call" | custom-call | tf_op jit(solution)/shard_map/shell/pallas_call | solution.py:867
  113.3 2.9 %all-to-all-start.2 = ((f32[32,1,256]{2,1,0:T(1,128)}), f32[32,1,256]{2,1,0:T(1,128)S(1)}, u32[]{:S(2)}, u32[]{:S(2)}) async-start(f32[32,1,256]{2,1,0:T(1,128)} %get-tuple-element.38.refs_8_), calls=%async_computation.2 | async-start | bytes 65536 | tf_op jit(solution)/shard_map/all_to_all | solution.py:863
  117.3 7.9 %fluid_end.1 = (f32[32,32,1024]{2,1,0:T(8,128)}, f32[8,128]{1,0:T(8,128)}) custom-call(f32[32,32,1024]{2,1,0:T(8,128)} %refs_0_.5, f32[32,32,1024]{2,1,0:T(8,128)} %refs_1_.5, f32[36,8,1024]{2,1,0:T(8,128)} %copy-done.1, f32[36,8,1024]{2,1,0:T(8,128)} %copy-done.2, f32[4,8,56,128]{3,2,1,0:T(8,128)} %get-tuple-element.32.refs_4_, ...), custom_call_target="tpu_custom_call", output_to_operand_aliasing={{0}: (7, {})} | custom-call | flops 23592960 | bytes 5898240 | tf_op jit(solution)/shard_map/fluid_end/pallas_call | solution.py:818
  125.8 5.8 %solve.1 = f32[64,512]{1,0:T(8,128)} custom-call(f32[32,1,256]{2,1,0:T(1,128)} %copy-done.16, f32[64,512]{1,0:T(8,128)} %get-tuple-element.40.resp_ref, f32[4,64,512]{2,1,0:T(8,128)} %copy-done.4, f32[40,64,512]{2,1,0:T(8,128)} %w_ref.1, f32[8,128]{1,0:T(8,128)} %get-tuple-element.41.after_ref), custom_call_target="tpu_custom_call" | custom-call | tf_op jit(solution)/shard_map/solve/pallas_call | solution.py:867
  (45 shorter events, 5.3 us)
Async XLA Ops:
  1.4 68.0 %copy-start.7 = (s32[64,128]{1,0:T(8,128)}, s32[64,128]{1,0:T(8,128)S(1)}, u32[]{:S(2)}) copy-start(s32[64,128]{1,0:T(8,128)S(1)} %pad_add_fusion.numbers_ref) | copy-start | bytes 98308
  2.5 18.7 %copy-start.4 = (f32[4,64,512]{2,1,0:T(8,128)}, f32[4,64,512]{2,1,0:T(8,128)S(1)}, u32[]{:S(2)}) copy-start(f32[4,64,512]{2,1,0:T(8,128)S(1)} %pad_maximum_fusion.small_ref) | copy-start | bytes 1572868
  21.2 12.5 %collective-permute-start = (f32[36,8,1024]{2,1,0:T(8,128)S(1)}, f32[36,8,1024]{2,1,0:T(8,128)S(1)}, u32[]{:S(2)}, u32[]{:S(2)}) collective-permute-start(f32[36,8,1024]{2,1,0:T(8,128)S(1)} %get-tuple-element.22), channel_id=1, source_target_pairs={{1,0},{2,1},{3,2},{5,4},{6,5},{7,6},{9,8},{10,9},{11,10},{13,12},{... | collective-permute-start | bytes 3538952 | tf_op jit(solution)/shard_map/ppermute | solution.py:860
  22.5 11.3 %collective-permute-start.1 = (f32[36,8,1024]{2,1,0:T(8,128)S(1)}, f32[36,8,1024]{2,1,0:T(8,128)S(1)}, u32[]{:S(2)}, u32[]{:S(2)}) collective-permute-start(f32[36,8,1024]{2,1,0:T(8,128)S(1)} %get-tuple-element.23), channel_id=1, source_target_pairs={{0,1},{1,2},{2,3},{4,5},{5,6},{6,7},{8,9},{9,10},{10,11},{12,13},{... | collective-permute-start | bytes 3538952 | tf_op jit(solution)/shard_map/ppermute | solution.py:860
  25.6 31.4 %collective-permute-start.2 = (f32[30,8,1024]{2,1,0:T(8,128)S(1)}, f32[30,8,1024]{2,1,0:T(8,128)S(1)}, u32[]{:S(2)}, u32[]{:S(2)}) collective-permute-start(f32[30,8,1024]{2,1,0:T(8,128)S(1)} %get-tuple-element.24), channel_id=1, source_target_pairs={{0,4},{1,5},{2,6},{3,7},{4,8},{5,9},{6,10},{7,11},{8,12},{9,13},{1... | collective-permute-start | bytes 2949128 | tf_op jit(solution)/shard_map/ppermute | solution.py:860
  28.2 21.7 %collective-permute-start.3 = (f32[4,8,1024]{2,1,0:T(8,128)S(1)}, f32[4,8,1024]{2,1,0:T(8,128)S(1)}, u32[]{:S(2)}, u32[]{:S(2)}) collective-permute-start(f32[4,8,1024]{2,1,0:T(8,128)S(1)} %get-tuple-element.25), channel_id=1, source_target_pairs={{1,4},{2,5},{3,6},{5,8},{6,9},{7,10},{9,12},{10,13},{11,14},{13,16... | collective-permute-start | bytes 393224 | tf_op jit(solution)/shard_map/ppermute | solution.py:860
  28.9 28.1 %collective-permute-start.4 = (f32[4,8,1024]{2,1,0:T(8,128)S(1)}, f32[4,8,1024]{2,1,0:T(8,128)S(1)}, u32[]{:S(2)}, u32[]{:S(2)}) collective-permute-start(f32[4,8,1024]{2,1,0:T(8,128)S(1)} %get-tuple-element.26), channel_id=1, source_target_pairs={{0,5},{1,6},{2,7},{4,9},{5,10},{6,11},{8,13},{9,14},{10,15},{12,17... | collective-permute-start | bytes 393224 | tf_op jit(solution)/shard_map/ppermute | solution.py:860
  33.8 23.3 %copy-start.1 = (f32[36,8,1024]{2,1,0:T(8,128)}, f32[36,8,1024]{2,1,0:T(8,128)S(1)}, u32[]{:S(2)}) copy-start(f32[36,8,1024]{2,1,0:T(8,128)S(1)} %collective-permute-done.up_ref.refs_2_) | copy-start | bytes 3538948
  33.8 10.7 %copy-start.2 = (f32[36,8,1024]{2,1,0:T(8,128)}, f32[36,8,1024]{2,1,0:T(8,128)S(1)}, u32[]{:S(2)}) copy-start(f32[36,8,1024]{2,1,0:T(8,128)S(1)} %collective-permute-done.1.down_ref.refs_3_) | copy-start | bytes 3538948
  33.9 23.2 %collective-permute-start.5 = (f32[4,8,1024]{2,1,0:T(8,128)S(1)}, f32[4,8,1024]{2,1,0:T(8,128)S(1)}, u32[]{:S(2)}, u32[]{:S(2)}) collective-permute-start(f32[4,8,1024]{2,1,0:T(8,128)S(1)} %pad_maximum_fusion.1), channel_id=1, source_target_pairs={{4,0},{5,1},{6,2},{7,3},{8,4},{9,5},{10,6},{11,7},{12,8},{13,9},{1... | collective-permute-start | bytes 393224 | tf_op jit(solution)/shard_map/ppermute | solution.py:860
  35.3 2.5 %copy-start.3 = (f32[40,64,512]{2,1,0:T(8,128)S(1)}, f32[40,64,512]{2,1,0:T(8,128)}, u32[]{:S(2)}) copy-start(f32[40,64,512]{2,1,0:T(8,128)} %v_ref.3) | copy-start | bytes 15728644
  37.8 6.7 %copy-start = (f32[32,32,1024]{2,1,0:T(8,128)S(1)}, f32[32,32,1024]{2,1,0:T(8,128)}, u32[]{:S(2)}) copy-start(f32[32,32,1024]{2,1,0:T(8,128)} %refs_0_.5) | copy-start | bytes 12582916
  49.9 15.9 %copy-start.10 = (f32[4,8,1024]{2,1,0:T(8,128)}, f32[4,8,1024]{2,1,0:T(8,128)S(1)}, u32[]{:S(2)}) copy-start(f32[4,8,1024]{2,1,0:T(8,128)S(1)} %collective-permute-done.3.refs_6_.low_up_ref) | copy-start | bytes 393220
  57.0 8.9 %copy-start.11 = (f32[4,8,1024]{2,1,0:T(8,128)}, f32[4,8,1024]{2,1,0:T(8,128)S(1)}, u32[]{:S(2)}) copy-start(f32[4,8,1024]{2,1,0:T(8,128)S(1)} %collective-permute-done.4.refs_7_.low_down_ref) | copy-start | bytes 393220
  57.0 8.9 %copy-start.5 = (f32[30,8,1024]{2,1,0:T(8,128)}, f32[30,8,1024]{2,1,0:T(8,128)S(1)}, u32[]{:S(2)}) copy-start(f32[30,8,1024]{2,1,0:T(8,128)S(1)} %collective-permute-done.2.refs_5_.low_ref) | copy-start | bytes 2949124
  57.0 8.9 %copy-start.12 = (f32[4,8,1024]{2,1,0:T(8,128)}, f32[4,8,1024]{2,1,0:T(8,128)S(1)}, u32[]{:S(2)}) copy-start(f32[4,8,1024]{2,1,0:T(8,128)S(1)} %collective-permute-done.5.refs_8_.high_ref) | copy-start | bytes 393220
  65.9 0.9 copy-start.8
  66.9 1.0 copy-start.9
  67.9 11.5 %copy-start.6 = (f32[4,32,1024]{2,1,0:T(8,128)}, f32[4,32,1024]{2,1,0:T(8,128)S(1)}, u32[]{:S(2)}) copy-start(f32[4,32,1024]{2,1,0:T(8,128)S(1)} %get-tuple-element.30.wet_ref.refs_6_) | copy-start | bytes 1572868
  67.9 48.4 %collective-permute-start.6 = (f32[7,40,1024]{2,1,0:T(8,128)}, f32[7,40,1024]{2,1,0:T(8,128)S(1)}, u32[]{:S(2)}, u32[]{:S(2)}) collective-permute-start(f32[7,40,1024]{2,1,0:T(8,128)} %get-tuple-element.34), channel_id=1, source_target_pairs={{4,0},{5,1},{6,2},{7,3},{8,4},{9,5},{10,6},{11,7},{12,8},{13,9},{1... | collective-permute-start | bytes 3440648 | tf_op jit(solution)/shard_map/ppermute | solution.py:860
  73.2 30.5 %all-to-all-start.1 = ((f32[32,1,1280]{2,1,0:T(1,128)}), f32[32,1,1280]{2,1,0:T(1,128)S(1)}, u32[]{:S(2)}, u32[]{:S(2)}) async-start(f32[32,1,1280]{2,1,0:T(1,128)} %get-tuple-element.36), calls=%async_computation.1 | async-start | bytes 327680 | tf_op jit(solution)/shard_map/all_to_all | solution.py:863
  103.6 0.7 copy-start.15
  113.3 11.8 %all-to-all-start.2 = ((f32[32,1,256]{2,1,0:T(1,128)}), f32[32,1,256]{2,1,0:T(1,128)S(1)}, u32[]{:S(2)}, u32[]{:S(2)}) async-start(f32[32,1,256]{2,1,0:T(1,128)} %get-tuple-element.38.refs_8_), calls=%async_computation.2 | async-start | bytes 65536 | tf_op jit(solution)/shard_map/all_to_all | solution.py:863
  116.3 1.0 copy-start.14
  (2 other events, 1.2 us)

commit v11 on v10

--- a/solution.py
+++ b/solution.py
@@ -669,6 +669,8 @@
     outs = []
     if kind == "middle":
         outs.append(copy(r["wet"], r["out"].at[pl.ds(0, x0)]))
+    if kind == "wet":
+        outs.append(copy(r["forced"], r["send"]))
     upper = lax.broadcasted_iota(jnp.int32, (8, cz), 0) < 4
 
     def set_kappa_edge(i, up, down):
@@ -780,9 +782,7 @@
     if kind != "end":
         outs.append(copy(a.at[pl.ds(planes - 4, 4)], r["next_a"]))
         outs.append(copy(b.at[pl.ds(planes - 5, 4)], r["next_b"]))
-    if kind == "wet":
-        outs.append(copy(r["forced"], r["send"]))
-    else:
+    if kind != "wet":
         r["token"][...] = jnp.zeros((8, 128), F32)
     loop(4, planes - 4, final)
     for made in outs:

time: 133 us -> 132 us (level)
  no operation moved by 1% of the time
where the time goes in v11:
time: 132 us
  Pallas kernels  72.3 us (55%)
  starting transfers between devices  24.6 us (19%)
  blocking collectives  14.4 us (11%)
  waiting for transfers between devices  9.99 us (8%)
  local copies, waits for them, and re-layouts  7.3 us (6%)
  other arithmetic  1.89 us (1%)
    pallas_call x3, Pallas kernels, fluid_call(): pl.pallas_call(functools.partial(fluid, x0, x1, cx, cy, cz, kind), in_spe...  38 us
    pallas_call x6, Pallas kernels, call(): pl.pallas_call(body, in_specs=specs, out_specs=vmem_specs(len(out_shape))...  31.3 us
    ppermute x7, starting transfers between devices, shift(): return lax.ppermute(value, axes, shifted_pairs(n_gx, n_gy, dx, dy))  15.5 us
    all_to_all x1, blocking collectives, exchange(): return lax.all_to_all(value, axes, split_axis=0, concat_axis=0, tiled=True)  14.4 us
    all_to_all x2, starting transfers between devices, exchange(): return lax.all_to_all(value, axes, split_axis=0, concat_axis=0, tiled=True)  9.14 us
    unnamed x34, local copies, waits for them, and re-layouts  7.29 us
    ppermute x7, waiting for transfers between devices, shift(): return lax.ppermute(value, axes, shifted_pairs(n_gx, n_gy, dx, dy))  7.08 us
    pallas_call x1, Pallas kernels, packed(): pl.pallas_call(pack, in_specs=hbm_specs(2) + any_specs(1) + vmem_specs(2)...  3.04 us
  transfers between devices with their start and end apart: 9, of which 2 were waited for; matrix products, arithmetic and copies ran while one was open for 0% of the time, Pallas kernels for 41%

profile of v11, /device:TPU:0, one launch (start us, length us, event | category | flops | bytes accessed | tf_op | source)
XLA Modules:
  0.0 131.7 jit_solution(11555227655749673390)
XLA Ops:
  1.4 1.1 pad_maximum_fusion.small_ref
  2.5 1.2 gather_disp.1
  3.7 14.4 %all_to_all.15.after_ref.disp_ref = f32[32,1,384]{2,1,0:T(1,128)S(1)} all-to-all(f32[32,1,384]{2,1,0:T(1,128)S(1)} %gather_disp.1), channel_id=1, replica_groups=mesh['gx'=8,'gy'=4] {'gx','gy'}, dimensions={0} | all-to-all | bytes 98304 | tf_op jit(solution)/shard_map/all_to_all | solution.py:863
  18.2 3.0 %pack.1 = (f32[36,8,1024]{2,1,0:T(8,128)S(1)}, f32[36,8,1024]{2,1,0:T(8,128)S(1)}, f32[30,8,1024]{2,1,0:T(8,128)S(1)}, f32[4,8,1024]{2,1,0:T(8,128)S(1)}, f32[4,...) custom-call(f32[32,32,1024]{2,1,0:T(8,128)} %refs_0_.5, f32[32,32,1024]{2,1,0:T(8,128)} %refs_1_.5, ...), custom_call_target="tpu_custom_call" | custom-call | tf_op jit(solution)/shard_map/pack/pallas_call | solution.py:585
  21.2 1.3 collective-permute-start
  22.5 3.1 %collective-permute-start.1 = (f32[36,8,1024]{2,1,0:T(8,128)S(1)}, f32[36,8,1024]{2,1,0:T(8,128)S(1)}, u32[]{:S(2)}, u32[]{:S(2)}) collective-permute-start(f32[36,8,1024]{2,1,0:T(8,128)S(1)} %get-tuple-element.23), channel_id=1, source_target_pairs={{0,1},{1,2},{2,3},{4,5},{5,6},{6,7},{8,9},{9,10},{10,11},{12,13},{... | collective-permute-start | bytes 3538952 | tf_op jit(solution)/shard_map/ppermute | solution.py:860
  25.6 2.5 %collective-permute-start.2 = (f32[30,8,1024]{2,1,0:T(8,128)S(1)}, f32[30,8,1024]{2,1,0:T(8,128)S(1)}, u32[]{:S(2)}, u32[]{:S(2)}) collective-permute-start(f32[30,8,1024]{2,1,0:T(8,128)S(1)} %get-tuple-element.24), channel_id=1, source_target_pairs={{0,4},{1,5},{2,6},{3,7},{4,8},{5,9},{6,10},{7,11},{8,12},{9,13},{1... | collective-permute-start | bytes 2949128 | tf_op jit(solution)/shard_map/ppermute | solution.py:860
  28.9 4.9 %collective-permute-start.4 = (f32[4,8,1024]{2,1,0:T(8,128)S(1)}, f32[4,8,1024]{2,1,0:T(8,128)S(1)}, u32[]{:S(2)}, u32[]{:S(2)}) collective-permute-start(f32[4,8,1024]{2,1,0:T(8,128)S(1)} %get-tuple-element.26), channel_id=1, source_target_pairs={{0,5},{1,6},{2,7},{4,9},{5,10},{6,11},{8,13},{9,14},{10,15},{12,17... | collective-permute-start | bytes 393224 | tf_op jit(solution)/shard_map/ppermute | solution.py:860
  33.9 1.5 %collective-permute-start.5 = (f32[4,8,1024]{2,1,0:T(8,128)S(1)}, f32[4,8,1024]{2,1,0:T(8,128)S(1)}, u32[]{:S(2)}, u32[]{:S(2)}) collective-permute-start(f32[4,8,1024]{2,1,0:T(8,128)S(1)} %pad_maximum_fusion.1), channel_id=1, source_target_pairs={{4,0},{5,1},{6,2},{7,3},{8,4},{9,5},{10,6},{11,7},{12,8},{13,9},{1... | collective-permute-start | bytes 393224 | tf_op jit(solution)/shard_map/ppermute | solution.py:860
  35.3 2.5 %copy-done.3 = f32[40,64,512]{2,1,0:T(8,128)S(1)} copy-done((f32[40,64,512]{2,1,0:T(8,128)S(1)}, f32[40,64,512]{2,1,0:T(8,128)}, u32[]{:S(2)}) %copy-start.3) | copy-done | bytes 5242904
  37.8 6.7 %gram_rows.1.refs_9_.gram_ref = f32[32,128]{1,0:T(8,128)S(1)} custom-call(f32[40,64,512]{2,1,0:T(8,128)S(1)} %copy-done.3), custom_call_target="tpu_custom_call" | custom-call | tf_op jit(solution)/shard_map/gram_rows/pallas_call | solution.py:867
  44.5 5.4 %scatter_disp.1.refs_4_ = f32[7,40,1024]{2,1,0:T(8,128)S(1)} custom-call(f32[32,1,384]{2,1,0:T(1,128)S(1)} %all_to_all.15.after_ref.disp_ref, s32[64,128]{1,0:T(8,128)S(1)} %pad_add_fusion.numbers_ref, f32[36,8,1024]{2,1,0:T(8,128)S(1)} %collective-permute-done.up_ref.refs_2_, f32[36,8,1024]{2,1,0:T(8,128)S(1)} %collective-permute-done.1.down_ref.refs_3_, ...), custom_call_target="tpu_custom_call" | custom-call | tf_op jit(solution)/shard_map/scatter_disp/pallas_call | solution.py:867
  50.0 7.1 %collective-permute-done.4.refs_7_.low_down_ref = f32[4,8,1024]{2,1,0:T(8,128)S(1)} collective-permute-done((f32[4,8,1024]{2,1,0:T(8,128)S(1)}, f32[4,8,1024]{2,1,0:T(8,128)S(1)}, u32[]{:S(2)}, u32[]{:S(2)}) %collective-permute-start.4) | collective-permute-done | bytes 131104 | tf_op jit(solution)/shard_map/ppermute | solution.py:860
  57.1 8.8 %fluid_wet.1 = (f32[4,32,1024]{2,1,0:T(8,128)S(1)}, f32[4,8,56,128]{3,2,1,0:T(8,128)S(1)}, f32[4,8,56,128]{3,2,1,0:T(8,128)S(1)}, f32[7,40,1024]{2,1,0:T(8,128)}) custom-call(f32[32,32,1024]{2,1,0:T(8,128)} %refs_0_.5, f32[32,32,1024]{2,1,0:T(8,128)} %refs_1_.5, f32[36,8,1024]{2,1,0:T(8,128)S(1)} %collective-permute-done.up_ref.refs_2_, ...), custom_call_target="tpu_custom_call" | custom-call | flops 23592960 | bytes 5898240 | tf_op jit(solution)/shard_map/fluid_wet/pallas_call | solution.py:818
  66.8 1.0 copy-done.9
  67.8 1.5 %collective-permute-start.6 = (f32[7,40,1024]{2,1,0:T(8,128)}, f32[7,40,1024]{2,1,0:T(8,128)S(1)}, u32[]{:S(2)}, u32[]{:S(2)}) collective-permute-start(f32[7,40,1024]{2,1,0:T(8,128)} %get-tuple-element.34), channel_id=1, source_target_pairs={{4,0},{5,1},{6,2},{7,3},{8,4},{9,5},{10,6},{11,7},{12,8},{13,9},{1... | collective-permute-start | bytes 3440648 | tf_op jit(solution)/shard_map/ppermute | solution.py:860
  69.4 3.2 %gather_press.1 = (f32[32,1,1280]{2,1,0:T(1,128)}, f32[8,128]{1,0:T(8,128)S(1)}) custom-call(f32[4,32,1024]{2,1,0:T(8,128)S(1)} %get-tuple-element.30.wet_ref.refs_6_, s32[64,128]{1,0:T(8,128)S(1)} %pad_add_fusion.numbers_ref, f32[32,128]{1,0:T(8,128)S(1)} %gram_rows.1.refs_9_.gram_ref), custom_call_target="tpu_custom_call" | custom-call | tf_op jit(solution)/shard_map/gather_press/pallas_call | solution.py:867
  73.1 6.2 %all-to-all-start.1 = ((f32[32,1,1280]{2,1,0:T(1,128)}), f32[32,1,1280]{2,1,0:T(1,128)S(1)}, u32[]{:S(2)}, u32[]{:S(2)}) async-start(f32[32,1,1280]{2,1,0:T(1,128)} %get-tuple-element.36), calls=%async_computation.1 | async-start | bytes 327680 | tf_op jit(solution)/shard_map/all_to_all | solution.py:863
  79.3 21.3 %fluid_middle.1 = (f32[32,32,1024]{2,1,0:T(8,128)}, f32[4,8,56,128]{3,2,1,0:T(8,128)}, f32[4,8,56,128]{3,2,1,0:T(8,128)}, f32[8,128]{1,0:T(8,128)}) custom-call(f32[32,32,1024]{2,1,0:T(8,128)} %refs_0_.5, f32[32,32,1024]{2,1,0:T(8,128)} %refs_1_.5, f32[36,8,1024]{2,1,0:T(8,128)} %copy-done.1, f32[36,8,1024]{2,1,0:T(8,128)} %copy-done.2, ...), custom_call_target="tpu_custom_call" | custom-call | flops 62914560 | bytes 15728640 | tf_op jit(solution)/shard_map/fluid_middle/pallas_call | solution.py:818
  100.7 2.9 %all-to-all-done.1.recv_ref = f32[32,1,1280]{2,1,0:T(1,128)S(1)} async-done(((f32[32,1,1280]{2,1,0:T(1,128)}), f32[32,1,1280]{2,1,0:T(1,128)S(1)}, u32[]{:S(2)}, u32[]{:S(2)}) %all-to-all-start.1) | async-done | bytes 163872 | tf_op jit(solution)/shard_map/all_to_all | solution.py:863
  104.3 9.0 %shell.1 = (f32[64,512]{1,0:T(8,128)}, f32[32,1,256]{2,1,0:T(1,128)}) custom-call(f32[32,1,1280]{2,1,0:T(1,128)} %copy-done.15, s32[64,128]{1,0:T(8,128)} %copy-done.7, f32[4,64,512]{2,1,0:T(8,128)} %copy-done.4, f32[36,8,1024]{2,1,0:T(8,128)} %copy-done.1, f32[36,8,1024]{2,1,0:T(8,128)} %copy-done.2, f32[30,8,1024]{2,1,0:T(8,128)} %copy-done.5, ...), custom_call_target="tpu_custom_call" | custom-call | tf_op jit(solution)/shard_map/shell/pallas_call | solution.py:867
  113.3 2.9 %all-to-all-start.2 = ((f32[32,1,256]{2,1,0:T(1,128)}), f32[32,1,256]{2,1,0:T(1,128)S(1)}, u32[]{:S(2)}, u32[]{:S(2)}) async-start(f32[32,1,256]{2,1,0:T(1,128)} %get-tuple-element.38.refs_8_), calls=%async_computation.2 | async-start | bytes 65536 | tf_op jit(solution)/shard_map/all_to_all | solution.py:863
  117.3 7.9 %fluid_end.1 = (f32[32,32,1024]{2,1,0:T(8,128)}, f32[8,128]{1,0:T(8,128)}) custom-call(f32[32,32,1024]{2,1,0:T(8,128)} %refs_0_.5, f32[32,32,1024]{2,1,0:T(8,128)} %refs_1_.5, f32[36,8,1024]{2,1,0:T(8,128)} %copy-done.1, f32[36,8,1024]{2,1,0:T(8,128)} %copy-done.2, f32[4,8,56,128]{3,2,1,0:T(8,128)} %get-tuple-element.32.refs_4_, ...), custom_call_target="tpu_custom_call", output_to_operand_aliasing={{0}: (7, {})} | custom-call | flops 23592960 | bytes 5898240 | tf_op jit(solution)/shard_map/fluid_end/pallas_call | solution.py:818
  125.7 5.8 %solve.1 = f32[64,512]{1,0:T(8,128)} custom-call(f32[32,1,256]{2,1,0:T(1,128)} %copy-done.16, f32[64,512]{1,0:T(8,128)} %get-tuple-element.40.resp_ref, f32[4,64,512]{2,1,0:T(8,128)} %copy-done.4, f32[40,64,512]{2,1,0:T(8,128)} %w_ref.1, f32[8,128]{1,0:T(8,128)} %get-tuple-element.41.after_ref), custom_call_target="tpu_custom_call" | custom-call | tf_op jit(solution)/shard_map/solve/pallas_call | solution.py:867
  (45 shorter events, 5.3 us)
Async XLA Ops:
  1.4 68.0 %copy-start.7 = (s32[64,128]{1,0:T(8,128)}, s32[64,128]{1,0:T(8,128)S(1)}, u32[]{:S(2)}) copy-start(s32[64,128]{1,0:T(8,128)S(1)} %pad_add_fusion.numbers_ref) | copy-start | bytes 98308
  2.5 18.7 %copy-start.4 = (f32[4,64,512]{2,1,0:T(8,128)}, f32[4,64,512]{2,1,0:T(8,128)S(1)}, u32[]{:S(2)}) copy-start(f32[4,64,512]{2,1,0:T(8,128)S(1)} %pad_maximum_fusion.small_ref) | copy-start | bytes 1572868
  21.2 12.5 %collective-permute-start = (f32[36,8,1024]{2,1,0:T(8,128)S(1)}, f32[36,8,1024]{2,1,0:T(8,128)S(1)}, u32[]{:S(2)}, u32[]{:S(2)}) collective-permute-start(f32[36,8,1024]{2,1,0:T(8,128)S(1)} %get-tuple-element.22), channel_id=1, source_target_pairs={{1,0},{2,1},{3,2},{5,4},{6,5},{7,6},{9,8},{10,9},{11,10},{13,12},{... | collective-permute-start | bytes 3538952 | tf_op jit(solution)/shard_map/ppermute | solution.py:860
  22.5 11.3 %collective-permute-start.1 = (f32[36,8,1024]{2,1,0:T(8,128)S(1)}, f32[36,8,1024]{2,1,0:T(8,128)S(1)}, u32[]{:S(2)}, u32[]{:S(2)}) collective-permute-start(f32[36,8,1024]{2,1,0:T(8,128)S(1)} %get-tuple-element.23), channel_id=1, source_target_pairs={{0,1},{1,2},{2,3},{4,5},{5,6},{6,7},{8,9},{9,10},{10,11},{12,13},{... | collective-permute-start | bytes 3538952 | tf_op jit(solution)/shard_map/ppermute | solution.py:860
  25.6 31.4 %collective-permute-start.2 = (f32[30,8,1024]{2,1,0:T(8,128)S(1)}, f32[30,8,1024]{2,1,0:T(8,128)S(1)}, u32[]{:S(2)}, u32[]{:S(2)}) collective-permute-start(f32[30,8,1024]{2,1,0:T(8,128)S(1)} %get-tuple-element.24), channel_id=1, source_target_pairs={{0,4},{1,5},{2,6},{3,7},{4,8},{5,9},{6,10},{7,11},{8,12},{9,13},{1... | collective-permute-start | bytes 2949128 | tf_op jit(solution)/shard_map/ppermute | solution.py:860
  28.2 21.7 %collective-permute-start.3 = (f32[4,8,1024]{2,1,0:T(8,128)S(1)}, f32[4,8,1024]{2,1,0:T(8,128)S(1)}, u32[]{:S(2)}, u32[]{:S(2)}) collective-permute-start(f32[4,8,1024]{2,1,0:T(8,128)S(1)} %get-tuple-element.25), channel_id=1, source_target_pairs={{1,4},{2,5},{3,6},{5,8},{6,9},{7,10},{9,12},{10,13},{11,14},{13,16... | collective-permute-start | bytes 393224 | tf_op jit(solution)/shard_map/ppermute | solution.py:860
  28.9 28.1 %collective-permute-start.4 = (f32[4,8,1024]{2,1,0:T(8,128)S(1)}, f32[4,8,1024]{2,1,0:T(8,128)S(1)}, u32[]{:S(2)}, u32[]{:S(2)}) collective-permute-start(f32[4,8,1024]{2,1,0:T(8,128)S(1)} %get-tuple-element.26), channel_id=1, source_target_pairs={{0,5},{1,6},{2,7},{4,9},{5,10},{6,11},{8,13},{9,14},{10,15},{12,17... | collective-permute-start | bytes 393224 | tf_op jit(solution)/shard_map/ppermute | solution.py:860
  33.8 23.3 %copy-start.1 = (f32[36,8,1024]{2,1,0:T(8,128)}, f32[36,8,1024]{2,1,0:T(8,128)S(1)}, u32[]{:S(2)}) copy-start(f32[36,8,1024]{2,1,0:T(8,128)S(1)} %collective-permute-done.up_ref.refs_2_) | copy-start | bytes 3538948
  33.8 10.7 %copy-start.2 = (f32[36,8,1024]{2,1,0:T(8,128)}, f32[36,8,1024]{2,1,0:T(8,128)S(1)}, u32[]{:S(2)}) copy-start(f32[36,8,1024]{2,1,0:T(8,128)S(1)} %collective-permute-done.1.down_ref.refs_3_) | copy-start | bytes 3538948
  33.9 23.2 %collective-permute-start.5 = (f32[4,8,1024]{2,1,0:T(8,128)S(1)}, f32[4,8,1024]{2,1,0:T(8,128)S(1)}, u32[]{:S(2)}, u32[]{:S(2)}) collective-permute-start(f32[4,8,1024]{2,1,0:T(8,128)S(1)} %pad_maximum_fusion.1), channel_id=1, source_target_pairs={{4,0},{5,1},{6,2},{7,3},{8,4},{9,5},{10,6},{11,7},{12,8},{13,9},{1... | collective-permute-start | bytes 393224 | tf_op jit(solution)/shard_map/ppermute | solution.py:860
  35.3 2.5 %copy-start.3 = (f32[40,64,512]{2,1,0:T(8,128)S(1)}, f32[40,64,512]{2,1,0:T(8,128)}, u32[]{:S(2)}) copy-start(f32[40,64,512]{2,1,0:T(8,128)} %v_ref.3) | copy-start | bytes 15728644
  37.8 6.7 %copy-start = (f32[32,32,1024]{2,1,0:T(8,128)S(1)}, f32[32,32,1024]{2,1,0:T(8,128)}, u32[]{:S(2)}) copy-start(f32[32,32,1024]{2,1,0:T(8,128)} %refs_0_.5) | copy-start | bytes 12582916
  49.9 15.9 %copy-start.10 = (f32[4,8,1024]{2,1,0:T(8,128)}, f32[4,8,1024]{2,1,0:T(8,128)S(1)}, u32[]{:S(2)}) copy-start(f32[4,8,1024]{2,1,0:T(8,128)S(1)} %collective-permute-done.3.refs_6_.low_up_ref) | copy-start | bytes 393220
  57.0 8.9 %copy-start.11 = (f32[4,8,1024]{2,1,0:T(8,128)}, f32[4,8,1024]{2,1,0:T(8,128)S(1)}, u32[]{:S(2)}) copy-start(f32[4,8,1024]{2,1,0:T(8,128)S(1)} %collective-permute-done.4.refs_7_.low_down_ref) | copy-start | bytes 393220
  57.0 8.9 %copy-start.5 = (f32[30,8,1024]{2,1,0:T(8,128)}, f32[30,8,1024]{2,1,0:T(8,128)S(1)}, u32[]{:S(2)}) copy-start(f32[30,8,1024]{2,1,0:T(8,128)S(1)} %collective-permute-done.2.refs_5_.low_ref) | copy-start | bytes 2949124
  57.0 8.9 %copy-start.12 = (f32[4,8,1024]{2,1,0:T(8,128)}, f32[4,8,1024]{2,1,0:T(8,128)S(1)}, u32[]{:S(2)}) copy-start(f32[4,8,1024]{2,1,0:T(8,128)S(1)} %collective-permute-done.5.refs_8_.high_ref) | copy-start | bytes 393220
  65.9 0.9 copy-start.8
  66.8 1.0 copy-start.9
  67.8 11.5 %copy-start.6 = (f32[4,32,1024]{2,1,0:T(8,128)}, f32[4,32,1024]{2,1,0:T(8,128)S(1)}, u32[]{:S(2)}) copy-start(f32[4,32,1024]{2,1,0:T(8,128)S(1)} %get-tuple-element.30.wet_ref.refs_6_) | copy-start | bytes 1572868
  67.8 48.4 %collective-permute-start.6 = (f32[7,40,1024]{2,1,0:T(8,128)}, f32[7,40,1024]{2,1,0:T(8,128)S(1)}, u32[]{:S(2)}, u32[]{:S(2)}) collective-permute-start(f32[7,40,1024]{2,1,0:T(8,128)} %get-tuple-element.34), channel_id=1, source_target_pairs={{4,0},{5,1},{6,2},{7,3},{8,4},{9,5},{10,6},{11,7},{12,8},{13,9},{1... | collective-permute-start | bytes 3440648 | tf_op jit(solution)/shard_map/ppermute | solution.py:860
  73.1 30.5 %all-to-all-start.1 = ((f32[32,1,1280]{2,1,0:T(1,128)}), f32[32,1,1280]{2,1,0:T(1,128)S(1)}, u32[]{:S(2)}, u32[]{:S(2)}) async-start(f32[32,1,1280]{2,1,0:T(1,128)} %get-tuple-element.36), calls=%async_computation.1 | async-start | bytes 327680 | tf_op jit(solution)/shard_map/all_to_all | solution.py:863
  103.6 0.7 copy-start.15
  113.3 11.8 %all-to-all-start.2 = ((f32[32,1,256]{2,1,0:T(1,128)}), f32[32,1,256]{2,1,0:T(1,128)S(1)}, u32[]{:S(2)}, u32[]{:S(2)}) async-start(f32[32,1,256]{2,1,0:T(1,128)} %get-tuple-element.38.refs_8_), calls=%async_computation.2 | async-start | bytes 65536 | tf_op jit(solution)/shard_map/all_to_all | solution.py:863
  116.3 1.0 copy-start.14
  (2 other events, 1.2 us)
